TPU v7x, 32 devices: a whole 2x2x4 slice. The times are simulated.
32 devices in a mesh: tm: 4 (over y, core), sx: 4 (over z), sy: 2 (over x).
Axes of the slice: x: 2, y: 2, z: 4, core: 2. Of those that a mesh axis runs over, the one named last changes fastest.
Arguments:
- snapshots: bfloat16 [1536, 4, 4096], P('tm', None, ('sx', 'sy')), may hold values from -12 to 12, as said below
- weights: float32 [4096], P(('sx', 'sy')), may hold values from 0.2 to 18, as said below
- block_order: int32 [4], replicated, may hold values from 0 to 3, each once
- owner: int32 [8, 4], P(('sx', 'sy')), may hold values from 0 to 3, as said below
- offsets: int32 [11], replicated, may hold values from 0 to 1280, as said below
Outputs:
- modes: bfloat16 [2, 128, 11, 4, 4096], P(None, None, None, 'tm', ('sx', 'sy'))
- gram: float32 [2, 128, 11, 11], P(None, ('sx', 'sy'))
Inputs may be any that keep to these rules, and one draw needn't show every extreme that they name: snapshots: noisy records with a few time signals in common across points. Positive weights. `block_order`: a permutation of the time blocks. `owner`: each row a permutation of the slots. Strictly increasing; offsets[0] = 0 and offsets[10] = 1280.
All inputs are finite; a program needn't handle non-finite values.
Results may differ from a plain program's by a relative error of at most 0.012.
Values may be sent and summed in bfloat16 or wider, within the bound.
No kernel may reach another device: no remote copies, remote signals or barrier semaphores. Data moves between devices by JAX's collectives and lax.ppermute only.
A program may use at most 64 MiB of HBM per device.

v0:
```python
import functools
import math

import jax
import jax.numpy as jnp
import numpy as np
from jax import lax
from jax.experimental import pallas as pl
from jax.experimental.pallas import tpu as pltpu
from jax.sharding import PartitionSpec as P

NFFT = 256
ROOT_STEPS = 5
NFREQ = 128
NBLK = 11
LANE = 128
SUB = 8
HALF_ROWS = NBLK * SUB
GROUPS = NFREQ // SUB
PAIRS = (NBLK + 1) // 2
PAIR_ROWS = 24
PACKED = PAIRS * PAIR_ROWS
STACK = 4
BF16 = jnp.bfloat16
F32 = jnp.float32


def fourier_tables():
    n = np.arange(NFFT)
    k = np.arange(NFREQ)
    angles = 2.0 * np.pi * ((k[:, None] * n[None, :]) % NFFT) / NFFT
    scaled = (0.5 - 0.5 * np.cos(2.0 * np.pi * n / NFFT)) / math.sqrt(0.375 * NFFT)
    table = np.concatenate([np.cos(angles) * scaled, -np.sin(angles) * scaled], axis=0)
    high = table.astype(jnp.bfloat16)
    low = (table - high.astype(np.float64)).astype(jnp.bfloat16)
    return np.stack([high, low])


def packed_rows():
    rows = {}
    for pair in range(PAIRS):
        row = pair * PAIR_ROWS
        for a in sorted({pair, NBLK - 1 - pair}):
            for e in range(a, NBLK):
                rows[0, a, e] = row
                row += 1
            for e in range(a + 1, NBLK):
                rows[1, a, e] = row
                row += 1
    return rows


def pick_table():
    pick = np.zeros((NBLK, PAIR_ROWS, 2 * LANE), np.float32)
    for (part, a, e), row in packed_rows().items():
        start = part * LANE + e * SUB
        pick[a, row % PAIR_ROWS, start : start + SUB] = 1.0
    return pick.astype(jnp.bfloat16)


def spread_table():
    spread = np.zeros((STACK, 2, LANE, 2 * HALF_ROWS), np.float32)
    for m in range(STACK):
        for b in range(NBLK):
            real = m * 32 + b
            imag = m * 32 + 16 + b
            first = slice(b * SUB, b * SUB + SUB)
            second = slice(HALF_ROWS + b * SUB, HALF_ROWS + b * SUB + SUB)
            spread[m, 0, real, first] = 1.0
            spread[m, 0, imag, second] = 1.0
            spread[m, 1, imag, first] = -1.0
            spread[m, 1, real, second] = 1.0
    return spread.reshape(STACK * 2, LANE, 2 * HALF_ROWS).astype(jnp.bfloat16)


def split(x):
    high = x.astype(BF16)
    return high, (x - high.astype(F32)).astype(BF16)


def dot(a, b):
    return jnp.dot(a, b, preferred_element_type=F32)


def dot_nt(a, b):
    return lax.dot_general(a, b, (((1,), (1,)), ((), ())), preferred_element_type=F32)


def spec(shape):
    return pl.BlockSpec(shape, lambda *_: (0,) * len(shape))


SMEM = pl.BlockSpec(memory_space=pltpu.SMEM)


def pack_kernel(owner_ref, x_ref, *out_refs):
    steps, lanes, width = x_ref.shape
    me = lax.axis_index("tm")
    rows = 2 * LANE // lanes
    out_row = lax.broadcasted_iota(jnp.int32, (2 * LANE, 2 * LANE), 0)
    in_row = lax.broadcasted_iota(jnp.int32, (2 * LANE, 2 * LANE), 1)
    want = jnp.zeros_like(out_row)
    for d in range(lanes):
        slot = me ^ d
        source = jnp.int32(0)
        for lane in range(lanes):
            source = source + jnp.where(owner_ref[0, lane] == slot, lane, 0)
        want = jnp.where(out_row // rows == d, source, want)
    pick = jnp.where(in_row == (out_row % rows) * lanes + want, 1.0, 0.0).astype(BF16)
    x = x_ref[...].reshape(steps * lanes, width)
    for i in range(steps // rows):
        y = dot(pick, x[i * 2 * LANE : (i + 1) * 2 * LANE]).astype(BF16)
        for d in range(lanes):
            out_refs[d][i * rows : (i + 1) * rows, :] = y[d * rows : (d + 1) * rows]


def pack(owner, snapshots, chunk):
    steps, lanes, _ = snapshots.shape
    return pl.pallas_call(
        pack_kernel,
        grid=(1,),
        out_shape=[jax.ShapeDtypeStruct((steps, LANE), BF16)] * lanes,
        in_specs=[SMEM, pl.BlockSpec((steps, lanes, LANE), lambda i: (0, 0, chunk))],
        out_specs=[spec((steps, LANE))] * lanes,
        compiler_params=pltpu.CompilerParams(vmem_limit_bytes=16 * 2**20),
    )(owner, snapshots)


def gram_kernel(lanes, scale, first, last, *refs):
    order_ref, offsets_ref, w_ref, f_ref, pick_ref = refs[:5]
    pieces = refs[5 : 5 + lanes]
    rest = refs[5 + lanes :]
    if not first:
        before_ref, *rest = rest
    s_ref, packed_ref, record, masked = rest
    steps = pieces[0].shape[0]
    me = lax.axis_index("tm")
    for d in range(lanes):
        start = pl.multiple_of(order_ref[me ^ d] * steps, steps)
        record[pl.ds(start, steps), :] = pieces[d][...].astype(F32)
    for b in range(0, NBLK, 2):
        pair = range(b, min(b + 2, NBLK))
        x = [record[pl.ds(offsets_ref[i], NFFT), :].astype(BF16) for i in pair]
        x = jnp.concatenate(x, axis=1) if len(x) > 1 else x[0]
        y = dot(f_ref[0], x) + dot(f_ref[1], x)
        for at, i in enumerate(pair):
            cols = slice(at * LANE, (at + 1) * LANE)
            s_ref[i] = y[:NFREQ, cols]
            s_ref[NBLK + i] = y[NFREQ:, cols]
    w = w_ref[...]
    row = lax.broadcasted_iota(jnp.int32, (HALF_ROWS, LANE), 0)
    col = lax.broadcasted_iota(jnp.int32, (HALF_ROWS, LANE), 1)
    same = row % SUB == col % SUB
    pad = jnp.zeros((LANE - HALF_ROWS, LANE), F32)
    for g in range(GROUPS):
        at = slice(g * SUB, (g + 1) * SUB)
        s = s_ref[:, at, :].reshape(2 * HALF_ROWS, LANE)
        other = jnp.concatenate([s[:HALF_ROWS], pad, s[HALF_ROWS:], pad], axis=0)
        full = dot_nt((s * w).astype(BF16), other.astype(BF16))
        real = full[:HALF_ROWS, :LANE] + full[HALF_ROWS:, LANE:]
        imag = full[:HALF_ROWS, LANE:] - full[HALF_ROWS:, :LANE]
        masked[:, at, :LANE] = jnp.where(same, real, 0.0).reshape(NBLK, SUB, LANE)
        masked[:, at, LANE:] = jnp.where(same, imag, 0.0).reshape(NBLK, SUB, LANE)
    for pair in range(PAIRS):
        total = jnp.zeros((PAIR_ROWS, NFREQ), F32)
        for a in sorted({pair, NBLK - 1 - pair}):
            high, low = split(masked[a])
            total = total + dot_nt(pick_ref[a], high) + dot_nt(pick_ref[a], low)
        rows = slice(pair * PAIR_ROWS, (pair + 1) * PAIR_ROWS)
        total = total * scale
        if not first:
            total = total + before_ref[rows, :]
        packed_ref[rows, :] = total.astype(packed_ref.dtype)


def gram_part(order, offsets, weights, tables, pieces, before, chunk, scale, last):
    lanes = len(pieces)
    steps = pieces[0].shape[0]
    first = before is None
    args = [order, offsets, weights, *tables, *pieces] + ([] if first else [before])
    in_specs = [SMEM, SMEM, pl.BlockSpec((1, LANE), lambda i: (0, chunk))]
    in_specs += [spec(a.shape) for a in args[3:]]
    return pl.pallas_call(
        functools.partial(gram_kernel, lanes, scale, first, last),
        grid=(1,),
        out_shape=[
            jax.ShapeDtypeStruct((2 * NBLK, NFREQ, LANE), F32),
            jax.ShapeDtypeStruct((PACKED, NFREQ), BF16 if last else F32),
        ],
        in_specs=in_specs,
        out_specs=[spec((2 * NBLK, NFREQ, LANE)), spec((PACKED, NFREQ))],
        scratch_shapes=[
            pltpu.VMEM((lanes * steps, LANE), F32),
            pltpu.VMEM((NBLK, NFREQ, 2 * LANE), F32),
        ],
        compiler_params=pltpu.CompilerParams(vmem_limit_bytes=24 * 2**20),
        cost_estimate=pl.CostEstimate(
            flops=2 * 10**9, bytes_accessed=6 * 10**6, transcendentals=0
        ),
    )(*args)


def product(x, y, store):
    xr, xi = x
    yr, yi = y

    @pl.loop(0, NBLK)
    def _(a):
        real = jnp.zeros((16, NFREQ), F32)
        imag = jnp.zeros((16, NFREQ), F32)
        for b in range(NBLK):
            pr = xr[a, pl.ds(b, 1), :]
            pi = xi[a, pl.ds(b, 1), :]
            qr = yr[b]
            qi = yi[b]
            real = real + (pr * qr - pi * qi)
            imag = imag + (pr * qi + pi * qr)
        store(a, real, imag)


def inverse_root(y, z, p, y2, z2):
    sub = lax.broadcasted_iota(jnp.int32, (16, NFREQ), 0)

    def to(dst):
        def store(a, real, imag):
            dst[0][a] = real
            dst[1][a] = imag

        return store

    def factor(a, real, imag):
        p[0][a] = jnp.where(sub == a, 1.5, 0.0) - 0.5 * real
        p[1][a] = -0.5 * imag

    for step in range(ROOT_STEPS):
        if step == 0:
            for a in range(NBLK):
                real = jnp.where(sub == a, 1.5, 0.0) - 0.5 * y[0][a]
                imag = -0.5 * y[1][a]
                p[0][a] = real
                p[1][a] = imag
                z2[0][a] = real
                z2[1][a] = imag
        else:
            product(z, y, factor)
            product(p, z, to(z2))
        if step < ROOT_STEPS - 1:
            product(y, p, to(y2))
        y, y2 = y2, y
        z, z2 = z2, z
    return z


def mode_kernel(parts, chunks, share, *refs):
    part_refs = refs[:parts]
    spread_ref = refs[parts]
    s_refs = refs[parts + 1 : parts + 1 + chunks]
    out_ref, gram_ref, packed, v, *mats = refs[parts + 1 + chunks :]
    step = pl.program_id(0)

    @pl.when(step == 0)
    def _():
        terms = [r[...].astype(F32) for r in part_refs]
        while len(terms) > 1:
            terms = [a + b for a, b in zip(terms[::2], terms[1::2])]
        packed[...] = terms[0]
        y, z, p, y2, z2 = [(mats[2 * i], mats[2 * i + 1]) for i in range(5)]
        for ref in mats:
            ref[:, 8:, :] = jnp.zeros((NBLK, 8, NFREQ), F32)
        trace = jnp.zeros((1, NFREQ), F32)
        rows = packed_rows()
        for a in range(NBLK):
            line = packed[pl.ds(rows[0, a, a], 1), :]
            trace = trace + line
            y[0][a, pl.ds(a, 1), :] = line
            y[1][a, pl.ds(a, 1), :] = jnp.zeros_like(line)
            for e in range(a + 1, NBLK):
                line = packed[pl.ds(rows[0, a, e], 1), :]
                y[0][a, pl.ds(e, 1), :] = line
                y[0][e, pl.ds(a, 1), :] = line
                line = packed[pl.ds(rows[1, a, e], 1), :]
                y[1][a, pl.ds(e, 1), :] = line
                y[1][e, pl.ds(a, 1), :] = -line
        trace = 2.0 * trace
        at = lax.axis_index("sx") * lax.axis_size("sy") + lax.axis_index("sy")
        back = (NFREQ - at * share) % NFREQ
        for c in range(2):
            for a in range(NBLK):
                gram_ref[c, a] = pltpu.roll(y[c][a], back, 1)
                y[c][a] = y[c][a] / trace
        root = inverse_root(y, z, p, y2, z2)
        norm = 1.0 / jnp.sqrt(trace)
        row = lax.broadcasted_iota(jnp.int32, (NFREQ, 2 * HALF_ROWS), 0)
        col = lax.broadcasted_iota(jnp.int32, (NFREQ, 2 * HALF_ROWS), 1)
        same = row % SUB == col % SUB
        for m0 in range(0, NBLK, STACK):
            modes = range(m0, min(m0 + STACK, NBLK))
            stack = [root[c][m] * norm for m in modes for c in range(2)]
            stack += [jnp.zeros((16, NFREQ), F32)] * (2 * STACK - len(stack))
            high, low = split(jnp.concatenate(stack, axis=0).T)
            for m in modes:
                for c in range(2):
                    table = spread_ref[(m - m0) * 2 + c]
                    wide = dot(high, table) + dot(low, table)
                    v[c * NBLK + m] = jnp.where(same, wide, 0.0)

    fields = []
    for h in range(2):
        start = pl.multiple_of(step * 16 + h * SUB, SUB)
        v_high, v_low = split(v[:, pl.ds(start, SUB), :].reshape(2 * HALF_ROWS, 2 * HALF_ROWS))
        s = jnp.concatenate(
            [r[:, h * SUB : (h + 1) * SUB, :].reshape(2 * HALF_ROWS, LANE) for r in s_refs], axis=1
        )
        s_high, s_low = split(s)
        field = dot(v_high, s_high) + (dot(v_high, s_low) + dot(v_low, s_high))
        fields.append(field.reshape(2 * NBLK, SUB, chunks * LANE))
    both = jnp.concatenate(fields, axis=1).astype(BF16)
    out_ref[...] = both.reshape(2, NBLK, 16, chunks * LANE)


def mode_fields(parts, spread, spectra, share):
    chunks = len(spectra)
    width = chunks * LANE
    mat = pltpu.VMEM((NBLK, 16, NFREQ), F32)
    return pl.pallas_call(
        functools.partial(mode_kernel, len(parts), chunks, share),
        grid=(NFREQ // 16,),
        out_shape=[
            jax.ShapeDtypeStruct((2, NBLK, NFREQ, width), BF16),
            jax.ShapeDtypeStruct((2, NBLK, 16, NFREQ), F32),
        ],
        in_specs=[spec(a.shape) for a in parts]
        + [spec(spread.shape)]
        + [pl.BlockSpec((2 * NBLK, 16, LANE), lambda i: (0, i, 0))] * chunks,
        out_specs=[
            pl.BlockSpec((2, NBLK, 16, width), lambda i: (0, 0, i, 0)),
            spec((2, NBLK, 16, NFREQ)),
        ],
        scratch_shapes=[
            pltpu.VMEM((PACKED, NFREQ), F32),
            pltpu.VMEM((2 * NBLK, NFREQ, 2 * HALF_ROWS), F32),
        ]
        + [mat] * 10,
        compiler_params=pltpu.CompilerParams(vmem_limit_bytes=24 * 2**20),
    )(*parts, spread, *spectra)


def swap(x, axes, mask, size):
    return lax.ppermute(x, axes, [(i, i ^ mask) for i in range(size)])


def body(snapshots, weights, block_order, owner, offsets):
    lanes = lax.axis_size("tm")
    sx = lax.axis_size("sx")
    sy = lax.axis_size("sy")
    groups = sx * sy
    chunks = snapshots.shape[2] // LANE
    scale = 1.0 / (lanes * groups * weights.shape[0])
    tables = (jnp.asarray(fourier_tables()), jnp.asarray(pick_table()))
    weights = weights.reshape(1, -1)

    arrived = []
    for q in range(chunks):
        packed = pack(owner, snapshots, q)
        pieces = [packed[0]]
        for d in range(1, lanes):
            pieces.append(swap(packed[d], "tm", d, lanes))
        arrived.append(pieces)

    spectra = []
    total = None
    for q in range(chunks):
        s, total = gram_part(
            block_order, offsets, weights, tables, arrived[q], total, q, scale, q == chunks - 1
        )
        spectra.append(s)

    bits = [b * groups for b in powers(lanes)] + powers(groups)
    size = lanes * groups
    terms = [total]
    for at in range(0, len(bits), 2):
        here = bits[at : at + 2]
        masks = [0, here[0]] + ([here[1], here[0] + here[1]] if len(here) > 1 else [])
        own = total_of(terms)
        terms = [own] + [swap(own, ("tm", "sx", "sy"), m, size) for m in masks[1:]]

    share = NFREQ // groups
    modes, gram = mode_fields(terms, jnp.asarray(spread_table()), spectra, share)
    modes = jnp.transpose(modes, (0, 2, 1, 3))[:, :, :, None, :]
    gram = jnp.transpose(gram[:, :, :NBLK, :share], (0, 3, 1, 2))
    return modes, gram


def powers(size):
    return [1 << i for i in range(size.bit_length() - 1)]


def total_of(terms):
    if len(terms) == 1:
        return terms[0]
    terms = [t.astype(F32) for t in terms]
    while len(terms) > 1:
        terms = [a + b for a, b in zip(terms[::2], terms[1::2])]
    return terms[0].astype(BF16)


def solution(mesh):
    placed = (P("tm", None, ("sx", "sy")), P(("sx", "sy")), P(), P(("sx", "sy"), None), P())
    return jax.shard_map(
        body,
        mesh=mesh,
        in_specs=placed,
        out_specs=(P(None, None, None, "tm", ("sx", "sy")), P(None, ("sx", "sy"), None, None)),
        check_vma=False,
    )
```

profile of v0, /device:TPU:0, one launch (start us, length us, event | category | flops | bytes accessed | tf_op | source)
XLA Modules:
  0.0 58.7 jit_solution(7335323380302954414)
XLA Ops:
  0.6 0.0 copy-start
  0.6 1.4 %copy-done = bf16[384,4,512]{2,1,0:T(4,128)(2,1)S(1)} copy-done((bf16[384,4,512]{2,1,0:T(4,128)(2,1)S(1)}, bf16[384,4,512]{2,1,0:T(4,128)(2,1)}, u32[]{:S(2)}) %copy-start) | copy-done | bytes 1572888
  2.0 0.0 copy-start.2
  2.0 0.7 %copy-done.2 = s32[1,4]{1,0:T(1,128)S(1)} copy-done((s32[1,4]{1,0:T(1,128)S(1)}, s32[1,4]{1,0:T(1,128)}, u32[]{:S(2)}) %copy-start.2) | copy-done | bytes 40
  2.7 0.9 %shard_map.98 = (bf16[384,128]{1,0:T(8,128)(2,1)S(1)}, bf16[384,128]{1,0:T(8,128)(2,1)S(1)}, bf16[384,128]{1,0:T(8,128)(2,1)S(1)}, bf16[384,128]{1,0:T(8,128)(2,1)S(1)}) custom-call(s32[1,4]{1,0:T(1,128)S(1)} %copy-done.2, bf16[384,4,512]{2,1,0:T(4,128)(2,1)S(1)} %copy-done), custom_call_target="tpu_custom_call" | custom-call | tf_op jit(solution)/shard_map/pallas_call | solution.py:119
  3.6 0.5 collective-permute-start.9
  4.2 2.6 %collective-permute-start.10 = (bf16[384,128]{1,0:T(8,128)(2,1)S(1)}, bf16[384,128]{1,0:T(8,128)(2,1)S(1)}, u32[]{:S(2)}, u32[]{:S(2)}) collective-permute-start(bf16[384,128]{1,0:T(8,128)(2,1)S(1)} %get-tuple-element.42), channel_id=1, source_target_pairs={{0,16},{8,24},{16,0},{24,8},{1,17},{9,25},{17,1},{25,9},{2,18},{10... | collective-permute-start | bytes 294920 | tf_op jit(solution)/shard_map/ppermute | solution.py:349
  6.7 0.1 collective-permute-start.11
  6.8 0.9 %shard_map.96 = (bf16[384,128]{1,0:T(8,128)(2,1)S(1)}, bf16[384,128]{1,0:T(8,128)(2,1)S(1)}, bf16[384,128]{1,0:T(8,128)(2,1)S(1)}, bf16[384,128]{1,0:T(8,128)(2,1)S(1)}) custom-call(s32[1,4]{1,0:T(1,128)S(1)} %copy-done.2, bf16[384,4,512]{2,1,0:T(4,128)(2,1)S(1)} %copy-done), custom_call_target="tpu_custom_call" | custom-call | tf_op jit(solution)/shard_map/pallas_call | solution.py:119
  7.8 0.2 collective-permute-start.3
  8.0 0.0 copy-start.3
  8.0 0.0 copy-start.4
  8.0 0.0 copy-start.5
  8.0 0.0 copy-start.6
  8.0 0.0 copy-start.7
  8.0 2.0 %collective-permute-start.4 = (bf16[384,128]{1,0:T(8,128)(2,1)S(1)}, bf16[384,128]{1,0:T(8,128)(2,1)S(1)}, u32[]{:S(2)}, u32[]{:S(2)}) collective-permute-start(bf16[384,128]{1,0:T(8,128)(2,1)S(1)} %get-tuple-element.34), channel_id=1, source_target_pairs={{0,16},{8,24},{16,0},{24,8},{1,17},{9,25},{17,1},{25,9},{2,18},{10... | collective-permute-start | bytes 294920 | tf_op jit(solution)/shard_map/ppermute | solution.py:349
  10.0 0.9 %shard_map.95 = (bf16[384,128]{1,0:T(8,128)(2,1)S(1)}, bf16[384,128]{1,0:T(8,128)(2,1)S(1)}, bf16[384,128]{1,0:T(8,128)(2,1)S(1)}, bf16[384,128]{1,0:T(8,128)(2,1)S(1)}) custom-call(s32[1,4]{1,0:T(1,128)S(1)} %copy-done.2, bf16[384,4,512]{2,1,0:T(4,128)(2,1)S(1)} %copy-done), custom_call_target="tpu_custom_call" | custom-call | tf_op jit(solution)/shard_map/pallas_call | solution.py:119
  10.9 0.9 %shard_map.97 = (bf16[384,128]{1,0:T(8,128)(2,1)S(1)}, bf16[384,128]{1,0:T(8,128)(2,1)S(1)}, bf16[384,128]{1,0:T(8,128)(2,1)S(1)}, bf16[384,128]{1,0:T(8,128)(2,1)S(1)}) custom-call(s32[1,4]{1,0:T(1,128)S(1)} %copy-done.2, bf16[384,4,512]{2,1,0:T(4,128)(2,1)S(1)} %copy-done), custom_call_target="tpu_custom_call" | custom-call | tf_op jit(solution)/shard_map/pallas_call | solution.py:119
  11.9 0.0 collective-permute-done.9.refs_6_
  11.9 0.1 collective-permute-start.6
  11.9 0.0 collective-permute-done.10.refs_7_
  12.0 0.4 collective-permute-start.7
  12.3 0.0 collective-permute-done.11.refs_8_
  12.3 1.5 %collective-permute-start.8 = (bf16[384,128]{1,0:T(8,128)(2,1)S(1)}, bf16[384,128]{1,0:T(8,128)(2,1)S(1)}, u32[]{:S(2)}, u32[]{:S(2)}) collective-permute-start(bf16[384,128]{1,0:T(8,128)(2,1)S(1)} %get-tuple-element.39), channel_id=1, source_target_pairs={{0,24},{8,16},{16,8},{24,0},{1,25},{9,17},{17,9},{25,1},{2,26},{10... | collective-permute-start | bytes 294920 | tf_op jit(solution)/shard_map/ppermute | solution.py:349
  13.9 0.0 copy-done.3
  13.9 0.0 copy-done.4
  13.9 0.0 copy-done.5
  13.9 0.0 copy-done.6
  13.9 0.0 copy-done.7
  13.9 2.6 %shard_map.99 = (f32[22,128,128]{2,1,0:T(8,128)S(1)}, f32[144,128]{1,0:T(8,128)S(1)}) custom-call(s32[4]{0:T(128)S(1)} %copy-done.4, s32[11]{0:T(128)S(1)} %copy-done.5, f32[1,512]{1,0:T(1,128)S(1)} %bitcast.8, bf16[2,256,256]{2,1,0:T(8,128)(2,1)S(1)} %copy-done.6, bf16[11,24,256]{2,1,0:T(8,128)(2,1)S(1)} %copy-done.7, ...), custom_call_target="tpu_custom_call" | custom-call | flops 2000000000 | bytes 6000000 | tf_op jit(solution)/shard_map/pallas_call | solution.py:183
  16.5 0.0 collective-permute-done.6.refs_6_
  16.5 0.3 collective-permute-start.5
  16.8 0.8 %collective-permute-done.7.refs_7_ = bf16[384,128]{1,0:T(8,128)(2,1)S(1)} collective-permute-done((bf16[384,128]{1,0:T(8,128)(2,1)S(1)}, bf16[384,128]{1,0:T(8,128)(2,1)S(1)}, u32[]{:S(2)}, u32[]{:S(2)}) %collective-permute-start.7) | collective-permute-done | bytes 98336 | tf_op jit(solution)/shard_map/ppermute | solution.py:349
  17.6 0.0 collective-permute-start
  17.6 1.2 %collective-permute-done.8.refs_8_ = bf16[384,128]{1,0:T(8,128)(2,1)S(1)} collective-permute-done((bf16[384,128]{1,0:T(8,128)(2,1)S(1)}, bf16[384,128]{1,0:T(8,128)(2,1)S(1)}, u32[]{:S(2)}, u32[]{:S(2)}) %collective-permute-start.8) | collective-permute-done | bytes 98336 | tf_op jit(solution)/shard_map/ppermute | solution.py:349
  18.8 1.1 %collective-permute-start.1 = (bf16[384,128]{1,0:T(8,128)(2,1)S(1)}, bf16[384,128]{1,0:T(8,128)(2,1)S(1)}, u32[]{:S(2)}, u32[]{:S(2)}) collective-permute-start(bf16[384,128]{1,0:T(8,128)(2,1)S(1)} %get-tuple-element.30), channel_id=1, source_target_pairs={{0,16},{8,24},{16,0},{24,8},{1,17},{9,25},{17,1},{25,9},{2,18},{10... | collective-permute-start | bytes 294920 | tf_op jit(solution)/shard_map/ppermute | solution.py:349
  19.9 2.6 %shard_map.100 = (f32[22,128,128]{2,1,0:T(8,128)S(1)}, f32[144,128]{1,0:T(8,128)S(1)}) custom-call(s32[4]{0:T(128)S(1)} %copy-done.4, s32[11]{0:T(128)S(1)} %copy-done.5, f32[1,512]{1,0:T(1,128)S(1)} %bitcast.9, bf16[2,256,256]{2,1,0:T(8,128)(2,1)S(1)} %copy-done.6, bf16[11,24,256]{2,1,0:T(8,128)(2,1)S(1)} %copy-done.7, ...), custom_call_target="tpu_custom_call" | custom-call | flops 2000000000 | bytes 6000000 | tf_op jit(solution)/shard_map/pallas_call | solution.py:183
  22.5 0.0 collective-permute-done.3.refs_6_
  22.5 0.7 %collective-permute-start.2 = (bf16[384,128]{1,0:T(8,128)(2,1)S(1)}, bf16[384,128]{1,0:T(8,128)(2,1)S(1)}, u32[]{:S(2)}, u32[]{:S(2)}) collective-permute-start(bf16[384,128]{1,0:T(8,128)(2,1)S(1)} %get-tuple-element.31), channel_id=1, source_target_pairs={{0,24},{8,16},{16,8},{24,0},{1,25},{9,17},{17,9},{25,1},{2,26},{10... | collective-permute-start | bytes 294920 | tf_op jit(solution)/shard_map/ppermute | solution.py:349
  23.2 0.0 collective-permute-done.4.refs_7_
  23.2 0.0 collective-permute-done.5.refs_8_
  23.2 2.6 %shard_map.101 = (f32[22,128,128]{2,1,0:T(8,128)S(1)}, f32[144,128]{1,0:T(8,128)S(1)}) custom-call(s32[4]{0:T(128)S(1)} %copy-done.4, s32[11]{0:T(128)S(1)} %copy-done.5, f32[1,512]{1,0:T(1,128)S(1)} %bitcast.10, bf16[2,256,256]{2,1,0:T(8,128)(2,1)S(1)} %copy-done.6, bf16[11,24,256]{2,1,0:T(8,128)(2,1)S(1)} %copy-done.7, ...), custom_call_target="tpu_custom_call" | custom-call | flops 2000000000 | bytes 6000000 | tf_op jit(solution)/shard_map/pallas_call | solution.py:183
  25.8 0.0 collective-permute-done.refs_6_
  25.8 0.0 collective-permute-done.1.refs_7_
  25.8 0.9 %collective-permute-done.2.refs_8_ = bf16[384,128]{1,0:T(8,128)(2,1)S(1)} collective-permute-done((bf16[384,128]{1,0:T(8,128)(2,1)S(1)}, bf16[384,128]{1,0:T(8,128)(2,1)S(1)}, u32[]{:S(2)}, u32[]{:S(2)}) %collective-permute-start.2) | collective-permute-done | bytes 98336 | tf_op jit(solution)/shard_map/ppermute | solution.py:349
  26.8 0.0 copy-start.1
  26.8 2.6 %shard_map.102 = (f32[22,128,128]{2,1,0:T(8,128)S(1)}, bf16[144,128]{1,0:T(8,128)(2,1)S(1)}) custom-call(s32[4]{0:T(128)S(1)} %copy-done.4, s32[11]{0:T(128)S(1)} %copy-done.5, f32[1,512]{1,0:T(1,128)S(1)} %bitcast.11, bf16[2,256,256]{2,1,0:T(8,128)(2,1)S(1)} %copy-done.6, bf16[11,24,256]{2,1,0:T(8,128)(2,1)S(1)} %copy-done.7, ...), custom_call_target="tpu_custom_call" | custom-call | flops 2000000000 | bytes 6000000 | tf_op jit(solution)/shard_map/pallas_call | solution.py:183
  29.4 1.4 %collective-permute-start.14 = (bf16[144,128]{1,0:T(8,128)(2,1)S(1)}, bf16[144,128]{1,0:T(8,128)(2,1)S(1)}, u32[]{:S(2)}, u32[]{:S(2)}) collective-permute-start(bf16[144,128]{1,0:T(8,128)(2,1)S(1)} %get-tuple-element.47), channel_id=1, source_target_pairs={{0,24},{1,25},{2,26},{3,27},{4,28},{5,29},{6,30},{7,31},{8,16},{9,... | collective-permute-start | bytes 110600 | tf_op jit(solution)/shard_map/ppermute | solution.py:349
  30.7 1.0 %collective-permute-start.13 = (bf16[144,128]{1,0:T(8,128)(2,1)S(1)}, bf16[144,128]{1,0:T(8,128)(2,1)S(1)}, u32[]{:S(2)}, u32[]{:S(2)}) collective-permute-start(bf16[144,128]{1,0:T(8,128)(2,1)S(1)} %get-tuple-element.47), channel_id=1, source_target_pairs={{0,16},{1,17},{2,18},{3,19},{4,20},{5,21},{6,22},{7,23},{8,24},{9,... | collective-permute-start | bytes 110600 | tf_op jit(solution)/shard_map/ppermute | solution.py:349
  31.8 0.0 collective-permute-start.12
  31.8 1.0 %collective-permute-done.14 = bf16[144,128]{1,0:T(8,128)(2,1)S(1)} collective-permute-done((bf16[144,128]{1,0:T(8,128)(2,1)S(1)}, bf16[144,128]{1,0:T(8,128)(2,1)S(1)}, u32[]{:S(2)}, u32[]{:S(2)}) %collective-permute-start.14) | collective-permute-done | bytes 36896 | tf_op jit(solution)/shard_map/ppermute | solution.py:349
  32.8 1.9 %collective-permute-done.13 = bf16[144,128]{1,0:T(8,128)(2,1)S(1)} collective-permute-done((bf16[144,128]{1,0:T(8,128)(2,1)S(1)}, bf16[144,128]{1,0:T(8,128)(2,1)S(1)}, u32[]{:S(2)}, u32[]{:S(2)}) %collective-permute-start.13) | collective-permute-done | bytes 36896 | tf_op jit(solution)/shard_map/ppermute | solution.py:349
  34.7 0.0 collective-permute-done.12
  34.7 2.7 %collective-permute-start.17 = (bf16[144,128]{1,0:T(8,128)(2,1)S(1)}, bf16[144,128]{1,0:T(8,128)(2,1)S(1)}, u32[]{:S(2)}, u32[]{:S(2)}) collective-permute-start(bf16[144,128]{1,0:T(8,128)(2,1)S(1)} %add_convert_fusion.1), channel_id=1, source_target_pairs={{0,3},{1,2},{2,1},{3,0},{4,7},{5,6},{6,5},{7,4},{8,11},{9,10},{10,... | collective-permute-start | bytes 110600 | tf_op jit(solution)/shard_map/ppermute | solution.py:349
  37.4 0.4 collective-permute-start.16
  37.9 0.4 collective-permute-start.15
  38.3 1.5 %collective-permute-done.17 = bf16[144,128]{1,0:T(8,128)(2,1)S(1)} collective-permute-done((bf16[144,128]{1,0:T(8,128)(2,1)S(1)}, bf16[144,128]{1,0:T(8,128)(2,1)S(1)}, u32[]{:S(2)}, u32[]{:S(2)}) %collective-permute-start.17) | collective-permute-done | bytes 36896 | tf_op jit(solution)/shard_map/ppermute | solution.py:349
  39.8 1.6 %collective-permute-done.16 = bf16[144,128]{1,0:T(8,128)(2,1)S(1)} collective-permute-done((bf16[144,128]{1,0:T(8,128)(2,1)S(1)}, bf16[144,128]{1,0:T(8,128)(2,1)S(1)}, u32[]{:S(2)}, u32[]{:S(2)}) %collective-permute-start.16) | collective-permute-done | bytes 36896 | tf_op jit(solution)/shard_map/ppermute | solution.py:349
  41.4 0.4 collective-permute-done.15
  41.8 2.6 %collective-permute-start.18 = (bf16[144,128]{1,0:T(8,128)(2,1)S(1)}, bf16[144,128]{1,0:T(8,128)(2,1)S(1)}, u32[]{:S(2)}, u32[]{:S(2)}) collective-permute-start(bf16[144,128]{1,0:T(8,128)(2,1)S(1)} %add_convert_fusion.refs_0_), channel_id=1, source_target_pairs={{0,4},{1,5},{2,6},{3,7},{4,0},{5,1},{6,2},{7,3},{8,12},{9,13},{10,... | collective-permute-start | bytes 110600 | tf_op jit(solution)/shard_map/ppermute | solution.py:349
  44.4 2.3 %collective-permute-done.18.refs_1_ = bf16[144,128]{1,0:T(8,128)(2,1)S(1)} collective-permute-done((bf16[144,128]{1,0:T(8,128)(2,1)S(1)}, bf16[144,128]{1,0:T(8,128)(2,1)S(1)}, u32[]{:S(2)}, u32[]{:S(2)}) %collective-permute-start.18) | collective-permute-done | bytes 36896 | tf_op jit(solution)/shard_map/ppermute | solution.py:349
  46.8 0.0 copy-done.1
  46.8 11.3 %shard_map.103 = (bf16[2,11,128,512]{3,2,1,0:T(8,128)(2,1)}, f32[2,11,16,128]{3,2,1,0:T(8,128)S(1)}) custom-call(bf16[144,128]{1,0:T(8,128)(2,1)S(1)} %add_convert_fusion.refs_0_, bf16[144,128]{1,0:T(8,128)(2,1)S(1)} %collective-permute-done.18.refs_1_, bf16[8,128,176]{2,1,0:T(8,128)(2,1)S(1)} %copy-done.1, f32[22,128,128]{2,1,0:T(8,128)S(1)} %get-tuple-element.48.refs_3_, ...), custom_call_target="tpu_custom_call" | custom-call | tf_op jit(solution)/shard_map/pallas_call | solution.py:325
  58.0 0.7 %copy.11 = f32[2,16,11,11]{1,0,3,2:T(2,128)} copy(f32[2,16,11,11]{1,3,2,0:T(8,128)S(1)} %slice_bitcast_fusion) | data formatting | bytes 30976
  (3 shorter events, 0.1 us)
Async XLA Ops:
  0.6 1.4 %copy-start = (bf16[384,4,512]{2,1,0:T(4,128)(2,1)S(1)}, bf16[384,4,512]{2,1,0:T(4,128)(2,1)}, u32[]{:S(2)}) copy-start(bf16[384,4,512]{2,1,0:T(4,128)(2,1)} %x_ref.7) | copy-start | bytes 4718596
  2.0 0.7 %copy-start.2 = (s32[1,4]{1,0:T(1,128)S(1)}, s32[1,4]{1,0:T(1,128)}, u32[]{:S(2)}) copy-start(s32[1,4]{1,0:T(1,128)} %owner_ref.7) | copy-start | bytes 52
  3.6 8.2 %collective-permute-start.9 = (bf16[384,128]{1,0:T(8,128)(2,1)S(1)}, bf16[384,128]{1,0:T(8,128)(2,1)S(1)}, u32[]{:S(2)}, u32[]{:S(2)}) collective-permute-start(bf16[384,128]{1,0:T(8,128)(2,1)S(1)} %get-tuple-element.41), channel_id=1, source_target_pairs={{0,8},{8,0},{16,24},{24,16},{1,9},{9,1},{17,25},{25,17},{2,10},{10... | collective-permute-start | bytes 294920 | tf_op jit(solution)/shard_map/ppermute | solution.py:349
  4.2 7.8 %collective-permute-start.10 = (bf16[384,128]{1,0:T(8,128)(2,1)S(1)}, bf16[384,128]{1,0:T(8,128)(2,1)S(1)}, u32[]{:S(2)}, u32[]{:S(2)}) collective-permute-start(bf16[384,128]{1,0:T(8,128)(2,1)S(1)} %get-tuple-element.42), channel_id=1, source_target_pairs={{0,16},{8,24},{16,0},{24,8},{1,17},{9,25},{17,1},{25,9},{2,18},{10... | collective-permute-start | bytes 294920 | tf_op jit(solution)/shard_map/ppermute | solution.py:349
  6.7 5.6 %collective-permute-start.11 = (bf16[384,128]{1,0:T(8,128)(2,1)S(1)}, bf16[384,128]{1,0:T(8,128)(2,1)S(1)}, u32[]{:S(2)}, u32[]{:S(2)}) collective-permute-start(bf16[384,128]{1,0:T(8,128)(2,1)S(1)} %get-tuple-element.43), channel_id=1, source_target_pairs={{0,24},{8,16},{16,8},{24,0},{1,25},{9,17},{17,9},{25,1},{2,26},{10... | collective-permute-start | bytes 294920 | tf_op jit(solution)/shard_map/ppermute | solution.py:349
  7.8 14.7 %collective-permute-start.3 = (bf16[384,128]{1,0:T(8,128)(2,1)S(1)}, bf16[384,128]{1,0:T(8,128)(2,1)S(1)}, u32[]{:S(2)}, u32[]{:S(2)}) collective-permute-start(bf16[384,128]{1,0:T(8,128)(2,1)S(1)} %get-tuple-element.33), channel_id=1, source_target_pairs={{0,8},{8,0},{16,24},{24,16},{1,9},{9,1},{17,25},{25,17},{2,10},{10... | collective-permute-start | bytes 294920 | tf_op jit(solution)/shard_map/ppermute | solution.py:349
  8.0 5.9 %copy-start.3 = (f32[512]{0:T(512)S(1)}, f32[512]{0:T(512)}, u32[]{:S(2)}) copy-start(f32[512]{0:T(512)} %param.9) | copy-start | bytes 6148
  8.0 5.9 %copy-start.4 = (s32[4]{0:T(128)S(1)}, s32[4]{0:T(128)}, u32[]{:S(2)}) copy-start(s32[4]{0:T(128)} %refs_0_.7) | copy-start | bytes 52
  8.0 5.9 %copy-start.5 = (s32[11]{0:T(128)S(1)}, s32[11]{0:T(128)}, u32[]{:S(2)}) copy-start(s32[11]{0:T(128)} %refs_1_.7) | copy-start | bytes 136
  8.0 5.9 %copy-start.6 = (bf16[2,256,256]{2,1,0:T(8,128)(2,1)S(1)}, bf16[2,256,256]{2,1,0:T(8,128)(2,1)}, u32[]{:S(2)}) copy-start(bf16[2,256,256]{2,1,0:T(8,128)(2,1)} %constant.6.clone.refs_3_) | copy-start | bytes 786436
  8.0 5.9 %copy-start.7 = (bf16[11,24,256]{2,1,0:T(8,128)(2,1)S(1)}, bf16[11,24,256]{2,1,0:T(8,128)(2,1)}, u32[]{:S(2)}) copy-start(bf16[11,24,256]{2,1,0:T(8,128)(2,1)} %constant.7.clone.refs_4_) | copy-start | bytes 405508
  8.0 15.2 %collective-permute-start.4 = (bf16[384,128]{1,0:T(8,128)(2,1)S(1)}, bf16[384,128]{1,0:T(8,128)(2,1)S(1)}, u32[]{:S(2)}, u32[]{:S(2)}) collective-permute-start(bf16[384,128]{1,0:T(8,128)(2,1)S(1)} %get-tuple-element.34), channel_id=1, source_target_pairs={{0,16},{8,24},{16,0},{24,8},{1,17},{9,25},{17,1},{25,9},{2,18},{10... | collective-permute-start | bytes 294920 | tf_op jit(solution)/shard_map/ppermute | solution.py:349
  11.9 4.6 %collective-permute-start.6 = (bf16[384,128]{1,0:T(8,128)(2,1)S(1)}, bf16[384,128]{1,0:T(8,128)(2,1)S(1)}, u32[]{:S(2)}, u32[]{:S(2)}) collective-permute-start(bf16[384,128]{1,0:T(8,128)(2,1)S(1)} %get-tuple-element.37), channel_id=1, source_target_pairs={{0,8},{8,0},{16,24},{24,16},{1,9},{9,1},{17,25},{25,17},{2,10},{10... | collective-permute-start | bytes 294920 | tf_op jit(solution)/shard_map/ppermute | solution.py:349
  12.0 5.7 %collective-permute-start.7 = (bf16[384,128]{1,0:T(8,128)(2,1)S(1)}, bf16[384,128]{1,0:T(8,128)(2,1)S(1)}, u32[]{:S(2)}, u32[]{:S(2)}) collective-permute-start(bf16[384,128]{1,0:T(8,128)(2,1)S(1)} %get-tuple-element.38), channel_id=1, source_target_pairs={{0,16},{8,24},{16,0},{24,8},{1,17},{9,25},{17,1},{25,9},{2,18},{10... | collective-permute-start | bytes 294920 | tf_op jit(solution)/shard_map/ppermute | solution.py:349
  12.3 6.5 %collective-permute-start.8 = (bf16[384,128]{1,0:T(8,128)(2,1)S(1)}, bf16[384,128]{1,0:T(8,128)(2,1)S(1)}, u32[]{:S(2)}, u32[]{:S(2)}) collective-permute-start(bf16[384,128]{1,0:T(8,128)(2,1)S(1)} %get-tuple-element.39), channel_id=1, source_target_pairs={{0,24},{8,16},{16,8},{24,0},{1,25},{9,17},{17,9},{25,1},{2,26},{10... | collective-permute-start | bytes 294920 | tf_op jit(solution)/shard_map/ppermute | solution.py:349
  16.5 6.7 %collective-permute-start.5 = (bf16[384,128]{1,0:T(8,128)(2,1)S(1)}, bf16[384,128]{1,0:T(8,128)(2,1)S(1)}, u32[]{:S(2)}, u32[]{:S(2)}) collective-permute-start(bf16[384,128]{1,0:T(8,128)(2,1)S(1)} %get-tuple-element.35), channel_id=1, source_target_pairs={{0,24},{8,16},{16,8},{24,0},{1,25},{9,17},{17,9},{25,1},{2,26},{10... | collective-permute-start | bytes 294920 | tf_op jit(solution)/shard_map/ppermute | solution.py:349
  17.6 8.2 %collective-permute-start = (bf16[384,128]{1,0:T(8,128)(2,1)S(1)}, bf16[384,128]{1,0:T(8,128)(2,1)S(1)}, u32[]{:S(2)}, u32[]{:S(2)}) collective-permute-start(bf16[384,128]{1,0:T(8,128)(2,1)S(1)} %get-tuple-element.29), channel_id=1, source_target_pairs={{0,8},{8,0},{16,24},{24,16},{1,9},{9,1},{17,25},{25,17},{2,10},{10... | collective-permute-start | bytes 294920 | tf_op jit(solution)/shard_map/ppermute | solution.py:349
  18.8 7.0 %collective-permute-start.1 = (bf16[384,128]{1,0:T(8,128)(2,1)S(1)}, bf16[384,128]{1,0:T(8,128)(2,1)S(1)}, u32[]{:S(2)}, u32[]{:S(2)}) collective-permute-start(bf16[384,128]{1,0:T(8,128)(2,1)S(1)} %get-tuple-element.30), channel_id=1, source_target_pairs={{0,16},{8,24},{16,0},{24,8},{1,17},{9,25},{17,1},{25,9},{2,18},{10... | collective-permute-start | bytes 294920 | tf_op jit(solution)/shard_map/ppermute | solution.py:349
  22.5 4.3 %collective-permute-start.2 = (bf16[384,128]{1,0:T(8,128)(2,1)S(1)}, bf16[384,128]{1,0:T(8,128)(2,1)S(1)}, u32[]{:S(2)}, u32[]{:S(2)}) collective-permute-start(bf16[384,128]{1,0:T(8,128)(2,1)S(1)} %get-tuple-element.31), channel_id=1, source_target_pairs={{0,24},{8,16},{16,8},{24,0},{1,25},{9,17},{17,9},{25,1},{2,26},{10... | collective-permute-start | bytes 294920 | tf_op jit(solution)/shard_map/ppermute | solution.py:349
  26.8 20.0 %copy-start.1 = (bf16[8,128,176]{2,1,0:T(8,128)(2,1)S(1)}, bf16[8,128,176]{2,1,0:T(8,128)(2,1)}, u32[]{:S(2)}) copy-start(bf16[8,128,176]{2,1,0:T(8,128)(2,1)} %constant.8.clone.refs_2_) | copy-start | bytes 1081348
  29.4 3.4 %collective-permute-start.14 = (bf16[144,128]{1,0:T(8,128)(2,1)S(1)}, bf16[144,128]{1,0:T(8,128)(2,1)S(1)}, u32[]{:S(2)}, u32[]{:S(2)}) collective-permute-start(bf16[144,128]{1,0:T(8,128)(2,1)S(1)} %get-tuple-element.47), channel_id=1, source_target_pairs={{0,24},{1,25},{2,26},{3,27},{4,28},{5,29},{6,30},{7,31},{8,16},{9,... | collective-permute-start | bytes 110600 | tf_op jit(solution)/shard_map/ppermute | solution.py:349
  30.7 4.0 %collective-permute-start.13 = (bf16[144,128]{1,0:T(8,128)(2,1)S(1)}, bf16[144,128]{1,0:T(8,128)(2,1)S(1)}, u32[]{:S(2)}, u32[]{:S(2)}) collective-permute-start(bf16[144,128]{1,0:T(8,128)(2,1)S(1)} %get-tuple-element.47), channel_id=1, source_target_pairs={{0,16},{1,17},{2,18},{3,19},{4,20},{5,21},{6,22},{7,23},{8,24},{9,... | collective-permute-start | bytes 110600 | tf_op jit(solution)/shard_map/ppermute | solution.py:349
  31.8 2.9 %collective-permute-start.12 = (bf16[144,128]{1,0:T(8,128)(2,1)S(1)}, bf16[144,128]{1,0:T(8,128)(2,1)S(1)}, u32[]{:S(2)}, u32[]{:S(2)}) collective-permute-start(bf16[144,128]{1,0:T(8,128)(2,1)S(1)} %get-tuple-element.47), channel_id=1, source_target_pairs={{0,8},{1,9},{2,10},{3,11},{4,12},{5,13},{6,14},{7,15},{8,0},{9,1},... | collective-permute-start | bytes 110600 | tf_op jit(solution)/shard_map/ppermute | solution.py:349
  34.7 5.0 %collective-permute-start.17 = (bf16[144,128]{1,0:T(8,128)(2,1)S(1)}, bf16[144,128]{1,0:T(8,128)(2,1)S(1)}, u32[]{:S(2)}, u32[]{:S(2)}) collective-permute-start(bf16[144,128]{1,0:T(8,128)(2,1)S(1)} %add_convert_fusion.1), channel_id=1, source_target_pairs={{0,3},{1,2},{2,1},{3,0},{4,7},{5,6},{6,5},{7,4},{8,11},{9,10},{10,... | collective-permute-start | bytes 110600 | tf_op jit(solution)/shard_map/ppermute | solution.py:349
  37.4 4.0 %collective-permute-start.16 = (bf16[144,128]{1,0:T(8,128)(2,1)S(1)}, bf16[144,128]{1,0:T(8,128)(2,1)S(1)}, u32[]{:S(2)}, u32[]{:S(2)}) collective-permute-start(bf16[144,128]{1,0:T(8,128)(2,1)S(1)} %add_convert_fusion.1), channel_id=1, source_target_pairs={{0,2},{1,3},{2,0},{3,1},{4,6},{5,7},{6,4},{7,5},{8,10},{9,11},{10,... | collective-permute-start | bytes 110600 | tf_op jit(solution)/shard_map/ppermute | solution.py:349
  37.9 4.0 %collective-permute-start.15 = (bf16[144,128]{1,0:T(8,128)(2,1)S(1)}, bf16[144,128]{1,0:T(8,128)(2,1)S(1)}, u32[]{:S(2)}, u32[]{:S(2)}) collective-permute-start(bf16[144,128]{1,0:T(8,128)(2,1)S(1)} %add_convert_fusion.1), channel_id=1, source_target_pairs={{0,1},{1,0},{2,3},{3,2},{4,5},{5,4},{6,7},{7,6},{8,9},{9,8},{10,11... | collective-permute-start | bytes 110600 | tf_op jit(solution)/shard_map/ppermute | solution.py:349
  41.8 4.9 %collective-permute-start.18 = (bf16[144,128]{1,0:T(8,128)(2,1)S(1)}, bf16[144,128]{1,0:T(8,128)(2,1)S(1)}, u32[]{:S(2)}, u32[]{:S(2)}) collective-permute-start(bf16[144,128]{1,0:T(8,128)(2,1)S(1)} %add_convert_fusion.refs_0_), channel_id=1, source_target_pairs={{0,4},{1,5},{2,6},{3,7},{4,0},{5,1},{6,2},{7,3},{8,12},{9,13},{10,... | collective-permute-start | bytes 110600 | tf_op jit(solution)/shard_map/ppermute | solution.py:349
where the time goes:
time: 58.9 us; the launch traced here: 58.7 us
  Pallas kernels  25.4 us (43%)
  starting transfers between devices  18 us (31%)
  waiting for transfers between devices  11.7 us (20%)
  local copies, waits for them, and re-layouts  2.81 us (5%)
  between operations  0.77 us (1%)
    ppermute x19, starting transfers between devices, swap(): return lax.ppermute(x, axes, [(i, i ^ mask) for i in range(size)])  18 us
    ppermute x19, waiting for transfers between devices, swap(): return lax.ppermute(x, axes, [(i, i ^ mask) for i in range(size)])  11.7 us
    pallas_call x1, Pallas kernels, mode_fields(): pl.pallas_call(functools.partial(mode_kernel, len(parts), chunks, share),...  11.3 us
    pallas_call x4, Pallas kernels, gram_part(): pl.pallas_call(functools.partial(gram_kernel, lanes, scale, first, last),...  10.5 us
    pallas_call x4, Pallas kernels, pack(): pl.pallas_call(pack_kernel, grid=(1,), out_shape=[jax.ShapeDtypeStruct((s...  3.73 us
    unnamed x17, local copies, waits for them, and re-layouts  2.79 us
  transfers between devices with their start and end apart: 19, of which 9 were waited for; matrix products, arithmetic and copies ran while one was open for 0% of the time, Pallas kernels for 18%

commit v1 on v0

v1 whole, which is shorter than its diff:
```python
import functools
import math

import jax
import jax.numpy as jnp
import numpy as np
from jax import lax
from jax.experimental import pallas as pl
from jax.experimental.pallas import tpu as pltpu
from jax.sharding import PartitionSpec as P

NFFT = 256
ROOT_STEPS = 5
NFREQ = 128
NBLK = 11
LANE = 128
SUB = 8
HALF_ROWS = NBLK * SUB
GROUPS = NFREQ // SUB
PAIRS = (NBLK + 1) // 2
PAIR_ROWS = 24
PACKED = PAIRS * PAIR_ROWS
STACK = 4
FIRST_LIMIT = 64 * 2**20
BF16 = jnp.bfloat16
F32 = jnp.float32


def fourier_tables():
    n = np.arange(NFFT)
    k = np.arange(NFREQ)
    angles = 2.0 * np.pi * ((k[:, None] * n[None, :]) % NFFT) / NFFT
    scaled = (0.5 - 0.5 * np.cos(2.0 * np.pi * n / NFFT)) / math.sqrt(0.375 * NFFT)
    table = np.concatenate([np.cos(angles) * scaled, -np.sin(angles) * scaled], axis=0)
    high = table.astype(jnp.bfloat16)
    low = (table - high.astype(np.float64)).astype(jnp.bfloat16)
    return np.stack([high, low])


def packed_rows():
    rows = {}
    for pair in range(PAIRS):
        row = pair * PAIR_ROWS
        for a in sorted({pair, NBLK - 1 - pair}):
            for e in range(a, NBLK):
                rows[0, a, e] = row
                row += 1
            for e in range(a + 1, NBLK):
                rows[1, a, e] = row
                row += 1
    return rows


def pick_table():
    pick = np.zeros((NBLK, PAIR_ROWS, 2 * LANE), np.float32)
    for (part, a, e), row in packed_rows().items():
        start = part * LANE + e * SUB
        pick[a, row % PAIR_ROWS, start : start + SUB] = 1.0
    return pick.astype(jnp.bfloat16)


def spread_table():
    spread = np.zeros((STACK, 2, LANE, 2 * HALF_ROWS), np.float32)
    for m in range(STACK):
        for b in range(NBLK):
            real = m * 32 + b
            imag = m * 32 + 16 + b
            first = slice(b * SUB, b * SUB + SUB)
            second = slice(HALF_ROWS + b * SUB, HALF_ROWS + b * SUB + SUB)
            spread[m, 0, real, first] = 1.0
            spread[m, 0, imag, second] = 1.0
            spread[m, 1, imag, first] = -1.0
            spread[m, 1, real, second] = 1.0
    return spread.reshape(STACK * 2, LANE, 2 * HALF_ROWS).astype(jnp.bfloat16)


def split(x):
    high = x.astype(BF16)
    return high, (x - high.astype(F32)).astype(BF16)


def dot(a, b):
    return jnp.dot(a, b, preferred_element_type=F32)


def dot_nt(a, b):
    return lax.dot_general(a, b, (((1,), (1,)), ((), ())), preferred_element_type=F32)


def spec(shape):
    return pl.BlockSpec(shape, lambda *_: (0,) * len(shape))


SMEM = pl.BlockSpec(memory_space=pltpu.SMEM)


def pack_kernel(base, follows, owner_hbm, x_hbm, *refs):
    lanes = x_hbm.shape[1]
    refs = refs[follows:]
    out_refs = refs[:lanes]
    owner, x_ref, owner_sem, x_sem = refs[lanes:]
    steps, _, width = x_ref.shape
    copies = []
    for i, at in enumerate(range(0, width, LANE)):
        copies.append(
            pltpu.make_async_copy(
                x_hbm.at[:, :, base + at : base + at + LANE],
                x_ref.at[:, :, at : at + LANE],
                x_sem.at[i],
            )
        )
    owner_copy = pltpu.make_async_copy(owner_hbm, owner, owner_sem)
    owner_copy.start()
    for copy in copies:
        copy.start()
    me = lax.axis_index("tm")
    rows = 2 * LANE // lanes
    out_row = lax.broadcasted_iota(jnp.int32, (2 * LANE, 2 * LANE), 0)
    in_row = lax.broadcasted_iota(jnp.int32, (2 * LANE, 2 * LANE), 1)
    want = jnp.zeros_like(out_row)
    owner_copy.wait()
    for d in range(lanes):
        slot = me ^ d
        source = jnp.int32(0)
        for lane in range(lanes):
            source = source + jnp.where(owner[0, lane] == slot, lane, 0)
        want = jnp.where(out_row // rows == d, source, want)
    pick = jnp.where(in_row == (out_row % rows) * lanes + want, 1.0, 0.0).astype(BF16)
    for c, copy in enumerate(copies):
        copy.wait()
        cols = slice(c * LANE, (c + 1) * LANE)
        x = x_ref[:, :, cols].reshape(steps * lanes, LANE)
        for i in range(steps // rows):
            y = dot(pick, x[i * 2 * LANE : (i + 1) * 2 * LANE]).astype(BF16)
            for d in range(lanes):
                out_refs[d][i * rows : (i + 1) * rows, cols] = y[d * rows : (d + 1) * rows]


def pack(owner, snapshots, base, width, after):
    steps, lanes, _ = snapshots.shape
    limit = 24 * 2**20 if after else FIRST_LIMIT
    return pl.pallas_call(
        functools.partial(pack_kernel, base, len(after)),
        out_shape=[jax.ShapeDtypeStruct((steps, width), BF16)] * lanes,
        in_specs=[pl.BlockSpec(memory_space=pltpu.HBM)] * (2 + len(after)),
        out_specs=[pl.BlockSpec(memory_space=pltpu.VMEM)] * lanes,
        scratch_shapes=[
            pltpu.SMEM(owner.shape, jnp.int32),
            pltpu.VMEM((steps, lanes, width), BF16),
            pltpu.SemaphoreType.DMA,
            pltpu.SemaphoreType.DMA((width // LANE,)),
        ],
        compiler_params=pltpu.CompilerParams(vmem_limit_bytes=limit),
        cost_estimate=pl.CostEstimate(
            flops=2 * 256 * steps * lanes * width,
            bytes_accessed=4 * steps * lanes * width,
            transcendentals=0,
        ),
    )(owner, snapshots, *after)


def gram_kernel(lanes, scale, first, *refs):
    order_ref, offsets_ref, w_ref, f_ref, pick_ref = refs[:5]
    pieces = refs[5 : 5 + lanes]
    rest = refs[5 + lanes :]
    if not first:
        before_ref, *rest = rest
    high_ref, low_ref, packed_ref, record, s_ref, masked = rest
    steps, width = pieces[0].shape
    me = lax.axis_index("tm")
    for d in range(lanes):
        start = pl.multiple_of(order_ref[me ^ d] * steps, steps)
        for c in range(width // LANE):
            cols = slice(c * LANE, (c + 1) * LANE)
            record[c, pl.ds(start, steps), :] = pieces[d][:, cols].astype(F32)
    wanted = [(i, c) for i in range(NBLK) for c in range(width // LANE)]
    for at in range(0, len(wanted), 2):
        pair = wanted[at : at + 2]
        x = [record[c, pl.ds(offsets_ref[i], NFFT), :].astype(BF16) for i, c in pair]
        x = jnp.concatenate(x, axis=1) if len(x) > 1 else x[0]
        y = dot(f_ref[0], x) + dot(f_ref[1], x)
        for j, (i, c) in enumerate(pair):
            cols = slice(j * LANE, (j + 1) * LANE)
            out = slice(c * LANE, (c + 1) * LANE)
            s_ref[i, :, out] = y[:NFREQ, cols]
            s_ref[NBLK + i, :, out] = y[NFREQ:, cols]
    w = w_ref[...]
    row = lax.broadcasted_iota(jnp.int32, (HALF_ROWS, LANE), 0)
    col = lax.broadcasted_iota(jnp.int32, (HALF_ROWS, LANE), 1)
    same = row % SUB == col % SUB
    pad = jnp.zeros((LANE - HALF_ROWS, width), F32)
    for g in range(GROUPS):
        at = slice(g * SUB, (g + 1) * SUB)
        s = s_ref[:, at, :].reshape(2 * HALF_ROWS, width)
        high, low = split(s)
        high_ref[g] = high
        low_ref[g] = low
        other = jnp.concatenate([s[:HALF_ROWS], pad, s[HALF_ROWS:], pad], axis=0)
        full = dot_nt((s * w).astype(BF16), other.astype(BF16))
        real = full[:HALF_ROWS, :LANE] + full[HALF_ROWS:, LANE:]
        imag = full[:HALF_ROWS, LANE:] - full[HALF_ROWS:, :LANE]
        masked[:, at, :LANE] = jnp.where(same, real, 0.0).reshape(NBLK, SUB, LANE)
        masked[:, at, LANE:] = jnp.where(same, imag, 0.0).reshape(NBLK, SUB, LANE)
    for pair in range(PAIRS):
        total = jnp.zeros((PAIR_ROWS, NFREQ), F32)
        for a in sorted({pair, NBLK - 1 - pair}):
            high, low = split(masked[a])
            total = total + dot_nt(pick_ref[a], high) + dot_nt(pick_ref[a], low)
        rows = slice(pair * PAIR_ROWS, (pair + 1) * PAIR_ROWS)
        total = total * scale
        if not first:
            total = total + before_ref[rows, :]
        packed_ref[rows, :] = total


def gram_part(order, offsets, weights, tables, pieces, before, base, scale):
    lanes = len(pieces)
    steps, width = pieces[0].shape
    first = before is None
    args = [order, offsets, weights[:, base : base + width], *tables, *pieces]
    args += [] if first else [before]
    vmem = pl.BlockSpec(memory_space=pltpu.VMEM)
    return pl.pallas_call(
        functools.partial(gram_kernel, lanes, scale, first),
        out_shape=[
            jax.ShapeDtypeStruct((GROUPS, 2 * HALF_ROWS, width), BF16),
            jax.ShapeDtypeStruct((GROUPS, 2 * HALF_ROWS, width), BF16),
            jax.ShapeDtypeStruct((PACKED, NFREQ), F32),
        ],
        in_specs=[SMEM, SMEM] + [vmem] * (len(args) - 2),
        out_specs=[vmem] * 3,
        scratch_shapes=[
            pltpu.VMEM((width // LANE, lanes * steps, LANE), F32),
            pltpu.VMEM((2 * NBLK, NFREQ, width), F32),
            pltpu.VMEM((NBLK, NFREQ, 2 * LANE), F32),
        ],
        compiler_params=pltpu.CompilerParams(vmem_limit_bytes=24 * 2**20),
        cost_estimate=pl.CostEstimate(
            flops=10**10 * width // LANE // 4, bytes_accessed=6 * 10**6, transcendentals=0
        ),
    )(*args)


def product(x, y, store):
    xr, xi = x
    yr, yi = y

    @pl.loop(0, NBLK)
    def _(a):
        real = jnp.zeros((16, NFREQ), F32)
        imag = jnp.zeros((16, NFREQ), F32)
        for b in range(NBLK):
            pr = xr[a, pl.ds(b, 1), :]
            pi = xi[a, pl.ds(b, 1), :]
            qr = yr[b]
            qi = yi[b]
            real = real + (pr * qr - pi * qi)
            imag = imag + (pr * qi + pi * qr)
        store(a, real, imag)


def inverse_root(y, z, p, y2, z2):
    sub = lax.broadcasted_iota(jnp.int32, (16, NFREQ), 0)

    def to(dst):
        def store(a, real, imag):
            dst[0][a] = real
            dst[1][a] = imag

        return store

    def factor(a, real, imag):
        p[0][a] = jnp.where(sub == a, 1.5, 0.0) - 0.5 * real
        p[1][a] = -0.5 * imag

    for step in range(ROOT_STEPS):
        if step == 0:
            for a in range(NBLK):
                real = jnp.where(sub == a, 1.5, 0.0) - 0.5 * y[0][a]
                imag = -0.5 * y[1][a]
                p[0][a] = real
                p[1][a] = imag
                z2[0][a] = real
                z2[1][a] = imag
        else:
            product(z, y, factor)
            product(p, z, to(z2))
        if step < ROOT_STEPS - 1:
            product(y, p, to(y2))
        y, y2 = y2, y
        z, z2 = z2, z
    return z


def root_kernel(parts, share, *refs):
    part_refs = refs[:parts]
    stack_ref, gram_ref, packed, *mats = refs[parts:]
    terms = [r[...].astype(F32) for r in part_refs]
    while len(terms) > 1:
        terms = [a + b for a, b in zip(terms[::2], terms[1::2])]
    packed[...] = terms[0]
    y, z, p, y2, z2 = [(mats[2 * i], mats[2 * i + 1]) for i in range(5)]
    for ref in mats:
        ref[:, 8:, :] = jnp.zeros((NBLK, 8, NFREQ), F32)
    trace = jnp.zeros((1, NFREQ), F32)
    rows = packed_rows()
    for a in range(NBLK):
        line = packed[pl.ds(rows[0, a, a], 1), :]
        trace = trace + line
        y[0][a, pl.ds(a, 1), :] = line
        y[1][a, pl.ds(a, 1), :] = jnp.zeros_like(line)
        for e in range(a + 1, NBLK):
            line = packed[pl.ds(rows[0, a, e], 1), :]
            y[0][a, pl.ds(e, 1), :] = line
            y[0][e, pl.ds(a, 1), :] = line
            line = packed[pl.ds(rows[1, a, e], 1), :]
            y[1][a, pl.ds(e, 1), :] = line
            y[1][e, pl.ds(a, 1), :] = -line
    trace = 2.0 * trace
    at = lax.axis_index("sx") * lax.axis_size("sy") + lax.axis_index("sy")
    back = (NFREQ - at * share) % NFREQ
    for c in range(2):
        for a in range(NBLK):
            gram_ref[a, :, c, :] = pltpu.roll(y[c][a], back, 1)[:NBLK, :share]
            y[c][a] = y[c][a] / trace
    root = inverse_root(y, z, p, y2, z2)
    norm = 1.0 / jnp.sqrt(trace)
    for at, m0 in enumerate(range(0, NBLK, STACK)):
        modes = range(m0, min(m0 + STACK, NBLK))
        stack = [root[c][m] * norm for m in modes for c in range(2)]
        stack += [jnp.zeros((16, NFREQ), F32)] * (2 * STACK - len(stack))
        stack_ref[at] = jnp.concatenate(stack, axis=0).T


def roots(parts, share):
    stacks = -(-NBLK // STACK)
    vmem = pl.BlockSpec(memory_space=pltpu.VMEM)
    return pl.pallas_call(
        functools.partial(root_kernel, len(parts), share),
        out_shape=[
            jax.ShapeDtypeStruct((stacks, NFREQ, LANE), F32),
            jax.ShapeDtypeStruct((NBLK, NBLK, 2, share), F32),
        ],
        in_specs=[vmem] * len(parts),
        out_specs=[vmem] * 2,
        scratch_shapes=[pltpu.VMEM((PACKED, NFREQ), F32)]
        + [pltpu.VMEM((NBLK, 16, NFREQ), F32)] * 10,
        compiler_params=pltpu.CompilerParams(vmem_limit_bytes=24 * 2**20),
    )(*parts)


def mode_kernel(chunks, stack_ref, spread_ref, *refs):
    high_refs = refs[:chunks]
    low_refs = refs[chunks : 2 * chunks]
    out_ref, v = refs[2 * chunks :]
    step = pl.program_id(0)

    @pl.when(step == 0)
    def _():
        row = lax.broadcasted_iota(jnp.int32, (NFREQ, 2 * HALF_ROWS), 0)
        col = lax.broadcasted_iota(jnp.int32, (NFREQ, 2 * HALF_ROWS), 1)
        same = row % SUB == col % SUB
        for at, m0 in enumerate(range(0, NBLK, STACK)):
            high, low = split(stack_ref[at])
            for m in range(m0, min(m0 + STACK, NBLK)):
                for c in range(2):
                    table = spread_ref[(m - m0) * 2 + c]
                    wide = dot(high, table) + dot(low, table)
                    v[c * NBLK + m] = jnp.where(same, wide, 0.0)

    fields = []
    for h in range(2):
        start = pl.multiple_of(step * 16 + h * SUB, SUB)
        v_high, v_low = split(v[:, pl.ds(start, SUB), :].reshape(2 * HALF_ROWS, 2 * HALF_ROWS))
        s_high = jnp.concatenate([r[h] for r in high_refs], axis=1)
        s_low = jnp.concatenate([r[h] for r in low_refs], axis=1)
        field = dot(v_high, s_high) + (dot(v_high, s_low) + dot(v_low, s_high))
        fields.append(field.reshape(2 * NBLK, SUB, -1))
    both = jnp.concatenate(fields, axis=1).astype(BF16)
    out_ref[...] = both.reshape(out_ref.shape)


def mode_fields(stacks, spread, highs, lows):
    width = sum(s.shape[2] for s in highs)
    return pl.pallas_call(
        functools.partial(mode_kernel, len(highs)),
        grid=(NFREQ // 16,),
        out_shape=jax.ShapeDtypeStruct((2, NBLK, NFREQ, width), BF16),
        in_specs=[spec(stacks.shape), spec(spread.shape)]
        + [
            pl.BlockSpec((2, 2 * HALF_ROWS, s.shape[2]), lambda i: (i, 0, 0))
            for s in highs + lows
        ],
        out_specs=pl.BlockSpec((2, NBLK, 16, width), lambda i: (0, 0, i, 0)),
        scratch_shapes=[pltpu.VMEM((2 * NBLK, NFREQ, 2 * HALF_ROWS), F32)],
        compiler_params=pltpu.CompilerParams(vmem_limit_bytes=24 * 2**20),
    )(stacks, spread, *highs, *lows)


def swap(x, axes, mask, size):
    return lax.ppermute(x, axes, [(i, i ^ mask) for i in range(size)])


def body(snapshots, weights, block_order, owner, offsets):
    lanes = lax.axis_size("tm")
    groups = lax.axis_size("sx") * lax.axis_size("sy")
    points = snapshots.shape[2]
    widths = [points // 2, points // 4, points // 4]
    scale = 1.0 / (lanes * groups * points)
    tables = (jnp.asarray(fourier_tables()), jnp.asarray(pick_table()))
    weights = weights.reshape(1, -1)

    arrived = []
    base = 0
    for width in widths:
        packed = pack(owner, snapshots, base, width, [p[0] for _, p in arrived[-1:]])
        moved = [swap(packed[d], "tm", d, lanes) for d in reversed(range(1, lanes))]
        pieces = [packed[0]] + moved[::-1]
        arrived.append((base, pieces))
        base += width

    highs, lows = [], []
    total = None
    for base, pieces in arrived:
        high, low, total = gram_part(
            block_order, offsets, weights, tables, pieces, total, base, scale
        )
        highs.append(high)
        lows.append(low)

    total = lax.psum(total, ("tm", "sx", "sy"))
    stacks, gram = roots([total], NFREQ // groups)
    modes = mode_fields(stacks, jnp.asarray(spread_table()), highs, lows)
    modes = jnp.transpose(modes, (0, 2, 1, 3))[:, :, :, None, :]
    return modes, jnp.transpose(gram, (2, 3, 0, 1))


def solution(mesh):
    placed = (P("tm", None, ("sx", "sy")), P(("sx", "sy")), P(), P(("sx", "sy"), None), P())
    return jax.shard_map(
        body,
        mesh=mesh,
        in_specs=placed,
        out_specs=(P(None, None, None, "tm", ("sx", "sy")), P(None, ("sx", "sy"), None, None)),
        check_vma=False,
    )
```

time: 58.9 us -> 182 us (3.09)
  waiting for transfers between devices: 11.7 us -> 122 us
  between operations: 0.77 us -> 14.1 us
  starting transfers between devices: 18 us -> 7.5 us
  local copies, waits for them, and re-layouts: 2.81 us -> 11.9 us
    psum x0 -> x1, waiting for transfers between devices: none -> 120 us  [body(): total = lax.psum(total, ('tm', 'sx', 'sy'))]
    ppermute x19 -> x9, starting transfers between devices: 18 us -> 7.46 us  [swap(): return lax.ppermute(x, axes, [(i, i ^ mask) for i in range(size)])]
    ppermute x19 -> x9, waiting for transfers between devices: 11.7 us -> 2.3 us  [swap(): return lax.ppermute(x, axes, [(i, i ^ mask) for i in range(size)])]
    unnamed x17 -> x38, local copies, waits for them, and re-layouts: 2.79 us -> 11.9 us
    pallas_call x9 -> x8, Pallas kernels: 25.4 us -> 24.5 us  [the longest x3 8.62 us: gram_part(): pl.pallas_call(functools.partial(gram_kernel, lanes, scale, first), out_s...]
  transfers between devices with their start and end apart: 19 -> 10, of which waited for: 9 -> 2; matrix products, arithmetic and copies ran while one was open for 0% -> 0% of each run, Pallas kernels for 18% -> 4%
where the time goes in v1:
time: 182 us; the launch traced here: 180 us
  waiting for transfers between devices  122 us (67%)
  Pallas kernels  24.5 us (13%)
  between operations  14.1 us (8%)
  local copies, waits for them, and re-layouts  11.9 us (7%)
  starting transfers between devices  7.5 us (4%)
    psum x1, waiting for transfers between devices, body(): total = lax.psum(total, ('tm', 'sx', 'sy'))  120 us
    unnamed x38, local copies, waits for them, and re-layouts  11.9 us
    pallas_call x3, Pallas kernels, gram_part(): pl.pallas_call(functools.partial(gram_kernel, lanes, scale, first), out_s...  8.62 us
    ppermute x9, starting transfers between devices, swap(): return lax.ppermute(x, axes, [(i, i ^ mask) for i in range(size)])  7.46 us
    pallas_call x1, Pallas kernels, mode_fields(): pl.pallas_call(functools.partial(mode_kernel, len(highs)), grid=(NFREQ //...  6.07 us
    pallas_call x1, Pallas kernels, roots(): pl.pallas_call(functools.partial(root_kernel, len(parts), share), out_sha...  5.31 us
    pallas_call x3, Pallas kernels, pack(): pl.pallas_call(functools.partial(pack_kernel, base, len(after)), out_shap...  4.53 us
  transfers between devices with their start and end apart: 10, of which 2 were waited for; matrix products, arithmetic and copies ran while one was open for 0% of the time, Pallas kernels for 4%

profile of v1, /device:TPU:0, one launch (start us, length us, event | category | flops | bytes accessed | tf_op | source)
XLA Modules:
  0.0 180.3 jit_solution(775421602887559169)
XLA Ops:
  7.2 0.0 all-reduce.2.cloned.1.call-start
  7.2 2.6 %shard_map.95 = (bf16[384,256]{1,0:T(8,128)(2,1)}, bf16[384,256]{1,0:T(8,128)(2,1)}, bf16[384,256]{1,0:T(8,128)(2,1)}, bf16[384,256]{1,0:T(8,128)(2,1)}) custom-call(s32[1,4]{1,0:T(1,128)} %owner_hbm.5, bf16[384,4,512]{2,1,0:T(4,128)(2,1)} %x_hbm.5), custom_call_target="tpu_custom_call" | custom-call | flops 201326592 | bytes 1572864 | tf_op jit(solution)/shard_map/pallas_call | solution.py:142
  9.8 0.0 copy-start.18
  9.8 0.5 collective-permute-start.6
  10.4 2.6 %collective-permute-start.7 = (bf16[384,256]{1,0:T(8,128)(2,1)}, bf16[384,256]{1,0:T(8,128)(2,1)S(1)}, u32[]{:S(2)}, u32[]{:S(2)}) collective-permute-start(bf16[384,256]{1,0:T(8,128)(2,1)} %get-tuple-element.35), channel_id=1, source_target_pairs={{0,16},{8,24},{16,0},{24,8},{1,17},{9,25},{17,1},{25,9},{2,18},{10... | collective-permute-start | bytes 589832 | tf_op jit(solution)/shard_map/ppermute | solution.py:401
  12.9 0.1 collective-permute-start.8
  13.0 0.0 copy-start
  13.0 1.4 copy-done
  14.4 0.0 copy-start.10
  14.4 0.9 copy-done.10
  15.4 0.0 copy-start.13
  15.4 0.7 copy-done.13
  16.0 0.0 copy-start.11
  16.0 0.0 copy-start.14
  16.0 0.0 copy-start.15
  16.0 0.0 copy-start.16
  16.0 0.0 copy-start.17
  16.0 1.0 shard_map.96
  17.0 0.2 collective-permute-start.3
  17.2 1.9 %collective-permute-start.4 = (bf16[384,128]{1,0:T(8,128)(2,1)S(1)}, bf16[384,128]{1,0:T(8,128)(2,1)S(1)}, u32[]{:S(2)}, u32[]{:S(2)}) collective-permute-start(bf16[384,128]{1,0:T(8,128)(2,1)S(1)} %get-tuple-element.32), channel_id=1, source_target_pairs={{0,16},{8,24},{16,0},{24,8},{1,17},{9,25},{17,1},{25,9},{2,18},{10... | collective-permute-start | bytes 294920 | tf_op jit(solution)/shard_map/ppermute | solution.py:401
  19.1 0.0 copy-done.18
  19.1 1.0 shard_map.97
  20.1 0.0 collective-permute-done.6.refs_6_
  20.1 0.1 collective-permute-start.5
  20.2 0.0 collective-permute-done.7.refs_7_
  20.2 0.2 collective-permute-start
  20.4 2.3 %collective-permute-done.8.refs_8_ = bf16[384,256]{1,0:T(8,128)(2,1)S(1)} collective-permute-done((bf16[384,256]{1,0:T(8,128)(2,1)}, bf16[384,256]{1,0:T(8,128)(2,1)S(1)}, u32[]{:S(2)}, u32[]{:S(2)}) %collective-permute-start.8) | collective-permute-done | bytes 196640 | tf_op jit(solution)/shard_map/ppermute | solution.py:401
  22.7 1.5 collective-permute-start.1
  24.2 0.0 copy-done.11
  24.2 0.0 copy-done.14
  24.2 0.0 copy-done.15
  24.2 0.0 copy-done.16
  24.2 0.0 copy-done.17
  24.2 3.1 %shard_map.98 = (bf16[16,176,256]{2,1,0:T(8,128)(2,1)S(1)}, bf16[16,176,256]{2,1,0:T(8,128)(2,1)S(1)}, f32[144,128]{1,0:T(8,128)S(1)}) custom-call(s32[4]{0:T(128)S(1)} %copy-done.14, s32[11]{0:T(128)S(1)} %copy-done.15, f32[1,256]{1,0:T(1,128)S(1)} %slice.14.refs_2_, bf16[2,256,256]{2,1,0:T(8,128)(2,1)S(1)} %copy-done.16, ...), custom_call_target="tpu_custom_call" | custom-call | flops 5000000000 | bytes 6000000 | tf_op jit(solution)/shard_map/pallas_call | solution.py:223
  27.3 0.0 collective-permute-done.3.refs_6_
  27.3 0.4 collective-permute-start.2
  27.7 0.0 collective-permute-done.4.refs_7_
  27.7 0.0 collective-permute-done.5.refs_8_
  27.7 2.4 %shard_map.99 = (bf16[16,176,128]{2,1,0:T(8,128)(2,1)S(1)}, bf16[16,176,128]{2,1,0:T(8,128)(2,1)S(1)}, f32[144,128]{1,0:T(8,128)S(1)}) custom-call(s32[4]{0:T(128)S(1)} %copy-done.14, s32[11]{0:T(128)S(1)} %copy-done.15, f32[1,128]{1,0:T(1,128)S(1)} %get-tuple-element.50.refs_2_, bf16[2,256,256]{2,1,0:T(8,128)(2,1)S(1)} %copy-done.16, ...), custom_call_target="tpu_custom_call" | custom-call | flops 2500000000 | bytes 6000000 | tf_op jit(solution)/shard_map/pallas_call | solution.py:223
  30.1 0.0 copy-start.1
  30.1 0.9 copy-done.1
  31.0 0.0 copy-start.3
  31.0 0.9 copy-done.3
  31.9 0.0 collective-permute-done.refs_6_
  31.9 0.0 collective-permute-done.1.refs_7_
  31.9 0.0 collective-permute-done.2.refs_8_
  31.9 0.0 copy-start.9
  31.9 3.1 %shard_map.100 = (bf16[16,176,128]{2,1,0:T(8,128)(2,1)S(1)}, bf16[16,176,128]{2,1,0:T(8,128)(2,1)S(1)}, f32[144,128]{1,0:T(8,128)}) custom-call(s32[4]{0:T(128)S(1)} %copy-done.14, s32[11]{0:T(128)S(1)} %copy-done.15, f32[1,128]{1,0:T(1,128)S(1)} %get-tuple-element.51.refs_2_, bf16[2,256,256]{2,1,0:T(8,128)(2,1)S(1)} %copy-done.16, ...), custom_call_target="tpu_custom_call" | custom-call | flops 2500000000 | bytes 6000000 | tf_op jit(solution)/shard_map/pallas_call | solution.py:223
  35.0 0.9 copy-done.5
  35.9 0.9 copy-done.7
  36.8 0.0 all-reduce.2.cloned.1.call-update
  36.8 119.9 %all-reduce.2.cloned.1.call-done.refs_0_ = f32[144,128]{1,0:T(8,128)} async-done(((f32[144,128]{1,0:T(8,128)}), f32[144,128]{1,0:T(8,128)}) %all-reduce.2.cloned.1.call-update) | async-done | bytes 73744 | tf_op jit(solution)/shard_map/psum | solution.py:431
  156.7 0.0 copy-start.12
  156.7 0.9 copy-done.12
  157.6 5.3 %shard_map.101 = (f32[3,128,128]{2,1,0:T(8,128)S(1)}, f32[11,11,2,16]{3,2,1,0:T(2,128)}) custom-call(f32[144,128]{1,0:T(8,128)S(1)} %copy-done.12), custom_call_target="tpu_custom_call" | custom-call | tf_op jit(solution)/shard_map/pallas_call | solution.py:338
  162.9 0.0 copy-done.9
  162.9 0.0 copy-start.2
  162.9 1.1 copy-done.2
  164.0 0.0 copy-start.4
  164.0 1.1 copy-done.4
  165.1 0.0 copy-start.6
  165.1 1.1 copy-done.6
  166.2 1.1 copy-done.8
  167.4 6.1 %shard_map.102 = bf16[2,11,128,512]{3,2,1,0:T(8,128)(2,1)} custom-call(f32[3,128,128]{2,1,0:T(8,128)S(1)} %get-tuple-element.40.stack_ref, bf16[8,128,176]{2,1,0:T(8,128)(2,1)S(1)} %copy-done.9, bf16[16,176,256]{2,1,0:T(8,128)(2,1)S(1)} %get-tuple-element.41.refs_0_, bf16[16,176,128]{2,1,0:T(8,128)(2,1)S(1)} %copy-done.2, ...), custom_call_target="tpu_custom_call" | custom-call | tf_op jit(solution)/shard_map/pallas_call | solution.py:385
  (5 shorter events, 0.0 us)
Async XLA Ops:
  7.2 149.5 %all-reduce.2.cloned.1.call-start = ((), (), s32[]{:S(2)}) async-start(), calls=%async_computation | async-start | bytes 147456 | tf_op jit(solution)/shard_map/psum | solution.py:431
  9.8 9.3 %copy-start.18 = (f32[512]{0:T(512)S(1)}, f32[512]{0:T(512)}, u32[]{:S(2)}) copy-start(f32[512]{0:T(512)} %param.9) | copy-start | bytes 6148
  9.8 10.3 %collective-permute-start.6 = (bf16[384,256]{1,0:T(8,128)(2,1)}, bf16[384,256]{1,0:T(8,128)(2,1)S(1)}, u32[]{:S(2)}, u32[]{:S(2)}) collective-permute-start(bf16[384,256]{1,0:T(8,128)(2,1)} %get-tuple-element.34), channel_id=1, source_target_pairs={{0,8},{8,0},{16,24},{24,16},{1,9},{9,1},{17,25},{25,17},{2,10},{10... | collective-permute-start | bytes 589832 | tf_op jit(solution)/shard_map/ppermute | solution.py:401
  10.4 9.9 %collective-permute-start.7 = (bf16[384,256]{1,0:T(8,128)(2,1)}, bf16[384,256]{1,0:T(8,128)(2,1)S(1)}, u32[]{:S(2)}, u32[]{:S(2)}) collective-permute-start(bf16[384,256]{1,0:T(8,128)(2,1)} %get-tuple-element.35), channel_id=1, source_target_pairs={{0,16},{8,24},{16,0},{24,8},{1,17},{9,25},{17,1},{25,9},{2,18},{10... | collective-permute-start | bytes 589832 | tf_op jit(solution)/shard_map/ppermute | solution.py:401
  12.9 9.8 %collective-permute-start.8 = (bf16[384,256]{1,0:T(8,128)(2,1)}, bf16[384,256]{1,0:T(8,128)(2,1)S(1)}, u32[]{:S(2)}, u32[]{:S(2)}) collective-permute-start(bf16[384,256]{1,0:T(8,128)(2,1)} %get-tuple-element.36), channel_id=1, source_target_pairs={{0,24},{8,16},{16,8},{24,0},{1,25},{9,17},{17,9},{25,1},{2,26},{10... | collective-permute-start | bytes 589832 | tf_op jit(solution)/shard_map/ppermute | solution.py:401
  13.0 1.4 copy-start
  14.4 0.9 copy-start.10
  15.4 0.7 copy-start.13
  16.0 8.2 %copy-start.11 = (bf16[384,256]{1,0:T(8,128)(2,1)S(1)}, bf16[384,256]{1,0:T(8,128)(2,1)}, u32[]{:S(2)}) copy-start(bf16[384,256]{1,0:T(8,128)(2,1)} %get-tuple-element.25.refs_0_.refs_5_) | copy-start | bytes 589828
  16.0 8.2 %copy-start.14 = (s32[4]{0:T(128)S(1)}, s32[4]{0:T(128)}, u32[]{:S(2)}) copy-start(s32[4]{0:T(128)} %refs_0_.5) | copy-start | bytes 52
  16.0 8.2 %copy-start.15 = (s32[11]{0:T(128)S(1)}, s32[11]{0:T(128)}, u32[]{:S(2)}) copy-start(s32[11]{0:T(128)} %refs_1_.5) | copy-start | bytes 136
  16.0 8.2 %copy-start.16 = (bf16[2,256,256]{2,1,0:T(8,128)(2,1)S(1)}, bf16[2,256,256]{2,1,0:T(8,128)(2,1)}, u32[]{:S(2)}) copy-start(bf16[2,256,256]{2,1,0:T(8,128)(2,1)} %constant.6.clone.refs_3_) | copy-start | bytes 786436
  16.0 8.2 %copy-start.17 = (bf16[11,24,256]{2,1,0:T(8,128)(2,1)S(1)}, bf16[11,24,256]{2,1,0:T(8,128)(2,1)}, u32[]{:S(2)}) copy-start(bf16[11,24,256]{2,1,0:T(8,128)(2,1)} %constant.7.clone.refs_4_) | copy-start | bytes 405508
  17.0 10.3 %collective-permute-start.3 = (bf16[384,128]{1,0:T(8,128)(2,1)S(1)}, bf16[384,128]{1,0:T(8,128)(2,1)S(1)}, u32[]{:S(2)}, u32[]{:S(2)}) collective-permute-start(bf16[384,128]{1,0:T(8,128)(2,1)S(1)} %get-tuple-element.31), channel_id=1, source_target_pairs={{0,8},{8,0},{16,24},{24,16},{1,9},{9,1},{17,25},{25,17},{2,10},{10... | collective-permute-start | bytes 294920 | tf_op jit(solution)/shard_map/ppermute | solution.py:401
  17.2 10.5 %collective-permute-start.4 = (bf16[384,128]{1,0:T(8,128)(2,1)S(1)}, bf16[384,128]{1,0:T(8,128)(2,1)S(1)}, u32[]{:S(2)}, u32[]{:S(2)}) collective-permute-start(bf16[384,128]{1,0:T(8,128)(2,1)S(1)} %get-tuple-element.32), channel_id=1, source_target_pairs={{0,16},{8,24},{16,0},{24,8},{1,17},{9,25},{17,1},{25,9},{2,18},{10... | collective-permute-start | bytes 294920 | tf_op jit(solution)/shard_map/ppermute | solution.py:401
  20.1 7.5 %collective-permute-start.5 = (bf16[384,128]{1,0:T(8,128)(2,1)S(1)}, bf16[384,128]{1,0:T(8,128)(2,1)S(1)}, u32[]{:S(2)}, u32[]{:S(2)}) collective-permute-start(bf16[384,128]{1,0:T(8,128)(2,1)S(1)} %get-tuple-element.33), channel_id=1, source_target_pairs={{0,24},{8,16},{16,8},{24,0},{1,25},{9,17},{17,9},{25,1},{2,26},{10... | collective-permute-start | bytes 294920 | tf_op jit(solution)/shard_map/ppermute | solution.py:401
  20.2 11.7 %collective-permute-start = (bf16[384,128]{1,0:T(8,128)(2,1)S(1)}, bf16[384,128]{1,0:T(8,128)(2,1)S(1)}, u32[]{:S(2)}, u32[]{:S(2)}) collective-permute-start(bf16[384,128]{1,0:T(8,128)(2,1)S(1)} %get-tuple-element.28), channel_id=1, source_target_pairs={{0,8},{8,0},{16,24},{24,16},{1,9},{9,1},{17,25},{25,17},{2,10},{10... | collective-permute-start | bytes 294920 | tf_op jit(solution)/shard_map/ppermute | solution.py:401
  22.7 9.2 %collective-permute-start.1 = (bf16[384,128]{1,0:T(8,128)(2,1)S(1)}, bf16[384,128]{1,0:T(8,128)(2,1)S(1)}, u32[]{:S(2)}, u32[]{:S(2)}) collective-permute-start(bf16[384,128]{1,0:T(8,128)(2,1)S(1)} %get-tuple-element.29), channel_id=1, source_target_pairs={{0,16},{8,24},{16,0},{24,8},{1,17},{9,25},{17,1},{25,9},{2,18},{10... | collective-permute-start | bytes 294920 | tf_op jit(solution)/shard_map/ppermute | solution.py:401
  27.3 4.6 %collective-permute-start.2 = (bf16[384,128]{1,0:T(8,128)(2,1)S(1)}, bf16[384,128]{1,0:T(8,128)(2,1)S(1)}, u32[]{:S(2)}, u32[]{:S(2)}) collective-permute-start(bf16[384,128]{1,0:T(8,128)(2,1)S(1)} %get-tuple-element.30), channel_id=1, source_target_pairs={{0,24},{8,16},{16,8},{24,0},{1,25},{9,17},{17,9},{25,1},{2,26},{10... | collective-permute-start | bytes 294920 | tf_op jit(solution)/shard_map/ppermute | solution.py:401
  30.1 0.9 copy-start.1
  31.0 0.9 copy-start.3
  31.9 131.0 %copy-start.9 = (bf16[8,128,176]{2,1,0:T(8,128)(2,1)S(1)}, bf16[8,128,176]{2,1,0:T(8,128)(2,1)}, u32[]{:S(2)}) copy-start(bf16[8,128,176]{2,1,0:T(8,128)(2,1)} %constant.8.clone.spread_ref) | copy-start | bytes 1081348
  35.0 0.9 copy-start.5
  35.9 0.9 copy-start.7
  156.7 0.9 copy-start.12
  162.9 1.1 copy-start.2
  164.0 1.1 copy-start.4
  165.1 1.1 copy-start.6
  166.2 1.1 copy-start.8
Sparse Core Ops, SparseCore 0:
  36.9 119.7 all-reduce.1

commit v2 on v1

--- a/solution.py
+++ b/solution.py
@@ -17,9 +17,7 @@
 SUB = 8
 HALF_ROWS = NBLK * SUB
 GROUPS = NFREQ // SUB
-PAIRS = (NBLK + 1) // 2
-PAIR_ROWS = 24
-PACKED = PAIRS * PAIR_ROWS
+PACKED = 128
 STACK = 4
 FIRST_LIMIT = 64 * 2**20
 BF16 = jnp.bfloat16
@@ -39,23 +37,19 @@
 
 def packed_rows():
     rows = {}
-    for pair in range(PAIRS):
-        row = pair * PAIR_ROWS
-        for a in sorted({pair, NBLK - 1 - pair}):
-            for e in range(a, NBLK):
-                rows[0, a, e] = row
-                row += 1
-            for e in range(a + 1, NBLK):
-                rows[1, a, e] = row
-                row += 1
+    for a in range(NBLK):
+        for e in range(a, NBLK):
+            rows[0, a, e] = len(rows)
+        for e in range(a + 1, NBLK):
+            rows[1, a, e] = len(rows)
     return rows
 
 
 def pick_table():
-    pick = np.zeros((NBLK, PAIR_ROWS, 2 * LANE), np.float32)
+    pick = np.zeros((NBLK, PACKED, 2 * LANE), np.float32)
     for (part, a, e), row in packed_rows().items():
         start = part * LANE + e * SUB
-        pick[a, row % PAIR_ROWS, start : start + SUB] = 1.0
+        pick[a, row, start : start + SUB] = 1.0
     return pick.astype(jnp.bfloat16)
 
 
@@ -201,16 +195,13 @@
         imag = full[:HALF_ROWS, LANE:] - full[HALF_ROWS:, :LANE]
         masked[:, at, :LANE] = jnp.where(same, real, 0.0).reshape(NBLK, SUB, LANE)
         masked[:, at, LANE:] = jnp.where(same, imag, 0.0).reshape(NBLK, SUB, LANE)
-    for pair in range(PAIRS):
-        total = jnp.zeros((PAIR_ROWS, NFREQ), F32)
-        for a in sorted({pair, NBLK - 1 - pair}):
-            high, low = split(masked[a])
-            total = total + dot_nt(pick_ref[a], high) + dot_nt(pick_ref[a], low)
-        rows = slice(pair * PAIR_ROWS, (pair + 1) * PAIR_ROWS)
-        total = total * scale
-        if not first:
-            total = total + before_ref[rows, :]
-        packed_ref[rows, :] = total
+    total = jnp.zeros((PACKED, NFREQ), F32)
+    for a in range(NBLK):
+        total = total + dot_nt(pick_ref[a], masked[a].astype(BF16))
+    total = total * scale
+    if not first:
+        total = total + before_ref[...]
+    packed_ref[...] = total
 
 
 def gram_part(order, offsets, weights, tables, pieces, before, base, scale):
@@ -428,7 +419,13 @@
         highs.append(high)
         lows.append(low)
 
-    total = lax.psum(total, ("tm", "sx", "sy"))
+    axes = ("tm", "sx", "sy")
+    size = lanes * groups
+    total = total.reshape(size, -1, min(LANE, PACKED * NFREQ // size))
+    total = lax.all_to_all(total, axes, split_axis=0, concat_axis=0, tiled=True)
+    total = jnp.broadcast_to(jnp.sum(total, axis=0, keepdims=True), total.shape)
+    total = lax.all_to_all(total, axes, split_axis=0, concat_axis=0, tiled=True)
+    total = total.reshape(PACKED, NFREQ)
     stacks, gram = roots([total], NFREQ // groups)
     modes = mode_fields(stacks, jnp.asarray(spread_table()), highs, lows)
     modes = jnp.transpose(modes, (0, 2, 1, 3))[:, :, :, None, :]

time: 182 us -> 68.1 us (0.37)
  waiting for transfers between devices: 122 us -> 2.3 us
  blocking collectives: 0 us -> 22.1 us
  between operations: 14.1 us -> 0.8 us
    psum x1 -> x0, waiting for transfers between devices: 120 us -> none  [body(): total = lax.psum(total, ('tm', 'sx', 'sy'))]
    all_to_all x0 -> x2, blocking collectives: none -> 22.1 us  [body(): total = lax.all_to_all(total, axes, split_axis=0, concat_axis=0, tiled=True)]
    unnamed x38 -> x36, local copies, waits for them, and re-layouts: 11.9 us -> 10.9 us
  transfers between devices with their start and end apart: 10 -> 9, of which waited for: 2 -> 1; matrix products, arithmetic and copies ran while one was open for 0% -> 0% of each run, Pallas kernels for 4% -> 11%
where the time goes in v2:
time: 68.1 us; the launch traced here: 67.7 us
  Pallas kernels  24.1 us (35%)
  blocking collectives  22.1 us (32%)
  local copies, waits for them, and re-layouts  10.9 us (16%)
  starting transfers between devices  7.48 us (11%)
  waiting for transfers between devices  2.3 us (3%)
  between operations  0.8 us (1%)
    all_to_all x2, blocking collectives, body(): total = lax.all_to_all(total, axes, split_axis=0, concat_axis=0, tiled=True)  22.1 us
    unnamed x36, local copies, waits for them, and re-layouts  10.9 us
    pallas_call x3, Pallas kernels, gram_part(): pl.pallas_call(functools.partial(gram_kernel, lanes, scale, first), out_s...  8.21 us
    ppermute x9, starting transfers between devices, swap(): return lax.ppermute(x, axes, [(i, i ^ mask) for i in range(size)])  7.48 us
    pallas_call x1, Pallas kernels, mode_fields(): pl.pallas_call(functools.partial(mode_kernel, len(highs)), grid=(NFREQ //...  6.07 us
    pallas_call x1, Pallas kernels, roots(): pl.pallas_call(functools.partial(root_kernel, len(parts), share), out_sha...  5.25 us
    pallas_call x3, Pallas kernels, pack(): pl.pallas_call(functools.partial(pack_kernel, base, len(after)), out_shap...  4.53 us
    ppermute x9, waiting for transfers between devices, swap(): return lax.ppermute(x, axes, [(i, i ^ mask) for i in range(size)])  2.3 us
  transfers between devices with their start and end apart: 9, of which 1 were waited for; matrix products, arithmetic and copies ran while one was open for 0% of the time, Pallas kernels for 11%

profile of v2, /device:TPU:0, one launch (start us, length us, event | category | flops | bytes accessed | tf_op | source)
XLA Modules:
  0.0 67.7 jit_solution(9564749951216286707)
XLA Ops:
  0.6 2.6 %shard_map.95 = (bf16[384,256]{1,0:T(8,128)(2,1)}, bf16[384,256]{1,0:T(8,128)(2,1)}, bf16[384,256]{1,0:T(8,128)(2,1)}, bf16[384,256]{1,0:T(8,128)(2,1)}) custom-call(s32[1,4]{1,0:T(1,128)} %owner_hbm.5, bf16[384,4,512]{2,1,0:T(4,128)(2,1)} %x_hbm.5), custom_call_target="tpu_custom_call" | custom-call | flops 201326592 | bytes 1572864 | tf_op jit(solution)/shard_map/pallas_call | solution.py:136
  3.2 0.0 copy-start.17
  3.3 0.5 collective-permute-start.6
  3.8 2.6 %collective-permute-start.7 = (bf16[384,256]{1,0:T(8,128)(2,1)}, bf16[384,256]{1,0:T(8,128)(2,1)S(1)}, u32[]{:S(2)}, u32[]{:S(2)}) collective-permute-start(bf16[384,256]{1,0:T(8,128)(2,1)} %get-tuple-element.35), channel_id=1, source_target_pairs={{0,16},{8,24},{16,0},{24,8},{1,17},{9,25},{17,1},{25,9},{2,18},{10... | collective-permute-start | bytes 589832 | tf_op jit(solution)/shard_map/ppermute | solution.py:392
  6.4 0.1 collective-permute-start.8
  6.4 0.0 copy-start
  6.4 1.4 %copy-done = bf16[384,4,512]{2,1,0:T(4,128)(2,1)S(1)} copy-done((bf16[384,4,512]{2,1,0:T(4,128)(2,1)S(1)}, bf16[384,4,512]{2,1,0:T(4,128)(2,1)}, u32[]{:S(2)}) %copy-start) | copy-done | bytes 1572888
  7.9 0.0 copy-start.10
  7.9 0.9 %copy-done.10 = bf16[384,256]{1,0:T(8,128)(2,1)S(1)} copy-done((bf16[384,256]{1,0:T(8,128)(2,1)S(1)}, bf16[384,256]{1,0:T(8,128)(2,1)}, u32[]{:S(2)}) %copy-start.10) | copy-done | bytes 196632
  8.8 0.0 copy-start.12
  8.8 0.7 copy-done.12
  9.4 0.0 copy-start.11
  9.4 0.0 copy-start.13
  9.4 0.0 copy-start.14
  9.4 0.0 copy-start.15
  9.4 0.0 copy-start.16
  9.5 1.0 %shard_map.96 = (bf16[384,128]{1,0:T(8,128)(2,1)S(1)}, bf16[384,128]{1,0:T(8,128)(2,1)S(1)}, bf16[384,128]{1,0:T(8,128)(2,1)S(1)}, bf16[384,128]{1,0:T(8,128)(2,1)S(1)}) custom-call(s32[1,4]{1,0:T(1,128)S(1)} %copy-done.12, bf16[384,4,512]{2,1,0:T(4,128)(2,1)S(1)} %copy-done, bf16[384,256]{1,0:T(8,128)(2,1)S(1)} %copy-done.10), custom_call_target="tpu_custom_call" | custom-call | flops 100663296 | bytes 786432 | tf_op jit(solution)/shard_map/pallas_call | solution.py:136
  10.4 0.2 collective-permute-start.3
  10.6 1.9 %collective-permute-start.4 = (bf16[384,128]{1,0:T(8,128)(2,1)S(1)}, bf16[384,128]{1,0:T(8,128)(2,1)S(1)}, u32[]{:S(2)}, u32[]{:S(2)}) collective-permute-start(bf16[384,128]{1,0:T(8,128)(2,1)S(1)} %get-tuple-element.32), channel_id=1, source_target_pairs={{0,16},{8,24},{16,0},{24,8},{1,17},{9,25},{17,1},{25,9},{2,18},{10... | collective-permute-start | bytes 294920 | tf_op jit(solution)/shard_map/ppermute | solution.py:392
  12.6 0.0 copy-done.17
  12.6 1.0 %shard_map.97 = (bf16[384,128]{1,0:T(8,128)(2,1)S(1)}, bf16[384,128]{1,0:T(8,128)(2,1)S(1)}, bf16[384,128]{1,0:T(8,128)(2,1)S(1)}, bf16[384,128]{1,0:T(8,128)(2,1)S(1)}) custom-call(s32[1,4]{1,0:T(1,128)S(1)} %copy-done.12, bf16[384,4,512]{2,1,0:T(4,128)(2,1)S(1)} %copy-done, bf16[384,128]{1,0:T(8,128)(2,1)S(1)} %get-tuple-element.26.refs_0_.refs_5_), custom_call_target="tpu_custom_call" | custom-call | flops 100663296 | bytes 786432 | tf_op jit(solution)/shard_map/pallas_call | solution.py:136
  13.5 0.0 collective-permute-done.6.refs_6_
  13.6 0.1 collective-permute-start.5
  13.6 0.0 collective-permute-done.7.refs_7_
  13.6 0.2 collective-permute-start
  13.8 2.3 %collective-permute-done.8.refs_8_ = bf16[384,256]{1,0:T(8,128)(2,1)S(1)} collective-permute-done((bf16[384,256]{1,0:T(8,128)(2,1)}, bf16[384,256]{1,0:T(8,128)(2,1)S(1)}, u32[]{:S(2)}, u32[]{:S(2)}) %collective-permute-start.8) | collective-permute-done | bytes 196640 | tf_op jit(solution)/shard_map/ppermute | solution.py:392
  16.1 1.5 %collective-permute-start.1 = (bf16[384,128]{1,0:T(8,128)(2,1)S(1)}, bf16[384,128]{1,0:T(8,128)(2,1)S(1)}, u32[]{:S(2)}, u32[]{:S(2)}) collective-permute-start(bf16[384,128]{1,0:T(8,128)(2,1)S(1)} %get-tuple-element.29), channel_id=1, source_target_pairs={{0,16},{8,24},{16,0},{24,8},{1,17},{9,25},{17,1},{25,9},{2,18},{10... | collective-permute-start | bytes 294920 | tf_op jit(solution)/shard_map/ppermute | solution.py:392
  17.6 0.0 copy-done.11
  17.6 0.0 copy-done.13
  17.6 0.0 copy-done.14
  17.6 0.0 copy-done.15
  17.6 0.0 copy-done.16
  17.6 3.1 %shard_map.98 = (bf16[16,176,256]{2,1,0:T(8,128)(2,1)S(1)}, bf16[16,176,256]{2,1,0:T(8,128)(2,1)S(1)}, f32[128,128]{1,0:T(8,128)S(1)}) custom-call(s32[4]{0:T(128)S(1)} %copy-done.13, s32[11]{0:T(128)S(1)} %copy-done.14, f32[1,256]{1,0:T(1,128)S(1)} %slice.14.refs_2_, bf16[2,256,256]{2,1,0:T(8,128)(2,1)S(1)} %copy-done.16, ...), custom_call_target="tpu_custom_call" | custom-call | flops 5000000000 | bytes 6000000 | tf_op jit(solution)/shard_map/pallas_call | solution.py:214
  20.7 0.0 collective-permute-done.3.refs_6_
  20.7 0.4 collective-permute-start.2
  21.2 0.0 collective-permute-done.4.refs_7_
  21.2 0.0 collective-permute-done.5.refs_8_
  21.2 2.5 %shard_map.99 = (bf16[16,176,128]{2,1,0:T(8,128)(2,1)S(1)}, bf16[16,176,128]{2,1,0:T(8,128)(2,1)S(1)}, f32[128,128]{1,0:T(8,128)S(1)}) custom-call(s32[4]{0:T(128)S(1)} %copy-done.13, s32[11]{0:T(128)S(1)} %copy-done.14, f32[1,128]{1,0:T(1,128)S(1)} %get-tuple-element.50.refs_2_, bf16[2,256,256]{2,1,0:T(8,128)(2,1)S(1)} %copy-done.16, ...), custom_call_target="tpu_custom_call" | custom-call | flops 2500000000 | bytes 6000000 | tf_op jit(solution)/shard_map/pallas_call | solution.py:214
  23.7 0.0 copy-start.1
  23.7 0.8 %copy-done.1 = bf16[16,176,128]{2,1,0:T(8,128)(2,1)} copy-done((bf16[16,176,128]{2,1,0:T(8,128)(2,1)}, bf16[16,176,128]{2,1,0:T(8,128)(2,1)S(1)}, u32[]{:S(2)}) %copy-start.1) | copy-done | bytes 720920
  24.6 0.0 copy-start.3
  24.6 0.9 %copy-done.3 = bf16[16,176,128]{2,1,0:T(8,128)(2,1)} copy-done((bf16[16,176,128]{2,1,0:T(8,128)(2,1)}, bf16[16,176,128]{2,1,0:T(8,128)(2,1)S(1)}, u32[]{:S(2)}) %copy-start.3) | copy-done | bytes 720920
  25.5 0.0 collective-permute-done.refs_6_
  25.5 0.0 collective-permute-done.1.refs_7_
  25.5 0.0 collective-permute-done.2.refs_8_
  25.5 0.0 copy-start.9
  25.5 2.6 %shard_map.100 = (bf16[16,176,128]{2,1,0:T(8,128)(2,1)S(1)}, bf16[16,176,128]{2,1,0:T(8,128)(2,1)S(1)}, f32[128,128]{1,0:T(8,128)S(1)}) custom-call(s32[4]{0:T(128)S(1)} %copy-done.13, s32[11]{0:T(128)S(1)} %copy-done.14, f32[1,128]{1,0:T(1,128)S(1)} %get-tuple-element.51.refs_2_, bf16[2,256,256]{2,1,0:T(8,128)(2,1)S(1)} %copy-done.16, ...), custom_call_target="tpu_custom_call" | custom-call | flops 2500000000 | bytes 6000000 | tf_op jit(solution)/shard_map/pallas_call | solution.py:214
  28.1 0.0 copy-start.5
  28.1 0.9 %copy-done.5 = bf16[16,176,128]{2,1,0:T(8,128)(2,1)} copy-done((bf16[16,176,128]{2,1,0:T(8,128)(2,1)}, bf16[16,176,128]{2,1,0:T(8,128)(2,1)S(1)}, u32[]{:S(2)}) %copy-start.5) | copy-done | bytes 720920
  28.9 0.0 copy-start.7
  28.9 0.8 %copy-done.7 = bf16[16,176,128]{2,1,0:T(8,128)(2,1)} copy-done((bf16[16,176,128]{2,1,0:T(8,128)(2,1)}, bf16[16,176,128]{2,1,0:T(8,128)(2,1)S(1)}, u32[]{:S(2)}) %copy-start.7) | copy-done | bytes 720920
  29.8 13.1 %all_to_all.10 = f32[32,4,128]{2,1,0:T(4,128)S(1)} all-to-all(f32[32,4,128]{2,1,0:T(4,128)S(1)} %bitcast.10), channel_id=1, replica_groups=mesh['tm'=4,'sx'=4,'sy'=2] {'tm','sx','sy'}, dimensions={0} | all-to-all | bytes 131072 | tf_op jit(solution)/shard_map/all_to_all | solution.py:425
  43.0 9.0 %all_to_all.11 = f32[32,4,128]{2,1,0:T(4,128)S(1)} all-to-all(f32[32,4,128]{2,1,0:T(4,128)S(1)} %broadcast_in_dim.4), channel_id=1, replica_groups=mesh['tm'=4,'sx'=4,'sy'=2] {'tm','sx','sy'}, dimensions={0} | all-to-all | bytes 131072 | tf_op jit(solution)/shard_map/all_to_all | solution.py:427
  52.0 5.3 %shard_map.101 = (f32[3,128,128]{2,1,0:T(8,128)S(1)}, f32[11,11,2,16]{3,2,1,0:T(2,128)}) custom-call(f32[128,128]{1,0:T(8,128)S(1)} %bitcast.9), custom_call_target="tpu_custom_call" | custom-call | tf_op jit(solution)/shard_map/pallas_call | solution.py:329
  57.2 0.0 copy-done.9
  57.2 0.0 copy-start.2
  57.2 1.1 %copy-done.2 = bf16[16,176,128]{2,1,0:T(8,128)(2,1)S(1)} copy-done((bf16[16,176,128]{2,1,0:T(8,128)(2,1)S(1)}, bf16[16,176,128]{2,1,0:T(8,128)(2,1)}, u32[]{:S(2)}) %copy-start.2) | copy-done | bytes 720920
  58.3 0.0 copy-start.4
  58.3 1.1 %copy-done.4 = bf16[16,176,128]{2,1,0:T(8,128)(2,1)S(1)} copy-done((bf16[16,176,128]{2,1,0:T(8,128)(2,1)S(1)}, bf16[16,176,128]{2,1,0:T(8,128)(2,1)}, u32[]{:S(2)}) %copy-start.4) | copy-done | bytes 720920
  59.4 0.0 copy-start.6
  59.4 1.1 %copy-done.6 = bf16[16,176,128]{2,1,0:T(8,128)(2,1)S(1)} copy-done((bf16[16,176,128]{2,1,0:T(8,128)(2,1)S(1)}, bf16[16,176,128]{2,1,0:T(8,128)(2,1)}, u32[]{:S(2)}) %copy-start.6) | copy-done | bytes 720920
  60.6 0.0 copy-start.8
  60.6 1.1 %copy-done.8 = bf16[16,176,128]{2,1,0:T(8,128)(2,1)S(1)} copy-done((bf16[16,176,128]{2,1,0:T(8,128)(2,1)S(1)}, bf16[16,176,128]{2,1,0:T(8,128)(2,1)}, u32[]{:S(2)}) %copy-start.8) | copy-done | bytes 720920
  61.7 6.1 %shard_map.102 = bf16[2,11,128,512]{3,2,1,0:T(8,128)(2,1)} custom-call(f32[3,128,128]{2,1,0:T(8,128)S(1)} %get-tuple-element.40.stack_ref, bf16[8,128,176]{2,1,0:T(8,128)(2,1)S(1)} %copy-done.9, bf16[16,176,256]{2,1,0:T(8,128)(2,1)S(1)} %get-tuple-element.41.refs_0_, bf16[16,176,128]{2,1,0:T(8,128)(2,1)S(1)} %copy-done.2, ...), custom_call_target="tpu_custom_call" | custom-call | tf_op jit(solution)/shard_map/pallas_call | solution.py:376
  (4 shorter events, 0.1 us)
Async XLA Ops:
  3.2 9.3 %copy-start.17 = (f32[512]{0:T(512)S(1)}, f32[512]{0:T(512)}, u32[]{:S(2)}) copy-start(f32[512]{0:T(512)} %param.9) | copy-start | bytes 6148
  3.3 10.3 %collective-permute-start.6 = (bf16[384,256]{1,0:T(8,128)(2,1)}, bf16[384,256]{1,0:T(8,128)(2,1)S(1)}, u32[]{:S(2)}, u32[]{:S(2)}) collective-permute-start(bf16[384,256]{1,0:T(8,128)(2,1)} %get-tuple-element.34), channel_id=1, source_target_pairs={{0,8},{8,0},{16,24},{24,16},{1,9},{9,1},{17,25},{25,17},{2,10},{10... | collective-permute-start | bytes 589832 | tf_op jit(solution)/shard_map/ppermute | solution.py:392
  3.8 9.9 %collective-permute-start.7 = (bf16[384,256]{1,0:T(8,128)(2,1)}, bf16[384,256]{1,0:T(8,128)(2,1)S(1)}, u32[]{:S(2)}, u32[]{:S(2)}) collective-permute-start(bf16[384,256]{1,0:T(8,128)(2,1)} %get-tuple-element.35), channel_id=1, source_target_pairs={{0,16},{8,24},{16,0},{24,8},{1,17},{9,25},{17,1},{25,9},{2,18},{10... | collective-permute-start | bytes 589832 | tf_op jit(solution)/shard_map/ppermute | solution.py:392
  6.4 9.8 %collective-permute-start.8 = (bf16[384,256]{1,0:T(8,128)(2,1)}, bf16[384,256]{1,0:T(8,128)(2,1)S(1)}, u32[]{:S(2)}, u32[]{:S(2)}) collective-permute-start(bf16[384,256]{1,0:T(8,128)(2,1)} %get-tuple-element.36), channel_id=1, source_target_pairs={{0,24},{8,16},{16,8},{24,0},{1,25},{9,17},{17,9},{25,1},{2,26},{10... | collective-permute-start | bytes 589832 | tf_op jit(solution)/shard_map/ppermute | solution.py:392
  6.4 1.4 %copy-start = (bf16[384,4,512]{2,1,0:T(4,128)(2,1)S(1)}, bf16[384,4,512]{2,1,0:T(4,128)(2,1)}, u32[]{:S(2)}) copy-start(bf16[384,4,512]{2,1,0:T(4,128)(2,1)} %x_hbm.5) | copy-start | bytes 4718596
  7.9 0.9 %copy-start.10 = (bf16[384,256]{1,0:T(8,128)(2,1)S(1)}, bf16[384,256]{1,0:T(8,128)(2,1)}, u32[]{:S(2)}) copy-start(bf16[384,256]{1,0:T(8,128)(2,1)} %get-tuple-element.25.refs_0_.refs_5_) | copy-start | bytes 589828
  8.8 0.7 copy-start.12
  9.4 8.2 %copy-start.11 = (bf16[384,256]{1,0:T(8,128)(2,1)S(1)}, bf16[384,256]{1,0:T(8,128)(2,1)}, u32[]{:S(2)}) copy-start(bf16[384,256]{1,0:T(8,128)(2,1)} %get-tuple-element.25.refs_0_.refs_5_) | copy-start | bytes 589828
  9.4 8.2 %copy-start.13 = (s32[4]{0:T(128)S(1)}, s32[4]{0:T(128)}, u32[]{:S(2)}) copy-start(s32[4]{0:T(128)} %refs_0_.5) | copy-start | bytes 52
  9.4 8.2 %copy-start.14 = (s32[11]{0:T(128)S(1)}, s32[11]{0:T(128)}, u32[]{:S(2)}) copy-start(s32[11]{0:T(128)} %refs_1_.5) | copy-start | bytes 136
  9.4 8.2 %copy-start.15 = (bf16[11,128,256]{2,1,0:T(8,128)(2,1)S(1)}, bf16[11,128,256]{2,1,0:T(8,128)(2,1)}, u32[]{:S(2)}) copy-start(bf16[11,128,256]{2,1,0:T(8,128)(2,1)} %constant.9.clone.refs_4_) | copy-start | bytes 2162692
  9.4 8.2 %copy-start.16 = (bf16[2,256,256]{2,1,0:T(8,128)(2,1)S(1)}, bf16[2,256,256]{2,1,0:T(8,128)(2,1)}, u32[]{:S(2)}) copy-start(bf16[2,256,256]{2,1,0:T(8,128)(2,1)} %constant.8.clone.refs_3_) | copy-start | bytes 786436
  10.4 10.3 %collective-permute-start.3 = (bf16[384,128]{1,0:T(8,128)(2,1)S(1)}, bf16[384,128]{1,0:T(8,128)(2,1)S(1)}, u32[]{:S(2)}, u32[]{:S(2)}) collective-permute-start(bf16[384,128]{1,0:T(8,128)(2,1)S(1)} %get-tuple-element.31), channel_id=1, source_target_pairs={{0,8},{8,0},{16,24},{24,16},{1,9},{9,1},{17,25},{25,17},{2,10},{10... | collective-permute-start | bytes 294920 | tf_op jit(solution)/shard_map/ppermute | solution.py:392
  10.6 10.5 %collective-permute-start.4 = (bf16[384,128]{1,0:T(8,128)(2,1)S(1)}, bf16[384,128]{1,0:T(8,128)(2,1)S(1)}, u32[]{:S(2)}, u32[]{:S(2)}) collective-permute-start(bf16[384,128]{1,0:T(8,128)(2,1)S(1)} %get-tuple-element.32), channel_id=1, source_target_pairs={{0,16},{8,24},{16,0},{24,8},{1,17},{9,25},{17,1},{25,9},{2,18},{10... | collective-permute-start | bytes 294920 | tf_op jit(solution)/shard_map/ppermute | solution.py:392
  13.6 7.6 %collective-permute-start.5 = (bf16[384,128]{1,0:T(8,128)(2,1)S(1)}, bf16[384,128]{1,0:T(8,128)(2,1)S(1)}, u32[]{:S(2)}, u32[]{:S(2)}) collective-permute-start(bf16[384,128]{1,0:T(8,128)(2,1)S(1)} %get-tuple-element.33), channel_id=1, source_target_pairs={{0,24},{8,16},{16,8},{24,0},{1,25},{9,17},{17,9},{25,1},{2,26},{10... | collective-permute-start | bytes 294920 | tf_op jit(solution)/shard_map/ppermute | solution.py:392
  13.6 11.8 %collective-permute-start = (bf16[384,128]{1,0:T(8,128)(2,1)S(1)}, bf16[384,128]{1,0:T(8,128)(2,1)S(1)}, u32[]{:S(2)}, u32[]{:S(2)}) collective-permute-start(bf16[384,128]{1,0:T(8,128)(2,1)S(1)} %get-tuple-element.28), channel_id=1, source_target_pairs={{0,8},{8,0},{16,24},{24,16},{1,9},{9,1},{17,25},{25,17},{2,10},{10... | collective-permute-start | bytes 294920 | tf_op jit(solution)/shard_map/ppermute | solution.py:392
  16.1 9.4 %collective-permute-start.1 = (bf16[384,128]{1,0:T(8,128)(2,1)S(1)}, bf16[384,128]{1,0:T(8,128)(2,1)S(1)}, u32[]{:S(2)}, u32[]{:S(2)}) collective-permute-start(bf16[384,128]{1,0:T(8,128)(2,1)S(1)} %get-tuple-element.29), channel_id=1, source_target_pairs={{0,16},{8,24},{16,0},{24,8},{1,17},{9,25},{17,1},{25,9},{2,18},{10... | collective-permute-start | bytes 294920 | tf_op jit(solution)/shard_map/ppermute | solution.py:392
  20.7 4.7 %collective-permute-start.2 = (bf16[384,128]{1,0:T(8,128)(2,1)S(1)}, bf16[384,128]{1,0:T(8,128)(2,1)S(1)}, u32[]{:S(2)}, u32[]{:S(2)}) collective-permute-start(bf16[384,128]{1,0:T(8,128)(2,1)S(1)} %get-tuple-element.30), channel_id=1, source_target_pairs={{0,24},{8,16},{16,8},{24,0},{1,25},{9,17},{17,9},{25,1},{2,26},{10... | collective-permute-start | bytes 294920 | tf_op jit(solution)/shard_map/ppermute | solution.py:392
  23.7 0.9 %copy-start.1 = (bf16[16,176,128]{2,1,0:T(8,128)(2,1)}, bf16[16,176,128]{2,1,0:T(8,128)(2,1)S(1)}, u32[]{:S(2)}) copy-start(bf16[16,176,128]{2,1,0:T(8,128)(2,1)S(1)} %get-tuple-element.42.refs_1_) | copy-start | bytes 2162692
  24.6 0.9 %copy-start.3 = (bf16[16,176,128]{2,1,0:T(8,128)(2,1)}, bf16[16,176,128]{2,1,0:T(8,128)(2,1)S(1)}, u32[]{:S(2)}) copy-start(bf16[16,176,128]{2,1,0:T(8,128)(2,1)S(1)} %get-tuple-element.45.refs_4_) | copy-start | bytes 2162692
  25.5 31.7 %copy-start.9 = (bf16[8,128,176]{2,1,0:T(8,128)(2,1)S(1)}, bf16[8,128,176]{2,1,0:T(8,128)(2,1)}, u32[]{:S(2)}) copy-start(bf16[8,128,176]{2,1,0:T(8,128)(2,1)} %constant.10.clone.spread_ref) | copy-start | bytes 1081348
  28.1 0.9 %copy-start.5 = (bf16[16,176,128]{2,1,0:T(8,128)(2,1)}, bf16[16,176,128]{2,1,0:T(8,128)(2,1)S(1)}, u32[]{:S(2)}) copy-start(bf16[16,176,128]{2,1,0:T(8,128)(2,1)S(1)} %get-tuple-element.43.refs_2_) | copy-start | bytes 2162692
  28.9 0.9 %copy-start.7 = (bf16[16,176,128]{2,1,0:T(8,128)(2,1)}, bf16[16,176,128]{2,1,0:T(8,128)(2,1)S(1)}, u32[]{:S(2)}) copy-start(bf16[16,176,128]{2,1,0:T(8,128)(2,1)S(1)} %get-tuple-element.46.refs_5_) | copy-start | bytes 2162692
  57.2 1.1 %copy-start.2 = (bf16[16,176,128]{2,1,0:T(8,128)(2,1)S(1)}, bf16[16,176,128]{2,1,0:T(8,128)(2,1)}, u32[]{:S(2)}) copy-start(bf16[16,176,128]{2,1,0:T(8,128)(2,1)} %copy-done.1) | copy-start | bytes 2162692
  58.3 1.1 %copy-start.4 = (bf16[16,176,128]{2,1,0:T(8,128)(2,1)S(1)}, bf16[16,176,128]{2,1,0:T(8,128)(2,1)}, u32[]{:S(2)}) copy-start(bf16[16,176,128]{2,1,0:T(8,128)(2,1)} %copy-done.3) | copy-start | bytes 2162692
  59.4 1.1 %copy-start.6 = (bf16[16,176,128]{2,1,0:T(8,128)(2,1)S(1)}, bf16[16,176,128]{2,1,0:T(8,128)(2,1)}, u32[]{:S(2)}) copy-start(bf16[16,176,128]{2,1,0:T(8,128)(2,1)} %copy-done.5) | copy-start | bytes 2162692
  60.6 1.1 %copy-start.8 = (bf16[16,176,128]{2,1,0:T(8,128)(2,1)S(1)}, bf16[16,176,128]{2,1,0:T(8,128)(2,1)}, u32[]{:S(2)}) copy-start(bf16[16,176,128]{2,1,0:T(8,128)(2,1)} %copy-done.7) | copy-start | bytes 2162692

commit v3 on v2

v3 whole, which is shorter than its diff:
```python
import functools
import math

import jax
import jax.numpy as jnp
import numpy as np
from jax import lax
from jax.experimental import pallas as pl
from jax.experimental.pallas import tpu as pltpu
from jax.sharding import PartitionSpec as P

NFFT = 256
ROOT_STEPS = 5
NFREQ = 128
NBLK = 11
LANE = 128
SUB = 8
HALF_ROWS = NBLK * SUB
GROUPS = NFREQ // SUB
PACKED = 128
STACK = 4
CORNER = NBLK - SUB
WIDE = 2 * LANE
FIRST_LIMIT = 64 * 2**20
SECOND_LIMIT = FIRST_LIMIT - 1450 * 2**10
BF16 = jnp.bfloat16
F32 = jnp.float32


def fourier_tables():
    n = np.arange(NFFT)
    k = np.arange(NFREQ)
    angles = 2.0 * np.pi * ((k[:, None] * n[None, :]) % NFFT) / NFFT
    scaled = (0.5 - 0.5 * np.cos(2.0 * np.pi * n / NFFT)) / math.sqrt(0.375 * NFFT)
    table = np.concatenate([np.cos(angles) * scaled, -np.sin(angles) * scaled], axis=0)
    high = table.astype(jnp.bfloat16)
    low = (table - high.astype(np.float64)).astype(jnp.bfloat16)
    return np.stack([high, low])


def packed_rows():
    rows = {}
    for a in range(NBLK):
        for e in range(a, NBLK):
            rows[0, a, e] = len(rows)
        for e in range(a + 1, NBLK):
            rows[1, a, e] = len(rows)
    return rows


ROWS = packed_rows()


def pick_table():
    pick = np.zeros((NBLK, 2, LANE, PACKED), np.float32)
    for (part, a, e), row in ROWS.items():
        pick[a, part, e * SUB : (e + 1) * SUB, row] = 1.0
    return pick.reshape(NBLK * WIDE, PACKED).astype(jnp.bfloat16)


def spread_table():
    spread = np.zeros((STACK, 2, LANE, 2 * HALF_ROWS), np.float32)
    for m in range(STACK):
        for b in range(NBLK):
            real = m * 32 + b
            imag = m * 32 + 16 + b
            first = slice(b * SUB, b * SUB + SUB)
            second = slice(HALF_ROWS + b * SUB, HALF_ROWS + b * SUB + SUB)
            spread[m, 0, real, first] = 1.0
            spread[m, 0, imag, second] = 1.0
            spread[m, 1, imag, first] = -1.0
            spread[m, 1, real, second] = 1.0
    spread = np.concatenate([spread, spread], axis=2)
    return spread.reshape(STACK * 2, WIDE, 2 * HALF_ROWS).astype(jnp.bfloat16)


def split(x):
    high = x.astype(BF16)
    return high, (x - high.astype(F32)).astype(BF16)


def dot(a, b):
    return jnp.dot(a, b, preferred_element_type=F32)


def dot_nt(a, b):
    return lax.dot_general(a, b, (((1,), (1,)), ((), ())), preferred_element_type=F32)


def spec(shape):
    return pl.BlockSpec(shape, lambda *_: (0,) * len(shape))


SMEM = pl.BlockSpec(memory_space=pltpu.SMEM)
VMEM = pl.BlockSpec(memory_space=pltpu.VMEM)
HBM = pl.BlockSpec(memory_space=pltpu.HBM)


def lane_pick(owner, lanes):
    me = lax.axis_index("tm")
    rows = WIDE // lanes
    out_row = lax.broadcasted_iota(jnp.int32, (WIDE, WIDE), 0)
    in_row = lax.broadcasted_iota(jnp.int32, (WIDE, WIDE), 1)
    row_of = (out_row % rows) * lanes
    for d in range(lanes):
        slot = me ^ d
        source = jnp.int32(0)
        for lane in range(lanes):
            source = source + jnp.where(owner[0, lane] == slot, lane, 0)
        row_of = jnp.where(out_row // rows == d, row_of + source, row_of)
    return jnp.where(in_row == row_of, 1.0, 0.0).astype(BF16)


def pack_kernel(base, parts, first, table_hbm, x_hbm, *refs):
    lanes = x_hbm.shape[1]
    out_refs = refs[:lanes]
    if first:
        pick, table, x_ref, table_sem, x_sem = refs[lanes:]
    else:
        pick, x_ref, table_sem, x_sem = refs[lanes:]
        table = pick
    steps, _, width = x_ref.shape
    part = steps // parts
    table_copy = pltpu.make_async_copy(table_hbm, table, table_sem)
    table_copy.start()
    copies = []
    for i in range(parts):
        at = slice(i * part, (i + 1) * part)
        source = x_hbm.at[at, :, base : base + width]
        copies.append(pltpu.make_async_copy(source, x_ref.at[at], x_sem.at[i]))
        copies[-1].start()
    table_copy.wait()
    if first:
        pick[...] = lane_pick(table, lanes)
    rows = WIDE // lanes
    for i in range(steps // rows):
        if i * rows % part == 0:
            copies[i * rows // part].wait()
        at = slice(i * rows, (i + 1) * rows)
        y = dot(pick[...], x_ref[at].reshape(WIDE, width)).astype(BF16)
        for d in range(lanes):
            out_refs[d][at, :] = y[d * rows : (d + 1) * rows]


def pack(table, snapshots, base, width, first):
    steps, lanes, _ = snapshots.shape
    parts = math.gcd(steps * lanes // WIDE, 3)
    outs = [jax.ShapeDtypeStruct((steps, width), BF16)] * lanes
    scratch = [
        pltpu.VMEM((steps, lanes, width), BF16),
        pltpu.SemaphoreType.DMA,
        pltpu.SemaphoreType.DMA((parts,)),
    ]
    if first:
        outs.append(jax.ShapeDtypeStruct((WIDE, WIDE), BF16))
        scratch = [pltpu.SMEM(table.shape, jnp.int32)] + scratch
    else:
        scratch = [pltpu.VMEM(table.shape, BF16)] + scratch
    return pl.pallas_call(
        functools.partial(pack_kernel, base, parts, first),
        out_shape=outs,
        in_specs=[HBM] * 2,
        out_specs=[VMEM] * len(outs),
        scratch_shapes=scratch,
        compiler_params=pltpu.CompilerParams(
            vmem_limit_bytes=FIRST_LIMIT if first else SECOND_LIMIT
        ),
        cost_estimate=pl.CostEstimate(
            flops=2 * WIDE * steps * lanes * width,
            bytes_accessed=4 * steps * lanes * width,
            transcendentals=0,
        ),
    )(table, snapshots)


def fill_record(order_ref, pieces, record, factor):
    steps, width = pieces[0].shape
    me = lax.axis_index("tm")
    for d, piece in enumerate(pieces):
        partner = me ^ (len(pieces) - d if d else 0)
        start = pl.multiple_of(order_ref[partner] * steps, steps)
        for c in range(width // LANE):
            cols = slice(c * LANE, (c + 1) * LANE)
            part = piece[:, cols].astype(F32)
            record[c, pl.ds(start, steps), :] = part if factor is None else part * factor[:, cols]


def transform(offsets_ref, f_ref, record, s_ref):
    for i in range(NBLK):
        x = [record[c, pl.ds(offsets_ref[i], NFFT), :].astype(BF16) for c in range(record.shape[0])]
        x = jnp.concatenate(x, axis=1)
        y = dot(f_ref[0], x) + dot(f_ref[1], x)
        s_ref[i] = y[:NFREQ]
        s_ref[NBLK + i] = y[NFREQ:]


def gram_kernel(lanes, scale, first, order_ref, offsets_ref, w_ref, f_ref, pick_ref, *refs):
    pieces = refs[:lanes]
    rest = refs[lanes:]
    if not first:
        before_ref, _, *rest = rest
    packed_ref, record, s_ref, masked = rest
    fill_record(order_ref, pieces, record, jnp.sqrt(w_ref[...]))
    transform(offsets_ref, f_ref, record, s_ref)
    row = lax.broadcasted_iota(jnp.int32, (HALF_ROWS, LANE), 0)
    col = lax.broadcasted_iota(jnp.int32, (HALF_ROWS, LANE), 1)
    same = row % SUB == col % SUB
    pad = jnp.zeros((LANE - HALF_ROWS, s_ref.shape[2]), F32)
    for g in range(GROUPS):
        at = slice(g * SUB, (g + 1) * SUB)
        s = s_ref[:, at, :].reshape(2 * HALF_ROWS, -1)
        other = jnp.concatenate([s[:HALF_ROWS], pad, s[HALF_ROWS:], pad], axis=0)
        full = dot_nt(s.astype(BF16), other.astype(BF16))
        real = full[:HALF_ROWS, :LANE] + full[HALF_ROWS:, LANE:]
        imag = full[:HALF_ROWS, LANE:] - full[HALF_ROWS:, :LANE]
        real = jnp.where(same, real, 0.0)
        imag = jnp.where(same, imag, 0.0)
        for a in range(NBLK):
            rows = slice(a * SUB, (a + 1) * SUB)
            masked[at, a * WIDE : a * WIDE + LANE] = real[rows]
            masked[at, a * WIDE + LANE : (a + 1) * WIDE] = imag[rows]
    total = dot(masked[...].astype(BF16), pick_ref[...]).T * scale
    if not first:
        total = total + before_ref[...]
    packed_ref[...] = total.astype(packed_ref.dtype)


def gram_part(order, offsets, weights, tables, pieces, before, scale):
    lanes = len(pieces)
    steps, width = pieces[0].shape
    first = not before
    args = [order, offsets, weights, *tables, *pieces, *before]
    return pl.pallas_call(
        functools.partial(gram_kernel, lanes, scale, first),
        out_shape=jax.ShapeDtypeStruct((PACKED, NFREQ), F32 if first else BF16),
        in_specs=[SMEM, SMEM] + [VMEM] * (len(args) - 2),
        out_specs=VMEM,
        scratch_shapes=[
            pltpu.VMEM((width // LANE, lanes * steps, LANE), F32),
            pltpu.VMEM((2 * NBLK, NFREQ, width), F32),
            pltpu.VMEM((NFREQ, NBLK * WIDE), F32),
        ],
        compiler_params=pltpu.CompilerParams(vmem_limit_bytes=32 * 2**20),
        cost_estimate=pl.CostEstimate(
            flops=25 * 10**8, bytes_accessed=3 * 10**6, transcendentals=0
        ),
    )(*args)


def spectrum_kernel(lanes, order_ref, offsets_ref, f_ref, *refs):
    high_ref, low_ref, record, s_ref = refs[-4:]
    fill_record(order_ref, refs[:lanes], record, None)
    transform(offsets_ref, f_ref, record, s_ref)
    for g in range(GROUPS):
        s = s_ref[:, g * SUB : (g + 1) * SUB, :].reshape(2 * HALF_ROWS, -1)
        high_ref[g], low_ref[g] = split(s)


def spectrum(order, offsets, fourier, pieces, after):
    lanes = len(pieces)
    steps, width = pieces[0].shape
    args = [order, offsets, fourier, *pieces, *after]
    part = jax.ShapeDtypeStruct((GROUPS, 2 * HALF_ROWS, width), BF16)
    return pl.pallas_call(
        functools.partial(spectrum_kernel, lanes),
        out_shape=[part, part],
        in_specs=[SMEM, SMEM] + [VMEM] * (len(args) - 2),
        out_specs=[VMEM, VMEM],
        scratch_shapes=[
            pltpu.VMEM((width // LANE, lanes * steps, LANE), F32),
            pltpu.VMEM((2 * NBLK, NFREQ, width), F32),
        ],
        compiler_params=pltpu.CompilerParams(vmem_limit_bytes=32 * 2**20),
        cost_estimate=pl.CostEstimate(
            flops=25 * 10**8, bytes_accessed=3 * 10**6, transcendentals=0
        ),
    )(*args)


class Hermitian:
    def __init__(self, main, corner):
        self.main = main
        self.corner = corner

    def entry(self, a, e):
        if e < SUB:
            return self.main[0, a, pl.ds(e, 1), :], self.main[1, a, pl.ds(e, 1), :], 1
        if a < SUB:
            return self.main[0, e, pl.ds(a, 1), :], self.main[1, e, pl.ds(a, 1), :], -1
        at = pl.ds(e - SUB, 1)
        return self.corner[0, a - SUB, at, :], self.corner[1, a - SUB, at, :], 1

    def put(self, a, e, real, imag):
        if e < SUB:
            self.main[0, a, pl.ds(e, 1), :] = real
            self.main[1, a, pl.ds(e, 1), :] = imag
        elif a >= SUB:
            at = pl.ds(e - SUB, 1)
            self.corner[0, a - SUB, at, :] = real
            self.corner[1, a - SUB, at, :] = imag


def product(x, y, out, diagonal=0.0, factor=1.0):
    sub = lax.broadcasted_iota(jnp.int32, (SUB, NFREQ), 0)
    yr = [y.main[0, b] for b in range(NBLK)]
    yi = [y.main[1, b] for b in range(NBLK)]
    for a in range(NBLK):
        real = imag = None
        for b in range(NBLK):
            pr, pi, sign = x.entry(a, b)
            tr, ti = pi * yi[b], pi * yr[b]
            if sign > 0:
                tr, ti = pr * yr[b] - tr, pr * yi[b] + ti
            else:
                tr, ti = pr * yr[b] + tr, pr * yi[b] - ti
            real = tr if real is None else real + tr
            imag = ti if imag is None else imag + ti
        if factor != 1.0:
            real, imag = factor * real, factor * imag
        if diagonal and a < SUB:
            real = real + jnp.where(sub == a, diagonal, 0.0)
        out.main[0, a] = real
        out.main[1, a] = imag
    ar = [[x.main[0, SUB + a], x.corner[0, a]] for a in range(CORNER)]
    ai = [[x.main[1, SUB + a], x.corner[1, a]] for a in range(CORNER)]
    er = [[yr[SUB + e], y.corner[0, e]] for e in range(CORNER)]
    ei = [[yi[SUB + e], y.corner[1, e]] for e in range(CORNER)]
    for a in range(CORNER):
        for e in range(a, CORNER):
            real = sum(ar[a][h] * er[e][h] + ai[a][h] * ei[e][h] for h in range(2))
            real = factor * jnp.sum(real, axis=0, keepdims=True)
            if a == e:
                real = real + diagonal
                out.put(SUB + a, SUB + a, real, jnp.zeros_like(real))
            else:
                imag = sum(ai[a][h] * er[e][h] - ar[a][h] * ei[e][h] for h in range(2))
                imag = factor * jnp.sum(imag, axis=0, keepdims=True)
                out.put(SUB + a, SUB + e, real, imag)
                out.put(SUB + e, SUB + a, real, -imag)


def affine(x, outs):
    sub = lax.broadcasted_iota(jnp.int32, (SUB, NFREQ), 0)
    for a in range(NBLK):
        real = -0.5 * x.main[0, a]
        imag = -0.5 * x.main[1, a]
        if a < SUB:
            real = real + jnp.where(sub == a, 1.5, 0.0)
        for out in outs:
            out.main[0, a] = real
            out.main[1, a] = imag
    for a in range(CORNER):
        real = jnp.where(sub == a, 1.5, 0.0) - 0.5 * x.corner[0, a]
        imag = -0.5 * x.corner[1, a]
        for out in outs:
            out.corner[0, a] = real
            out.corner[1, a] = imag


def root_kernel(parts, share, *refs):
    part_refs = refs[:parts]
    stack_ref, gram_ref, packed, rolled, *mats = refs[parts:]
    terms = [r[...].astype(F32) for r in part_refs]
    packed[...] = terms[0] + terms[1]
    at = lax.axis_index("sx") * lax.axis_size("sy") + lax.axis_index("sy")
    rolled[...] = pltpu.roll(packed[...], (NFREQ - at * share) % NFREQ, 1)
    y, z, p, y2, z2 = [Hermitian(mats[2 * i], mats[2 * i + 1]) for i in range(5)]
    for ref in mats[1::2]:
        ref[...] = jnp.zeros_like(ref)

    def row(ref, part, a, e):
        return ref[pl.ds(ROWS[part, a, e], 1), :]

    trace = 2.0 * sum(row(packed, 0, a, a) for a in range(NBLK))
    norm = 1.0 / jnp.sqrt(trace)
    packed[...] = packed[...] / trace
    zero = jnp.zeros((1, NFREQ), F32)
    for a in range(NBLK):
        y.put(a, a, row(packed, 0, a, a), zero)
        gram_ref[a, a, 0:1, :] = row(rolled, 0, a, a)[:, :share]
        gram_ref[a, a, 1:2, :] = zero[:, :share]
        for e in range(a + 1, NBLK):
            real, imag = row(packed, 0, a, e), row(packed, 1, a, e)
            y.put(a, e, real, imag)
            y.put(e, a, real, -imag)
            real, imag = row(rolled, 0, a, e)[:, :share], row(rolled, 1, a, e)[:, :share]
            gram_ref[a, e, 0:1, :] = real
            gram_ref[e, a, 0:1, :] = real
            gram_ref[a, e, 1:2, :] = imag
            gram_ref[e, a, 1:2, :] = -imag
    for step in range(ROOT_STEPS):
        if step == 0:
            affine(y, [p, z2])
        else:
            product(z, y, p, 1.5, -0.5)
            product(p, z, z2)
        if step < ROOT_STEPS - 1:
            product(y, p, y2)
        y, y2 = y2, y
        z, z2 = z2, z
    none = jnp.zeros((SUB - CORNER, NFREQ), F32)
    for at, m0 in enumerate(range(0, NBLK, STACK)):
        modes = range(m0, min(m0 + STACK, NBLK))
        stack = []
        for m in modes:
            for c in range(2):
                stack.append(z.main[c, m] * norm)
                for b in range(SUB, NBLK):
                    real, imag, sign = z.entry(m, b)
                    stack.append((imag * sign if c else real) * norm)
                stack.append(none)
        stack += [jnp.zeros((32, NFREQ), F32)] * (STACK - len(modes))
        stack_ref[at] = jnp.concatenate(stack, axis=0).T


def roots(parts, share):
    stacks = -(-NBLK // STACK)
    return pl.pallas_call(
        functools.partial(root_kernel, len(parts), share),
        out_shape=[
            jax.ShapeDtypeStruct((stacks, NFREQ, LANE), F32),
            jax.ShapeDtypeStruct((NBLK, NBLK, 2, share), F32),
        ],
        in_specs=[VMEM] * len(parts),
        out_specs=[VMEM] * 2,
        scratch_shapes=[pltpu.VMEM((PACKED, NFREQ), F32)] * 2
        + [
            pltpu.VMEM((2, NBLK, SUB, NFREQ), F32),
            pltpu.VMEM((2, CORNER, SUB, NFREQ), F32),
        ]
        * 5,
        compiler_params=pltpu.CompilerParams(vmem_limit_bytes=32 * 2**20),
    )(*parts)


def mode_kernel(chunks, stack_ref, spread_ref, *refs):
    high_refs = refs[:chunks]
    low_refs = refs[chunks : 2 * chunks]
    out_ref, v = refs[2 * chunks :]
    step = pl.program_id(0)

    @pl.when(step == 0)
    def _():
        row = lax.broadcasted_iota(jnp.int32, (NFREQ, 2 * HALF_ROWS), 0)
        col = lax.broadcasted_iota(jnp.int32, (NFREQ, 2 * HALF_ROWS), 1)
        same = row % SUB == col % SUB
        for at, m0 in enumerate(range(0, NBLK, STACK)):
            both = jnp.concatenate(split(stack_ref[at]), axis=1)
            for m in range(m0, min(m0 + STACK, NBLK)):
                for c in range(2):
                    wide = dot(both, spread_ref[(m - m0) * 2 + c])
                    v[c * NBLK + m] = jnp.where(same, wide, 0.0)

    fields = []
    for h in range(2):
        g = step * 2 + h
        start = pl.multiple_of(g * SUB, SUB)
        v_high, v_low = split(v[:, pl.ds(start, SUB), :].reshape(2 * HALF_ROWS, 2 * HALF_ROWS))
        s_high = jnp.concatenate([r[g] for r in high_refs], axis=1)
        s_low = jnp.concatenate([r[g] for r in low_refs], axis=1)
        field = dot(jnp.concatenate([v_high, v_low], axis=0), s_high)
        field = field[: 2 * HALF_ROWS] + (field[2 * HALF_ROWS :] + dot(v_high, s_low))
        fields.append(field.reshape(2 * NBLK, SUB, -1))
    both = jnp.concatenate(fields, axis=1).astype(BF16)
    out_ref[...] = both.reshape(out_ref.shape)


def mode_fields(stacks, spread, highs, lows):
    width = sum(s.shape[2] for s in highs)
    return pl.pallas_call(
        functools.partial(mode_kernel, len(highs)),
        grid=(NFREQ // 16,),
        out_shape=jax.ShapeDtypeStruct((2, NBLK, NFREQ, width), BF16),
        in_specs=[VMEM] * (2 + 2 * len(highs)),
        out_specs=pl.BlockSpec((2, NBLK, 16, width), lambda i: (0, 0, i, 0)),
        scratch_shapes=[pltpu.VMEM((2 * NBLK, NFREQ, 2 * HALF_ROWS), F32)],
        compiler_params=pltpu.CompilerParams(vmem_limit_bytes=32 * 2**20),
    )(stacks, spread, *highs, *lows)


def swap(x, axes, mask, size):
    return lax.ppermute(x, axes, [(i, i ^ mask) for i in range(size)])


def powers(size):
    return [1 << i for i in range(size.bit_length() - 1)]


def body(snapshots, weights, block_order, owner, offsets):
    lanes = lax.axis_size("tm")
    groups = lax.axis_size("sx") * lax.axis_size("sy")
    points = snapshots.shape[2]
    width = points // 2
    scale = 1.0 / (lanes * groups * points)
    tables = (jnp.asarray(fourier_tables()), jnp.asarray(pick_table()))
    weights = weights.reshape(1, -1)

    arrived = []
    table = owner
    for base in range(0, points, width):
        packed = pack(table, snapshots, base, width, base == 0)
        table = packed[lanes] if base == 0 else table
        moved = [swap(packed[d], "tm", d, lanes) for d in reversed(range(1, lanes))]
        arrived.append([packed[0]] + moved)

    highs, lows = [], []
    before = []
    for at, pieces in enumerate(arrived):
        here = weights[:, at * width : (at + 1) * width]
        total = gram_part(block_order, offsets, here, tables, pieces, before, scale)
        after = [total] if at == len(arrived) - 1 else []
        high, low = spectrum(block_order, offsets, tables[0], pieces, after)
        highs.append(high)
        lows.append(low)
        before = [total, high]

    axes = ("tm", "sx", "sy")
    size = lanes * groups
    masks = [b * groups for b in powers(lanes)] + powers(groups)
    other = swap(total, axes, masks[0], size)
    for mask in masks[1:]:
        total = (total.astype(F32) + other.astype(F32)).astype(BF16)
        other = swap(total, axes, mask, size)

    stacks, gram = roots([total, other], NFREQ // groups)
    modes = mode_fields(stacks, jnp.asarray(spread_table()), highs, lows)
    modes = jnp.transpose(modes, (0, 2, 1, 3))[:, :, :, None, :]
    return modes, jnp.transpose(gram, (2, 3, 0, 1))


def solution(mesh):
    placed = (P("tm", None, ("sx", "sy")), P(("sx", "sy")), P(), P(("sx", "sy"), None), P())
    return jax.shard_map(
        body,
        mesh=mesh,
        in_specs=placed,
        out_specs=(P(None, None, None, "tm", ("sx", "sy")), P(None, ("sx", "sy"), None, None)),
        check_vma=False,
    )
```

time: 68.1 us -> 53.9 us (0.79)
  blocking collectives: 22.1 us -> 0 us
  waiting for transfers between devices: 2.3 us -> 14.7 us
  local copies, waits for them, and re-layouts: 10.9 us -> 0.05 us
  starting transfers between devices: 7.48 us -> 15.8 us
  Pallas kernels: 24.1 us -> 22.4 us
    all_to_all x2 -> x0, blocking collectives: 22.1 us -> none  [body(): total = lax.all_to_all(total, axes, split_axis=0, concat_axis=0, tiled=True)]
    ppermute x9 -> x11, waiting for transfers between devices: 2.3 us -> 14.7 us  [swap(): return lax.ppermute(x, axes, [(i, i ^ mask) for i in range(size)])]
    unnamed x36 -> x16, local copies, waits for them, and re-layouts: 10.9 us -> 0.05 us
    ppermute x9 -> x11, starting transfers between devices: 7.48 us -> 15.8 us  [swap(): return lax.ppermute(x, axes, [(i, i ^ mask) for i in range(size)])]
    pallas_call x3 -> x4, Pallas kernels: 4.53 us -> 8.51 us  [the longest x2 5.18 us: pack(): pl.pallas_call(functools.partial(pack_kernel, base, parts, first), out_sh...]
    pallas_call x3 -> x2, Pallas kernels: 8.21 us -> 5.56 us  [gram_part(): pl.pallas_call(functools.partial(gram_kernel, lanes, scale, first), out_s...]
    pallas_call x1, Pallas kernels: 5.25 us -> 2.66 us  [roots(): pl.pallas_call(functools.partial(root_kernel, len(parts), share), out_sha...]
  transfers between devices with their start and end apart: 9 -> 11, of which waited for: 1 -> 8; matrix products, arithmetic and copies ran while one was open for 0% -> 0% of each run, Pallas kernels for 11% -> 16%
where the time goes in v3:
time: 53.9 us; the launch traced here: 53.8 us
  Pallas kernels  22.4 us (42%)
  starting transfers between devices  15.8 us (29%)
  waiting for transfers between devices  14.7 us (27%)
  between operations  0.8 us (1%)
    ppermute x11, starting transfers between devices, swap(): return lax.ppermute(x, axes, [(i, i ^ mask) for i in range(size)])  15.8 us
    ppermute x11, waiting for transfers between devices, swap(): return lax.ppermute(x, axes, [(i, i ^ mask) for i in range(size)])  14.7 us
    pallas_call x1, Pallas kernels, mode_fields(): pl.pallas_call(functools.partial(mode_kernel, len(highs)), grid=(NFREQ //...  5.7 us
    pallas_call x2, Pallas kernels, gram_part(): pl.pallas_call(functools.partial(gram_kernel, lanes, scale, first), out_s...  5.56 us
    pallas_call x2, Pallas kernels, pack(): pl.pallas_call(functools.partial(pack_kernel, base, parts, first), out_sh...  5.18 us
    pallas_call x2, Pallas kernels, spectrum(): pl.pallas_call(functools.partial(spectrum_kernel, lanes), out_shape=[part...  3.33 us
    pallas_call x1, Pallas kernels, roots(): pl.pallas_call(functools.partial(root_kernel, len(parts), share), out_sha...  2.66 us
  transfers between devices with their start and end apart: 11, of which 8 were waited for; matrix products, arithmetic and copies ran while one was open for 0% of the time, Pallas kernels for 16%

profile of v3, /device:TPU:0, one launch (start us, length us, event | category | flops | bytes accessed | tf_op | source)
XLA Modules:
  0.0 53.8 jit_solution(2644216713363458753)
XLA Ops:
  0.6 2.5 %shard_map.95 = (bf16[384,256]{1,0:T(8,128)(2,1)}, bf16[384,256]{1,0:T(8,128)(2,1)}, bf16[384,256]{1,0:T(8,128)(2,1)}, bf16[384,256]{1,0:T(8,128)(2,1)}, bf16[256,256]{1,0:T(8,128)(2,1)}) custom-call(s32[1,4]{1,0:T(1,128)} %table_hbm.1, bf16[384,4,512]{2,1,0:T(4,128)(2,1)} %x_hbm.3), custom_call_target="tpu_custom_call" | custom-call | flops 201326592 | bytes 1572864 | tf_op jit(solution)/shard_map/pallas_call | solution.py:159
  3.2 0.0 copy-start.7
  3.2 0.0 copy-start.2
  3.2 0.0 copy-start.3
  3.2 0.0 copy-start.4
  3.2 0.0 copy-start.6
  3.2 2.5 %collective-permute-start.3 = (bf16[384,256]{1,0:T(8,128)(2,1)}, bf16[384,256]{1,0:T(8,128)(2,1)S(1)}, u32[]{:S(2)}, u32[]{:S(2)}) collective-permute-start(bf16[384,256]{1,0:T(8,128)(2,1)} %get-tuple-element.23), channel_id=1, source_target_pairs={{0,24},{8,16},{16,8},{24,0},{1,25},{9,17},{17,9},{25,1},{2,26},{10... | collective-permute-start | bytes 589832 | tf_op jit(solution)/shard_map/ppermute | solution.py:482
  5.7 0.6 %collective-permute-start.4 = (bf16[384,256]{1,0:T(8,128)(2,1)}, bf16[384,256]{1,0:T(8,128)(2,1)S(1)}, u32[]{:S(2)}, u32[]{:S(2)}) collective-permute-start(bf16[384,256]{1,0:T(8,128)(2,1)} %get-tuple-element.24), channel_id=1, source_target_pairs={{0,16},{8,24},{16,0},{24,8},{1,17},{9,25},{17,1},{25,9},{2,18},{10... | collective-permute-start | bytes 589832 | tf_op jit(solution)/shard_map/ppermute | solution.py:482
  6.3 0.0 collective-permute-start.5
  6.4 2.6 %shard_map.96 = (bf16[384,256]{1,0:T(8,128)(2,1)}, bf16[384,256]{1,0:T(8,128)(2,1)}, bf16[384,256]{1,0:T(8,128)(2,1)}, bf16[384,256]{1,0:T(8,128)(2,1)}) custom-call(bf16[256,256]{1,0:T(8,128)(2,1)} %get-tuple-element.17.table_hbm, bf16[384,4,512]{2,1,0:T(4,128)(2,1)} %x_hbm.3), custom_call_target="tpu_custom_call" | custom-call | flops 201326592 | bytes 1572864 | tf_op jit(solution)/shard_map/pallas_call | solution.py:159
  9.0 1.5 %collective-permute-start = (bf16[384,256]{1,0:T(8,128)(2,1)}, bf16[384,256]{1,0:T(8,128)(2,1)S(1)}, u32[]{:S(2)}, u32[]{:S(2)}) collective-permute-start(bf16[384,256]{1,0:T(8,128)(2,1)} %get-tuple-element.19), channel_id=1, source_target_pairs={{0,24},{8,16},{16,8},{24,0},{1,25},{9,17},{17,9},{25,1},{2,26},{10... | collective-permute-start | bytes 589832 | tf_op jit(solution)/shard_map/ppermute | solution.py:482
  10.6 0.6 %collective-permute-start.1 = (bf16[384,256]{1,0:T(8,128)(2,1)}, bf16[384,256]{1,0:T(8,128)(2,1)S(1)}, u32[]{:S(2)}, u32[]{:S(2)}) collective-permute-start(bf16[384,256]{1,0:T(8,128)(2,1)} %get-tuple-element.20), channel_id=1, source_target_pairs={{0,16},{8,24},{16,0},{24,8},{1,17},{9,25},{17,1},{25,9},{2,18},{10... | collective-permute-start | bytes 589832 | tf_op jit(solution)/shard_map/ppermute | solution.py:482
  11.2 0.0 copy-done.7
  11.2 0.1 collective-permute-done.3.refs_1_
  11.3 0.7 %collective-permute-start.2 = (bf16[384,256]{1,0:T(8,128)(2,1)}, bf16[384,256]{1,0:T(8,128)(2,1)S(1)}, u32[]{:S(2)}, u32[]{:S(2)}) collective-permute-start(bf16[384,256]{1,0:T(8,128)(2,1)} %get-tuple-element.21), channel_id=1, source_target_pairs={{0,8},{8,0},{16,24},{24,16},{1,9},{9,1},{17,25},{25,17},{2,10},{10... | collective-permute-start | bytes 589832 | tf_op jit(solution)/shard_map/ppermute | solution.py:482
  12.0 4.4 %collective-permute-done.4.refs_2_ = bf16[384,256]{1,0:T(8,128)(2,1)S(1)} collective-permute-done((bf16[384,256]{1,0:T(8,128)(2,1)}, bf16[384,256]{1,0:T(8,128)(2,1)S(1)}, u32[]{:S(2)}, u32[]{:S(2)}) %collective-permute-start.4) | collective-permute-done | bytes 196640 | tf_op jit(solution)/shard_map/ppermute | solution.py:482
  16.4 0.0 collective-permute-done.5.refs_3_
  16.4 0.0 copy-done.2
  16.4 0.0 copy-done.3
  16.4 0.0 copy-done.4
  16.4 0.0 copy-done.6
  16.5 0.0 copy-start.5
  16.5 1.7 %shard_map.98 = (bf16[16,176,256]{2,1,0:T(8,128)(2,1)S(1)}, bf16[16,176,256]{2,1,0:T(8,128)(2,1)S(1)}) custom-call(s32[4]{0:T(128)S(1)} %copy-done.3, s32[11]{0:T(128)S(1)} %copy-done.4, bf16[2,256,256]{2,1,0:T(8,128)(2,1)S(1)} %copy-done.6, bf16[384,256]{1,0:T(8,128)(2,1)S(1)} %copy-done.2, bf16[384,256]{1,0:T(8,128)(2,1)S(1)} %collective-permute-done.3.refs_1_, ...), custom_call_target="tpu_custom_call" | custom-call | flops 2500000000 | bytes 3000000 | tf_op jit(solution)/shard_map/pallas_call | solution.py:264
  18.1 0.0 copy-done.5
  18.2 0.0 copy-start.1
  18.2 2.8 %shard_map.97.refs_4_ = f32[128,128]{1,0:T(8,128)S(1)} custom-call(s32[4]{0:T(128)S(1)} %copy-done.3, s32[11]{0:T(128)S(1)} %copy-done.4, f32[1,256]{1,0:T(1,128)S(1)} %get-tuple-element.34.w_ref, bf16[2,256,256]{2,1,0:T(8,128)(2,1)S(1)} %copy-done.6, bf16[2816,128]{1,0:T(8,128)(2,1)S(1)} %copy-done.5, bf16[384,256]{1,0:T(8,128)(2,1)S(1)} %copy-done.2, ...), custom_call_target="tpu_custom_call" | custom-call | flops 2500000000 | bytes 3000000 | tf_op jit(solution)/shard_map/pallas_call | solution.py:233
  21.0 0.0 collective-permute-done.refs_1_
  21.0 3.1 %collective-permute-done.1.refs_2_ = bf16[384,256]{1,0:T(8,128)(2,1)S(1)} collective-permute-done((bf16[384,256]{1,0:T(8,128)(2,1)}, bf16[384,256]{1,0:T(8,128)(2,1)S(1)}, u32[]{:S(2)}, u32[]{:S(2)}) %collective-permute-start.1) | collective-permute-done | bytes 196640 | tf_op jit(solution)/shard_map/ppermute | solution.py:482
  24.0 0.0 collective-permute-done.2.refs_3_
  24.0 0.0 copy-done.1
  24.0 2.8 %shard_map.99.refs_4_ = bf16[128,128]{1,0:T(8,128)(2,1)S(1)} custom-call(s32[4]{0:T(128)S(1)} %copy-done.3, s32[11]{0:T(128)S(1)} %copy-done.4, f32[1,256]{1,0:T(1,128)S(1)} %get-tuple-element.35.w_ref, bf16[2,256,256]{2,1,0:T(8,128)(2,1)S(1)} %copy-done.6, bf16[2816,128]{1,0:T(8,128)(2,1)S(1)} %copy-done.5, bf16[384,256]{1,0:T(8,128)(2,1)S(1)} %copy-done.1, ...), custom_call_target="tpu_custom_call" | custom-call | flops 2500000000 | bytes 3000000 | tf_op jit(solution)/shard_map/pallas_call | solution.py:233
  26.8 0.1 collective-permute-start.6
  26.9 1.2 %collective-permute-done.6 = bf16[128,128]{1,0:T(8,128)(2,1)S(1)} collective-permute-done((bf16[128,128]{1,0:T(8,128)(2,1)S(1)}, bf16[128,128]{1,0:T(8,128)(2,1)S(1)}, u32[]{:S(2)}, u32[]{:S(2)}) %collective-permute-start.6) | collective-permute-done | bytes 32800 | tf_op jit(solution)/shard_map/ppermute | solution.py:482
  28.1 2.4 %collective-permute-start.7 = (bf16[128,128]{1,0:T(8,128)(2,1)S(1)}, bf16[128,128]{1,0:T(8,128)(2,1)S(1)}, u32[]{:S(2)}, u32[]{:S(2)}) collective-permute-start(bf16[128,128]{1,0:T(8,128)(2,1)S(1)} %add_convert_fusion.3), channel_id=1, source_target_pairs={{0,16},{1,17},{2,18},{3,19},{4,20},{5,21},{6,22},{7,23},{8,24},{9,... | collective-permute-start | bytes 98312 | tf_op jit(solution)/shard_map/ppermute | solution.py:482
  30.5 1.9 %collective-permute-done.7 = bf16[128,128]{1,0:T(8,128)(2,1)S(1)} collective-permute-done((bf16[128,128]{1,0:T(8,128)(2,1)S(1)}, bf16[128,128]{1,0:T(8,128)(2,1)S(1)}, u32[]{:S(2)}, u32[]{:S(2)}) %collective-permute-start.7) | collective-permute-done | bytes 32800 | tf_op jit(solution)/shard_map/ppermute | solution.py:482
  32.4 2.1 %collective-permute-start.8 = (bf16[128,128]{1,0:T(8,128)(2,1)S(1)}, bf16[128,128]{1,0:T(8,128)(2,1)S(1)}, u32[]{:S(2)}, u32[]{:S(2)}) collective-permute-start(bf16[128,128]{1,0:T(8,128)(2,1)S(1)} %add_convert_fusion.2), channel_id=1, source_target_pairs={{0,1},{1,0},{2,3},{3,2},{4,5},{5,4},{6,7},{7,6},{8,9},{9,8},{10,11... | collective-permute-start | bytes 98312 | tf_op jit(solution)/shard_map/ppermute | solution.py:482
  34.4 1.9 %collective-permute-done.8 = bf16[128,128]{1,0:T(8,128)(2,1)S(1)} collective-permute-done((bf16[128,128]{1,0:T(8,128)(2,1)S(1)}, bf16[128,128]{1,0:T(8,128)(2,1)S(1)}, u32[]{:S(2)}, u32[]{:S(2)}) %collective-permute-start.8) | collective-permute-done | bytes 32800 | tf_op jit(solution)/shard_map/ppermute | solution.py:482
  36.4 2.1 %collective-permute-start.9 = (bf16[128,128]{1,0:T(8,128)(2,1)S(1)}, bf16[128,128]{1,0:T(8,128)(2,1)S(1)}, u32[]{:S(2)}, u32[]{:S(2)}) collective-permute-start(bf16[128,128]{1,0:T(8,128)(2,1)S(1)} %add_convert_fusion.1), channel_id=1, source_target_pairs={{0,2},{1,3},{2,0},{3,1},{4,6},{5,7},{6,4},{7,5},{8,10},{9,11},{10,... | collective-permute-start | bytes 98312 | tf_op jit(solution)/shard_map/ppermute | solution.py:482
  38.5 1.9 %collective-permute-done.9 = bf16[128,128]{1,0:T(8,128)(2,1)S(1)} collective-permute-done((bf16[128,128]{1,0:T(8,128)(2,1)S(1)}, bf16[128,128]{1,0:T(8,128)(2,1)S(1)}, u32[]{:S(2)}, u32[]{:S(2)}) %collective-permute-start.9) | collective-permute-done | bytes 32800 | tf_op jit(solution)/shard_map/ppermute | solution.py:482
  40.4 0.0 copy-start
  40.4 3.1 %collective-permute-start.10 = (bf16[128,128]{1,0:T(8,128)(2,1)S(1)}, bf16[128,128]{1,0:T(8,128)(2,1)S(1)}, u32[]{:S(2)}, u32[]{:S(2)}) collective-permute-start(bf16[128,128]{1,0:T(8,128)(2,1)S(1)} %add_convert_fusion.refs_0_), channel_id=1, source_target_pairs={{0,4},{1,5},{2,6},{3,7},{4,0},{5,1},{6,2},{7,3},{8,12},{9,13},{10,... | collective-permute-start | bytes 98312 | tf_op jit(solution)/shard_map/ppermute | solution.py:482
  43.5 1.7 %shard_map.101 = (bf16[16,176,256]{2,1,0:T(8,128)(2,1)S(1)}, bf16[16,176,256]{2,1,0:T(8,128)(2,1)S(1)}) custom-call(s32[4]{0:T(128)S(1)} %copy-done.3, s32[11]{0:T(128)S(1)} %copy-done.4, bf16[2,256,256]{2,1,0:T(8,128)(2,1)S(1)} %copy-done.6, bf16[384,256]{1,0:T(8,128)(2,1)S(1)} %copy-done.1, bf16[384,256]{1,0:T(8,128)(2,1)S(1)} %collective-permute-done.refs_1_, ...), custom_call_target="tpu_custom_call" | custom-call | flops 2500000000 | bytes 3000000 | tf_op jit(solution)/shard_map/pallas_call | solution.py:264
  45.2 0.2 collective-permute-done.10.refs_1_
  45.4 2.7 %shard_map.100 = (f32[3,128,128]{2,1,0:T(8,128)S(1)}, f32[11,11,2,16]{3,2,1,0:T(2,128)}) custom-call(bf16[128,128]{1,0:T(8,128)(2,1)S(1)} %add_convert_fusion.refs_0_, bf16[128,128]{1,0:T(8,128)(2,1)S(1)} %collective-permute-done.10.refs_1_), custom_call_target="tpu_custom_call" | custom-call | tf_op jit(solution)/shard_map/pallas_call | solution.py:418
  48.1 0.0 copy-done
  48.1 5.7 %shard_map.102 = bf16[2,11,128,512]{3,2,1,0:T(8,128)(2,1)} custom-call(f32[3,128,128]{2,1,0:T(8,128)S(1)} %get-tuple-element.27.stack_ref, bf16[8,256,176]{2,1,0:T(8,128)(2,1)S(1)} %copy-done, bf16[16,176,256]{2,1,0:T(8,128)(2,1)S(1)} %get-tuple-element.26.refs_5_.refs_0_, bf16[16,176,256]{2,1,0:T(8,128)(2,1)S(1)} %get-tuple-element.28.refs_1_, ...), custom_call_target="tpu_custom_call" | custom-call | tf_op jit(solution)/shard_map/pallas_call | solution.py:470
  (5 shorter events, 0.1 us)
Async XLA Ops:
  3.2 8.0 %copy-start.7 = (f32[512]{0:T(512)S(1)}, f32[512]{0:T(512)}, u32[]{:S(2)}) copy-start(f32[512]{0:T(512)} %param.9) | copy-start | bytes 6148
  3.2 13.2 %copy-start.2 = (bf16[384,256]{1,0:T(8,128)(2,1)S(1)}, bf16[384,256]{1,0:T(8,128)(2,1)}, u32[]{:S(2)}) copy-start(bf16[384,256]{1,0:T(8,128)(2,1)} %get-tuple-element.22.refs_0_) | copy-start | bytes 589828
  3.2 13.2 %copy-start.3 = (s32[4]{0:T(128)S(1)}, s32[4]{0:T(128)}, u32[]{:S(2)}) copy-start(s32[4]{0:T(128)} %order_ref.7) | copy-start | bytes 52
  3.2 13.2 %copy-start.4 = (s32[11]{0:T(128)S(1)}, s32[11]{0:T(128)}, u32[]{:S(2)}) copy-start(s32[11]{0:T(128)} %offsets_ref.7) | copy-start | bytes 136
  3.2 13.2 %copy-start.6 = (bf16[2,256,256]{2,1,0:T(8,128)(2,1)S(1)}, bf16[2,256,256]{2,1,0:T(8,128)(2,1)}, u32[]{:S(2)}) copy-start(bf16[2,256,256]{2,1,0:T(8,128)(2,1)} %constant.6.clone.f_ref) | copy-start | bytes 786436
  3.2 8.1 %collective-permute-start.3 = (bf16[384,256]{1,0:T(8,128)(2,1)}, bf16[384,256]{1,0:T(8,128)(2,1)S(1)}, u32[]{:S(2)}, u32[]{:S(2)}) collective-permute-start(bf16[384,256]{1,0:T(8,128)(2,1)} %get-tuple-element.23), channel_id=1, source_target_pairs={{0,24},{8,16},{16,8},{24,0},{1,25},{9,17},{17,9},{25,1},{2,26},{10... | collective-permute-start | bytes 589832 | tf_op jit(solution)/shard_map/ppermute | solution.py:482
  5.7 10.7 %collective-permute-start.4 = (bf16[384,256]{1,0:T(8,128)(2,1)}, bf16[384,256]{1,0:T(8,128)(2,1)S(1)}, u32[]{:S(2)}, u32[]{:S(2)}) collective-permute-start(bf16[384,256]{1,0:T(8,128)(2,1)} %get-tuple-element.24), channel_id=1, source_target_pairs={{0,16},{8,24},{16,0},{24,8},{1,17},{9,25},{17,1},{25,9},{2,18},{10... | collective-permute-start | bytes 589832 | tf_op jit(solution)/shard_map/ppermute | solution.py:482
  6.3 10.1 %collective-permute-start.5 = (bf16[384,256]{1,0:T(8,128)(2,1)}, bf16[384,256]{1,0:T(8,128)(2,1)S(1)}, u32[]{:S(2)}, u32[]{:S(2)}) collective-permute-start(bf16[384,256]{1,0:T(8,128)(2,1)} %get-tuple-element.25), channel_id=1, source_target_pairs={{0,8},{8,0},{16,24},{24,16},{1,9},{9,1},{17,25},{25,17},{2,10},{10... | collective-permute-start | bytes 589832 | tf_op jit(solution)/shard_map/ppermute | solution.py:482
  9.0 11.9 %collective-permute-start = (bf16[384,256]{1,0:T(8,128)(2,1)}, bf16[384,256]{1,0:T(8,128)(2,1)S(1)}, u32[]{:S(2)}, u32[]{:S(2)}) collective-permute-start(bf16[384,256]{1,0:T(8,128)(2,1)} %get-tuple-element.19), channel_id=1, source_target_pairs={{0,24},{8,16},{16,8},{24,0},{1,25},{9,17},{17,9},{25,1},{2,26},{10... | collective-permute-start | bytes 589832 | tf_op jit(solution)/shard_map/ppermute | solution.py:482
  10.6 13.5 %collective-permute-start.1 = (bf16[384,256]{1,0:T(8,128)(2,1)}, bf16[384,256]{1,0:T(8,128)(2,1)S(1)}, u32[]{:S(2)}, u32[]{:S(2)}) collective-permute-start(bf16[384,256]{1,0:T(8,128)(2,1)} %get-tuple-element.20), channel_id=1, source_target_pairs={{0,16},{8,24},{16,0},{24,8},{1,17},{9,25},{17,1},{25,9},{2,18},{10... | collective-permute-start | bytes 589832 | tf_op jit(solution)/shard_map/ppermute | solution.py:482
  11.3 12.7 %collective-permute-start.2 = (bf16[384,256]{1,0:T(8,128)(2,1)}, bf16[384,256]{1,0:T(8,128)(2,1)S(1)}, u32[]{:S(2)}, u32[]{:S(2)}) collective-permute-start(bf16[384,256]{1,0:T(8,128)(2,1)} %get-tuple-element.21), channel_id=1, source_target_pairs={{0,8},{8,0},{16,24},{24,16},{1,9},{9,1},{17,25},{25,17},{2,10},{10... | collective-permute-start | bytes 589832 | tf_op jit(solution)/shard_map/ppermute | solution.py:482
  16.5 1.7 %copy-start.5 = (bf16[2816,128]{1,0:T(8,128)(2,1)S(1)}, bf16[2816,128]{1,0:T(8,128)(2,1)}, u32[]{:S(2)}) copy-start(bf16[2816,128]{1,0:T(8,128)(2,1)} %constant.7.clone.pick_ref) | copy-start | bytes 2162692
  18.2 5.9 %copy-start.1 = (bf16[384,256]{1,0:T(8,128)(2,1)S(1)}, bf16[384,256]{1,0:T(8,128)(2,1)}, u32[]{:S(2)}) copy-start(bf16[384,256]{1,0:T(8,128)(2,1)} %get-tuple-element.18.refs_0_) | copy-start | bytes 589828
  26.8 1.3 %collective-permute-start.6 = (bf16[128,128]{1,0:T(8,128)(2,1)S(1)}, bf16[128,128]{1,0:T(8,128)(2,1)S(1)}, u32[]{:S(2)}, u32[]{:S(2)}) collective-permute-start(bf16[128,128]{1,0:T(8,128)(2,1)S(1)} %shard_map.99.refs_4_), channel_id=1, source_target_pairs={{0,8},{1,9},{2,10},{3,11},{4,12},{5,13},{6,14},{7,15},{8,0},{9,1},... | collective-permute-start | bytes 98312 | tf_op jit(solution)/shard_map/ppermute | solution.py:482
  28.1 4.3 %collective-permute-start.7 = (bf16[128,128]{1,0:T(8,128)(2,1)S(1)}, bf16[128,128]{1,0:T(8,128)(2,1)S(1)}, u32[]{:S(2)}, u32[]{:S(2)}) collective-permute-start(bf16[128,128]{1,0:T(8,128)(2,1)S(1)} %add_convert_fusion.3), channel_id=1, source_target_pairs={{0,16},{1,17},{2,18},{3,19},{4,20},{5,21},{6,22},{7,23},{8,24},{9,... | collective-permute-start | bytes 98312 | tf_op jit(solution)/shard_map/ppermute | solution.py:482
  32.4 4.0 %collective-permute-start.8 = (bf16[128,128]{1,0:T(8,128)(2,1)S(1)}, bf16[128,128]{1,0:T(8,128)(2,1)S(1)}, u32[]{:S(2)}, u32[]{:S(2)}) collective-permute-start(bf16[128,128]{1,0:T(8,128)(2,1)S(1)} %add_convert_fusion.2), channel_id=1, source_target_pairs={{0,1},{1,0},{2,3},{3,2},{4,5},{5,4},{6,7},{7,6},{8,9},{9,8},{10,11... | collective-permute-start | bytes 98312 | tf_op jit(solution)/shard_map/ppermute | solution.py:482
  36.4 4.0 %collective-permute-start.9 = (bf16[128,128]{1,0:T(8,128)(2,1)S(1)}, bf16[128,128]{1,0:T(8,128)(2,1)S(1)}, u32[]{:S(2)}, u32[]{:S(2)}) collective-permute-start(bf16[128,128]{1,0:T(8,128)(2,1)S(1)} %add_convert_fusion.1), channel_id=1, source_target_pairs={{0,2},{1,3},{2,0},{3,1},{4,6},{5,7},{6,4},{7,5},{8,10},{9,11},{10,... | collective-permute-start | bytes 98312 | tf_op jit(solution)/shard_map/ppermute | solution.py:482
  40.4 7.7 %copy-start = (bf16[8,256,176]{2,1,0:T(8,128)(2,1)S(1)}, bf16[8,256,176]{2,1,0:T(8,128)(2,1)}, u32[]{:S(2)}) copy-start(bf16[8,256,176]{2,1,0:T(8,128)(2,1)} %constant.8.clone.spread_ref) | copy-start | bytes 2162692
  40.4 5.0 %collective-permute-start.10 = (bf16[128,128]{1,0:T(8,128)(2,1)S(1)}, bf16[128,128]{1,0:T(8,128)(2,1)S(1)}, u32[]{:S(2)}, u32[]{:S(2)}) collective-permute-start(bf16[128,128]{1,0:T(8,128)(2,1)S(1)} %add_convert_fusion.refs_0_), channel_id=1, source_target_pairs={{0,4},{1,5},{2,6},{3,7},{4,0},{5,1},{6,2},{7,3},{8,12},{9,13},{10,... | collective-permute-start | bytes 98312 | tf_op jit(solution)/shard_map/ppermute | solution.py:482

commit v4 on v3

--- a/solution.py
+++ b/solution.py
@@ -17,7 +17,9 @@
 SUB = 8
 HALF_ROWS = NBLK * SUB
 GROUPS = NFREQ // SUB
+STEP_GROUPS = 4
 PACKED = 128
+HALF = PACKED // 2
 STACK = 4
 CORNER = NBLK - SUB
 WIDE = 2 * LANE
@@ -35,7 +37,7 @@
     table = np.concatenate([np.cos(angles) * scaled, -np.sin(angles) * scaled], axis=0)
     high = table.astype(jnp.bfloat16)
     low = (table - high.astype(np.float64)).astype(jnp.bfloat16)
-    return np.stack([high, low])
+    return np.concatenate([high, low], axis=1)
 
 
 def packed_rows():
@@ -189,7 +191,7 @@
     for i in range(NBLK):
         x = [record[c, pl.ds(offsets_ref[i], NFFT), :].astype(BF16) for c in range(record.shape[0])]
         x = jnp.concatenate(x, axis=1)
-        y = dot(f_ref[0], x) + dot(f_ref[1], x)
+        y = dot(f_ref[...], jnp.concatenate([x, x], axis=0))
         s_ref[i] = y[:NFREQ]
         s_ref[NBLK + i] = y[NFREQ:]
 
@@ -199,7 +201,7 @@
     rest = refs[lanes:]
     if not first:
         before_ref, _, *rest = rest
-    packed_ref, record, s_ref, masked = rest
+    *packed_refs, record, s_ref, masked = rest
     fill_record(order_ref, pieces, record, jnp.sqrt(w_ref[...]))
     transform(offsets_ref, f_ref, record, s_ref)
     row = lax.broadcasted_iota(jnp.int32, (HALF_ROWS, LANE), 0)
@@ -220,9 +222,14 @@
             masked[at, a * WIDE : a * WIDE + LANE] = real[rows]
             masked[at, a * WIDE + LANE : (a + 1) * WIDE] = imag[rows]
     total = dot(masked[...].astype(BF16), pick_ref[...]).T * scale
-    if not first:
-        total = total + before_ref[...]
-    packed_ref[...] = total.astype(packed_ref.dtype)
+    if first:
+        packed_refs[0][...] = total
+        return
+    keep_ref, send_ref = packed_refs
+    total = total + before_ref[...]
+    other = lax.axis_index("tm") % 2 == 1
+    keep_ref[...] = jnp.where(other, total[HALF:], total[:HALF]).astype(BF16)
+    send_ref[...] = jnp.where(other, total[:HALF], total[HALF:]).astype(BF16)
 
 
 def gram_part(order, offsets, weights, tables, pieces, before, scale):
@@ -232,9 +239,11 @@
     args = [order, offsets, weights, *tables, *pieces, *before]
     return pl.pallas_call(
         functools.partial(gram_kernel, lanes, scale, first),
-        out_shape=jax.ShapeDtypeStruct((PACKED, NFREQ), F32 if first else BF16),
+        out_shape=[jax.ShapeDtypeStruct((PACKED, NFREQ), F32)]
+        if first
+        else [jax.ShapeDtypeStruct((HALF, NFREQ), BF16)] * 2,
         in_specs=[SMEM, SMEM] + [VMEM] * (len(args) - 2),
-        out_specs=VMEM,
+        out_specs=[VMEM] * (1 if first else 2),
         scratch_shapes=[
             pltpu.VMEM((width // LANE, lanes * steps, LANE), F32),
             pltpu.VMEM((2 * NBLK, NFREQ, width), F32),
@@ -357,11 +366,10 @@
             out.corner[1, a] = imag
 
 
-def root_kernel(parts, share, *refs):
-    part_refs = refs[:parts]
-    stack_ref, gram_ref, packed, rolled, *mats = refs[parts:]
-    terms = [r[...].astype(F32) for r in part_refs]
-    packed[...] = terms[0] + terms[1]
+def root_kernel(share, half_ref, other_ref, stack_ref, gram_ref, packed, rolled, *mats):
+    core = lax.axis_index("tm") % 2
+    packed[pl.ds(pl.multiple_of(core * HALF, HALF), HALF), :] = half_ref[...]
+    packed[pl.ds(pl.multiple_of((1 - core) * HALF, HALF), HALF), :] = other_ref[...]
     at = lax.axis_index("sx") * lax.axis_size("sy") + lax.axis_index("sy")
     rolled[...] = pltpu.roll(packed[...], (NFREQ - at * share) % NFREQ, 1)
     y, z, p, y2, z2 = [Hermitian(mats[2 * i], mats[2 * i + 1]) for i in range(5)]
@@ -413,15 +421,15 @@
         stack_ref[at] = jnp.concatenate(stack, axis=0).T
 
 
-def roots(parts, share):
+def roots(half, other, share):
     stacks = -(-NBLK // STACK)
     return pl.pallas_call(
-        functools.partial(root_kernel, len(parts), share),
+        functools.partial(root_kernel, share),
         out_shape=[
             jax.ShapeDtypeStruct((stacks, NFREQ, LANE), F32),
             jax.ShapeDtypeStruct((NBLK, NBLK, 2, share), F32),
         ],
-        in_specs=[VMEM] * len(parts),
+        in_specs=[VMEM] * 2,
         out_specs=[VMEM] * 2,
         scratch_shapes=[pltpu.VMEM((PACKED, NFREQ), F32)] * 2
         + [
@@ -430,7 +438,7 @@
         ]
         * 5,
         compiler_params=pltpu.CompilerParams(vmem_limit_bytes=32 * 2**20),
-    )(*parts)
+    )(half, other)
 
 
 def mode_kernel(chunks, stack_ref, spread_ref, *refs):
@@ -452,8 +460,8 @@
                     v[c * NBLK + m] = jnp.where(same, wide, 0.0)
 
     fields = []
-    for h in range(2):
-        g = step * 2 + h
+    for h in range(STEP_GROUPS):
+        g = step * STEP_GROUPS + h
         start = pl.multiple_of(g * SUB, SUB)
         v_high, v_low = split(v[:, pl.ds(start, SUB), :].reshape(2 * HALF_ROWS, 2 * HALF_ROWS))
         s_high = jnp.concatenate([r[g] for r in high_refs], axis=1)
@@ -469,10 +477,12 @@
     width = sum(s.shape[2] for s in highs)
     return pl.pallas_call(
         functools.partial(mode_kernel, len(highs)),
-        grid=(NFREQ // 16,),
+        grid=(GROUPS // STEP_GROUPS,),
         out_shape=jax.ShapeDtypeStruct((2, NBLK, NFREQ, width), BF16),
         in_specs=[VMEM] * (2 + 2 * len(highs)),
-        out_specs=pl.BlockSpec((2, NBLK, 16, width), lambda i: (0, 0, i, 0)),
+        out_specs=pl.BlockSpec(
+            (2, NBLK, STEP_GROUPS * SUB, width), lambda i: (0, 0, i, 0)
+        ),
         scratch_shapes=[pltpu.VMEM((2 * NBLK, NFREQ, 2 * HALF_ROWS), F32)],
         compiler_params=pltpu.CompilerParams(vmem_limit_bytes=32 * 2**20),
     )(stacks, spread, *highs, *lows)
@@ -508,21 +518,30 @@
     for at, pieces in enumerate(arrived):
         here = weights[:, at * width : (at + 1) * width]
         total = gram_part(block_order, offsets, here, tables, pieces, before, scale)
-        after = [total] if at == len(arrived) - 1 else []
+        after = total if at == len(arrived) - 1 else []
         high, low = spectrum(block_order, offsets, tables[0], pieces, after)
         highs.append(high)
         lows.append(low)
-        before = [total, high]
+        before = [total[0], high]
 
     axes = ("tm", "sx", "sy")
     size = lanes * groups
-    masks = [b * groups for b in powers(lanes)] + powers(groups)
-    other = swap(total, axes, masks[0], size)
-    for mask in masks[1:]:
-        total = (total.astype(F32) + other.astype(F32)).astype(BF16)
-        other = swap(total, axes, mask, size)
-
-    stacks, gram = roots([total, other], NFREQ // groups)
+    bits = [b * groups for b in powers(lanes)] + powers(groups)
+    keep, send = total
+    half = keep.astype(F32) + swap(send, axes, bits[0], size).astype(F32)
+    for at in range(1, len(bits), 2):
+        masks = bits[at : at + 2]
+        if len(masks) == 2:
+            masks.append(masks[0] ^ masks[1])
+        half = half.astype(BF16)
+        terms = [half] + [swap(half, axes, mask, size) for mask in masks]
+        terms = [t.astype(F32) for t in terms]
+        while len(terms) > 1:
+            terms = [a + b for a, b in zip(terms[::2], terms[1::2])]
+        half = terms[0]
+    other = swap(half, axes, bits[0], size)
+
+    stacks, gram = roots(half, other, NFREQ // groups)
     modes = mode_fields(stacks, jnp.asarray(spread_table()), highs, lows)
     modes = jnp.transpose(modes, (0, 2, 1, 3))[:, :, :, None, :]
     return modes, jnp.transpose(gram, (2, 3, 0, 1))

time: 53.9 us -> 53 us (0.983)
  waiting for transfers between devices: 14.7 us -> 16.2 us
  starting transfers between devices: 15.8 us -> 14.6 us
  Pallas kernels: 22.4 us -> 21.2 us
    ppermute x11 -> x14, waiting for transfers between devices: 14.7 us -> 16.2 us  [swap(): return lax.ppermute(x, axes, [(i, i ^ mask) for i in range(size)])]
    pallas_call x2, Pallas kernels: 8.35 us -> 7.12 us  [the longest x1 4.45 us: mode_fields(): pl.pallas_call(functools.partial(mode_kernel, len(highs)), grid=(GROUPS /...]
    ppermute x11 -> x14, starting transfers between devices: 15.8 us -> 14.6 us  [swap(): return lax.ppermute(x, axes, [(i, i ^ mask) for i in range(size)])]
  transfers between devices with their start and end apart: 11 -> 14, of which waited for: 8 -> 9; matrix products, arithmetic and copies ran while one was open for 0% -> 0% of each run, Pallas kernels for 16% -> 17%
where the time goes in v4:
time: 53 us; the launch traced here: 52.8 us
  Pallas kernels  21.2 us (40%)
  waiting for transfers between devices  16.2 us (31%)
  starting transfers between devices  14.6 us (28%)
  between operations  0.81 us (2%)
    ppermute x14, waiting for transfers between devices, swap(): return lax.ppermute(x, axes, [(i, i ^ mask) for i in range(size)])  16.2 us
    ppermute x14, starting transfers between devices, swap(): return lax.ppermute(x, axes, [(i, i ^ mask) for i in range(size)])  14.6 us
    pallas_call x2, Pallas kernels, gram_part(): pl.pallas_call(functools.partial(gram_kernel, lanes, scale, first), out_s...  5.54 us
    pallas_call x2, Pallas kernels, pack(): pl.pallas_call(functools.partial(pack_kernel, base, parts, first), out_sh...  5.2 us
    pallas_call x1, Pallas kernels, mode_fields(): pl.pallas_call(functools.partial(mode_kernel, len(highs)), grid=(GROUPS /...  4.45 us
    pallas_call x2, Pallas kernels, spectrum(): pl.pallas_call(functools.partial(spectrum_kernel, lanes), out_shape=[part...  3.32 us
    pallas_call x1, Pallas kernels, roots(): pl.pallas_call(functools.partial(root_kernel, share), out_shape=[jax.Shap...  2.67 us
  transfers between devices with their start and end apart: 14, of which 9 were waited for; matrix products, arithmetic and copies ran while one was open for 0% of the time, Pallas kernels for 17%

profile of v4, /device:TPU:0, one launch (start us, length us, event | category | flops | bytes accessed | tf_op | source)
XLA Modules:
  0.0 52.8 jit_solution(5228763292966530857)
XLA Ops:
  0.6 2.5 %shard_map.95 = (bf16[384,256]{1,0:T(8,128)(2,1)}, bf16[384,256]{1,0:T(8,128)(2,1)}, bf16[384,256]{1,0:T(8,128)(2,1)}, bf16[384,256]{1,0:T(8,128)(2,1)}, bf16[256,256]{1,0:T(8,128)(2,1)}) custom-call(s32[1,4]{1,0:T(1,128)} %table_hbm.1, bf16[384,4,512]{2,1,0:T(4,128)(2,1)} %x_hbm.3), custom_call_target="tpu_custom_call" | custom-call | flops 201326592 | bytes 1572864 | tf_op jit(solution)/shard_map/pallas_call | solution.py:161
  3.2 0.0 copy-start.7
  3.2 0.0 copy-start.2
  3.2 0.0 copy-start.3
  3.2 0.0 copy-start.4
  3.2 0.0 copy-start.6
  3.2 2.5 %collective-permute-start.3 = (bf16[384,256]{1,0:T(8,128)(2,1)}, bf16[384,256]{1,0:T(8,128)(2,1)S(1)}, u32[]{:S(2)}, u32[]{:S(2)}) collective-permute-start(bf16[384,256]{1,0:T(8,128)(2,1)} %get-tuple-element.25), channel_id=1, source_target_pairs={{0,24},{8,16},{16,8},{24,0},{1,25},{9,17},{17,9},{25,1},{2,26},{10... | collective-permute-start | bytes 589832 | tf_op jit(solution)/shard_map/ppermute | solution.py:492
  5.7 0.6 %collective-permute-start.4 = (bf16[384,256]{1,0:T(8,128)(2,1)}, bf16[384,256]{1,0:T(8,128)(2,1)S(1)}, u32[]{:S(2)}, u32[]{:S(2)}) collective-permute-start(bf16[384,256]{1,0:T(8,128)(2,1)} %get-tuple-element.26), channel_id=1, source_target_pairs={{0,16},{8,24},{16,0},{24,8},{1,17},{9,25},{17,1},{25,9},{2,18},{10... | collective-permute-start | bytes 589832 | tf_op jit(solution)/shard_map/ppermute | solution.py:492
  6.3 0.0 collective-permute-start.5
  6.4 2.7 %shard_map.96 = (bf16[384,256]{1,0:T(8,128)(2,1)}, bf16[384,256]{1,0:T(8,128)(2,1)}, bf16[384,256]{1,0:T(8,128)(2,1)}, bf16[384,256]{1,0:T(8,128)(2,1)}) custom-call(bf16[256,256]{1,0:T(8,128)(2,1)} %get-tuple-element.19.table_hbm, bf16[384,4,512]{2,1,0:T(4,128)(2,1)} %x_hbm.3), custom_call_target="tpu_custom_call" | custom-call | flops 201326592 | bytes 1572864 | tf_op jit(solution)/shard_map/pallas_call | solution.py:161
  9.1 1.5 %collective-permute-start = (bf16[384,256]{1,0:T(8,128)(2,1)}, bf16[384,256]{1,0:T(8,128)(2,1)S(1)}, u32[]{:S(2)}, u32[]{:S(2)}) collective-permute-start(bf16[384,256]{1,0:T(8,128)(2,1)} %get-tuple-element.21), channel_id=1, source_target_pairs={{0,24},{8,16},{16,8},{24,0},{1,25},{9,17},{17,9},{25,1},{2,26},{10... | collective-permute-start | bytes 589832 | tf_op jit(solution)/shard_map/ppermute | solution.py:492
  10.6 0.6 %collective-permute-start.1 = (bf16[384,256]{1,0:T(8,128)(2,1)}, bf16[384,256]{1,0:T(8,128)(2,1)S(1)}, u32[]{:S(2)}, u32[]{:S(2)}) collective-permute-start(bf16[384,256]{1,0:T(8,128)(2,1)} %get-tuple-element.22), channel_id=1, source_target_pairs={{0,16},{8,24},{16,0},{24,8},{1,17},{9,25},{17,1},{25,9},{2,18},{10... | collective-permute-start | bytes 589832 | tf_op jit(solution)/shard_map/ppermute | solution.py:492
  11.2 0.0 copy-done.7
  11.2 0.1 collective-permute-done.3.refs_1_
  11.3 0.7 %collective-permute-start.2 = (bf16[384,256]{1,0:T(8,128)(2,1)}, bf16[384,256]{1,0:T(8,128)(2,1)S(1)}, u32[]{:S(2)}, u32[]{:S(2)}) collective-permute-start(bf16[384,256]{1,0:T(8,128)(2,1)} %get-tuple-element.23), channel_id=1, source_target_pairs={{0,8},{8,0},{16,24},{24,16},{1,9},{9,1},{17,25},{25,17},{2,10},{10... | collective-permute-start | bytes 589832 | tf_op jit(solution)/shard_map/ppermute | solution.py:492
  12.0 4.4 %collective-permute-done.4.refs_2_ = bf16[384,256]{1,0:T(8,128)(2,1)S(1)} collective-permute-done((bf16[384,256]{1,0:T(8,128)(2,1)}, bf16[384,256]{1,0:T(8,128)(2,1)S(1)}, u32[]{:S(2)}, u32[]{:S(2)}) %collective-permute-start.4) | collective-permute-done | bytes 196640 | tf_op jit(solution)/shard_map/ppermute | solution.py:492
  16.4 0.0 collective-permute-done.5.refs_3_
  16.4 0.0 copy-done.2
  16.4 0.0 copy-done.3
  16.4 0.0 copy-done.4
  16.4 0.0 copy-done.6
  16.5 0.0 copy-start.5
  16.5 1.7 %shard_map.98 = (bf16[16,176,256]{2,1,0:T(8,128)(2,1)S(1)}, bf16[16,176,256]{2,1,0:T(8,128)(2,1)S(1)}) custom-call(s32[4]{0:T(128)S(1)} %copy-done.3, s32[11]{0:T(128)S(1)} %copy-done.4, bf16[256,512]{1,0:T(8,128)(2,1)S(1)} %copy-done.6, bf16[384,256]{1,0:T(8,128)(2,1)S(1)} %copy-done.2, bf16[384,256]{1,0:T(8,128)(2,1)S(1)} %collective-permute-done.3.refs_1_, ...), custom_call_target="tpu_custom_call" | custom-call | flops 2500000000 | bytes 3000000 | tf_op jit(solution)/shard_map/pallas_call | solution.py:273
  18.1 0.0 copy-done.5
  18.1 0.0 copy-start.1
  18.2 2.8 %shard_map.97.refs_4_ = f32[128,128]{1,0:T(8,128)S(1)} custom-call(s32[4]{0:T(128)S(1)} %copy-done.3, s32[11]{0:T(128)S(1)} %copy-done.4, f32[1,256]{1,0:T(1,128)S(1)} %get-tuple-element.38.w_ref, bf16[256,512]{1,0:T(8,128)(2,1)S(1)} %copy-done.6, bf16[2816,128]{1,0:T(8,128)(2,1)S(1)} %copy-done.5, bf16[384,256]{1,0:T(8,128)(2,1)S(1)} %copy-done.2, ...), custom_call_target="tpu_custom_call" | custom-call | flops 2500000000 | bytes 3000000 | tf_op jit(solution)/shard_map/pallas_call | solution.py:240
  20.9 0.0 collective-permute-done.refs_1_
  20.9 3.1 %collective-permute-done.1.refs_2_ = bf16[384,256]{1,0:T(8,128)(2,1)S(1)} collective-permute-done((bf16[384,256]{1,0:T(8,128)(2,1)}, bf16[384,256]{1,0:T(8,128)(2,1)S(1)}, u32[]{:S(2)}, u32[]{:S(2)}) %collective-permute-start.1) | collective-permute-done | bytes 196640 | tf_op jit(solution)/shard_map/ppermute | solution.py:492
  24.0 0.0 collective-permute-done.2.refs_3_
  24.0 0.0 copy-done.1
  24.0 2.8 %shard_map.99 = (bf16[64,128]{1,0:T(8,128)(2,1)S(1)}, bf16[64,128]{1,0:T(8,128)(2,1)S(1)}) custom-call(s32[4]{0:T(128)S(1)} %copy-done.3, s32[11]{0:T(128)S(1)} %copy-done.4, f32[1,256]{1,0:T(1,128)S(1)} %get-tuple-element.39.w_ref, bf16[256,512]{1,0:T(8,128)(2,1)S(1)} %copy-done.6, bf16[2816,128]{1,0:T(8,128)(2,1)S(1)} %copy-done.5, ...), custom_call_target="tpu_custom_call" | custom-call | flops 2500000000 | bytes 3000000 | tf_op jit(solution)/shard_map/pallas_call | solution.py:240
  26.8 0.1 collective-permute-start.6
  26.9 1.2 %collective-permute-done.6 = bf16[64,128]{1,0:T(8,128)(2,1)S(1)} collective-permute-done((bf16[64,128]{1,0:T(8,128)(2,1)S(1)}, bf16[64,128]{1,0:T(8,128)(2,1)S(1)}, u32[]{:S(2)}, u32[]{:S(2)}) %collective-permute-start.6) | collective-permute-done | bytes 16416 | tf_op jit(solution)/shard_map/ppermute | solution.py:492
  28.1 3.3 %collective-permute-start.9 = (bf16[64,128]{1,0:T(8,128)(2,1)S(1)}, bf16[64,128]{1,0:T(8,128)(2,1)S(1)}, u32[]{:S(2)}, u32[]{:S(2)}) collective-permute-start(bf16[64,128]{1,0:T(8,128)(2,1)S(1)} %add_convert_fusion.1), channel_id=1, source_target_pairs={{0,17},{1,16},{2,19},{3,18},{4,21},{5,20},{6,23},{7,22},{8,25},{9,... | collective-permute-start | bytes 49160 | tf_op jit(solution)/shard_map/ppermute | solution.py:492
  31.4 0.5 %collective-permute-start.8 = (bf16[64,128]{1,0:T(8,128)(2,1)S(1)}, bf16[64,128]{1,0:T(8,128)(2,1)S(1)}, u32[]{:S(2)}, u32[]{:S(2)}) collective-permute-start(bf16[64,128]{1,0:T(8,128)(2,1)S(1)} %add_convert_fusion.1), channel_id=1, source_target_pairs={{0,1},{1,0},{2,3},{3,2},{4,5},{5,4},{6,7},{7,6},{8,9},{9,8},{10,11... | collective-permute-start | bytes 49160 | tf_op jit(solution)/shard_map/ppermute | solution.py:492
  31.9 0.1 collective-permute-start.7
  32.0 1.1 %collective-permute-done.9 = bf16[64,128]{1,0:T(8,128)(2,1)S(1)} collective-permute-done((bf16[64,128]{1,0:T(8,128)(2,1)S(1)}, bf16[64,128]{1,0:T(8,128)(2,1)S(1)}, u32[]{:S(2)}, u32[]{:S(2)}) %collective-permute-start.9) | collective-permute-done | bytes 16416 | tf_op jit(solution)/shard_map/ppermute | solution.py:492
  33.1 2.0 %collective-permute-done.8 = bf16[64,128]{1,0:T(8,128)(2,1)S(1)} collective-permute-done((bf16[64,128]{1,0:T(8,128)(2,1)S(1)}, bf16[64,128]{1,0:T(8,128)(2,1)S(1)}, u32[]{:S(2)}, u32[]{:S(2)}) %collective-permute-start.8) | collective-permute-done | bytes 16416 | tf_op jit(solution)/shard_map/ppermute | solution.py:492
  35.1 0.5 %collective-permute-done.7 = bf16[64,128]{1,0:T(8,128)(2,1)S(1)} collective-permute-done((bf16[64,128]{1,0:T(8,128)(2,1)S(1)}, bf16[64,128]{1,0:T(8,128)(2,1)S(1)}, u32[]{:S(2)}, u32[]{:S(2)}) %collective-permute-start.7) | collective-permute-done | bytes 16416 | tf_op jit(solution)/shard_map/ppermute | solution.py:492
  35.7 3.6 %collective-permute-start.12 = (bf16[64,128]{1,0:T(8,128)(2,1)S(1)}, bf16[64,128]{1,0:T(8,128)(2,1)S(1)}, u32[]{:S(2)}, u32[]{:S(2)}) collective-permute-start(bf16[64,128]{1,0:T(8,128)(2,1)S(1)} %add_convert_fusion), channel_id=1, source_target_pairs={{0,6},{1,7},{2,4},{3,5},{4,2},{5,3},{6,0},{7,1},{8,14},{9,15},{10,... | collective-permute-start | bytes 49160 | tf_op jit(solution)/shard_map/ppermute | solution.py:492
  39.3 0.0 collective-permute-start.11
  39.3 0.8 %collective-permute-start.10 = (bf16[64,128]{1,0:T(8,128)(2,1)S(1)}, bf16[64,128]{1,0:T(8,128)(2,1)S(1)}, u32[]{:S(2)}, u32[]{:S(2)}) collective-permute-start(bf16[64,128]{1,0:T(8,128)(2,1)S(1)} %add_convert_fusion), channel_id=1, source_target_pairs={{0,2},{1,3},{2,0},{3,1},{4,6},{5,7},{6,4},{7,5},{8,10},{9,11},{10,... | collective-permute-start | bytes 49160 | tf_op jit(solution)/shard_map/ppermute | solution.py:492
  40.1 1.2 %collective-permute-done.12 = bf16[64,128]{1,0:T(8,128)(2,1)S(1)} collective-permute-done((bf16[64,128]{1,0:T(8,128)(2,1)S(1)}, bf16[64,128]{1,0:T(8,128)(2,1)S(1)}, u32[]{:S(2)}, u32[]{:S(2)}) %collective-permute-start.12) | collective-permute-done | bytes 16416 | tf_op jit(solution)/shard_map/ppermute | solution.py:492
  41.3 2.6 %collective-permute-done.11 = bf16[64,128]{1,0:T(8,128)(2,1)S(1)} collective-permute-done((bf16[64,128]{1,0:T(8,128)(2,1)S(1)}, bf16[64,128]{1,0:T(8,128)(2,1)S(1)}, u32[]{:S(2)}, u32[]{:S(2)}) %collective-permute-start.11) | collective-permute-done | bytes 16416 | tf_op jit(solution)/shard_map/ppermute | solution.py:492
  43.9 0.0 collective-permute-done.10
  44.0 0.0 copy-start
  44.0 0.1 collective-permute-start.13
  44.0 1.7 %shard_map.101 = (bf16[16,176,256]{2,1,0:T(8,128)(2,1)S(1)}, bf16[16,176,256]{2,1,0:T(8,128)(2,1)S(1)}) custom-call(s32[4]{0:T(128)S(1)} %copy-done.3, s32[11]{0:T(128)S(1)} %copy-done.4, bf16[256,512]{1,0:T(8,128)(2,1)S(1)} %copy-done.6, bf16[384,256]{1,0:T(8,128)(2,1)S(1)} %copy-done.1, bf16[384,256]{1,0:T(8,128)(2,1)S(1)} %collective-permute-done.refs_1_, ...), custom_call_target="tpu_custom_call" | custom-call | flops 2500000000 | bytes 3000000 | tf_op jit(solution)/shard_map/pallas_call | solution.py:273
  45.7 0.0 collective-permute-done.13.other_ref
  45.7 2.7 %shard_map.100 = (f32[3,128,128]{2,1,0:T(8,128)S(1)}, f32[11,11,2,16]{3,2,1,0:T(2,128)}) custom-call(f32[64,128]{1,0:T(8,128)S(1)} %add_add_fusion.half_ref, f32[64,128]{1,0:T(8,128)S(1)} %collective-permute-done.13.other_ref), custom_call_target="tpu_custom_call" | custom-call | tf_op jit(solution)/shard_map/pallas_call | solution.py:426
  48.4 0.0 copy-done
  48.4 4.5 %shard_map.102 = bf16[2,11,128,512]{3,2,1,0:T(8,128)(2,1)} custom-call(f32[3,128,128]{2,1,0:T(8,128)S(1)} %get-tuple-element.31.stack_ref, bf16[8,256,176]{2,1,0:T(8,128)(2,1)S(1)} %copy-done, bf16[16,176,256]{2,1,0:T(8,128)(2,1)S(1)} %get-tuple-element.28.refs_5_.refs_0_, bf16[16,176,256]{2,1,0:T(8,128)(2,1)S(1)} %get-tuple-element.32.refs_1_, ...), custom_call_target="tpu_custom_call" | custom-call | tf_op jit(solution)/shard_map/pallas_call | solution.py:478
  (4 shorter events, 0.0 us)
Async XLA Ops:
  3.2 8.1 %copy-start.7 = (f32[512]{0:T(512)S(1)}, f32[512]{0:T(512)}, u32[]{:S(2)}) copy-start(f32[512]{0:T(512)} %param.9) | copy-start | bytes 6148
  3.2 13.2 %copy-start.2 = (bf16[384,256]{1,0:T(8,128)(2,1)S(1)}, bf16[384,256]{1,0:T(8,128)(2,1)}, u32[]{:S(2)}) copy-start(bf16[384,256]{1,0:T(8,128)(2,1)} %get-tuple-element.24.refs_0_) | copy-start | bytes 589828
  3.2 13.2 %copy-start.3 = (s32[4]{0:T(128)S(1)}, s32[4]{0:T(128)}, u32[]{:S(2)}) copy-start(s32[4]{0:T(128)} %order_ref.7) | copy-start | bytes 52
  3.2 13.2 %copy-start.4 = (s32[11]{0:T(128)S(1)}, s32[11]{0:T(128)}, u32[]{:S(2)}) copy-start(s32[11]{0:T(128)} %offsets_ref.7) | copy-start | bytes 136
  3.2 13.2 %copy-start.6 = (bf16[256,512]{1,0:T(8,128)(2,1)S(1)}, bf16[256,512]{1,0:T(8,128)(2,1)}, u32[]{:S(2)}) copy-start(bf16[256,512]{1,0:T(8,128)(2,1)} %constant.6.clone.f_ref) | copy-start | bytes 786436
  3.2 8.1 %collective-permute-start.3 = (bf16[384,256]{1,0:T(8,128)(2,1)}, bf16[384,256]{1,0:T(8,128)(2,1)S(1)}, u32[]{:S(2)}, u32[]{:S(2)}) collective-permute-start(bf16[384,256]{1,0:T(8,128)(2,1)} %get-tuple-element.25), channel_id=1, source_target_pairs={{0,24},{8,16},{16,8},{24,0},{1,25},{9,17},{17,9},{25,1},{2,26},{10... | collective-permute-start | bytes 589832 | tf_op jit(solution)/shard_map/ppermute | solution.py:492
  5.7 10.7 %collective-permute-start.4 = (bf16[384,256]{1,0:T(8,128)(2,1)}, bf16[384,256]{1,0:T(8,128)(2,1)S(1)}, u32[]{:S(2)}, u32[]{:S(2)}) collective-permute-start(bf16[384,256]{1,0:T(8,128)(2,1)} %get-tuple-element.26), channel_id=1, source_target_pairs={{0,16},{8,24},{16,0},{24,8},{1,17},{9,25},{17,1},{25,9},{2,18},{10... | collective-permute-start | bytes 589832 | tf_op jit(solution)/shard_map/ppermute | solution.py:492
  6.3 10.1 %collective-permute-start.5 = (bf16[384,256]{1,0:T(8,128)(2,1)}, bf16[384,256]{1,0:T(8,128)(2,1)S(1)}, u32[]{:S(2)}, u32[]{:S(2)}) collective-permute-start(bf16[384,256]{1,0:T(8,128)(2,1)} %get-tuple-element.27), channel_id=1, source_target_pairs={{0,8},{8,0},{16,24},{24,16},{1,9},{9,1},{17,25},{25,17},{2,10},{10... | collective-permute-start | bytes 589832 | tf_op jit(solution)/shard_map/ppermute | solution.py:492
  9.1 11.9 %collective-permute-start = (bf16[384,256]{1,0:T(8,128)(2,1)}, bf16[384,256]{1,0:T(8,128)(2,1)S(1)}, u32[]{:S(2)}, u32[]{:S(2)}) collective-permute-start(bf16[384,256]{1,0:T(8,128)(2,1)} %get-tuple-element.21), channel_id=1, source_target_pairs={{0,24},{8,16},{16,8},{24,0},{1,25},{9,17},{17,9},{25,1},{2,26},{10... | collective-permute-start | bytes 589832 | tf_op jit(solution)/shard_map/ppermute | solution.py:492
  10.6 13.4 %collective-permute-start.1 = (bf16[384,256]{1,0:T(8,128)(2,1)}, bf16[384,256]{1,0:T(8,128)(2,1)S(1)}, u32[]{:S(2)}, u32[]{:S(2)}) collective-permute-start(bf16[384,256]{1,0:T(8,128)(2,1)} %get-tuple-element.22), channel_id=1, source_target_pairs={{0,16},{8,24},{16,0},{24,8},{1,17},{9,25},{17,1},{25,9},{2,18},{10... | collective-permute-start | bytes 589832 | tf_op jit(solution)/shard_map/ppermute | solution.py:492
  11.3 12.7 %collective-permute-start.2 = (bf16[384,256]{1,0:T(8,128)(2,1)}, bf16[384,256]{1,0:T(8,128)(2,1)S(1)}, u32[]{:S(2)}, u32[]{:S(2)}) collective-permute-start(bf16[384,256]{1,0:T(8,128)(2,1)} %get-tuple-element.23), channel_id=1, source_target_pairs={{0,8},{8,0},{16,24},{24,16},{1,9},{9,1},{17,25},{25,17},{2,10},{10... | collective-permute-start | bytes 589832 | tf_op jit(solution)/shard_map/ppermute | solution.py:492
  16.5 1.7 %copy-start.5 = (bf16[2816,128]{1,0:T(8,128)(2,1)S(1)}, bf16[2816,128]{1,0:T(8,128)(2,1)}, u32[]{:S(2)}) copy-start(bf16[2816,128]{1,0:T(8,128)(2,1)} %constant.7.clone.pick_ref) | copy-start | bytes 2162692
  18.1 5.9 %copy-start.1 = (bf16[384,256]{1,0:T(8,128)(2,1)S(1)}, bf16[384,256]{1,0:T(8,128)(2,1)}, u32[]{:S(2)}) copy-start(bf16[384,256]{1,0:T(8,128)(2,1)} %get-tuple-element.20.refs_0_) | copy-start | bytes 589828
  26.8 1.2 %collective-permute-start.6 = (bf16[64,128]{1,0:T(8,128)(2,1)S(1)}, bf16[64,128]{1,0:T(8,128)(2,1)S(1)}, u32[]{:S(2)}, u32[]{:S(2)}) collective-permute-start(bf16[64,128]{1,0:T(8,128)(2,1)S(1)} %get-tuple-element.30.refs_5_), channel_id=1, source_target_pairs={{0,8},{1,9},{2,10},{3,11},{4,12},{5,13},{6,14},{7,15},{8,0},{9,1},... | collective-permute-start | bytes 49160 | tf_op jit(solution)/shard_map/ppermute | solution.py:492
  28.1 5.0 %collective-permute-start.9 = (bf16[64,128]{1,0:T(8,128)(2,1)S(1)}, bf16[64,128]{1,0:T(8,128)(2,1)S(1)}, u32[]{:S(2)}, u32[]{:S(2)}) collective-permute-start(bf16[64,128]{1,0:T(8,128)(2,1)S(1)} %add_convert_fusion.1), channel_id=1, source_target_pairs={{0,17},{1,16},{2,19},{3,18},{4,21},{5,20},{6,23},{7,22},{8,25},{9,... | collective-permute-start | bytes 49160 | tf_op jit(solution)/shard_map/ppermute | solution.py:492
  31.4 3.7 %collective-permute-start.8 = (bf16[64,128]{1,0:T(8,128)(2,1)S(1)}, bf16[64,128]{1,0:T(8,128)(2,1)S(1)}, u32[]{:S(2)}, u32[]{:S(2)}) collective-permute-start(bf16[64,128]{1,0:T(8,128)(2,1)S(1)} %add_convert_fusion.1), channel_id=1, source_target_pairs={{0,1},{1,0},{2,3},{3,2},{4,5},{5,4},{6,7},{7,6},{8,9},{9,8},{10,11... | collective-permute-start | bytes 49160 | tf_op jit(solution)/shard_map/ppermute | solution.py:492
  31.9 3.7 %collective-permute-start.7 = (bf16[64,128]{1,0:T(8,128)(2,1)S(1)}, bf16[64,128]{1,0:T(8,128)(2,1)S(1)}, u32[]{:S(2)}, u32[]{:S(2)}) collective-permute-start(bf16[64,128]{1,0:T(8,128)(2,1)S(1)} %add_convert_fusion.1), channel_id=1, source_target_pairs={{0,16},{1,17},{2,18},{3,19},{4,20},{5,21},{6,22},{7,23},{8,24},{9,... | collective-permute-start | bytes 49160 | tf_op jit(solution)/shard_map/ppermute | solution.py:492
  35.7 5.7 %collective-permute-start.12 = (bf16[64,128]{1,0:T(8,128)(2,1)S(1)}, bf16[64,128]{1,0:T(8,128)(2,1)S(1)}, u32[]{:S(2)}, u32[]{:S(2)}) collective-permute-start(bf16[64,128]{1,0:T(8,128)(2,1)S(1)} %add_convert_fusion), channel_id=1, source_target_pairs={{0,6},{1,7},{2,4},{3,5},{4,2},{5,3},{6,0},{7,1},{8,14},{9,15},{10,... | collective-permute-start | bytes 49160 | tf_op jit(solution)/shard_map/ppermute | solution.py:492
  39.3 4.6 %collective-permute-start.11 = (bf16[64,128]{1,0:T(8,128)(2,1)S(1)}, bf16[64,128]{1,0:T(8,128)(2,1)S(1)}, u32[]{:S(2)}, u32[]{:S(2)}) collective-permute-start(bf16[64,128]{1,0:T(8,128)(2,1)S(1)} %add_convert_fusion), channel_id=1, source_target_pairs={{0,4},{1,5},{2,6},{3,7},{4,0},{5,1},{6,2},{7,3},{8,12},{9,13},{10,... | collective-permute-start | bytes 49160 | tf_op jit(solution)/shard_map/ppermute | solution.py:492
  39.3 4.6 %collective-permute-start.10 = (bf16[64,128]{1,0:T(8,128)(2,1)S(1)}, bf16[64,128]{1,0:T(8,128)(2,1)S(1)}, u32[]{:S(2)}, u32[]{:S(2)}) collective-permute-start(bf16[64,128]{1,0:T(8,128)(2,1)S(1)} %add_convert_fusion), channel_id=1, source_target_pairs={{0,2},{1,3},{2,0},{3,1},{4,6},{5,7},{6,4},{7,5},{8,10},{9,11},{10,... | collective-permute-start | bytes 49160 | tf_op jit(solution)/shard_map/ppermute | solution.py:492
  44.0 4.4 %copy-start = (bf16[8,256,176]{2,1,0:T(8,128)(2,1)S(1)}, bf16[8,256,176]{2,1,0:T(8,128)(2,1)}, u32[]{:S(2)}) copy-start(bf16[8,256,176]{2,1,0:T(8,128)(2,1)} %constant.8.clone.spread_ref) | copy-start | bytes 2162692
  44.0 1.7 %collective-permute-start.13 = (f32[64,128]{1,0:T(8,128)S(1)}, f32[64,128]{1,0:T(8,128)S(1)}, u32[]{:S(2)}, u32[]{:S(2)}) collective-permute-start(f32[64,128]{1,0:T(8,128)S(1)} %add_add_fusion.half_ref), channel_id=1, source_target_pairs={{0,8},{1,9},{2,10},{3,11},{4,12},{5,13},{6,14},{7,15},{8,0},{9,1},... | collective-permute-start | bytes 98312 | tf_op jit(solution)/shard_map/ppermute | solution.py:492

commit v5 on v4

--- a/solution.py
+++ b/solution.py
@@ -61,19 +61,19 @@
 
 
 def spread_table():
-    spread = np.zeros((STACK, 2, LANE, 2 * HALF_ROWS), np.float32)
+    spread = np.zeros((STACK, 2, LANE, WIDE), np.float32)
     for m in range(STACK):
         for b in range(NBLK):
             real = m * 32 + b
             imag = m * 32 + 16 + b
             first = slice(b * SUB, b * SUB + SUB)
-            second = slice(HALF_ROWS + b * SUB, HALF_ROWS + b * SUB + SUB)
+            second = slice(LANE + b * SUB, LANE + b * SUB + SUB)
             spread[m, 0, real, first] = 1.0
             spread[m, 0, imag, second] = 1.0
             spread[m, 1, imag, first] = -1.0
             spread[m, 1, real, second] = 1.0
     spread = np.concatenate([spread, spread], axis=2)
-    return spread.reshape(STACK * 2, WIDE, 2 * HALF_ROWS).astype(jnp.bfloat16)
+    return spread.reshape(STACK * 2, WIDE, WIDE).astype(jnp.bfloat16)
 
 
 def split(x):
@@ -116,11 +116,7 @@
 def pack_kernel(base, parts, first, table_hbm, x_hbm, *refs):
     lanes = x_hbm.shape[1]
     out_refs = refs[:lanes]
-    if first:
-        pick, table, x_ref, table_sem, x_sem = refs[lanes:]
-    else:
-        pick, x_ref, table_sem, x_sem = refs[lanes:]
-        table = pick
+    pick, table, x_ref, table_sem, x_sem = refs[lanes:]
     steps, _, width = x_ref.shape
     part = steps // parts
     table_copy = pltpu.make_async_copy(table_hbm, table, table_sem)
@@ -132,8 +128,7 @@
         copies.append(pltpu.make_async_copy(source, x_ref.at[at], x_sem.at[i]))
         copies[-1].start()
     table_copy.wait()
-    if first:
-        pick[...] = lane_pick(table, lanes)
+    pick[...] = lane_pick(table, lanes) if first else table[...]
     rows = WIDE // lanes
     for i in range(steps // rows):
         if i * rows % part == 0:
@@ -148,16 +143,13 @@
     steps, lanes, _ = snapshots.shape
     parts = math.gcd(steps * lanes // WIDE, 3)
     outs = [jax.ShapeDtypeStruct((steps, width), BF16)] * lanes
+    outs.append(jax.ShapeDtypeStruct((WIDE, WIDE), BF16))
     scratch = [
+        pltpu.SMEM(table.shape, jnp.int32) if first else pltpu.VMEM(table.shape, BF16),
         pltpu.VMEM((steps, lanes, width), BF16),
         pltpu.SemaphoreType.DMA,
         pltpu.SemaphoreType.DMA((parts,)),
     ]
-    if first:
-        outs.append(jax.ShapeDtypeStruct((WIDE, WIDE), BF16))
-        scratch = [pltpu.SMEM(table.shape, jnp.int32)] + scratch
-    else:
-        scratch = [pltpu.VMEM(table.shape, BF16)] + scratch
     return pl.pallas_call(
         functools.partial(pack_kernel, base, parts, first),
         out_shape=outs,
@@ -188,15 +180,27 @@
 
 
 def transform(offsets_ref, f_ref, record, s_ref):
-    for i in range(NBLK):
-        x = [record[c, pl.ds(offsets_ref[i], NFFT), :].astype(BF16) for c in range(record.shape[0])]
-        x = jnp.concatenate(x, axis=1)
+    wanted = [(i, c) for i in range(NBLK) for c in range(record.shape[0])]
+    for first in range(0, len(wanted), 2):
+        pair = wanted[first : first + 2]
+        x = [record[c, pl.ds(offsets_ref[i], NFFT), :].astype(BF16) for i, c in pair]
+        x = jnp.concatenate(x, axis=1) if len(x) > 1 else x[0]
         y = dot(f_ref[...], jnp.concatenate([x, x], axis=0))
-        s_ref[i] = y[:NFREQ]
-        s_ref[NBLK + i] = y[NFREQ:]
-
-
-def gram_kernel(lanes, scale, first, order_ref, offsets_ref, w_ref, f_ref, pick_ref, *refs):
+        for at, (i, c) in enumerate(pair):
+            cols = slice(c * LANE, (c + 1) * LANE)
+            s_ref[i, :, cols] = y[:NFREQ, at * LANE : (at + 1) * LANE]
+            s_ref[NBLK + i, :, cols] = y[NFREQ:, at * LANE : (at + 1) * LANE]
+
+
+def padded(s):
+    width = s.shape[2]
+    pad = jnp.zeros((LANE - HALF_ROWS, width), F32)
+    real = s[:NBLK].reshape(HALF_ROWS, width)
+    imag = s[NBLK:].reshape(HALF_ROWS, width)
+    return jnp.concatenate([real, pad, imag, pad], axis=0)
+
+
+def gram_kernel(lanes, scale, first, last, order_ref, offsets_ref, w_ref, f_ref, pick_ref, *refs):
     pieces = refs[:lanes]
     rest = refs[lanes:]
     if not first:
@@ -207,12 +211,10 @@
     row = lax.broadcasted_iota(jnp.int32, (HALF_ROWS, LANE), 0)
     col = lax.broadcasted_iota(jnp.int32, (HALF_ROWS, LANE), 1)
     same = row % SUB == col % SUB
-    pad = jnp.zeros((LANE - HALF_ROWS, s_ref.shape[2]), F32)
     for g in range(GROUPS):
         at = slice(g * SUB, (g + 1) * SUB)
-        s = s_ref[:, at, :].reshape(2 * HALF_ROWS, -1)
-        other = jnp.concatenate([s[:HALF_ROWS], pad, s[HALF_ROWS:], pad], axis=0)
-        full = dot_nt(s.astype(BF16), other.astype(BF16))
+        s = s_ref[:, at, :]
+        full = dot_nt(s.reshape(2 * HALF_ROWS, -1).astype(BF16), padded(s).astype(BF16))
         real = full[:HALF_ROWS, :LANE] + full[HALF_ROWS:, LANE:]
         imag = full[:HALF_ROWS, LANE:] - full[HALF_ROWS:, :LANE]
         real = jnp.where(same, real, 0.0)
@@ -222,28 +224,29 @@
             masked[at, a * WIDE : a * WIDE + LANE] = real[rows]
             masked[at, a * WIDE + LANE : (a + 1) * WIDE] = imag[rows]
     total = dot(masked[...].astype(BF16), pick_ref[...]).T * scale
-    if first:
+    if not first:
+        total = total + before_ref[...]
+    if not last:
         packed_refs[0][...] = total
         return
     keep_ref, send_ref = packed_refs
-    total = total + before_ref[...]
     other = lax.axis_index("tm") % 2 == 1
     keep_ref[...] = jnp.where(other, total[HALF:], total[:HALF]).astype(BF16)
     send_ref[...] = jnp.where(other, total[:HALF], total[HALF:]).astype(BF16)
 
 
-def gram_part(order, offsets, weights, tables, pieces, before, scale):
+def gram_part(order, offsets, weights, tables, pieces, before, last, scale):
     lanes = len(pieces)
     steps, width = pieces[0].shape
     first = not before
     args = [order, offsets, weights, *tables, *pieces, *before]
     return pl.pallas_call(
-        functools.partial(gram_kernel, lanes, scale, first),
-        out_shape=[jax.ShapeDtypeStruct((PACKED, NFREQ), F32)]
-        if first
-        else [jax.ShapeDtypeStruct((HALF, NFREQ), BF16)] * 2,
+        functools.partial(gram_kernel, lanes, scale, first, last),
+        out_shape=[jax.ShapeDtypeStruct((HALF, NFREQ), BF16)] * 2
+        if last
+        else [jax.ShapeDtypeStruct((PACKED, NFREQ), F32)],
         in_specs=[SMEM, SMEM] + [VMEM] * (len(args) - 2),
-        out_specs=[VMEM] * (1 if first else 2),
+        out_specs=[VMEM] * (2 if last else 1),
         scratch_shapes=[
             pltpu.VMEM((width // LANE, lanes * steps, LANE), F32),
             pltpu.VMEM((2 * NBLK, NFREQ, width), F32),
@@ -251,7 +254,7 @@
         ],
         compiler_params=pltpu.CompilerParams(vmem_limit_bytes=32 * 2**20),
         cost_estimate=pl.CostEstimate(
-            flops=25 * 10**8, bytes_accessed=3 * 10**6, transcendentals=0
+            flops=width * 10**7, bytes_accessed=3 * 10**6, transcendentals=0
         ),
     )(*args)
 
@@ -261,15 +264,14 @@
     fill_record(order_ref, refs[:lanes], record, None)
     transform(offsets_ref, f_ref, record, s_ref)
     for g in range(GROUPS):
-        s = s_ref[:, g * SUB : (g + 1) * SUB, :].reshape(2 * HALF_ROWS, -1)
-        high_ref[g], low_ref[g] = split(s)
+        high_ref[g], low_ref[g] = split(padded(s_ref[:, g * SUB : (g + 1) * SUB, :]))
 
 
 def spectrum(order, offsets, fourier, pieces, after):
     lanes = len(pieces)
     steps, width = pieces[0].shape
     args = [order, offsets, fourier, *pieces, *after]
-    part = jax.ShapeDtypeStruct((GROUPS, 2 * HALF_ROWS, width), BF16)
+    part = jax.ShapeDtypeStruct((GROUPS, WIDE, width), BF16)
     return pl.pallas_call(
         functools.partial(spectrum_kernel, lanes),
         out_shape=[part, part],
@@ -281,7 +283,7 @@
         ],
         compiler_params=pltpu.CompilerParams(vmem_limit_bytes=32 * 2**20),
         cost_estimate=pl.CostEstimate(
-            flops=25 * 10**8, bytes_accessed=3 * 10**6, transcendentals=0
+            flops=width * 10**7, bytes_accessed=3 * 10**6, transcendentals=0
         ),
     )(*args)
 
@@ -449,8 +451,8 @@
 
     @pl.when(step == 0)
     def _():
-        row = lax.broadcasted_iota(jnp.int32, (NFREQ, 2 * HALF_ROWS), 0)
-        col = lax.broadcasted_iota(jnp.int32, (NFREQ, 2 * HALF_ROWS), 1)
+        row = lax.broadcasted_iota(jnp.int32, (NFREQ, WIDE), 0)
+        col = lax.broadcasted_iota(jnp.int32, (NFREQ, WIDE), 1)
         same = row % SUB == col % SUB
         for at, m0 in enumerate(range(0, NBLK, STACK)):
             both = jnp.concatenate(split(stack_ref[at]), axis=1)
@@ -463,11 +465,13 @@
     for h in range(STEP_GROUPS):
         g = step * STEP_GROUPS + h
         start = pl.multiple_of(g * SUB, SUB)
-        v_high, v_low = split(v[:, pl.ds(start, SUB), :].reshape(2 * HALF_ROWS, 2 * HALF_ROWS))
+        v_high, v_low = split(v[:, pl.ds(start, SUB), :].reshape(2 * HALF_ROWS, WIDE))
         s_high = jnp.concatenate([r[g] for r in high_refs], axis=1)
         s_low = jnp.concatenate([r[g] for r in low_refs], axis=1)
-        field = dot(jnp.concatenate([v_high, v_low], axis=0), s_high)
-        field = field[: 2 * HALF_ROWS] + (field[2 * HALF_ROWS :] + dot(v_high, s_low))
+        field = dot(
+            jnp.concatenate([v_high, v_high, v_low], axis=1),
+            jnp.concatenate([s_high, s_low, s_high], axis=0),
+        )
         fields.append(field.reshape(2 * NBLK, SUB, -1))
     both = jnp.concatenate(fields, axis=1).astype(BF16)
     out_ref[...] = both.reshape(out_ref.shape)
@@ -483,7 +487,7 @@
         out_specs=pl.BlockSpec(
             (2, NBLK, STEP_GROUPS * SUB, width), lambda i: (0, 0, i, 0)
         ),
-        scratch_shapes=[pltpu.VMEM((2 * NBLK, NFREQ, 2 * HALF_ROWS), F32)],
+        scratch_shapes=[pltpu.VMEM((2 * NBLK, NFREQ, WIDE), F32)],
         compiler_params=pltpu.CompilerParams(vmem_limit_bytes=32 * 2**20),
     )(stacks, spread, *highs, *lows)
 
@@ -500,25 +504,27 @@
     lanes = lax.axis_size("tm")
     groups = lax.axis_size("sx") * lax.axis_size("sy")
     points = snapshots.shape[2]
-    width = points // 2
+    chunks = [(0, points // 2), (points // 2, points // 2)]
     scale = 1.0 / (lanes * groups * points)
     tables = (jnp.asarray(fourier_tables()), jnp.asarray(pick_table()))
     weights = weights.reshape(1, -1)
 
     arrived = []
     table = owner
-    for base in range(0, points, width):
+    for base, width in chunks:
         packed = pack(table, snapshots, base, width, base == 0)
-        table = packed[lanes] if base == 0 else table
+        table = packed[lanes]
         moved = [swap(packed[d], "tm", d, lanes) for d in reversed(range(1, lanes))]
         arrived.append([packed[0]] + moved)
 
     highs, lows = [], []
     before = []
     for at, pieces in enumerate(arrived):
-        here = weights[:, at * width : (at + 1) * width]
-        total = gram_part(block_order, offsets, here, tables, pieces, before, scale)
-        after = total if at == len(arrived) - 1 else []
+        base, width = chunks[at]
+        here = weights[:, base : base + width]
+        last = at == len(arrived) - 1
+        total = gram_part(block_order, offsets, here, tables, pieces, before, last, scale)
+        after = total if last else []
         high, low = spectrum(block_order, offsets, tables[0], pieces, after)
         highs.append(high)
         lows.append(low)
@@ -539,6 +545,7 @@
         while len(terms) > 1:
             terms = [a + b for a, b in zip(terms[::2], terms[1::2])]
         half = terms[0]
+    half, highs[-1] = lax.optimization_barrier((half, highs[-1]))
     other = swap(half, axes, bits[0], size)
 
     stacks, gram = roots(half, other, NFREQ // groups)

time: 53 us -> 52.7 us (level)
  local copies, waits for them, and re-layouts: 0.05 us -> 3.9 us
  waiting for transfers between devices: 16.2 us -> 12.5 us
  starting transfers between devices: 14.6 us -> 13.6 us
    ppermute x14, waiting for transfers between devices: 16.2 us -> 12.5 us  [swap(): return lax.ppermute(x, axes, [(i, i ^ mask) for i in range(size)])]
    unnamed x16 -> x14, local copies, waits for them, and re-layouts: 0.05 us -> 3.2 us
    ppermute x14, starting transfers between devices: 14.6 us -> 13.6 us  [swap(): return lax.ppermute(x, axes, [(i, i ^ mask) for i in range(size)])]
    slice x1, local copies, waits for them, and re-layouts: 0.01 us -> 0.7 us  [body(): here = weights[:, base:base + width]]
  transfers between devices with their start and end apart: 14 -> 14, of which waited for: 9 -> 7; matrix products, arithmetic and copies ran while one was open for 0% -> 1% of each run, Pallas kernels for 17% -> 17%
where the time goes in v5:
time: 52.7 us; the launch traced here: 52.4 us
  Pallas kernels  21.6 us (41%)
  starting transfers between devices  13.6 us (26%)
  waiting for transfers between devices  12.5 us (24%)
  local copies, waits for them, and re-layouts  3.9 us (7%)
  between operations  0.78 us (1%)
    ppermute x14, starting transfers between devices, swap(): return lax.ppermute(x, axes, [(i, i ^ mask) for i in range(size)])  13.6 us
    ppermute x14, waiting for transfers between devices, swap(): return lax.ppermute(x, axes, [(i, i ^ mask) for i in range(size)])  12.5 us
    pallas_call x2, Pallas kernels, gram_part(): pl.pallas_call(functools.partial(gram_kernel, lanes, scale, first, last),...  5.6 us
    pallas_call x2, Pallas kernels, pack(): pl.pallas_call(functools.partial(pack_kernel, base, parts, first), out_sh...  5.28 us
    pallas_call x1, Pallas kernels, mode_fields(): pl.pallas_call(functools.partial(mode_kernel, len(highs)), grid=(GROUPS /...  4.57 us
    pallas_call x2, Pallas kernels, spectrum(): pl.pallas_call(functools.partial(spectrum_kernel, lanes), out_shape=[part...  3.53 us
    unnamed x14, local copies, waits for them, and re-layouts  3.2 us
    pallas_call x1, Pallas kernels, roots(): pl.pallas_call(functools.partial(root_kernel, share), out_shape=[jax.Shap...  2.66 us
  transfers between devices with their start and end apart: 14, of which 7 were waited for; matrix products, arithmetic and copies ran while one was open for 1% of the time, Pallas kernels for 17%

profile of v5, /device:TPU:0, one launch (start us, length us, event | category | flops | bytes accessed | tf_op | source)
XLA Modules:
  0.0 52.4 jit_solution(7929683613231949569)
XLA Ops:
  0.6 2.5 %shard_map.95 = (bf16[384,256]{1,0:T(8,128)(2,1)}, bf16[384,256]{1,0:T(8,128)(2,1)}, bf16[384,256]{1,0:T(8,128)(2,1)}, bf16[384,256]{1,0:T(8,128)(2,1)}, bf16[256,256]{1,0:T(8,128)(2,1)}) custom-call(s32[1,4]{1,0:T(1,128)} %table_hbm.1, bf16[384,4,512]{2,1,0:T(4,128)(2,1)} %x_hbm.3), custom_call_target="tpu_custom_call" | custom-call | flops 201326592 | bytes 1572864 | tf_op jit(solution)/shard_map/pallas_call | solution.py:153
  3.2 2.5 %collective-permute-start.3 = (bf16[384,256]{1,0:T(8,128)(2,1)}, bf16[384,256]{1,0:T(8,128)(2,1)S(1)}, u32[]{:S(2)}, u32[]{:S(2)}) collective-permute-start(bf16[384,256]{1,0:T(8,128)(2,1)} %get-tuple-element.27), channel_id=1, source_target_pairs={{0,24},{8,16},{16,8},{24,0},{1,25},{9,17},{17,9},{25,1},{2,26},{10... | collective-permute-start | bytes 589832 | tf_op jit(solution)/shard_map/ppermute | solution.py:496
  5.6 0.6 %collective-permute-start.4 = (bf16[384,256]{1,0:T(8,128)(2,1)}, bf16[384,256]{1,0:T(8,128)(2,1)S(1)}, u32[]{:S(2)}, u32[]{:S(2)}) collective-permute-start(bf16[384,256]{1,0:T(8,128)(2,1)} %get-tuple-element.28), channel_id=1, source_target_pairs={{0,16},{8,24},{16,0},{24,8},{1,17},{9,25},{17,1},{25,9},{2,18},{10... | collective-permute-start | bytes 589832 | tf_op jit(solution)/shard_map/ppermute | solution.py:496
  6.3 0.0 collective-permute-start.5
  6.3 2.7 %shard_map.96 = (bf16[384,256]{1,0:T(8,128)(2,1)}, bf16[384,256]{1,0:T(8,128)(2,1)}, bf16[384,256]{1,0:T(8,128)(2,1)}, bf16[384,256]{1,0:T(8,128)(2,1)}, bf16[256,256]{1,0:T(8,128)(2,1)}) custom-call(bf16[256,256]{1,0:T(8,128)(2,1)} %get-tuple-element.21.table_hbm, bf16[384,4,512]{2,1,0:T(4,128)(2,1)} %x_hbm.3), custom_call_target="tpu_custom_call" | custom-call | flops 201326592 | bytes 1572864 | tf_op jit(solution)/shard_map/pallas_call | solution.py:153
  9.1 1.5 %collective-permute-start = (bf16[384,256]{1,0:T(8,128)(2,1)}, bf16[384,256]{1,0:T(8,128)(2,1)S(1)}, u32[]{:S(2)}, u32[]{:S(2)}) collective-permute-start(bf16[384,256]{1,0:T(8,128)(2,1)} %get-tuple-element.23), channel_id=1, source_target_pairs={{0,24},{8,16},{16,8},{24,0},{1,25},{9,17},{17,9},{25,1},{2,26},{10... | collective-permute-start | bytes 589832 | tf_op jit(solution)/shard_map/ppermute | solution.py:496
  10.6 0.6 %collective-permute-start.1 = (bf16[384,256]{1,0:T(8,128)(2,1)}, bf16[384,256]{1,0:T(8,128)(2,1)S(1)}, u32[]{:S(2)}, u32[]{:S(2)}) collective-permute-start(bf16[384,256]{1,0:T(8,128)(2,1)} %get-tuple-element.24), channel_id=1, source_target_pairs={{0,16},{8,24},{16,0},{24,8},{1,17},{9,25},{17,1},{25,9},{2,18},{10... | collective-permute-start | bytes 589832 | tf_op jit(solution)/shard_map/ppermute | solution.py:496
  11.2 0.7 %fusion = (f32[1,256]{1,0:T(1,128)S(1)}, f32[1,256]{1,0:T(1,128)S(1)}) fusion(f32[1,512]{1,0:T(1,128)} %bitcast.8), kind=kLoop, calls=%fused_computation.3 | loop fusion | bytes 4096 | tf_op jit(solution)/shard_map/slice | solution.py:524
  11.9 0.0 collective-permute-done.3.refs_1_
  11.9 0.0 collective-permute-start.2
  12.0 4.4 %collective-permute-done.4.refs_2_ = bf16[384,256]{1,0:T(8,128)(2,1)S(1)} collective-permute-done((bf16[384,256]{1,0:T(8,128)(2,1)}, bf16[384,256]{1,0:T(8,128)(2,1)S(1)}, u32[]{:S(2)}, u32[]{:S(2)}) %collective-permute-start.4) | collective-permute-done | bytes 196640 | tf_op jit(solution)/shard_map/ppermute | solution.py:496
  16.4 0.0 collective-permute-done.5.refs_3_
  16.4 0.0 copy-start.2
  16.4 0.9 %copy-done.2 = bf16[384,256]{1,0:T(8,128)(2,1)S(1)} copy-done((bf16[384,256]{1,0:T(8,128)(2,1)S(1)}, bf16[384,256]{1,0:T(8,128)(2,1)}, u32[]{:S(2)}) %copy-start.2) | copy-done | bytes 196632
  17.3 0.0 copy-start.3
  17.3 0.7 %copy-done.3 = s32[4]{0:T(128)S(1)} copy-done((s32[4]{0:T(128)S(1)}, s32[4]{0:T(128)}, u32[]{:S(2)}) %copy-start.3) | copy-done | bytes 40
  17.9 0.0 copy-start.4
  17.9 0.7 %copy-done.4 = s32[11]{0:T(128)S(1)} copy-done((s32[11]{0:T(128)S(1)}, s32[11]{0:T(128)}, u32[]{:S(2)}) %copy-start.4) | copy-done | bytes 68
  18.6 0.0 copy-start.6
  18.6 0.9 %copy-done.6 = bf16[256,512]{1,0:T(8,128)(2,1)S(1)} copy-done((bf16[256,512]{1,0:T(8,128)(2,1)S(1)}, bf16[256,512]{1,0:T(8,128)(2,1)}, u32[]{:S(2)}) %copy-start.6) | copy-done | bytes 262168
  19.6 0.0 copy-start.5
  19.6 1.8 %shard_map.98 = (bf16[16,256,256]{2,1,0:T(8,128)(2,1)S(1)}, bf16[16,256,256]{2,1,0:T(8,128)(2,1)S(1)}) custom-call(s32[4]{0:T(128)S(1)} %copy-done.3, s32[11]{0:T(128)S(1)} %copy-done.4, bf16[256,512]{1,0:T(8,128)(2,1)S(1)} %copy-done.6, bf16[384,256]{1,0:T(8,128)(2,1)S(1)} %copy-done.2, bf16[384,256]{1,0:T(8,128)(2,1)S(1)} %collective-permute-done.3.refs_1_, ...), custom_call_target="tpu_custom_call" | custom-call | flops 2560000000 | bytes 3000000 | tf_op jit(solution)/shard_map/pallas_call | solution.py:275
  21.3 0.0 copy-done.5
  21.3 0.0 copy-start.1
  21.4 2.8 %shard_map.97.refs_4_ = f32[128,128]{1,0:T(8,128)S(1)} custom-call(s32[4]{0:T(128)S(1)} %copy-done.3, s32[11]{0:T(128)S(1)} %copy-done.4, f32[1,256]{1,0:T(1,128)S(1)} %get-tuple-element.42.w_ref, bf16[256,512]{1,0:T(8,128)(2,1)S(1)} %copy-done.6, bf16[2816,128]{1,0:T(8,128)(2,1)S(1)} %copy-done.5, bf16[384,256]{1,0:T(8,128)(2,1)S(1)} %copy-done.2, ...), custom_call_target="tpu_custom_call" | custom-call | flops 2560000000 | bytes 3000000 | tf_op jit(solution)/shard_map/pallas_call | solution.py:243
  24.2 0.0 collective-permute-done.refs_1_
  24.2 0.0 collective-permute-done.1.refs_2_
  24.2 0.0 collective-permute-done.2.refs_3_
  24.2 0.0 copy-done.1
  24.2 2.8 %shard_map.99 = (bf16[64,128]{1,0:T(8,128)(2,1)S(1)}, bf16[64,128]{1,0:T(8,128)(2,1)S(1)}) custom-call(s32[4]{0:T(128)S(1)} %copy-done.3, s32[11]{0:T(128)S(1)} %copy-done.4, f32[1,256]{1,0:T(1,128)S(1)} %get-tuple-element.43.w_ref, bf16[256,512]{1,0:T(8,128)(2,1)S(1)} %copy-done.6, bf16[2816,128]{1,0:T(8,128)(2,1)S(1)} %copy-done.5, ...), custom_call_target="tpu_custom_call" | custom-call | flops 2560000000 | bytes 3000000 | tf_op jit(solution)/shard_map/pallas_call | solution.py:243
  27.0 0.1 collective-permute-start.6
  27.1 1.2 %collective-permute-done.6 = bf16[64,128]{1,0:T(8,128)(2,1)S(1)} collective-permute-done((bf16[64,128]{1,0:T(8,128)(2,1)S(1)}, bf16[64,128]{1,0:T(8,128)(2,1)S(1)}, u32[]{:S(2)}, u32[]{:S(2)}) %collective-permute-start.6) | collective-permute-done | bytes 16416 | tf_op jit(solution)/shard_map/ppermute | solution.py:496
  28.3 3.0 %collective-permute-start.9 = (bf16[64,128]{1,0:T(8,128)(2,1)S(1)}, bf16[64,128]{1,0:T(8,128)(2,1)S(1)}, u32[]{:S(2)}, u32[]{:S(2)}) collective-permute-start(bf16[64,128]{1,0:T(8,128)(2,1)S(1)} %add_convert_fusion.1), channel_id=1, source_target_pairs={{0,17},{1,16},{2,19},{3,18},{4,21},{5,20},{6,23},{7,22},{8,25},{9,... | collective-permute-start | bytes 49160 | tf_op jit(solution)/shard_map/ppermute | solution.py:496
  31.3 0.5 %collective-permute-start.8 = (bf16[64,128]{1,0:T(8,128)(2,1)S(1)}, bf16[64,128]{1,0:T(8,128)(2,1)S(1)}, u32[]{:S(2)}, u32[]{:S(2)}) collective-permute-start(bf16[64,128]{1,0:T(8,128)(2,1)S(1)} %add_convert_fusion.1), channel_id=1, source_target_pairs={{0,1},{1,0},{2,3},{3,2},{4,5},{5,4},{6,7},{7,6},{8,9},{9,8},{10,11... | collective-permute-start | bytes 49160 | tf_op jit(solution)/shard_map/ppermute | solution.py:496
  31.9 0.1 collective-permute-start.7
  32.0 1.1 %collective-permute-done.9 = bf16[64,128]{1,0:T(8,128)(2,1)S(1)} collective-permute-done((bf16[64,128]{1,0:T(8,128)(2,1)S(1)}, bf16[64,128]{1,0:T(8,128)(2,1)S(1)}, u32[]{:S(2)}, u32[]{:S(2)}) %collective-permute-start.9) | collective-permute-done | bytes 16416 | tf_op jit(solution)/shard_map/ppermute | solution.py:496
  33.0 2.0 %collective-permute-done.8 = bf16[64,128]{1,0:T(8,128)(2,1)S(1)} collective-permute-done((bf16[64,128]{1,0:T(8,128)(2,1)S(1)}, bf16[64,128]{1,0:T(8,128)(2,1)S(1)}, u32[]{:S(2)}, u32[]{:S(2)}) %collective-permute-start.8) | collective-permute-done | bytes 16416 | tf_op jit(solution)/shard_map/ppermute | solution.py:496
  35.1 0.5 %collective-permute-done.7 = bf16[64,128]{1,0:T(8,128)(2,1)S(1)} collective-permute-done((bf16[64,128]{1,0:T(8,128)(2,1)S(1)}, bf16[64,128]{1,0:T(8,128)(2,1)S(1)}, u32[]{:S(2)}, u32[]{:S(2)}) %collective-permute-start.7) | collective-permute-done | bytes 16416 | tf_op jit(solution)/shard_map/ppermute | solution.py:496
  35.6 0.0 copy-start
  35.6 3.6 %collective-permute-start.12 = (bf16[64,128]{1,0:T(8,128)(2,1)S(1)}, bf16[64,128]{1,0:T(8,128)(2,1)S(1)}, u32[]{:S(2)}, u32[]{:S(2)}) collective-permute-start(bf16[64,128]{1,0:T(8,128)(2,1)S(1)} %add_convert_fusion), channel_id=1, source_target_pairs={{0,6},{1,7},{2,4},{3,5},{4,2},{5,3},{6,0},{7,1},{8,14},{9,15},{10,... | collective-permute-start | bytes 49160 | tf_op jit(solution)/shard_map/ppermute | solution.py:496
  39.3 0.0 collective-permute-start.11
  39.3 0.8 %collective-permute-start.10 = (bf16[64,128]{1,0:T(8,128)(2,1)S(1)}, bf16[64,128]{1,0:T(8,128)(2,1)S(1)}, u32[]{:S(2)}, u32[]{:S(2)}) collective-permute-start(bf16[64,128]{1,0:T(8,128)(2,1)S(1)} %add_convert_fusion), channel_id=1, source_target_pairs={{0,2},{1,3},{2,0},{3,1},{4,6},{5,7},{6,4},{7,5},{8,10},{9,11},{10,... | collective-permute-start | bytes 49160 | tf_op jit(solution)/shard_map/ppermute | solution.py:496
  40.1 1.8 %shard_map.100 = (bf16[16,256,256]{2,1,0:T(8,128)(2,1)S(1)}, bf16[16,256,256]{2,1,0:T(8,128)(2,1)S(1)}) custom-call(s32[4]{0:T(128)S(1)} %copy-done.3, s32[11]{0:T(128)S(1)} %copy-done.4, bf16[256,512]{1,0:T(8,128)(2,1)S(1)} %copy-done.6, bf16[384,256]{1,0:T(8,128)(2,1)S(1)} %copy-done.1, bf16[384,256]{1,0:T(8,128)(2,1)S(1)} %collective-permute-done.refs_1_, ...), custom_call_target="tpu_custom_call" | custom-call | flops 2560000000 | bytes 3000000 | tf_op jit(solution)/shard_map/pallas_call | solution.py:275
  41.8 0.0 collective-permute-done.12
  41.8 2.1 %collective-permute-done.11 = bf16[64,128]{1,0:T(8,128)(2,1)S(1)} collective-permute-done((bf16[64,128]{1,0:T(8,128)(2,1)S(1)}, bf16[64,128]{1,0:T(8,128)(2,1)S(1)}, u32[]{:S(2)}, u32[]{:S(2)}) %collective-permute-start.11) | collective-permute-done | bytes 16416 | tf_op jit(solution)/shard_map/ppermute | solution.py:496
  43.9 0.0 collective-permute-done.10
  43.9 0.1 collective-permute-start.13
  44.0 1.2 %collective-permute-done.13.other_ref = f32[64,128]{1,0:T(8,128)S(1)} collective-permute-done((f32[64,128]{1,0:T(8,128)S(1)}, f32[64,128]{1,0:T(8,128)S(1)}, u32[]{:S(2)}, u32[]{:S(2)}) %collective-permute-start.13) | collective-permute-done | bytes 32800 | tf_op jit(solution)/shard_map/ppermute | solution.py:496
  45.2 2.7 %shard_map.101 = (f32[3,128,128]{2,1,0:T(8,128)S(1)}, f32[11,11,2,16]{3,2,1,0:T(2,128)}) custom-call(f32[64,128]{1,0:T(8,128)S(1)} %add_add_fusion.half_ref, f32[64,128]{1,0:T(8,128)S(1)} %collective-permute-done.13.other_ref), custom_call_target="tpu_custom_call" | custom-call | tf_op jit(solution)/shard_map/pallas_call | solution.py:428
  47.9 0.0 copy-done
  47.9 4.6 %shard_map.102 = bf16[2,11,128,512]{3,2,1,0:T(8,128)(2,1)} custom-call(f32[3,128,128]{2,1,0:T(8,128)S(1)} %get-tuple-element.35.stack_ref, bf16[8,256,256]{2,1,0:T(8,128)(2,1)S(1)} %copy-done, bf16[16,256,256]{2,1,0:T(8,128)(2,1)S(1)} %get-tuple-element.30.refs_5_.refs_0_, bf16[16,256,256]{2,1,0:T(8,128)(2,1)S(1)} %get-tuple-element.36.refs_1_, ...), custom_call_target="tpu_custom_call" | custom-call | tf_op jit(solution)/shard_map/pallas_call | solution.py:482
  (3 shorter events, 0.0 us)
Async XLA Ops:
  3.2 8.8 %collective-permute-start.3 = (bf16[384,256]{1,0:T(8,128)(2,1)}, bf16[384,256]{1,0:T(8,128)(2,1)S(1)}, u32[]{:S(2)}, u32[]{:S(2)}) collective-permute-start(bf16[384,256]{1,0:T(8,128)(2,1)} %get-tuple-element.27), channel_id=1, source_target_pairs={{0,24},{8,16},{16,8},{24,0},{1,25},{9,17},{17,9},{25,1},{2,26},{10... | collective-permute-start | bytes 589832 | tf_op jit(solution)/shard_map/ppermute | solution.py:496
  5.6 10.7 %collective-permute-start.4 = (bf16[384,256]{1,0:T(8,128)(2,1)}, bf16[384,256]{1,0:T(8,128)(2,1)S(1)}, u32[]{:S(2)}, u32[]{:S(2)}) collective-permute-start(bf16[384,256]{1,0:T(8,128)(2,1)} %get-tuple-element.28), channel_id=1, source_target_pairs={{0,16},{8,24},{16,0},{24,8},{1,17},{9,25},{17,1},{25,9},{2,18},{10... | collective-permute-start | bytes 589832 | tf_op jit(solution)/shard_map/ppermute | solution.py:496
  6.3 10.1 %collective-permute-start.5 = (bf16[384,256]{1,0:T(8,128)(2,1)}, bf16[384,256]{1,0:T(8,128)(2,1)S(1)}, u32[]{:S(2)}, u32[]{:S(2)}) collective-permute-start(bf16[384,256]{1,0:T(8,128)(2,1)} %get-tuple-element.29), channel_id=1, source_target_pairs={{0,8},{8,0},{16,24},{24,16},{1,9},{9,1},{17,25},{25,17},{2,10},{10... | collective-permute-start | bytes 589832 | tf_op jit(solution)/shard_map/ppermute | solution.py:496
  9.1 15.1 %collective-permute-start = (bf16[384,256]{1,0:T(8,128)(2,1)}, bf16[384,256]{1,0:T(8,128)(2,1)S(1)}, u32[]{:S(2)}, u32[]{:S(2)}) collective-permute-start(bf16[384,256]{1,0:T(8,128)(2,1)} %get-tuple-element.23), channel_id=1, source_target_pairs={{0,24},{8,16},{16,8},{24,0},{1,25},{9,17},{17,9},{25,1},{2,26},{10... | collective-permute-start | bytes 589832 | tf_op jit(solution)/shard_map/ppermute | solution.py:496
  10.6 13.6 %collective-permute-start.1 = (bf16[384,256]{1,0:T(8,128)(2,1)}, bf16[384,256]{1,0:T(8,128)(2,1)S(1)}, u32[]{:S(2)}, u32[]{:S(2)}) collective-permute-start(bf16[384,256]{1,0:T(8,128)(2,1)} %get-tuple-element.24), channel_id=1, source_target_pairs={{0,16},{8,24},{16,0},{24,8},{1,17},{9,25},{17,1},{25,9},{2,18},{10... | collective-permute-start | bytes 589832 | tf_op jit(solution)/shard_map/ppermute | solution.py:496
  11.9 12.2 %collective-permute-start.2 = (bf16[384,256]{1,0:T(8,128)(2,1)}, bf16[384,256]{1,0:T(8,128)(2,1)S(1)}, u32[]{:S(2)}, u32[]{:S(2)}) collective-permute-start(bf16[384,256]{1,0:T(8,128)(2,1)} %get-tuple-element.25), channel_id=1, source_target_pairs={{0,8},{8,0},{16,24},{24,16},{1,9},{9,1},{17,25},{25,17},{2,10},{10... | collective-permute-start | bytes 589832 | tf_op jit(solution)/shard_map/ppermute | solution.py:496
  16.4 0.9 %copy-start.2 = (bf16[384,256]{1,0:T(8,128)(2,1)S(1)}, bf16[384,256]{1,0:T(8,128)(2,1)}, u32[]{:S(2)}) copy-start(bf16[384,256]{1,0:T(8,128)(2,1)} %get-tuple-element.26.refs_0_) | copy-start | bytes 589828
  17.3 0.7 %copy-start.3 = (s32[4]{0:T(128)S(1)}, s32[4]{0:T(128)}, u32[]{:S(2)}) copy-start(s32[4]{0:T(128)} %order_ref.7) | copy-start | bytes 52
  17.9 0.7 %copy-start.4 = (s32[11]{0:T(128)S(1)}, s32[11]{0:T(128)}, u32[]{:S(2)}) copy-start(s32[11]{0:T(128)} %offsets_ref.7) | copy-start | bytes 136
  18.6 0.9 %copy-start.6 = (bf16[256,512]{1,0:T(8,128)(2,1)S(1)}, bf16[256,512]{1,0:T(8,128)(2,1)}, u32[]{:S(2)}) copy-start(bf16[256,512]{1,0:T(8,128)(2,1)} %constant.6.clone.f_ref) | copy-start | bytes 786436
  19.6 1.8 %copy-start.5 = (bf16[2816,128]{1,0:T(8,128)(2,1)S(1)}, bf16[2816,128]{1,0:T(8,128)(2,1)}, u32[]{:S(2)}) copy-start(bf16[2816,128]{1,0:T(8,128)(2,1)} %constant.7.clone.pick_ref) | copy-start | bytes 2162692
  21.3 2.8 %copy-start.1 = (bf16[384,256]{1,0:T(8,128)(2,1)S(1)}, bf16[384,256]{1,0:T(8,128)(2,1)}, u32[]{:S(2)}) copy-start(bf16[384,256]{1,0:T(8,128)(2,1)} %get-tuple-element.22.refs_0_) | copy-start | bytes 589828
  27.0 1.2 %collective-permute-start.6 = (bf16[64,128]{1,0:T(8,128)(2,1)S(1)}, bf16[64,128]{1,0:T(8,128)(2,1)S(1)}, u32[]{:S(2)}, u32[]{:S(2)}) collective-permute-start(bf16[64,128]{1,0:T(8,128)(2,1)S(1)} %get-tuple-element.32.refs_5_), channel_id=1, source_target_pairs={{0,8},{1,9},{2,10},{3,11},{4,12},{5,13},{6,14},{7,15},{8,0},{9,1},... | collective-permute-start | bytes 49160 | tf_op jit(solution)/shard_map/ppermute | solution.py:496
  28.3 4.8 %collective-permute-start.9 = (bf16[64,128]{1,0:T(8,128)(2,1)S(1)}, bf16[64,128]{1,0:T(8,128)(2,1)S(1)}, u32[]{:S(2)}, u32[]{:S(2)}) collective-permute-start(bf16[64,128]{1,0:T(8,128)(2,1)S(1)} %add_convert_fusion.1), channel_id=1, source_target_pairs={{0,17},{1,16},{2,19},{3,18},{4,21},{5,20},{6,23},{7,22},{8,25},{9,... | collective-permute-start | bytes 49160 | tf_op jit(solution)/shard_map/ppermute | solution.py:496
  31.3 3.7 %collective-permute-start.8 = (bf16[64,128]{1,0:T(8,128)(2,1)S(1)}, bf16[64,128]{1,0:T(8,128)(2,1)S(1)}, u32[]{:S(2)}, u32[]{:S(2)}) collective-permute-start(bf16[64,128]{1,0:T(8,128)(2,1)S(1)} %add_convert_fusion.1), channel_id=1, source_target_pairs={{0,1},{1,0},{2,3},{3,2},{4,5},{5,4},{6,7},{7,6},{8,9},{9,8},{10,11... | collective-permute-start | bytes 49160 | tf_op jit(solution)/shard_map/ppermute | solution.py:496
  31.9 3.7 %collective-permute-start.7 = (bf16[64,128]{1,0:T(8,128)(2,1)S(1)}, bf16[64,128]{1,0:T(8,128)(2,1)S(1)}, u32[]{:S(2)}, u32[]{:S(2)}) collective-permute-start(bf16[64,128]{1,0:T(8,128)(2,1)S(1)} %add_convert_fusion.1), channel_id=1, source_target_pairs={{0,16},{1,17},{2,18},{3,19},{4,20},{5,21},{6,22},{7,23},{8,24},{9,... | collective-permute-start | bytes 49160 | tf_op jit(solution)/shard_map/ppermute | solution.py:496
  35.6 12.3 %copy-start = (bf16[8,256,256]{2,1,0:T(8,128)(2,1)S(1)}, bf16[8,256,256]{2,1,0:T(8,128)(2,1)}, u32[]{:S(2)}) copy-start(bf16[8,256,256]{2,1,0:T(8,128)(2,1)} %constant.8.clone.spread_ref) | copy-start | bytes 3145732
  35.6 6.2 %collective-permute-start.12 = (bf16[64,128]{1,0:T(8,128)(2,1)S(1)}, bf16[64,128]{1,0:T(8,128)(2,1)S(1)}, u32[]{:S(2)}, u32[]{:S(2)}) collective-permute-start(bf16[64,128]{1,0:T(8,128)(2,1)S(1)} %add_convert_fusion), channel_id=1, source_target_pairs={{0,6},{1,7},{2,4},{3,5},{4,2},{5,3},{6,0},{7,1},{8,14},{9,15},{10,... | collective-permute-start | bytes 49160 | tf_op jit(solution)/shard_map/ppermute | solution.py:496
  39.3 4.6 %collective-permute-start.11 = (bf16[64,128]{1,0:T(8,128)(2,1)S(1)}, bf16[64,128]{1,0:T(8,128)(2,1)S(1)}, u32[]{:S(2)}, u32[]{:S(2)}) collective-permute-start(bf16[64,128]{1,0:T(8,128)(2,1)S(1)} %add_convert_fusion), channel_id=1, source_target_pairs={{0,4},{1,5},{2,6},{3,7},{4,0},{5,1},{6,2},{7,3},{8,12},{9,13},{10,... | collective-permute-start | bytes 49160 | tf_op jit(solution)/shard_map/ppermute | solution.py:496
  39.3 4.6 %collective-permute-start.10 = (bf16[64,128]{1,0:T(8,128)(2,1)S(1)}, bf16[64,128]{1,0:T(8,128)(2,1)S(1)}, u32[]{:S(2)}, u32[]{:S(2)}) collective-permute-start(bf16[64,128]{1,0:T(8,128)(2,1)S(1)} %add_convert_fusion), channel_id=1, source_target_pairs={{0,2},{1,3},{2,0},{3,1},{4,6},{5,7},{6,4},{7,5},{8,10},{9,11},{10,... | collective-permute-start | bytes 49160 | tf_op jit(solution)/shard_map/ppermute | solution.py:496
  43.9 1.3 %collective-permute-start.13 = (f32[64,128]{1,0:T(8,128)S(1)}, f32[64,128]{1,0:T(8,128)S(1)}, u32[]{:S(2)}, u32[]{:S(2)}) collective-permute-start(f32[64,128]{1,0:T(8,128)S(1)} %add_add_fusion.half_ref), channel_id=1, source_target_pairs={{0,8},{1,9},{2,10},{3,11},{4,12},{5,13},{6,14},{7,15},{8,0},{9,1},... | collective-permute-start | bytes 98312 | tf_op jit(solution)/shard_map/ppermute | solution.py:496

commit v6 on v5

--- a/solution.py
+++ b/solution.py
@@ -37,7 +37,7 @@
     table = np.concatenate([np.cos(angles) * scaled, -np.sin(angles) * scaled], axis=0)
     high = table.astype(jnp.bfloat16)
     low = (table - high.astype(np.float64)).astype(jnp.bfloat16)
-    return np.concatenate([high, low], axis=1)
+    return np.concatenate([high, low], axis=0)
 
 
 def packed_rows():
@@ -61,19 +61,19 @@
 
 
 def spread_table():
-    spread = np.zeros((STACK, 2, LANE, WIDE), np.float32)
+    spread = np.zeros((STACK, 2, LANE, 2 * HALF_ROWS), np.float32)
     for m in range(STACK):
         for b in range(NBLK):
             real = m * 32 + b
             imag = m * 32 + 16 + b
             first = slice(b * SUB, b * SUB + SUB)
-            second = slice(LANE + b * SUB, LANE + b * SUB + SUB)
+            second = slice(HALF_ROWS + b * SUB, HALF_ROWS + b * SUB + SUB)
             spread[m, 0, real, first] = 1.0
             spread[m, 0, imag, second] = 1.0
             spread[m, 1, imag, first] = -1.0
             spread[m, 1, real, second] = 1.0
     spread = np.concatenate([spread, spread], axis=2)
-    return spread.reshape(STACK * 2, WIDE, WIDE).astype(jnp.bfloat16)
+    return spread.reshape(STACK * 2, WIDE, 2 * HALF_ROWS).astype(jnp.bfloat16)
 
 
 def split(x):
@@ -116,7 +116,7 @@
 def pack_kernel(base, parts, first, table_hbm, x_hbm, *refs):
     lanes = x_hbm.shape[1]
     out_refs = refs[:lanes]
-    pick, table, x_ref, table_sem, x_sem = refs[lanes:]
+    pick, table, x_ref, staged, table_sem, x_sem, out_sem = refs[lanes:]
     steps, _, width = x_ref.shape
     part = steps // parts
     table_copy = pltpu.make_async_copy(table_hbm, table, table_sem)
@@ -130,13 +130,23 @@
     table_copy.wait()
     pick[...] = lane_pick(table, lanes) if first else table[...]
     rows = WIDE // lanes
-    for i in range(steps // rows):
-        if i * rows % part == 0:
-            copies[i * rows // part].wait()
-        at = slice(i * rows, (i + 1) * rows)
-        y = dot(pick[...], x_ref[at].reshape(WIDE, width)).astype(BF16)
+    stores = []
+    for i in range(parts):
+        copies[i].wait()
+        for start in range(i * part, (i + 1) * part, rows):
+            at = slice(start, start + rows)
+            y = dot(pick[...], x_ref[at].reshape(WIDE, width)).astype(BF16)
+            for d in range(lanes):
+                staged[d, at, :] = y[d * rows : (d + 1) * rows]
+        at = slice(i * part, (i + 1) * part)
         for d in range(lanes):
-            out_refs[d][at, :] = y[d * rows : (d + 1) * rows]
+            store = pltpu.make_async_copy(
+                staged.at[d, at], out_refs[d].at[at], out_sem.at[i * lanes + d]
+            )
+            store.start()
+            stores.append(store)
+    for store in stores:
+        store.wait()
 
 
 def pack(table, snapshots, base, width, first):
@@ -144,18 +154,19 @@
     parts = math.gcd(steps * lanes // WIDE, 3)
     outs = [jax.ShapeDtypeStruct((steps, width), BF16)] * lanes
     outs.append(jax.ShapeDtypeStruct((WIDE, WIDE), BF16))
-    scratch = [
-        pltpu.SMEM(table.shape, jnp.int32) if first else pltpu.VMEM(table.shape, BF16),
-        pltpu.VMEM((steps, lanes, width), BF16),
-        pltpu.SemaphoreType.DMA,
-        pltpu.SemaphoreType.DMA((parts,)),
-    ]
     return pl.pallas_call(
         functools.partial(pack_kernel, base, parts, first),
         out_shape=outs,
         in_specs=[HBM] * 2,
-        out_specs=[VMEM] * len(outs),
-        scratch_shapes=scratch,
+        out_specs=[HBM] * lanes + [VMEM],
+        scratch_shapes=[
+            pltpu.SMEM(table.shape, jnp.int32) if first else pltpu.VMEM(table.shape, BF16),
+            pltpu.VMEM((steps, lanes, width), BF16),
+            pltpu.VMEM((lanes, steps, width), BF16),
+            pltpu.SemaphoreType.DMA,
+            pltpu.SemaphoreType.DMA((parts,)),
+            pltpu.SemaphoreType.DMA((parts * lanes,)),
+        ],
         compiler_params=pltpu.CompilerParams(
             vmem_limit_bytes=FIRST_LIMIT if first else SECOND_LIMIT
         ),
@@ -185,7 +196,8 @@
         pair = wanted[first : first + 2]
         x = [record[c, pl.ds(offsets_ref[i], NFFT), :].astype(BF16) for i, c in pair]
         x = jnp.concatenate(x, axis=1) if len(x) > 1 else x[0]
-        y = dot(f_ref[...], jnp.concatenate([x, x], axis=0))
+        y = dot(f_ref[...], x)
+        y = y[:NFFT] + y[NFFT:]
         for at, (i, c) in enumerate(pair):
             cols = slice(c * LANE, (c + 1) * LANE)
             s_ref[i, :, cols] = y[:NFREQ, at * LANE : (at + 1) * LANE]
@@ -264,14 +276,15 @@
     fill_record(order_ref, refs[:lanes], record, None)
     transform(offsets_ref, f_ref, record, s_ref)
     for g in range(GROUPS):
-        high_ref[g], low_ref[g] = split(padded(s_ref[:, g * SUB : (g + 1) * SUB, :]))
+        s = s_ref[:, g * SUB : (g + 1) * SUB, :].reshape(2 * HALF_ROWS, -1)
+        high_ref[g], low_ref[g] = split(s)
 
 
 def spectrum(order, offsets, fourier, pieces, after):
     lanes = len(pieces)
     steps, width = pieces[0].shape
     args = [order, offsets, fourier, *pieces, *after]
-    part = jax.ShapeDtypeStruct((GROUPS, WIDE, width), BF16)
+    part = jax.ShapeDtypeStruct((GROUPS, 2 * HALF_ROWS, width), BF16)
     return pl.pallas_call(
         functools.partial(spectrum_kernel, lanes),
         out_shape=[part, part],
@@ -368,7 +381,7 @@
             out.corner[1, a] = imag
 
 
-def root_kernel(share, half_ref, other_ref, stack_ref, gram_ref, packed, rolled, *mats):
+def make_roots(share, half_ref, other_ref, gram_ref, packed, rolled, mats):
     core = lax.axis_index("tm") % 2
     packed[pl.ds(pl.multiple_of(core * HALF, HALF), HALF), :] = half_ref[...]
     packed[pl.ds(pl.multiple_of((1 - core) * HALF, HALF), HALF), :] = other_ref[...]
@@ -409,7 +422,8 @@
         y, y2 = y2, y
         z, z2 = z2, z
     none = jnp.zeros((SUB - CORNER, NFREQ), F32)
-    for at, m0 in enumerate(range(0, NBLK, STACK)):
+    stacks = []
+    for m0 in range(0, NBLK, STACK):
         modes = range(m0, min(m0 + STACK, NBLK))
         stack = []
         for m in modes:
@@ -420,76 +434,69 @@
                     stack.append((imag * sign if c else real) * norm)
                 stack.append(none)
         stack += [jnp.zeros((32, NFREQ), F32)] * (STACK - len(modes))
-        stack_ref[at] = jnp.concatenate(stack, axis=0).T
-
-
-def roots(half, other, share):
-    stacks = -(-NBLK // STACK)
+        stacks.append(jnp.concatenate(stack, axis=0).T)
+    return stacks
+
+
+def mode_kernel(chunks, share, half_ref, other_ref, spread_ref, *refs):
+    high_refs = refs[:chunks]
+    low_refs = refs[chunks : 2 * chunks]
+    out_ref, gram_ref, v, packed, rolled, *mats = refs[2 * chunks :]
+    step = pl.program_id(0)
+
+    @pl.when(step == 0)
+    def _():
+        stacks = make_roots(share, half_ref, other_ref, gram_ref, packed, rolled, mats)
+        row = lax.broadcasted_iota(jnp.int32, (NFREQ, 2 * HALF_ROWS), 0)
+        col = lax.broadcasted_iota(jnp.int32, (NFREQ, 2 * HALF_ROWS), 1)
+        same = row % SUB == col % SUB
+        for at, stack in enumerate(stacks):
+            both = jnp.concatenate(split(stack), axis=1)
+            for m in range(at * STACK, min((at + 1) * STACK, NBLK)):
+                for c in range(2):
+                    wide = dot(both, spread_ref[(m - at * STACK) * 2 + c])
+                    v[c * NBLK + m] = jnp.where(same, wide, 0.0)
+
+    fields = []
+    for h in range(STEP_GROUPS):
+        g = step * STEP_GROUPS + h
+        start = pl.multiple_of(g * SUB, SUB)
+        v_high, v_low = split(v[:, pl.ds(start, SUB), :].reshape(2 * HALF_ROWS, 2 * HALF_ROWS))
+        s_high = jnp.concatenate([r[g] for r in high_refs], axis=1)
+        s_low = jnp.concatenate([r[g] for r in low_refs], axis=1)
+        field = dot(jnp.concatenate([v_high, v_low], axis=0), s_high)
+        field = field[: 2 * HALF_ROWS] + (field[2 * HALF_ROWS :] + dot(v_high, s_low))
+        fields.append(field.reshape(2 * NBLK, SUB, -1))
+    both = jnp.concatenate(fields, axis=1).astype(BF16)
+    out_ref[...] = both.reshape(out_ref.shape)
+
+
+def mode_fields(half, other, spread, highs, lows, share):
+    width = sum(s.shape[2] for s in highs)
     return pl.pallas_call(
-        functools.partial(root_kernel, share),
+        functools.partial(mode_kernel, len(highs), share),
+        grid=(GROUPS // STEP_GROUPS,),
         out_shape=[
-            jax.ShapeDtypeStruct((stacks, NFREQ, LANE), F32),
+            jax.ShapeDtypeStruct((2, NBLK, NFREQ, width), BF16),
             jax.ShapeDtypeStruct((NBLK, NBLK, 2, share), F32),
         ],
-        in_specs=[VMEM] * 2,
-        out_specs=[VMEM] * 2,
-        scratch_shapes=[pltpu.VMEM((PACKED, NFREQ), F32)] * 2
+        in_specs=[VMEM] * (3 + 2 * len(highs)),
+        out_specs=[
+            pl.BlockSpec((2, NBLK, STEP_GROUPS * SUB, width), lambda i: (0, 0, i, 0)),
+            spec((NBLK, NBLK, 2, share)),
+        ],
+        scratch_shapes=[
+            pltpu.VMEM((2 * NBLK, NFREQ, 2 * HALF_ROWS), F32),
+            pltpu.VMEM((PACKED, NFREQ), F32),
+            pltpu.VMEM((PACKED, NFREQ), F32),
+        ]
         + [
             pltpu.VMEM((2, NBLK, SUB, NFREQ), F32),
             pltpu.VMEM((2, CORNER, SUB, NFREQ), F32),
         ]
         * 5,
         compiler_params=pltpu.CompilerParams(vmem_limit_bytes=32 * 2**20),
-    )(half, other)
-
-
-def mode_kernel(chunks, stack_ref, spread_ref, *refs):
-    high_refs = refs[:chunks]
-    low_refs = refs[chunks : 2 * chunks]
-    out_ref, v = refs[2 * chunks :]
-    step = pl.program_id(0)
-
-    @pl.when(step == 0)
-    def _():
-        row = lax.broadcasted_iota(jnp.int32, (NFREQ, WIDE), 0)
-        col = lax.broadcasted_iota(jnp.int32, (NFREQ, WIDE), 1)
-        same = row % SUB == col % SUB
-        for at, m0 in enumerate(range(0, NBLK, STACK)):
-            both = jnp.concatenate(split(stack_ref[at]), axis=1)
-            for m in range(m0, min(m0 + STACK, NBLK)):
-                for c in range(2):
-                    wide = dot(both, spread_ref[(m - m0) * 2 + c])
-                    v[c * NBLK + m] = jnp.where(same, wide, 0.0)
-
-    fields = []
-    for h in range(STEP_GROUPS):
-        g = step * STEP_GROUPS + h
-        start = pl.multiple_of(g * SUB, SUB)
-        v_high, v_low = split(v[:, pl.ds(start, SUB), :].reshape(2 * HALF_ROWS, WIDE))
-        s_high = jnp.concatenate([r[g] for r in high_refs], axis=1)
-        s_low = jnp.concatenate([r[g] for r in low_refs], axis=1)
-        field = dot(
-            jnp.concatenate([v_high, v_high, v_low], axis=1),
-            jnp.concatenate([s_high, s_low, s_high], axis=0),
-        )
-        fields.append(field.reshape(2 * NBLK, SUB, -1))
-    both = jnp.concatenate(fields, axis=1).astype(BF16)
-    out_ref[...] = both.reshape(out_ref.shape)
-
-
-def mode_fields(stacks, spread, highs, lows):
-    width = sum(s.shape[2] for s in highs)
-    return pl.pallas_call(
-        functools.partial(mode_kernel, len(highs)),
-        grid=(GROUPS // STEP_GROUPS,),
-        out_shape=jax.ShapeDtypeStruct((2, NBLK, NFREQ, width), BF16),
-        in_specs=[VMEM] * (2 + 2 * len(highs)),
-        out_specs=pl.BlockSpec(
-            (2, NBLK, STEP_GROUPS * SUB, width), lambda i: (0, 0, i, 0)
-        ),
-        scratch_shapes=[pltpu.VMEM((2 * NBLK, NFREQ, WIDE), F32)],
-        compiler_params=pltpu.CompilerParams(vmem_limit_bytes=32 * 2**20),
-    )(stacks, spread, *highs, *lows)
+    )(half, other, spread, *highs, *lows)
 
 
 def swap(x, axes, mask, size):
@@ -548,8 +555,8 @@
     half, highs[-1] = lax.optimization_barrier((half, highs[-1]))
     other = swap(half, axes, bits[0], size)
 
-    stacks, gram = roots(half, other, NFREQ // groups)
-    modes = mode_fields(stacks, jnp.asarray(spread_table()), highs, lows)
+    spread = jnp.asarray(spread_table())
+    modes, gram = mode_fields(half, other, spread, highs, lows, NFREQ // groups)
     modes = jnp.transpose(modes, (0, 2, 1, 3))[:, :, :, None, :]
     return modes, jnp.transpose(gram, (2, 3, 0, 1))
 

time: 52.7 us -> 52.5 us (level)
  local copies, waits for them, and re-layouts: 3.9 us -> 0.05 us
  waiting for transfers between devices: 12.5 us -> 15.7 us
    ppermute x14, waiting for transfers between devices: 12.5 us -> 15.7 us  [swap(): return lax.ppermute(x, axes, [(i, i ^ mask) for i in range(size)])]
    unnamed x14 -> x16, local copies, waits for them, and re-layouts: 3.2 us -> 0.05 us
    pallas_call x2, Pallas kernels: 5.28 us -> 6.41 us  [pack(): pl.pallas_call(functools.partial(pack_kernel, base, parts, first), out_sh...]
    pallas_call x2 -> x1, Pallas kernels: 7.23 us -> 6.45 us  [mode_fields(): pl.pallas_call(functools.partial(mode_kernel, len(highs), share), grid=(G...]
    slice x1, local copies, waits for them, and re-layouts: 0.7 us -> 0.01 us  [body(): here = weights[:, base:base + width]]
  transfers between devices with their start and end apart: 14 -> 14, of which waited for: 7 -> 8; matrix products, arithmetic and copies ran while one was open for 1% -> 0% of each run, Pallas kernels for 17% -> 18%
where the time goes in v6:
time: 52.5 us; the launch traced here: 52.3 us
  Pallas kernels  21.7 us (41%)
  waiting for transfers between devices  15.7 us (30%)
  starting transfers between devices  14.1 us (27%)
  between operations  0.81 us (2%)
    ppermute x14, waiting for transfers between devices, swap(): return lax.ppermute(x, axes, [(i, i ^ mask) for i in range(size)])  15.7 us
    ppermute x14, starting transfers between devices, swap(): return lax.ppermute(x, axes, [(i, i ^ mask) for i in range(size)])  14.1 us
    pallas_call x1, Pallas kernels, mode_fields(): pl.pallas_call(functools.partial(mode_kernel, len(highs), share), grid=(G...  6.45 us
    pallas_call x2, Pallas kernels, pack(): pl.pallas_call(functools.partial(pack_kernel, base, parts, first), out_sh...  6.41 us
    pallas_call x2, Pallas kernels, gram_part(): pl.pallas_call(functools.partial(gram_kernel, lanes, scale, first, last),...  5.52 us
    pallas_call x2, Pallas kernels, spectrum(): pl.pallas_call(functools.partial(spectrum_kernel, lanes), out_shape=[part...  3.29 us
  transfers between devices with their start and end apart: 14, of which 8 were waited for; matrix products, arithmetic and copies ran while one was open for 0% of the time, Pallas kernels for 18%

profile of v6, /device:TPU:0, one launch (start us, length us, event | category | flops | bytes accessed | tf_op | source)
XLA Modules:
  0.0 52.3 jit_solution(14447532001134093012)
XLA Ops:
  0.6 3.1 %shard_map.95 = (bf16[384,256]{1,0:T(8,128)(2,1)}, bf16[384,256]{1,0:T(8,128)(2,1)}, bf16[384,256]{1,0:T(8,128)(2,1)}, bf16[384,256]{1,0:T(8,128)(2,1)}, bf16[256,256]{1,0:T(8,128)(2,1)}) custom-call(s32[1,4]{1,0:T(1,128)} %table_hbm.1, bf16[384,4,512]{2,1,0:T(4,128)(2,1)} %x_hbm.3), custom_call_target="tpu_custom_call" | custom-call | flops 201326592 | bytes 1572864 | tf_op jit(solution)/shard_map/pallas_call | solution.py:157
  3.8 0.0 copy-start.7
  3.8 0.0 copy-start.2
  3.8 0.0 copy-start.3
  3.8 0.0 copy-start.4
  3.8 0.0 copy-start.6
  3.8 2.5 %collective-permute-start.3 = (bf16[384,256]{1,0:T(8,128)(2,1)}, bf16[384,256]{1,0:T(8,128)(2,1)S(1)}, u32[]{:S(2)}, u32[]{:S(2)}) collective-permute-start(bf16[384,256]{1,0:T(8,128)(2,1)} %get-tuple-element.27), channel_id=1, source_target_pairs={{0,24},{8,16},{16,8},{24,0},{1,25},{9,17},{17,9},{25,1},{2,26},{10... | collective-permute-start | bytes 589832 | tf_op jit(solution)/shard_map/ppermute | solution.py:503
  6.3 0.6 %collective-permute-start.4 = (bf16[384,256]{1,0:T(8,128)(2,1)}, bf16[384,256]{1,0:T(8,128)(2,1)S(1)}, u32[]{:S(2)}, u32[]{:S(2)}) collective-permute-start(bf16[384,256]{1,0:T(8,128)(2,1)} %get-tuple-element.28), channel_id=1, source_target_pairs={{0,16},{8,24},{16,0},{24,8},{1,17},{9,25},{17,1},{25,9},{2,18},{10... | collective-permute-start | bytes 589832 | tf_op jit(solution)/shard_map/ppermute | solution.py:503
  7.0 0.0 collective-permute-start.5
  7.0 3.3 %shard_map.96 = (bf16[384,256]{1,0:T(8,128)(2,1)}, bf16[384,256]{1,0:T(8,128)(2,1)}, bf16[384,256]{1,0:T(8,128)(2,1)}, bf16[384,256]{1,0:T(8,128)(2,1)}, bf16[256,256]{1,0:T(8,128)(2,1)}) custom-call(bf16[256,256]{1,0:T(8,128)(2,1)} %get-tuple-element.21.table_hbm, bf16[384,4,512]{2,1,0:T(4,128)(2,1)} %x_hbm.3), custom_call_target="tpu_custom_call" | custom-call | flops 201326592 | bytes 1572864 | tf_op jit(solution)/shard_map/pallas_call | solution.py:157
  10.3 1.5 %collective-permute-start = (bf16[384,256]{1,0:T(8,128)(2,1)}, bf16[384,256]{1,0:T(8,128)(2,1)S(1)}, u32[]{:S(2)}, u32[]{:S(2)}) collective-permute-start(bf16[384,256]{1,0:T(8,128)(2,1)} %get-tuple-element.23), channel_id=1, source_target_pairs={{0,24},{8,16},{16,8},{24,0},{1,25},{9,17},{17,9},{25,1},{2,26},{10... | collective-permute-start | bytes 589832 | tf_op jit(solution)/shard_map/ppermute | solution.py:503
  11.8 0.6 %collective-permute-start.1 = (bf16[384,256]{1,0:T(8,128)(2,1)}, bf16[384,256]{1,0:T(8,128)(2,1)S(1)}, u32[]{:S(2)}, u32[]{:S(2)}) collective-permute-start(bf16[384,256]{1,0:T(8,128)(2,1)} %get-tuple-element.24), channel_id=1, source_target_pairs={{0,16},{8,24},{16,0},{24,8},{1,17},{9,25},{17,1},{25,9},{2,18},{10... | collective-permute-start | bytes 589832 | tf_op jit(solution)/shard_map/ppermute | solution.py:503
  12.4 0.0 copy-done.7
  12.4 0.0 collective-permute-done.3.refs_1_
  12.4 0.2 collective-permute-start.2
  12.6 4.4 %collective-permute-done.4.refs_2_ = bf16[384,256]{1,0:T(8,128)(2,1)S(1)} collective-permute-done((bf16[384,256]{1,0:T(8,128)(2,1)}, bf16[384,256]{1,0:T(8,128)(2,1)S(1)}, u32[]{:S(2)}, u32[]{:S(2)}) %collective-permute-start.4) | collective-permute-done | bytes 196640 | tf_op jit(solution)/shard_map/ppermute | solution.py:503
  17.0 0.0 collective-permute-done.5.refs_3_
  17.0 0.0 copy-done.2
  17.0 0.0 copy-done.3
  17.0 0.0 copy-done.4
  17.0 0.0 copy-done.6
  17.1 0.0 copy-start.5
  17.1 1.6 %shard_map.98 = (bf16[16,176,256]{2,1,0:T(8,128)(2,1)S(1)}, bf16[16,176,256]{2,1,0:T(8,128)(2,1)S(1)}) custom-call(s32[4]{0:T(128)S(1)} %copy-done.3, s32[11]{0:T(128)S(1)} %copy-done.4, bf16[512,256]{1,0:T(8,128)(2,1)S(1)} %copy-done.6, bf16[384,256]{1,0:T(8,128)(2,1)S(1)} %copy-done.2, bf16[384,256]{1,0:T(8,128)(2,1)S(1)} %collective-permute-done.3.refs_1_, ...), custom_call_target="tpu_custom_call" | custom-call | flops 2560000000 | bytes 3000000 | tf_op jit(solution)/shard_map/pallas_call | solution.py:288
  18.7 0.0 copy-done.5
  18.7 0.0 copy-start.1
  18.7 2.8 %shard_map.97.refs_4_ = f32[128,128]{1,0:T(8,128)S(1)} custom-call(s32[4]{0:T(128)S(1)} %copy-done.3, s32[11]{0:T(128)S(1)} %copy-done.4, f32[1,256]{1,0:T(1,128)S(1)} %get-tuple-element.42.w_ref, bf16[512,256]{1,0:T(8,128)(2,1)S(1)} %copy-done.6, bf16[2816,128]{1,0:T(8,128)(2,1)S(1)} %copy-done.5, bf16[384,256]{1,0:T(8,128)(2,1)S(1)} %copy-done.2, ...), custom_call_target="tpu_custom_call" | custom-call | flops 2560000000 | bytes 3000000 | tf_op jit(solution)/shard_map/pallas_call | solution.py:255
  21.5 0.0 collective-permute-done.refs_1_
  21.5 3.1 %collective-permute-done.1.refs_2_ = bf16[384,256]{1,0:T(8,128)(2,1)S(1)} collective-permute-done((bf16[384,256]{1,0:T(8,128)(2,1)}, bf16[384,256]{1,0:T(8,128)(2,1)S(1)}, u32[]{:S(2)}, u32[]{:S(2)}) %collective-permute-start.1) | collective-permute-done | bytes 196640 | tf_op jit(solution)/shard_map/ppermute | solution.py:503
  24.6 0.0 collective-permute-done.2.refs_3_
  24.6 0.0 copy-done.1
  24.6 2.8 %shard_map.99 = (bf16[64,128]{1,0:T(8,128)(2,1)S(1)}, bf16[64,128]{1,0:T(8,128)(2,1)S(1)}) custom-call(s32[4]{0:T(128)S(1)} %copy-done.3, s32[11]{0:T(128)S(1)} %copy-done.4, f32[1,256]{1,0:T(1,128)S(1)} %get-tuple-element.43.w_ref, bf16[512,256]{1,0:T(8,128)(2,1)S(1)} %copy-done.6, bf16[2816,128]{1,0:T(8,128)(2,1)S(1)} %copy-done.5, ...), custom_call_target="tpu_custom_call" | custom-call | flops 2560000000 | bytes 3000000 | tf_op jit(solution)/shard_map/pallas_call | solution.py:255
  27.4 0.1 collective-permute-start.6
  27.5 1.2 %collective-permute-done.6 = bf16[64,128]{1,0:T(8,128)(2,1)S(1)} collective-permute-done((bf16[64,128]{1,0:T(8,128)(2,1)S(1)}, bf16[64,128]{1,0:T(8,128)(2,1)S(1)}, u32[]{:S(2)}, u32[]{:S(2)}) %collective-permute-start.6) | collective-permute-done | bytes 16416 | tf_op jit(solution)/shard_map/ppermute | solution.py:503
  28.7 3.3 %collective-permute-start.9 = (bf16[64,128]{1,0:T(8,128)(2,1)S(1)}, bf16[64,128]{1,0:T(8,128)(2,1)S(1)}, u32[]{:S(2)}, u32[]{:S(2)}) collective-permute-start(bf16[64,128]{1,0:T(8,128)(2,1)S(1)} %add_convert_fusion.1), channel_id=1, source_target_pairs={{0,17},{1,16},{2,19},{3,18},{4,21},{5,20},{6,23},{7,22},{8,25},{9,... | collective-permute-start | bytes 49160 | tf_op jit(solution)/shard_map/ppermute | solution.py:503
  32.0 0.5 %collective-permute-start.8 = (bf16[64,128]{1,0:T(8,128)(2,1)S(1)}, bf16[64,128]{1,0:T(8,128)(2,1)S(1)}, u32[]{:S(2)}, u32[]{:S(2)}) collective-permute-start(bf16[64,128]{1,0:T(8,128)(2,1)S(1)} %add_convert_fusion.1), channel_id=1, source_target_pairs={{0,1},{1,0},{2,3},{3,2},{4,5},{5,4},{6,7},{7,6},{8,9},{9,8},{10,11... | collective-permute-start | bytes 49160 | tf_op jit(solution)/shard_map/ppermute | solution.py:503
  32.5 0.1 collective-permute-start.7
  32.6 1.1 %collective-permute-done.9 = bf16[64,128]{1,0:T(8,128)(2,1)S(1)} collective-permute-done((bf16[64,128]{1,0:T(8,128)(2,1)S(1)}, bf16[64,128]{1,0:T(8,128)(2,1)S(1)}, u32[]{:S(2)}, u32[]{:S(2)}) %collective-permute-start.9) | collective-permute-done | bytes 16416 | tf_op jit(solution)/shard_map/ppermute | solution.py:503
  33.7 2.0 %collective-permute-done.8 = bf16[64,128]{1,0:T(8,128)(2,1)S(1)} collective-permute-done((bf16[64,128]{1,0:T(8,128)(2,1)S(1)}, bf16[64,128]{1,0:T(8,128)(2,1)S(1)}, u32[]{:S(2)}, u32[]{:S(2)}) %collective-permute-start.8) | collective-permute-done | bytes 16416 | tf_op jit(solution)/shard_map/ppermute | solution.py:503
  35.7 0.5 %collective-permute-done.7 = bf16[64,128]{1,0:T(8,128)(2,1)S(1)} collective-permute-done((bf16[64,128]{1,0:T(8,128)(2,1)S(1)}, bf16[64,128]{1,0:T(8,128)(2,1)S(1)}, u32[]{:S(2)}, u32[]{:S(2)}) %collective-permute-start.7) | collective-permute-done | bytes 16416 | tf_op jit(solution)/shard_map/ppermute | solution.py:503
  36.3 0.0 copy-start
  36.3 3.7 %collective-permute-start.12 = (bf16[64,128]{1,0:T(8,128)(2,1)S(1)}, bf16[64,128]{1,0:T(8,128)(2,1)S(1)}, u32[]{:S(2)}, u32[]{:S(2)}) collective-permute-start(bf16[64,128]{1,0:T(8,128)(2,1)S(1)} %add_convert_fusion), channel_id=1, source_target_pairs={{0,6},{1,7},{2,4},{3,5},{4,2},{5,3},{6,0},{7,1},{8,14},{9,15},{10,... | collective-permute-start | bytes 49160 | tf_op jit(solution)/shard_map/ppermute | solution.py:503
  39.9 0.0 collective-permute-start.11
  39.9 0.8 %collective-permute-start.10 = (bf16[64,128]{1,0:T(8,128)(2,1)S(1)}, bf16[64,128]{1,0:T(8,128)(2,1)S(1)}, u32[]{:S(2)}, u32[]{:S(2)}) collective-permute-start(bf16[64,128]{1,0:T(8,128)(2,1)S(1)} %add_convert_fusion), channel_id=1, source_target_pairs={{0,2},{1,3},{2,0},{3,1},{4,6},{5,7},{6,4},{7,5},{8,10},{9,11},{10,... | collective-permute-start | bytes 49160 | tf_op jit(solution)/shard_map/ppermute | solution.py:503
  40.7 1.6 %shard_map.100 = (bf16[16,176,256]{2,1,0:T(8,128)(2,1)S(1)}, bf16[16,176,256]{2,1,0:T(8,128)(2,1)S(1)}) custom-call(s32[4]{0:T(128)S(1)} %copy-done.3, s32[11]{0:T(128)S(1)} %copy-done.4, bf16[512,256]{1,0:T(8,128)(2,1)S(1)} %copy-done.6, bf16[384,256]{1,0:T(8,128)(2,1)S(1)} %copy-done.1, bf16[384,256]{1,0:T(8,128)(2,1)S(1)} %collective-permute-done.refs_1_, ...), custom_call_target="tpu_custom_call" | custom-call | flops 2560000000 | bytes 3000000 | tf_op jit(solution)/shard_map/pallas_call | solution.py:288
  42.4 0.0 collective-permute-done.12
  42.4 2.2 %collective-permute-done.11 = bf16[64,128]{1,0:T(8,128)(2,1)S(1)} collective-permute-done((bf16[64,128]{1,0:T(8,128)(2,1)S(1)}, bf16[64,128]{1,0:T(8,128)(2,1)S(1)}, u32[]{:S(2)}, u32[]{:S(2)}) %collective-permute-start.11) | collective-permute-done | bytes 16416 | tf_op jit(solution)/shard_map/ppermute | solution.py:503
  44.6 0.0 collective-permute-done.10
  44.6 0.1 collective-permute-start.13
  44.7 1.2 %collective-permute-done.13.other_ref = f32[64,128]{1,0:T(8,128)S(1)} collective-permute-done((f32[64,128]{1,0:T(8,128)S(1)}, f32[64,128]{1,0:T(8,128)S(1)}, u32[]{:S(2)}, u32[]{:S(2)}) %collective-permute-start.13) | collective-permute-done | bytes 32800 | tf_op jit(solution)/shard_map/ppermute | solution.py:503
  45.9 0.0 copy-done
  45.9 6.4 %shard_map.101 = (bf16[2,11,128,512]{3,2,1,0:T(8,128)(2,1)}, f32[11,11,2,16]{3,2,1,0:T(2,128)}) custom-call(f32[64,128]{1,0:T(8,128)S(1)} %add_add_fusion.half_ref, f32[64,128]{1,0:T(8,128)S(1)} %collective-permute-done.13.other_ref, bf16[8,256,176]{2,1,0:T(8,128)(2,1)S(1)} %copy-done, bf16[16,176,256]{2,1,0:T(8,128)(2,1)S(1)} %get-tuple-element.30.refs_5_.refs_0_, ...), custom_call_target="tpu_custom_call" | custom-call | tf_op jit(solution)/shard_map/pallas_call | solution.py:476
  (4 shorter events, 0.0 us)
Async XLA Ops:
  3.8 8.7 %copy-start.7 = (f32[512]{0:T(512)S(1)}, f32[512]{0:T(512)}, u32[]{:S(2)}) copy-start(f32[512]{0:T(512)} %param.9) | copy-start | bytes 6148
  3.8 13.2 %copy-start.2 = (bf16[384,256]{1,0:T(8,128)(2,1)S(1)}, bf16[384,256]{1,0:T(8,128)(2,1)}, u32[]{:S(2)}) copy-start(bf16[384,256]{1,0:T(8,128)(2,1)} %get-tuple-element.26.refs_0_) | copy-start | bytes 589828
  3.8 13.2 %copy-start.3 = (s32[4]{0:T(128)S(1)}, s32[4]{0:T(128)}, u32[]{:S(2)}) copy-start(s32[4]{0:T(128)} %order_ref.7) | copy-start | bytes 52
  3.8 13.2 %copy-start.4 = (s32[11]{0:T(128)S(1)}, s32[11]{0:T(128)}, u32[]{:S(2)}) copy-start(s32[11]{0:T(128)} %offsets_ref.7) | copy-start | bytes 136
  3.8 13.2 %copy-start.6 = (bf16[512,256]{1,0:T(8,128)(2,1)S(1)}, bf16[512,256]{1,0:T(8,128)(2,1)}, u32[]{:S(2)}) copy-start(bf16[512,256]{1,0:T(8,128)(2,1)} %constant.6.clone.f_ref) | copy-start | bytes 786436
  3.8 8.6 %collective-permute-start.3 = (bf16[384,256]{1,0:T(8,128)(2,1)}, bf16[384,256]{1,0:T(8,128)(2,1)S(1)}, u32[]{:S(2)}, u32[]{:S(2)}) collective-permute-start(bf16[384,256]{1,0:T(8,128)(2,1)} %get-tuple-element.27), channel_id=1, source_target_pairs={{0,24},{8,16},{16,8},{24,0},{1,25},{9,17},{17,9},{25,1},{2,26},{10... | collective-permute-start | bytes 589832 | tf_op jit(solution)/shard_map/ppermute | solution.py:503
  6.3 10.7 %collective-permute-start.4 = (bf16[384,256]{1,0:T(8,128)(2,1)}, bf16[384,256]{1,0:T(8,128)(2,1)S(1)}, u32[]{:S(2)}, u32[]{:S(2)}) collective-permute-start(bf16[384,256]{1,0:T(8,128)(2,1)} %get-tuple-element.28), channel_id=1, source_target_pairs={{0,16},{8,24},{16,0},{24,8},{1,17},{9,25},{17,1},{25,9},{2,18},{10... | collective-permute-start | bytes 589832 | tf_op jit(solution)/shard_map/ppermute | solution.py:503
  7.0 10.1 %collective-permute-start.5 = (bf16[384,256]{1,0:T(8,128)(2,1)}, bf16[384,256]{1,0:T(8,128)(2,1)S(1)}, u32[]{:S(2)}, u32[]{:S(2)}) collective-permute-start(bf16[384,256]{1,0:T(8,128)(2,1)} %get-tuple-element.29), channel_id=1, source_target_pairs={{0,8},{8,0},{16,24},{24,16},{1,9},{9,1},{17,25},{25,17},{2,10},{10... | collective-permute-start | bytes 589832 | tf_op jit(solution)/shard_map/ppermute | solution.py:503
  10.3 11.2 %collective-permute-start = (bf16[384,256]{1,0:T(8,128)(2,1)}, bf16[384,256]{1,0:T(8,128)(2,1)S(1)}, u32[]{:S(2)}, u32[]{:S(2)}) collective-permute-start(bf16[384,256]{1,0:T(8,128)(2,1)} %get-tuple-element.23), channel_id=1, source_target_pairs={{0,24},{8,16},{16,8},{24,0},{1,25},{9,17},{17,9},{25,1},{2,26},{10... | collective-permute-start | bytes 589832 | tf_op jit(solution)/shard_map/ppermute | solution.py:503
  11.8 12.8 %collective-permute-start.1 = (bf16[384,256]{1,0:T(8,128)(2,1)}, bf16[384,256]{1,0:T(8,128)(2,1)S(1)}, u32[]{:S(2)}, u32[]{:S(2)}) collective-permute-start(bf16[384,256]{1,0:T(8,128)(2,1)} %get-tuple-element.24), channel_id=1, source_target_pairs={{0,16},{8,24},{16,0},{24,8},{1,17},{9,25},{17,1},{25,9},{2,18},{10... | collective-permute-start | bytes 589832 | tf_op jit(solution)/shard_map/ppermute | solution.py:503
  12.4 12.2 %collective-permute-start.2 = (bf16[384,256]{1,0:T(8,128)(2,1)}, bf16[384,256]{1,0:T(8,128)(2,1)S(1)}, u32[]{:S(2)}, u32[]{:S(2)}) collective-permute-start(bf16[384,256]{1,0:T(8,128)(2,1)} %get-tuple-element.25), channel_id=1, source_target_pairs={{0,8},{8,0},{16,24},{24,16},{1,9},{9,1},{17,25},{25,17},{2,10},{10... | collective-permute-start | bytes 589832 | tf_op jit(solution)/shard_map/ppermute | solution.py:503
  17.1 1.7 %copy-start.5 = (bf16[2816,128]{1,0:T(8,128)(2,1)S(1)}, bf16[2816,128]{1,0:T(8,128)(2,1)}, u32[]{:S(2)}) copy-start(bf16[2816,128]{1,0:T(8,128)(2,1)} %constant.7.clone.pick_ref) | copy-start | bytes 2162692
  18.7 5.9 %copy-start.1 = (bf16[384,256]{1,0:T(8,128)(2,1)S(1)}, bf16[384,256]{1,0:T(8,128)(2,1)}, u32[]{:S(2)}) copy-start(bf16[384,256]{1,0:T(8,128)(2,1)} %get-tuple-element.22.refs_0_) | copy-start | bytes 589828
  27.4 1.2 %collective-permute-start.6 = (bf16[64,128]{1,0:T(8,128)(2,1)S(1)}, bf16[64,128]{1,0:T(8,128)(2,1)S(1)}, u32[]{:S(2)}, u32[]{:S(2)}) collective-permute-start(bf16[64,128]{1,0:T(8,128)(2,1)S(1)} %get-tuple-element.32.refs_5_), channel_id=1, source_target_pairs={{0,8},{1,9},{2,10},{3,11},{4,12},{5,13},{6,14},{7,15},{8,0},{9,1},... | collective-permute-start | bytes 49160 | tf_op jit(solution)/shard_map/ppermute | solution.py:503
  28.7 5.0 %collective-permute-start.9 = (bf16[64,128]{1,0:T(8,128)(2,1)S(1)}, bf16[64,128]{1,0:T(8,128)(2,1)S(1)}, u32[]{:S(2)}, u32[]{:S(2)}) collective-permute-start(bf16[64,128]{1,0:T(8,128)(2,1)S(1)} %add_convert_fusion.1), channel_id=1, source_target_pairs={{0,17},{1,16},{2,19},{3,18},{4,21},{5,20},{6,23},{7,22},{8,25},{9,... | collective-permute-start | bytes 49160 | tf_op jit(solution)/shard_map/ppermute | solution.py:503
  32.0 3.7 %collective-permute-start.8 = (bf16[64,128]{1,0:T(8,128)(2,1)S(1)}, bf16[64,128]{1,0:T(8,128)(2,1)S(1)}, u32[]{:S(2)}, u32[]{:S(2)}) collective-permute-start(bf16[64,128]{1,0:T(8,128)(2,1)S(1)} %add_convert_fusion.1), channel_id=1, source_target_pairs={{0,1},{1,0},{2,3},{3,2},{4,5},{5,4},{6,7},{7,6},{8,9},{9,8},{10,11... | collective-permute-start | bytes 49160 | tf_op jit(solution)/shard_map/ppermute | solution.py:503
  32.5 3.7 %collective-permute-start.7 = (bf16[64,128]{1,0:T(8,128)(2,1)S(1)}, bf16[64,128]{1,0:T(8,128)(2,1)S(1)}, u32[]{:S(2)}, u32[]{:S(2)}) collective-permute-start(bf16[64,128]{1,0:T(8,128)(2,1)S(1)} %add_convert_fusion.1), channel_id=1, source_target_pairs={{0,16},{1,17},{2,18},{3,19},{4,20},{5,21},{6,22},{7,23},{8,24},{9,... | collective-permute-start | bytes 49160 | tf_op jit(solution)/shard_map/ppermute | solution.py:503
  36.3 9.6 %copy-start = (bf16[8,256,176]{2,1,0:T(8,128)(2,1)S(1)}, bf16[8,256,176]{2,1,0:T(8,128)(2,1)}, u32[]{:S(2)}) copy-start(bf16[8,256,176]{2,1,0:T(8,128)(2,1)} %constant.8.clone.spread_ref) | copy-start | bytes 2162692
  36.3 6.1 %collective-permute-start.12 = (bf16[64,128]{1,0:T(8,128)(2,1)S(1)}, bf16[64,128]{1,0:T(8,128)(2,1)S(1)}, u32[]{:S(2)}, u32[]{:S(2)}) collective-permute-start(bf16[64,128]{1,0:T(8,128)(2,1)S(1)} %add_convert_fusion), channel_id=1, source_target_pairs={{0,6},{1,7},{2,4},{3,5},{4,2},{5,3},{6,0},{7,1},{8,14},{9,15},{10,... | collective-permute-start | bytes 49160 | tf_op jit(solution)/shard_map/ppermute | solution.py:503
  39.9 4.6 %collective-permute-start.11 = (bf16[64,128]{1,0:T(8,128)(2,1)S(1)}, bf16[64,128]{1,0:T(8,128)(2,1)S(1)}, u32[]{:S(2)}, u32[]{:S(2)}) collective-permute-start(bf16[64,128]{1,0:T(8,128)(2,1)S(1)} %add_convert_fusion), channel_id=1, source_target_pairs={{0,4},{1,5},{2,6},{3,7},{4,0},{5,1},{6,2},{7,3},{8,12},{9,13},{10,... | collective-permute-start | bytes 49160 | tf_op jit(solution)/shard_map/ppermute | solution.py:503
  39.9 4.6 %collective-permute-start.10 = (bf16[64,128]{1,0:T(8,128)(2,1)S(1)}, bf16[64,128]{1,0:T(8,128)(2,1)S(1)}, u32[]{:S(2)}, u32[]{:S(2)}) collective-permute-start(bf16[64,128]{1,0:T(8,128)(2,1)S(1)} %add_convert_fusion), channel_id=1, source_target_pairs={{0,2},{1,3},{2,0},{3,1},{4,6},{5,7},{6,4},{7,5},{8,10},{9,11},{10,... | collective-permute-start | bytes 49160 | tf_op jit(solution)/shard_map/ppermute | solution.py:503
  44.6 1.3 %collective-permute-start.13 = (f32[64,128]{1,0:T(8,128)S(1)}, f32[64,128]{1,0:T(8,128)S(1)}, u32[]{:S(2)}, u32[]{:S(2)}) collective-permute-start(f32[64,128]{1,0:T(8,128)S(1)} %add_add_fusion.half_ref), channel_id=1, source_target_pairs={{0,8},{1,9},{2,10},{3,11},{4,12},{5,13},{6,14},{7,15},{8,0},{9,1},... | collective-permute-start | bytes 98312 | tf_op jit(solution)/shard_map/ppermute | solution.py:503

commit v7 on v6

--- a/solution.py
+++ b/solution.py
@@ -23,6 +23,7 @@
 STACK = 4
 CORNER = NBLK - SUB
 WIDE = 2 * LANE
+LOW = 10 * SUB
 FIRST_LIMIT = 64 * 2**20
 SECOND_LIMIT = FIRST_LIMIT - 1450 * 2**10
 BF16 = jnp.bfloat16
@@ -61,19 +62,18 @@
 
 
 def spread_table():
-    spread = np.zeros((STACK, 2, LANE, 2 * HALF_ROWS), np.float32)
+    places = [[(0, q) for q in range(16)]]
+    places += [[(0, q) for q in range(16, 22)] + [(1, q) for q in range(at, at + 10)] for at in (0, 10)]
+    spread = np.zeros((STACK, 2, LANE, 2, 3, 16, SUB), np.float32)
     for m in range(STACK):
-        for b in range(NBLK):
-            real = m * 32 + b
-            imag = m * 32 + 16 + b
-            first = slice(b * SUB, b * SUB + SUB)
-            second = slice(HALF_ROWS + b * SUB, HALF_ROWS + b * SUB + SUB)
-            spread[m, 0, real, first] = 1.0
-            spread[m, 0, imag, second] = 1.0
-            spread[m, 1, imag, first] = -1.0
-            spread[m, 1, real, second] = 1.0
-    spread = np.concatenate([spread, spread], axis=2)
-    return spread.reshape(STACK * 2, WIDE, 2 * HALF_ROWS).astype(jnp.bfloat16)
+        for tile, inputs in enumerate(places):
+            for at, (low, q) in enumerate(inputs):
+                part, b = divmod(q, NBLK)
+                real = m * 32 + b
+                imag = m * 32 + 16 + b
+                spread[m, low, imag if part else real, 0, tile, at] = 1.0
+                spread[m, low, real if part else imag, 1, tile, at] = 1.0 if part else -1.0
+    return spread.reshape(STACK, WIDE, 6 * LANE).astype(jnp.bfloat16)
 
 
 def split(x):
@@ -113,66 +113,67 @@
     return jnp.where(in_row == row_of, 1.0, 0.0).astype(BF16)
 
 
-def pack_kernel(base, parts, first, table_hbm, x_hbm, *refs):
-    lanes = x_hbm.shape[1]
-    out_refs = refs[:lanes]
-    pick, table, x_ref, staged, table_sem, x_sem, out_sem = refs[lanes:]
-    steps, _, width = x_ref.shape
+def pack_kernel(jobs, parts, first, table_hbm, x_hbm, *refs):
+    steps, lanes, _ = x_hbm.shape
+    base = jobs[0][0]
+    table, x_ref, table_sem, x_sem = refs[-4:]
+    outs = list(refs[:-4])
     part = steps // parts
     table_copy = pltpu.make_async_copy(table_hbm, table, table_sem)
     table_copy.start()
     copies = []
     for i in range(parts):
         at = slice(i * part, (i + 1) * part)
-        source = x_hbm.at[at, :, base : base + width]
+        source = x_hbm.at[at, :, base : base + x_ref.shape[2]]
         copies.append(pltpu.make_async_copy(source, x_ref.at[at], x_sem.at[i]))
         copies[-1].start()
     table_copy.wait()
-    pick[...] = lane_pick(table, lanes) if first else table[...]
+    pick = table
+    if first:
+        pick = outs.pop()
+        pick[...] = lane_pick(table, lanes)
     rows = WIDE // lanes
-    stores = []
     for i in range(parts):
         copies[i].wait()
         for start in range(i * part, (i + 1) * part, rows):
             at = slice(start, start + rows)
-            y = dot(pick[...], x_ref[at].reshape(WIDE, width)).astype(BF16)
-            for d in range(lanes):
-                staged[d, at, :] = y[d * rows : (d + 1) * rows]
-        at = slice(i * part, (i + 1) * part)
-        for d in range(lanes):
-            store = pltpu.make_async_copy(
-                staged.at[d, at], out_refs[d].at[at], out_sem.at[i * lanes + d]
-            )
-            store.start()
-            stores.append(store)
-    for store in stores:
-        store.wait()
-
-
-def pack(table, snapshots, base, width, first):
+            x = x_ref[at].reshape(WIDE, x_ref.shape[2])
+            out = iter(outs)
+            for job, width, begin, end in jobs:
+                here = x[:, job - base : job - base + width]
+                y = dot(pick[begin * rows : end * rows, :], here).astype(BF16)
+                for d in range(end - begin):
+                    next(out)[at, :] = y[d * rows : (d + 1) * rows]
+
+
+def pack(table, snapshots, jobs, first):
     steps, lanes, _ = snapshots.shape
     parts = math.gcd(steps * lanes // WIDE, 3)
-    outs = [jax.ShapeDtypeStruct((steps, width), BF16)] * lanes
-    outs.append(jax.ShapeDtypeStruct((WIDE, WIDE), BF16))
+    outs = [
+        jax.ShapeDtypeStruct((steps, width), BF16)
+        for _, width, begin, end in jobs
+        for _ in range(begin, end)
+    ]
+    if first:
+        outs.append(jax.ShapeDtypeStruct((WIDE, WIDE), BF16))
+    columns = jobs[-1][0] + jobs[-1][1] - jobs[0][0]
     return pl.pallas_call(
-        functools.partial(pack_kernel, base, parts, first),
+        functools.partial(pack_kernel, jobs, parts, first),
         out_shape=outs,
         in_specs=[HBM] * 2,
-        out_specs=[HBM] * lanes + [VMEM],
+        out_specs=[VMEM] * len(outs),
         scratch_shapes=[
             pltpu.SMEM(table.shape, jnp.int32) if first else pltpu.VMEM(table.shape, BF16),
-            pltpu.VMEM((steps, lanes, width), BF16),
-            pltpu.VMEM((lanes, steps, width), BF16),
+            pltpu.VMEM((steps, lanes, columns), BF16),
             pltpu.SemaphoreType.DMA,
             pltpu.SemaphoreType.DMA((parts,)),
-            pltpu.SemaphoreType.DMA((parts * lanes,)),
         ],
         compiler_params=pltpu.CompilerParams(
             vmem_limit_bytes=FIRST_LIMIT if first else SECOND_LIMIT
         ),
         cost_estimate=pl.CostEstimate(
-            flops=2 * WIDE * steps * lanes * width,
-            bytes_accessed=4 * steps * lanes * width,
+            flops=2 * WIDE * steps * lanes * columns,
+            bytes_accessed=4 * steps * lanes * columns,
             transcendentals=0,
         ),
     )(table, snapshots)
@@ -190,14 +191,15 @@
             record[c, pl.ds(start, steps), :] = part if factor is None else part * factor[:, cols]
 
 
-def transform(offsets_ref, f_ref, record, s_ref):
+def transform(offsets_ref, f, record, s_ref):
     wanted = [(i, c) for i in range(NBLK) for c in range(record.shape[0])]
     for first in range(0, len(wanted), 2):
         pair = wanted[first : first + 2]
         x = [record[c, pl.ds(offsets_ref[i], NFFT), :].astype(BF16) for i, c in pair]
         x = jnp.concatenate(x, axis=1) if len(x) > 1 else x[0]
-        y = dot(f_ref[...], x)
-        y = y[:NFFT] + y[NFFT:]
+        y = dot(f, x)
+        if f.shape[0] > NFFT:
+            y = y[:NFFT] + y[NFFT:]
         for at, (i, c) in enumerate(pair):
             cols = slice(c * LANE, (c + 1) * LANE)
             s_ref[i, :, cols] = y[:NFREQ, at * LANE : (at + 1) * LANE]
@@ -219,7 +221,7 @@
         before_ref, _, *rest = rest
     *packed_refs, record, s_ref, masked = rest
     fill_record(order_ref, pieces, record, jnp.sqrt(w_ref[...]))
-    transform(offsets_ref, f_ref, record, s_ref)
+    transform(offsets_ref, f_ref[:NFFT] if last else f_ref[...], record, s_ref)
     row = lax.broadcasted_iota(jnp.int32, (HALF_ROWS, LANE), 0)
     col = lax.broadcasted_iota(jnp.int32, (HALF_ROWS, LANE), 1)
     same = row % SUB == col % SUB
@@ -274,7 +276,7 @@
 def spectrum_kernel(lanes, order_ref, offsets_ref, f_ref, *refs):
     high_ref, low_ref, record, s_ref = refs[-4:]
     fill_record(order_ref, refs[:lanes], record, None)
-    transform(offsets_ref, f_ref, record, s_ref)
+    transform(offsets_ref, f_ref[...], record, s_ref)
     for g in range(GROUPS):
         s = s_ref[:, g * SUB : (g + 1) * SUB, :].reshape(2 * HALF_ROWS, -1)
         high_ref[g], low_ref[g] = split(s)
@@ -447,26 +449,27 @@
     @pl.when(step == 0)
     def _():
         stacks = make_roots(share, half_ref, other_ref, gram_ref, packed, rolled, mats)
-        row = lax.broadcasted_iota(jnp.int32, (NFREQ, 2 * HALF_ROWS), 0)
-        col = lax.broadcasted_iota(jnp.int32, (NFREQ, 2 * HALF_ROWS), 1)
+        row = lax.broadcasted_iota(jnp.int32, (NFREQ, 3 * LANE), 0)
+        col = lax.broadcasted_iota(jnp.int32, (NFREQ, 3 * LANE), 1)
         same = row % SUB == col % SUB
         for at, stack in enumerate(stacks):
             both = jnp.concatenate(split(stack), axis=1)
             for m in range(at * STACK, min((at + 1) * STACK, NBLK)):
+                wide = dot(both, spread_ref[m - at * STACK])
                 for c in range(2):
-                    wide = dot(both, spread_ref[(m - at * STACK) * 2 + c])
-                    v[c * NBLK + m] = jnp.where(same, wide, 0.0)
+                    here = wide[:, c * 3 * LANE : (c + 1) * 3 * LANE]
+                    v[c * NBLK + m] = jnp.where(same, here, 0.0)
 
     fields = []
     for h in range(STEP_GROUPS):
         g = step * STEP_GROUPS + h
         start = pl.multiple_of(g * SUB, SUB)
-        v_high, v_low = split(v[:, pl.ds(start, SUB), :].reshape(2 * HALF_ROWS, 2 * HALF_ROWS))
-        s_high = jnp.concatenate([r[g] for r in high_refs], axis=1)
-        s_low = jnp.concatenate([r[g] for r in low_refs], axis=1)
-        field = dot(jnp.concatenate([v_high, v_low], axis=0), s_high)
-        field = field[: 2 * HALF_ROWS] + (field[2 * HALF_ROWS :] + dot(v_high, s_low))
-        fields.append(field.reshape(2 * NBLK, SUB, -1))
+        vg = v[:, pl.ds(start, SUB), :].reshape(2 * HALF_ROWS, 3 * LANE).astype(BF16)
+        vg = jnp.concatenate([vg[:, : 2 * LANE], vg[:, :LANE], vg[:, 2 * LANE :]], axis=1)
+        high = jnp.concatenate([r[g] for r in high_refs], axis=1)
+        low = jnp.concatenate([r[g] for r in low_refs], axis=1)
+        inputs = jnp.concatenate([high, high[:LOW], low, high[LOW : 2 * LOW]], axis=0)
+        fields.append(dot(vg, inputs).reshape(2 * NBLK, SUB, -1))
     both = jnp.concatenate(fields, axis=1).astype(BF16)
     out_ref[...] = both.reshape(out_ref.shape)
 
@@ -486,7 +489,7 @@
             spec((NBLK, NBLK, 2, share)),
         ],
         scratch_shapes=[
-            pltpu.VMEM((2 * NBLK, NFREQ, 2 * HALF_ROWS), F32),
+            pltpu.VMEM((2 * NBLK, NFREQ, 3 * LANE), F32),
             pltpu.VMEM((PACKED, NFREQ), F32),
             pltpu.VMEM((PACKED, NFREQ), F32),
         ]
@@ -516,11 +519,13 @@
     tables = (jnp.asarray(fourier_tables()), jnp.asarray(pick_table()))
     weights = weights.reshape(1, -1)
 
+    near = min(2, lanes)
+    (base, width), (next_base, next_width) = chunks
+    *far, table = pack(owner, snapshots, [(base, width, near, lanes)], True)
+    jobs = [(base, width, 0, near), (next_base, next_width, 0, lanes)]
+    rest = list(pack(table, snapshots, jobs, False))
     arrived = []
-    table = owner
-    for base, width in chunks:
-        packed = pack(table, snapshots, base, width, base == 0)
-        table = packed[lanes]
+    for packed in (rest[:near] + far, rest[near:]):
         moved = [swap(packed[d], "tm", d, lanes) for d in reversed(range(1, lanes))]
         arrived.append([packed[0]] + moved)
 

time: 52.5 us -> 51.1 us (0.973)
  Pallas kernels: 21.7 us -> 20 us
  local copies, waits for them, and re-layouts: 0.05 us -> 0.96 us
  waiting for transfers between devices: 15.7 us -> 14.8 us
    pallas_call x2, Pallas kernels: 6.41 us -> 5.37 us  [pack(): pl.pallas_call(functools.partial(pack_kernel, jobs, parts, first), out_sh...]
    ppermute x14, waiting for transfers between devices: 15.7 us -> 14.8 us  [swap(): return lax.ppermute(x, axes, [(i, i ^ mask) for i in range(size)])]
    unnamed x16, local copies, waits for them, and re-layouts: 0.05 us -> 0.96 us
where the time goes in v7:
time: 51.1 us; the launch traced here: 50.9 us
  Pallas kernels  20 us (39%)
  waiting for transfers between devices  14.8 us (29%)
  starting transfers between devices  14.3 us (28%)
  local copies, waits for them, and re-layouts  0.96 us (2%)
  between operations  0.8 us (2%)
    ppermute x14, waiting for transfers between devices, swap(): return lax.ppermute(x, axes, [(i, i ^ mask) for i in range(size)])  14.8 us
    ppermute x14, starting transfers between devices, swap(): return lax.ppermute(x, axes, [(i, i ^ mask) for i in range(size)])  14.3 us
    pallas_call x1, Pallas kernels, mode_fields(): pl.pallas_call(functools.partial(mode_kernel, len(highs), share), grid=(G...  6.18 us
    pallas_call x2, Pallas kernels, pack(): pl.pallas_call(functools.partial(pack_kernel, jobs, parts, first), out_sh...  5.37 us
    pallas_call x2, Pallas kernels, gram_part(): pl.pallas_call(functools.partial(gram_kernel, lanes, scale, first, last),...  5.2 us
    pallas_call x2, Pallas kernels, spectrum(): pl.pallas_call(functools.partial(spectrum_kernel, lanes), out_shape=[part...  3.29 us
  transfers between devices with their start and end apart: 14, of which 8 were waited for; matrix products, arithmetic and copies ran while one was open for 0% of the time, Pallas kernels for 18%

profile of v7, /device:TPU:0, one launch (start us, length us, event | category | flops | bytes accessed | tf_op | source)
XLA Modules:
  0.0 50.9 jit_solution(8502268633136879267)
XLA Ops:
  0.6 2.3 %shard_map.95 = (bf16[384,256]{1,0:T(8,128)(2,1)}, bf16[384,256]{1,0:T(8,128)(2,1)}, bf16[256,256]{1,0:T(8,128)(2,1)}) custom-call(s32[1,4]{1,0:T(1,128)} %table_hbm.1, bf16[384,4,512]{2,1,0:T(4,128)(2,1)} %x_hbm.3), custom_call_target="tpu_custom_call" | custom-call | flops 201326592 | bytes 1572864 | tf_op jit(solution)/shard_map/pallas_call | solution.py:160
  3.0 0.0 copy-start.7
  3.0 0.0 copy-start.3
  3.0 0.0 copy-start.4
  3.0 0.0 copy-start.6
  3.0 2.5 %collective-permute-start.3 = (bf16[384,256]{1,0:T(8,128)(2,1)}, bf16[384,256]{1,0:T(8,128)(2,1)S(1)}, u32[]{:S(2)}, u32[]{:S(2)}) collective-permute-start(bf16[384,256]{1,0:T(8,128)(2,1)} %get-tuple-element.27), channel_id=1, source_target_pairs={{0,24},{8,16},{16,8},{24,0},{1,25},{9,17},{17,9},{25,1},{2,26},{10... | collective-permute-start | bytes 589832 | tf_op jit(solution)/shard_map/ppermute | solution.py:506
  5.5 0.6 %collective-permute-start.4 = (bf16[384,256]{1,0:T(8,128)(2,1)}, bf16[384,256]{1,0:T(8,128)(2,1)S(1)}, u32[]{:S(2)}, u32[]{:S(2)}) collective-permute-start(bf16[384,256]{1,0:T(8,128)(2,1)} %get-tuple-element.28), channel_id=1, source_target_pairs={{0,16},{8,24},{16,0},{24,8},{1,17},{9,25},{17,1},{25,9},{2,18},{10... | collective-permute-start | bytes 589832 | tf_op jit(solution)/shard_map/ppermute | solution.py:506
  6.1 3.0 %shard_map.96 = (bf16[384,256]{1,0:T(8,128)(2,1)}, bf16[384,256]{1,0:T(8,128)(2,1)}, bf16[384,256]{1,0:T(8,128)(2,1)}, bf16[384,256]{1,0:T(8,128)(2,1)}, bf16[38...) custom-call(bf16[256,256]{1,0:T(8,128)(2,1)} %get-tuple-element.21.table_hbm, bf16[384,4,512]{2,1,0:T(4,128)(2,1)} %x_hbm.3), custom_call_target="tpu_custom_call" | custom-call | flops 402653184 | bytes 3145728 | tf_op jit(solution)/shard_map/pallas_call | solution.py:160
  9.2 1.5 %collective-permute-start = (bf16[384,256]{1,0:T(8,128)(2,1)}, bf16[384,256]{1,0:T(8,128)(2,1)S(1)}, u32[]{:S(2)}, u32[]{:S(2)}) collective-permute-start(bf16[384,256]{1,0:T(8,128)(2,1)} %get-tuple-element.23), channel_id=1, source_target_pairs={{0,24},{8,16},{16,8},{24,0},{1,25},{9,17},{17,9},{25,1},{2,26},{10... | collective-permute-start | bytes 589832 | tf_op jit(solution)/shard_map/ppermute | solution.py:506
  10.6 0.3 collective-permute-start.1
  10.9 0.2 collective-permute-start.5
  11.1 0.0 copy-done.7
  11.1 0.0 collective-permute-done.3.refs_1_
  11.1 0.7 %collective-permute-start.2 = (bf16[384,256]{1,0:T(8,128)(2,1)}, bf16[384,256]{1,0:T(8,128)(2,1)S(1)}, u32[]{:S(2)}, u32[]{:S(2)}) collective-permute-start(bf16[384,256]{1,0:T(8,128)(2,1)} %get-tuple-element.25), channel_id=1, source_target_pairs={{0,8},{8,0},{16,24},{24,16},{1,9},{9,1},{17,25},{25,17},{2,10},{10... | collective-permute-start | bytes 589832 | tf_op jit(solution)/shard_map/ppermute | solution.py:506
  11.8 4.4 %collective-permute-done.4.refs_2_ = bf16[384,256]{1,0:T(8,128)(2,1)S(1)} collective-permute-done((bf16[384,256]{1,0:T(8,128)(2,1)}, bf16[384,256]{1,0:T(8,128)(2,1)S(1)}, u32[]{:S(2)}, u32[]{:S(2)}) %collective-permute-start.4) | collective-permute-done | bytes 196640 | tf_op jit(solution)/shard_map/ppermute | solution.py:506
  16.2 0.0 collective-permute-done.5.refs_3_
  16.2 0.0 copy-done.3
  16.2 0.0 copy-done.4
  16.2 0.0 copy-done.6
  16.2 0.0 copy-start.2
  16.2 0.9 %copy-done.2 = bf16[384,256]{1,0:T(8,128)(2,1)S(1)} copy-done((bf16[384,256]{1,0:T(8,128)(2,1)S(1)}, bf16[384,256]{1,0:T(8,128)(2,1)}, u32[]{:S(2)}) %copy-start.2) | copy-done | bytes 196632
  17.1 0.0 copy-start.5
  17.2 1.6 %shard_map.98 = (bf16[16,176,256]{2,1,0:T(8,128)(2,1)S(1)}, bf16[16,176,256]{2,1,0:T(8,128)(2,1)S(1)}) custom-call(s32[4]{0:T(128)S(1)} %copy-done.3, s32[11]{0:T(128)S(1)} %copy-done.4, bf16[512,256]{1,0:T(8,128)(2,1)S(1)} %copy-done.6, bf16[384,256]{1,0:T(8,128)(2,1)S(1)} %copy-done.2, bf16[384,256]{1,0:T(8,128)(2,1)S(1)} %collective-permute-done.3.refs_1_, ...), custom_call_target="tpu_custom_call" | custom-call | flops 2560000000 | bytes 3000000 | tf_op jit(solution)/shard_map/pallas_call | solution.py:290
  18.8 0.0 copy-done.5
  18.8 0.0 copy-start.1
  18.8 2.8 %shard_map.97.refs_4_ = f32[128,128]{1,0:T(8,128)S(1)} custom-call(s32[4]{0:T(128)S(1)} %copy-done.3, s32[11]{0:T(128)S(1)} %copy-done.4, f32[1,256]{1,0:T(1,128)S(1)} %get-tuple-element.42.w_ref, bf16[512,256]{1,0:T(8,128)(2,1)S(1)} %copy-done.6, bf16[2816,128]{1,0:T(8,128)(2,1)S(1)} %copy-done.5, bf16[384,256]{1,0:T(8,128)(2,1)S(1)} %copy-done.2, ...), custom_call_target="tpu_custom_call" | custom-call | flops 2560000000 | bytes 3000000 | tf_op jit(solution)/shard_map/pallas_call | solution.py:257
  21.6 0.0 collective-permute-done.refs_1_
  21.6 2.2 %collective-permute-done.1.refs_2_ = bf16[384,256]{1,0:T(8,128)(2,1)S(1)} collective-permute-done((bf16[384,256]{1,0:T(8,128)(2,1)}, bf16[384,256]{1,0:T(8,128)(2,1)S(1)}, u32[]{:S(2)}, u32[]{:S(2)}) %collective-permute-start.1) | collective-permute-done | bytes 196640 | tf_op jit(solution)/shard_map/ppermute | solution.py:506
  23.8 0.0 collective-permute-done.2.refs_3_
  23.8 0.0 copy-done.1
  23.8 2.4 %shard_map.99 = (bf16[64,128]{1,0:T(8,128)(2,1)S(1)}, bf16[64,128]{1,0:T(8,128)(2,1)S(1)}) custom-call(s32[4]{0:T(128)S(1)} %copy-done.3, s32[11]{0:T(128)S(1)} %copy-done.4, f32[1,256]{1,0:T(1,128)S(1)} %get-tuple-element.43.w_ref, bf16[512,256]{1,0:T(8,128)(2,1)S(1)} %copy-done.6, bf16[2816,128]{1,0:T(8,128)(2,1)S(1)} %copy-done.5, ...), custom_call_target="tpu_custom_call" | custom-call | flops 2560000000 | bytes 3000000 | tf_op jit(solution)/shard_map/pallas_call | solution.py:257
  26.2 0.1 collective-permute-start.6
  26.3 1.2 %collective-permute-done.6 = bf16[64,128]{1,0:T(8,128)(2,1)S(1)} collective-permute-done((bf16[64,128]{1,0:T(8,128)(2,1)S(1)}, bf16[64,128]{1,0:T(8,128)(2,1)S(1)}, u32[]{:S(2)}, u32[]{:S(2)}) %collective-permute-start.6) | collective-permute-done | bytes 16416 | tf_op jit(solution)/shard_map/ppermute | solution.py:506
  27.5 3.3 %collective-permute-start.9 = (bf16[64,128]{1,0:T(8,128)(2,1)S(1)}, bf16[64,128]{1,0:T(8,128)(2,1)S(1)}, u32[]{:S(2)}, u32[]{:S(2)}) collective-permute-start(bf16[64,128]{1,0:T(8,128)(2,1)S(1)} %add_convert_fusion.1), channel_id=1, source_target_pairs={{0,17},{1,16},{2,19},{3,18},{4,21},{5,20},{6,23},{7,22},{8,25},{9,... | collective-permute-start | bytes 49160 | tf_op jit(solution)/shard_map/ppermute | solution.py:506
  30.8 0.5 %collective-permute-start.8 = (bf16[64,128]{1,0:T(8,128)(2,1)S(1)}, bf16[64,128]{1,0:T(8,128)(2,1)S(1)}, u32[]{:S(2)}, u32[]{:S(2)}) collective-permute-start(bf16[64,128]{1,0:T(8,128)(2,1)S(1)} %add_convert_fusion.1), channel_id=1, source_target_pairs={{0,1},{1,0},{2,3},{3,2},{4,5},{5,4},{6,7},{7,6},{8,9},{9,8},{10,11... | collective-permute-start | bytes 49160 | tf_op jit(solution)/shard_map/ppermute | solution.py:506
  31.3 0.1 collective-permute-start.7
  31.4 1.1 %collective-permute-done.9 = bf16[64,128]{1,0:T(8,128)(2,1)S(1)} collective-permute-done((bf16[64,128]{1,0:T(8,128)(2,1)S(1)}, bf16[64,128]{1,0:T(8,128)(2,1)S(1)}, u32[]{:S(2)}, u32[]{:S(2)}) %collective-permute-start.9) | collective-permute-done | bytes 16416 | tf_op jit(solution)/shard_map/ppermute | solution.py:506
  32.5 2.0 %collective-permute-done.8 = bf16[64,128]{1,0:T(8,128)(2,1)S(1)} collective-permute-done((bf16[64,128]{1,0:T(8,128)(2,1)S(1)}, bf16[64,128]{1,0:T(8,128)(2,1)S(1)}, u32[]{:S(2)}, u32[]{:S(2)}) %collective-permute-start.8) | collective-permute-done | bytes 16416 | tf_op jit(solution)/shard_map/ppermute | solution.py:506
  34.5 0.5 %collective-permute-done.7 = bf16[64,128]{1,0:T(8,128)(2,1)S(1)} collective-permute-done((bf16[64,128]{1,0:T(8,128)(2,1)S(1)}, bf16[64,128]{1,0:T(8,128)(2,1)S(1)}, u32[]{:S(2)}, u32[]{:S(2)}) %collective-permute-start.7) | collective-permute-done | bytes 16416 | tf_op jit(solution)/shard_map/ppermute | solution.py:506
  35.1 0.0 copy-start
  35.1 3.7 %collective-permute-start.12 = (bf16[64,128]{1,0:T(8,128)(2,1)S(1)}, bf16[64,128]{1,0:T(8,128)(2,1)S(1)}, u32[]{:S(2)}, u32[]{:S(2)}) collective-permute-start(bf16[64,128]{1,0:T(8,128)(2,1)S(1)} %add_convert_fusion), channel_id=1, source_target_pairs={{0,6},{1,7},{2,4},{3,5},{4,2},{5,3},{6,0},{7,1},{8,14},{9,15},{10,... | collective-permute-start | bytes 49160 | tf_op jit(solution)/shard_map/ppermute | solution.py:506
  38.8 0.0 collective-permute-start.11
  38.8 0.8 %collective-permute-start.10 = (bf16[64,128]{1,0:T(8,128)(2,1)S(1)}, bf16[64,128]{1,0:T(8,128)(2,1)S(1)}, u32[]{:S(2)}, u32[]{:S(2)}) collective-permute-start(bf16[64,128]{1,0:T(8,128)(2,1)S(1)} %add_convert_fusion), channel_id=1, source_target_pairs={{0,2},{1,3},{2,0},{3,1},{4,6},{5,7},{6,4},{7,5},{8,10},{9,11},{10,... | collective-permute-start | bytes 49160 | tf_op jit(solution)/shard_map/ppermute | solution.py:506
  39.5 1.6 %shard_map.100 = (bf16[16,176,256]{2,1,0:T(8,128)(2,1)S(1)}, bf16[16,176,256]{2,1,0:T(8,128)(2,1)S(1)}) custom-call(s32[4]{0:T(128)S(1)} %copy-done.3, s32[11]{0:T(128)S(1)} %copy-done.4, bf16[512,256]{1,0:T(8,128)(2,1)S(1)} %copy-done.6, bf16[384,256]{1,0:T(8,128)(2,1)S(1)} %copy-done.1, bf16[384,256]{1,0:T(8,128)(2,1)S(1)} %collective-permute-done.refs_1_, ...), custom_call_target="tpu_custom_call" | custom-call | flops 2560000000 | bytes 3000000 | tf_op jit(solution)/shard_map/pallas_call | solution.py:290
  41.2 0.0 collective-permute-done.12
  41.2 2.2 %collective-permute-done.11 = bf16[64,128]{1,0:T(8,128)(2,1)S(1)} collective-permute-done((bf16[64,128]{1,0:T(8,128)(2,1)S(1)}, bf16[64,128]{1,0:T(8,128)(2,1)S(1)}, u32[]{:S(2)}, u32[]{:S(2)}) %collective-permute-start.11) | collective-permute-done | bytes 16416 | tf_op jit(solution)/shard_map/ppermute | solution.py:506
  43.4 0.0 collective-permute-done.10
  43.4 0.1 collective-permute-start.13
  43.5 1.2 %collective-permute-done.13.other_ref = f32[64,128]{1,0:T(8,128)S(1)} collective-permute-done((f32[64,128]{1,0:T(8,128)S(1)}, f32[64,128]{1,0:T(8,128)S(1)}, u32[]{:S(2)}, u32[]{:S(2)}) %collective-permute-start.13) | collective-permute-done | bytes 32800 | tf_op jit(solution)/shard_map/ppermute | solution.py:506
  44.7 0.0 copy-done
  44.7 6.2 %shard_map.101 = (bf16[2,11,128,512]{3,2,1,0:T(8,128)(2,1)}, f32[11,11,2,16]{3,2,1,0:T(2,128)}) custom-call(f32[64,128]{1,0:T(8,128)S(1)} %add_add_fusion.half_ref, f32[64,128]{1,0:T(8,128)S(1)} %collective-permute-done.13.other_ref, bf16[4,256,768]{2,1,0:T(8,128)(2,1)S(1)} %copy-done, bf16[16,176,256]{2,1,0:T(8,128)(2,1)S(1)} %get-tuple-element.30.refs_5_.refs_0_, ...), custom_call_target="tpu_custom_call" | custom-call | tf_op jit(solution)/shard_map/pallas_call | solution.py:479
  (4 shorter events, 0.0 us)
Async XLA Ops:
  3.0 8.1 %copy-start.7 = (f32[512]{0:T(512)S(1)}, f32[512]{0:T(512)}, u32[]{:S(2)}) copy-start(f32[512]{0:T(512)} %param.9) | copy-start | bytes 6148
  3.0 13.2 %copy-start.3 = (s32[4]{0:T(128)S(1)}, s32[4]{0:T(128)}, u32[]{:S(2)}) copy-start(s32[4]{0:T(128)} %order_ref.7) | copy-start | bytes 52
  3.0 13.2 %copy-start.4 = (s32[11]{0:T(128)S(1)}, s32[11]{0:T(128)}, u32[]{:S(2)}) copy-start(s32[11]{0:T(128)} %offsets_ref.7) | copy-start | bytes 136
  3.0 13.2 %copy-start.6 = (bf16[512,256]{1,0:T(8,128)(2,1)S(1)}, bf16[512,256]{1,0:T(8,128)(2,1)}, u32[]{:S(2)}) copy-start(bf16[512,256]{1,0:T(8,128)(2,1)} %constant.6.clone.f_ref) | copy-start | bytes 786436
  3.0 8.1 %collective-permute-start.3 = (bf16[384,256]{1,0:T(8,128)(2,1)}, bf16[384,256]{1,0:T(8,128)(2,1)S(1)}, u32[]{:S(2)}, u32[]{:S(2)}) collective-permute-start(bf16[384,256]{1,0:T(8,128)(2,1)} %get-tuple-element.27), channel_id=1, source_target_pairs={{0,24},{8,16},{16,8},{24,0},{1,25},{9,17},{17,9},{25,1},{2,26},{10... | collective-permute-start | bytes 589832 | tf_op jit(solution)/shard_map/ppermute | solution.py:506
  5.5 10.7 %collective-permute-start.4 = (bf16[384,256]{1,0:T(8,128)(2,1)}, bf16[384,256]{1,0:T(8,128)(2,1)S(1)}, u32[]{:S(2)}, u32[]{:S(2)}) collective-permute-start(bf16[384,256]{1,0:T(8,128)(2,1)} %get-tuple-element.28), channel_id=1, source_target_pairs={{0,16},{8,24},{16,0},{24,8},{1,17},{9,25},{17,1},{25,9},{2,18},{10... | collective-permute-start | bytes 589832 | tf_op jit(solution)/shard_map/ppermute | solution.py:506
  9.2 12.4 %collective-permute-start = (bf16[384,256]{1,0:T(8,128)(2,1)}, bf16[384,256]{1,0:T(8,128)(2,1)S(1)}, u32[]{:S(2)}, u32[]{:S(2)}) collective-permute-start(bf16[384,256]{1,0:T(8,128)(2,1)} %get-tuple-element.23), channel_id=1, source_target_pairs={{0,24},{8,16},{16,8},{24,0},{1,25},{9,17},{17,9},{25,1},{2,26},{10... | collective-permute-start | bytes 589832 | tf_op jit(solution)/shard_map/ppermute | solution.py:506
  10.6 13.2 %collective-permute-start.1 = (bf16[384,256]{1,0:T(8,128)(2,1)}, bf16[384,256]{1,0:T(8,128)(2,1)S(1)}, u32[]{:S(2)}, u32[]{:S(2)}) collective-permute-start(bf16[384,256]{1,0:T(8,128)(2,1)} %get-tuple-element.24), channel_id=1, source_target_pairs={{0,16},{8,24},{16,0},{24,8},{1,17},{9,25},{17,1},{25,9},{2,18},{10... | collective-permute-start | bytes 589832 | tf_op jit(solution)/shard_map/ppermute | solution.py:506
  10.9 5.3 %collective-permute-start.5 = (bf16[384,256]{1,0:T(8,128)(2,1)}, bf16[384,256]{1,0:T(8,128)(2,1)S(1)}, u32[]{:S(2)}, u32[]{:S(2)}) collective-permute-start(bf16[384,256]{1,0:T(8,128)(2,1)} %get-tuple-element.29), channel_id=1, source_target_pairs={{0,8},{8,0},{16,24},{24,16},{1,9},{9,1},{17,25},{25,17},{2,10},{10... | collective-permute-start | bytes 589832 | tf_op jit(solution)/shard_map/ppermute | solution.py:506
  11.1 12.7 %collective-permute-start.2 = (bf16[384,256]{1,0:T(8,128)(2,1)}, bf16[384,256]{1,0:T(8,128)(2,1)S(1)}, u32[]{:S(2)}, u32[]{:S(2)}) collective-permute-start(bf16[384,256]{1,0:T(8,128)(2,1)} %get-tuple-element.25), channel_id=1, source_target_pairs={{0,8},{8,0},{16,24},{24,16},{1,9},{9,1},{17,25},{25,17},{2,10},{10... | collective-permute-start | bytes 589832 | tf_op jit(solution)/shard_map/ppermute | solution.py:506
  16.2 0.9 %copy-start.2 = (bf16[384,256]{1,0:T(8,128)(2,1)S(1)}, bf16[384,256]{1,0:T(8,128)(2,1)}, u32[]{:S(2)}) copy-start(bf16[384,256]{1,0:T(8,128)(2,1)} %get-tuple-element.26.refs_0_) | copy-start | bytes 589828
  17.1 1.7 %copy-start.5 = (bf16[2816,128]{1,0:T(8,128)(2,1)S(1)}, bf16[2816,128]{1,0:T(8,128)(2,1)}, u32[]{:S(2)}) copy-start(bf16[2816,128]{1,0:T(8,128)(2,1)} %constant.7.clone.pick_ref) | copy-start | bytes 2162692
  18.8 5.0 %copy-start.1 = (bf16[384,256]{1,0:T(8,128)(2,1)S(1)}, bf16[384,256]{1,0:T(8,128)(2,1)}, u32[]{:S(2)}) copy-start(bf16[384,256]{1,0:T(8,128)(2,1)} %get-tuple-element.22.refs_0_) | copy-start | bytes 589828
  26.2 1.2 %collective-permute-start.6 = (bf16[64,128]{1,0:T(8,128)(2,1)S(1)}, bf16[64,128]{1,0:T(8,128)(2,1)S(1)}, u32[]{:S(2)}, u32[]{:S(2)}) collective-permute-start(bf16[64,128]{1,0:T(8,128)(2,1)S(1)} %get-tuple-element.32.refs_5_), channel_id=1, source_target_pairs={{0,8},{1,9},{2,10},{3,11},{4,12},{5,13},{6,14},{7,15},{8,0},{9,1},... | collective-permute-start | bytes 49160 | tf_op jit(solution)/shard_map/ppermute | solution.py:506
  27.5 5.0 %collective-permute-start.9 = (bf16[64,128]{1,0:T(8,128)(2,1)S(1)}, bf16[64,128]{1,0:T(8,128)(2,1)S(1)}, u32[]{:S(2)}, u32[]{:S(2)}) collective-permute-start(bf16[64,128]{1,0:T(8,128)(2,1)S(1)} %add_convert_fusion.1), channel_id=1, source_target_pairs={{0,17},{1,16},{2,19},{3,18},{4,21},{5,20},{6,23},{7,22},{8,25},{9,... | collective-permute-start | bytes 49160 | tf_op jit(solution)/shard_map/ppermute | solution.py:506
  30.8 3.7 %collective-permute-start.8 = (bf16[64,128]{1,0:T(8,128)(2,1)S(1)}, bf16[64,128]{1,0:T(8,128)(2,1)S(1)}, u32[]{:S(2)}, u32[]{:S(2)}) collective-permute-start(bf16[64,128]{1,0:T(8,128)(2,1)S(1)} %add_convert_fusion.1), channel_id=1, source_target_pairs={{0,1},{1,0},{2,3},{3,2},{4,5},{5,4},{6,7},{7,6},{8,9},{9,8},{10,11... | collective-permute-start | bytes 49160 | tf_op jit(solution)/shard_map/ppermute | solution.py:506
  31.3 3.7 %collective-permute-start.7 = (bf16[64,128]{1,0:T(8,128)(2,1)S(1)}, bf16[64,128]{1,0:T(8,128)(2,1)S(1)}, u32[]{:S(2)}, u32[]{:S(2)}) collective-permute-start(bf16[64,128]{1,0:T(8,128)(2,1)S(1)} %add_convert_fusion.1), channel_id=1, source_target_pairs={{0,16},{1,17},{2,18},{3,19},{4,20},{5,21},{6,22},{7,23},{8,24},{9,... | collective-permute-start | bytes 49160 | tf_op jit(solution)/shard_map/ppermute | solution.py:506
  35.1 9.6 %copy-start = (bf16[4,256,768]{2,1,0:T(8,128)(2,1)S(1)}, bf16[4,256,768]{2,1,0:T(8,128)(2,1)}, u32[]{:S(2)}) copy-start(bf16[4,256,768]{2,1,0:T(8,128)(2,1)} %constant.8.clone.spread_ref) | copy-start | bytes 4718596
  35.1 6.1 %collective-permute-start.12 = (bf16[64,128]{1,0:T(8,128)(2,1)S(1)}, bf16[64,128]{1,0:T(8,128)(2,1)S(1)}, u32[]{:S(2)}, u32[]{:S(2)}) collective-permute-start(bf16[64,128]{1,0:T(8,128)(2,1)S(1)} %add_convert_fusion), channel_id=1, source_target_pairs={{0,6},{1,7},{2,4},{3,5},{4,2},{5,3},{6,0},{7,1},{8,14},{9,15},{10,... | collective-permute-start | bytes 49160 | tf_op jit(solution)/shard_map/ppermute | solution.py:506
  38.8 4.6 %collective-permute-start.11 = (bf16[64,128]{1,0:T(8,128)(2,1)S(1)}, bf16[64,128]{1,0:T(8,128)(2,1)S(1)}, u32[]{:S(2)}, u32[]{:S(2)}) collective-permute-start(bf16[64,128]{1,0:T(8,128)(2,1)S(1)} %add_convert_fusion), channel_id=1, source_target_pairs={{0,4},{1,5},{2,6},{3,7},{4,0},{5,1},{6,2},{7,3},{8,12},{9,13},{10,... | collective-permute-start | bytes 49160 | tf_op jit(solution)/shard_map/ppermute | solution.py:506
  38.8 4.6 %collective-permute-start.10 = (bf16[64,128]{1,0:T(8,128)(2,1)S(1)}, bf16[64,128]{1,0:T(8,128)(2,1)S(1)}, u32[]{:S(2)}, u32[]{:S(2)}) collective-permute-start(bf16[64,128]{1,0:T(8,128)(2,1)S(1)} %add_convert_fusion), channel_id=1, source_target_pairs={{0,2},{1,3},{2,0},{3,1},{4,6},{5,7},{6,4},{7,5},{8,10},{9,11},{10,... | collective-permute-start | bytes 49160 | tf_op jit(solution)/shard_map/ppermute | solution.py:506
  43.4 1.3 %collective-permute-start.13 = (f32[64,128]{1,0:T(8,128)S(1)}, f32[64,128]{1,0:T(8,128)S(1)}, u32[]{:S(2)}, u32[]{:S(2)}) collective-permute-start(f32[64,128]{1,0:T(8,128)S(1)} %add_add_fusion.half_ref), channel_id=1, source_target_pairs={{0,8},{1,9},{2,10},{3,11},{4,12},{5,13},{6,14},{7,15},{8,0},{9,1},... | collective-permute-start | bytes 98312 | tf_op jit(solution)/shard_map/ppermute | solution.py:506

commit v8 on v7

--- a/solution.py
+++ b/solution.py
@@ -10,7 +10,6 @@
 from jax.sharding import PartitionSpec as P
 
 NFFT = 256
-ROOT_STEPS = 5
 NFREQ = 128
 NBLK = 11
 LANE = 128
@@ -18,12 +17,12 @@
 HALF_ROWS = NBLK * SUB
 GROUPS = NFREQ // SUB
 STEP_GROUPS = 4
+MATS = 7
 PACKED = 128
 HALF = PACKED // 2
 STACK = 4
 CORNER = NBLK - SUB
 WIDE = 2 * LANE
-LOW = 10 * SUB
 FIRST_LIMIT = 64 * 2**20
 SECOND_LIMIT = FIRST_LIMIT - 1450 * 2**10
 BF16 = jnp.bfloat16
@@ -62,23 +61,15 @@
 
 
 def spread_table():
-    places = [[(0, q) for q in range(16)]]
-    places += [[(0, q) for q in range(16, 22)] + [(1, q) for q in range(at, at + 10)] for at in (0, 10)]
-    spread = np.zeros((STACK, 2, LANE, 2, 3, 16, SUB), np.float32)
-    for m in range(STACK):
-        for tile, inputs in enumerate(places):
-            for at, (low, q) in enumerate(inputs):
-                part, b = divmod(q, NBLK)
-                real = m * 32 + b
-                imag = m * 32 + 16 + b
-                spread[m, low, imag if part else real, 0, tile, at] = 1.0
-                spread[m, low, real if part else imag, 1, tile, at] = 1.0 if part else -1.0
-    return spread.reshape(STACK, WIDE, 6 * LANE).astype(jnp.bfloat16)
-
-
-def split(x):
-    high = x.astype(BF16)
-    return high, (x - high.astype(F32)).astype(BF16)
+    spread = np.zeros((2, STACK, 2, 16, WIDE), np.float32)
+    for b in range(NBLK):
+        first = slice(b * SUB, b * SUB + SUB)
+        second = slice(HALF_ROWS + b * SUB, HALF_ROWS + b * SUB + SUB)
+        spread[0, :, 0, b, first] = 1.0
+        spread[0, :, 1, b, second] = 1.0
+        spread[1, :, 1, b, first] = -1.0
+        spread[1, :, 0, b, second] = 1.0
+    return spread.reshape(2, LANE, WIDE).astype(jnp.bfloat16)
 
 
 def dot(a, b):
@@ -274,28 +265,21 @@
 
 
 def spectrum_kernel(lanes, order_ref, offsets_ref, f_ref, *refs):
-    high_ref, low_ref, record, s_ref = refs[-4:]
+    s_ref, record = refs[-2:]
     fill_record(order_ref, refs[:lanes], record, None)
     transform(offsets_ref, f_ref[...], record, s_ref)
-    for g in range(GROUPS):
-        s = s_ref[:, g * SUB : (g + 1) * SUB, :].reshape(2 * HALF_ROWS, -1)
-        high_ref[g], low_ref[g] = split(s)
 
 
 def spectrum(order, offsets, fourier, pieces, after):
     lanes = len(pieces)
     steps, width = pieces[0].shape
     args = [order, offsets, fourier, *pieces, *after]
-    part = jax.ShapeDtypeStruct((GROUPS, 2 * HALF_ROWS, width), BF16)
     return pl.pallas_call(
         functools.partial(spectrum_kernel, lanes),
-        out_shape=[part, part],
+        out_shape=jax.ShapeDtypeStruct((2 * NBLK, NFREQ, width), F32),
         in_specs=[SMEM, SMEM] + [VMEM] * (len(args) - 2),
-        out_specs=[VMEM, VMEM],
-        scratch_shapes=[
-            pltpu.VMEM((width // LANE, lanes * steps, LANE), F32),
-            pltpu.VMEM((2 * NBLK, NFREQ, width), F32),
-        ],
+        out_specs=VMEM,
+        scratch_shapes=[pltpu.VMEM((width // LANE, lanes * steps, LANE), F32)],
         compiler_params=pltpu.CompilerParams(vmem_limit_bytes=32 * 2**20),
         cost_estimate=pl.CostEstimate(
             flops=width * 10**7, bytes_accessed=3 * 10**6, transcendentals=0
@@ -326,7 +310,7 @@
             self.corner[1, a - SUB, at, :] = imag
 
 
-def product(x, y, out, diagonal=0.0, factor=1.0):
+def product(x, y, out, diagonal=0.0, terms=()):
     sub = lax.broadcasted_iota(jnp.int32, (SUB, NFREQ), 0)
     yr = [y.main[0, b] for b in range(NBLK)]
     yi = [y.main[1, b] for b in range(NBLK)]
@@ -341,8 +325,9 @@
                 tr, ti = pr * yr[b] + tr, pr * yi[b] - ti
             real = tr if real is None else real + tr
             imag = ti if imag is None else imag + ti
-        if factor != 1.0:
-            real, imag = factor * real, factor * imag
+        for factor, term in terms:
+            real = real + factor * term.main[0, a]
+            imag = imag + factor * term.main[1, a]
         if diagonal and a < SUB:
             real = real + jnp.where(sub == a, diagonal, 0.0)
         out.main[0, a] = real
@@ -354,33 +339,54 @@
     for a in range(CORNER):
         for e in range(a, CORNER):
             real = sum(ar[a][h] * er[e][h] + ai[a][h] * ei[e][h] for h in range(2))
-            real = factor * jnp.sum(real, axis=0, keepdims=True)
+            real = jnp.sum(real, axis=0, keepdims=True)
+            imag = jnp.zeros_like(real)
+            if a != e:
+                imag = sum(ai[a][h] * er[e][h] - ar[a][h] * ei[e][h] for h in range(2))
+                imag = jnp.sum(imag, axis=0, keepdims=True)
+            for factor, term in terms:
+                r, i, _ = term.entry(SUB + a, SUB + e)
+                real, imag = real + factor * r, imag + factor * i
             if a == e:
-                real = real + diagonal
-                out.put(SUB + a, SUB + a, real, jnp.zeros_like(real))
+                out.put(SUB + a, SUB + a, real + diagonal, jnp.zeros_like(real))
             else:
-                imag = sum(ai[a][h] * er[e][h] - ar[a][h] * ei[e][h] for h in range(2))
-                imag = factor * jnp.sum(imag, axis=0, keepdims=True)
                 out.put(SUB + a, SUB + e, real, imag)
                 out.put(SUB + e, SUB + a, real, -imag)
 
 
-def affine(x, outs):
+def combine(out, diagonal, terms):
     sub = lax.broadcasted_iota(jnp.int32, (SUB, NFREQ), 0)
-    for a in range(NBLK):
-        real = -0.5 * x.main[0, a]
-        imag = -0.5 * x.main[1, a]
-        if a < SUB:
-            real = real + jnp.where(sub == a, 1.5, 0.0)
-        for out in outs:
-            out.main[0, a] = real
-            out.main[1, a] = imag
-    for a in range(CORNER):
-        real = jnp.where(sub == a, 1.5, 0.0) - 0.5 * x.corner[0, a]
-        imag = -0.5 * x.corner[1, a]
-        for out in outs:
-            out.corner[0, a] = real
-            out.corner[1, a] = imag
+    for name, rows in (("main", NBLK), ("corner", CORNER)):
+        target = getattr(out, name)
+        for a in range(rows):
+            real = sum(factor * getattr(term, name)[0, a] for factor, term in terms)
+            imag = sum(factor * getattr(term, name)[1, a] for factor, term in terms)
+            if diagonal and (name == "corner" or a < SUB):
+                real = real + jnp.where(sub == a, diagonal, 0.0)
+            target[0, a] = real
+            target[1, a] = imag
+
+
+TWO_STEPS = (2.25, -2.4375, 1.6875, -0.5625, 0.0625)
+
+
+def inverse_root(w, mats):
+    q, u, r, t, w2, z = mats
+    c0, c1, c2, c3, c4 = TWO_STEPS
+    product(w, w, q)
+    combine(u, 0.0, [(c3, w), (c4, q)])
+    product(q, u, z, c0, [(c1, w), (c2, q)])
+    product(z, z, t)
+    product(w, t, w2)
+    product(w2, w2, q)
+    combine(u, 0.0, [(c3, w2), (c4, q)])
+    product(q, u, r, c0, [(c1, w2), (c2, q)])
+    product(r, r, t)
+    product(z, r, u)
+    product(w2, t, q)
+    combine(q, 1.5, [(-0.5, q)])
+    product(u, q, z)
+    return z
 
 
 def make_roots(share, half_ref, other_ref, gram_ref, packed, rolled, mats):
@@ -389,7 +395,7 @@
     packed[pl.ds(pl.multiple_of((1 - core) * HALF, HALF), HALF), :] = other_ref[...]
     at = lax.axis_index("sx") * lax.axis_size("sy") + lax.axis_index("sy")
     rolled[...] = pltpu.roll(packed[...], (NFREQ - at * share) % NFREQ, 1)
-    y, z, p, y2, z2 = [Hermitian(mats[2 * i], mats[2 * i + 1]) for i in range(5)]
+    y, *free = [Hermitian(mats[2 * i], mats[2 * i + 1]) for i in range(MATS)]
     for ref in mats[1::2]:
         ref[...] = jnp.zeros_like(ref)
 
@@ -413,83 +419,83 @@
             gram_ref[e, a, 0:1, :] = real
             gram_ref[a, e, 1:2, :] = imag
             gram_ref[e, a, 1:2, :] = -imag
-    for step in range(ROOT_STEPS):
-        if step == 0:
-            affine(y, [p, z2])
-        else:
-            product(z, y, p, 1.5, -0.5)
-            product(p, z, z2)
-        if step < ROOT_STEPS - 1:
-            product(y, p, y2)
-        y, y2 = y2, y
-        z, z2 = z2, z
+    z = inverse_root(y, free)
+    mean = sum(z.entry(a, a)[0] for a in range(NBLK)) * (1.0 / NBLK)
+    sub = lax.broadcasted_iota(jnp.int32, (SUB, NFREQ), 0)
     none = jnp.zeros((SUB - CORNER, NFREQ), F32)
+    first = jnp.concatenate([mean * norm, none[1:]], axis=0)
     stacks = []
     for m0 in range(0, NBLK, STACK):
         modes = range(m0, min(m0 + STACK, NBLK))
         stack = []
         for m in modes:
             for c in range(2):
-                stack.append(z.main[c, m] * norm)
+                column = z.main[c, m]
+                if c == 0 and m < SUB:
+                    column = column - jnp.where(sub == m, mean, 0.0)
+                stack.append(column * norm)
                 for b in range(SUB, NBLK):
                     real, imag, sign = z.entry(m, b)
-                    stack.append((imag * sign if c else real) * norm)
-                stack.append(none)
+                    line = imag * sign if c else real
+                    if c == 0 and m == b:
+                        line = line - mean
+                    stack.append(line * norm)
+                stack.append(first if c == 0 and m == 0 else none)
         stack += [jnp.zeros((32, NFREQ), F32)] * (STACK - len(modes))
         stacks.append(jnp.concatenate(stack, axis=0).T)
     return stacks
 
 
 def mode_kernel(chunks, share, half_ref, other_ref, spread_ref, *refs):
-    high_refs = refs[:chunks]
-    low_refs = refs[chunks : 2 * chunks]
-    out_ref, gram_ref, v, packed, rolled, *mats = refs[2 * chunks :]
+    s_refs = refs[:chunks]
+    out_ref, gram_ref, v, mean, packed, rolled, *mats = refs[chunks:]
     step = pl.program_id(0)
 
     @pl.when(step == 0)
     def _():
         stacks = make_roots(share, half_ref, other_ref, gram_ref, packed, rolled, mats)
-        row = lax.broadcasted_iota(jnp.int32, (NFREQ, 3 * LANE), 0)
-        col = lax.broadcasted_iota(jnp.int32, (NFREQ, 3 * LANE), 1)
+        mean[...] = jnp.broadcast_to(stacks[0][:, NBLK : NBLK + 1], (NFREQ, LANE))
+        row = lax.broadcasted_iota(jnp.int32, (NFREQ, 2 * HALF_ROWS), 0)
+        col = lax.broadcasted_iota(jnp.int32, (NFREQ, 2 * HALF_ROWS), 1)
         same = row % SUB == col % SUB
-        for at, stack in enumerate(stacks):
-            both = jnp.concatenate(split(stack), axis=1)
-            for m in range(at * STACK, min((at + 1) * STACK, NBLK)):
-                wide = dot(both, spread_ref[m - at * STACK])
-                for c in range(2):
-                    here = wide[:, c * 3 * LANE : (c + 1) * 3 * LANE]
-                    v[c * NBLK + m] = jnp.where(same, here, 0.0)
+        place = lax.broadcasted_iota(jnp.int32, (NFREQ, LANE), 1) // 32
+        rows = [jnp.where(place == m % STACK, stacks[m // STACK], 0.0) for m in range(NBLK)]
+        rows = jnp.concatenate(rows, axis=0).astype(BF16)
+        for c in range(2):
+            wide = dot(rows, spread_ref[c])[:, : 2 * HALF_ROWS]
+            for m in range(NBLK):
+                here = wide[m * NFREQ : (m + 1) * NFREQ]
+                v[c * NBLK + m] = jnp.where(same, here, 0.0)
 
     fields = []
     for h in range(STEP_GROUPS):
-        g = step * STEP_GROUPS + h
-        start = pl.multiple_of(g * SUB, SUB)
-        vg = v[:, pl.ds(start, SUB), :].reshape(2 * HALF_ROWS, 3 * LANE).astype(BF16)
-        vg = jnp.concatenate([vg[:, : 2 * LANE], vg[:, :LANE], vg[:, 2 * LANE :]], axis=1)
-        high = jnp.concatenate([r[g] for r in high_refs], axis=1)
-        low = jnp.concatenate([r[g] for r in low_refs], axis=1)
-        inputs = jnp.concatenate([high, high[:LOW], low, high[LOW : 2 * LOW]], axis=0)
-        fields.append(dot(vg, inputs).reshape(2 * NBLK, SUB, -1))
+        at = pl.ds(pl.multiple_of((step * STEP_GROUPS + h) * SUB, SUB), SUB)
+        s = jnp.concatenate([r[:, at, :] for r in s_refs], axis=2)
+        flat = s.reshape(2 * HALF_ROWS, -1).astype(BF16)
+        field = dot(v[:, at, :].reshape(2 * HALF_ROWS, 2 * HALF_ROWS).astype(BF16), flat)
+        scale = jnp.concatenate([mean[at, :]] * (s.shape[2] // LANE), axis=1)
+        fields.append(field.reshape(s.shape) + s * scale[None])
     both = jnp.concatenate(fields, axis=1).astype(BF16)
     out_ref[...] = both.reshape(out_ref.shape)
 
 
-def mode_fields(half, other, spread, highs, lows, share):
-    width = sum(s.shape[2] for s in highs)
+def mode_fields(half, other, spread, spectra, share):
+    width = sum(s.shape[2] for s in spectra)
     return pl.pallas_call(
-        functools.partial(mode_kernel, len(highs), share),
+        functools.partial(mode_kernel, len(spectra), share),
         grid=(GROUPS // STEP_GROUPS,),
         out_shape=[
             jax.ShapeDtypeStruct((2, NBLK, NFREQ, width), BF16),
             jax.ShapeDtypeStruct((NBLK, NBLK, 2, share), F32),
         ],
-        in_specs=[VMEM] * (3 + 2 * len(highs)),
+        in_specs=[VMEM] * (3 + len(spectra)),
         out_specs=[
             pl.BlockSpec((2, NBLK, STEP_GROUPS * SUB, width), lambda i: (0, 0, i, 0)),
             spec((NBLK, NBLK, 2, share)),
         ],
         scratch_shapes=[
-            pltpu.VMEM((2 * NBLK, NFREQ, 3 * LANE), F32),
+            pltpu.VMEM((2 * NBLK, NFREQ, 2 * HALF_ROWS), F32),
+            pltpu.VMEM((NFREQ, LANE), F32),
             pltpu.VMEM((PACKED, NFREQ), F32),
             pltpu.VMEM((PACKED, NFREQ), F32),
         ]
@@ -497,9 +503,9 @@
             pltpu.VMEM((2, NBLK, SUB, NFREQ), F32),
             pltpu.VMEM((2, CORNER, SUB, NFREQ), F32),
         ]
-        * 5,
+        * MATS,
         compiler_params=pltpu.CompilerParams(vmem_limit_bytes=32 * 2**20),
-    )(half, other, spread, *highs, *lows)
+    )(half, other, spread, *spectra)
 
 
 def swap(x, axes, mask, size):
@@ -529,7 +535,7 @@
         moved = [swap(packed[d], "tm", d, lanes) for d in reversed(range(1, lanes))]
         arrived.append([packed[0]] + moved)
 
-    highs, lows = [], []
+    spectra = []
     before = []
     for at, pieces in enumerate(arrived):
         base, width = chunks[at]
@@ -537,10 +543,8 @@
         last = at == len(arrived) - 1
         total = gram_part(block_order, offsets, here, tables, pieces, before, last, scale)
         after = total if last else []
-        high, low = spectrum(block_order, offsets, tables[0], pieces, after)
-        highs.append(high)
-        lows.append(low)
-        before = [total[0], high]
+        spectra.append(spectrum(block_order, offsets, tables[0], pieces, after))
+        before = [total[0], spectra[-1]]
 
     axes = ("tm", "sx", "sy")
     size = lanes * groups
@@ -557,11 +561,11 @@
         while len(terms) > 1:
             terms = [a + b for a, b in zip(terms[::2], terms[1::2])]
         half = terms[0]
-    half, highs[-1] = lax.optimization_barrier((half, highs[-1]))
+    half, spectra[-1] = lax.optimization_barrier((half, spectra[-1]))
     other = swap(half, axes, bits[0], size)
 
     spread = jnp.asarray(spread_table())
-    modes, gram = mode_fields(half, other, spread, highs, lows, NFREQ // groups)
+    modes, gram = mode_fields(half, other, spread, spectra, NFREQ // groups)
     modes = jnp.transpose(modes, (0, 2, 1, 3))[:, :, :, None, :]
     return modes, jnp.transpose(gram, (2, 3, 0, 1))
 

time: 51.1 us -> 50 us (0.978)
  local copies, waits for them, and re-layouts: 0.96 us -> 3.9 us
  waiting for transfers between devices: 14.8 us -> 12.3 us
  Pallas kernels: 20 us -> 19 us
    ppermute x14, waiting for transfers between devices: 14.8 us -> 12.3 us  [swap(): return lax.ppermute(x, axes, [(i, i ^ mask) for i in range(size)])]
    unnamed x16 -> x14, local copies, waits for them, and re-layouts: 0.96 us -> 3.2 us
    pallas_call x3, Pallas kernels: 9.47 us -> 8.41 us  [the longest x1 5.15 us: mode_fields(): pl.pallas_call(functools.partial(mode_kernel, len(spectra), share), grid=...]
    slice x1, local copies, waits for them, and re-layouts: 0.01 us -> 0.7 us  [body(): here = weights[:, base:base + width]]
  transfers between devices with their start and end apart: 14 -> 14, of which waited for: 8 -> 7; matrix products, arithmetic and copies ran while one was open for 0% -> 1% of each run, Pallas kernels for 18% -> 18%
where the time goes in v8:
time: 50 us; the launch traced here: 49.8 us
  Pallas kernels  19 us (38%)
  starting transfers between devices  13.8 us (28%)
  waiting for transfers between devices  12.3 us (25%)
  local copies, waits for them, and re-layouts  3.9 us (8%)
  between operations  0.78 us (2%)
    ppermute x14, starting transfers between devices, swap(): return lax.ppermute(x, axes, [(i, i ^ mask) for i in range(size)])  13.8 us
    ppermute x14, waiting for transfers between devices, swap(): return lax.ppermute(x, axes, [(i, i ^ mask) for i in range(size)])  12.3 us
    pallas_call x2, Pallas kernels, pack(): pl.pallas_call(functools.partial(pack_kernel, jobs, parts, first), out_sh...  5.37 us
    pallas_call x2, Pallas kernels, gram_part(): pl.pallas_call(functools.partial(gram_kernel, lanes, scale, first, last),...  5.19 us
    pallas_call x1, Pallas kernels, mode_fields(): pl.pallas_call(functools.partial(mode_kernel, len(spectra), share), grid=...  5.15 us
    pallas_call x2, Pallas kernels, spectrum(): pl.pallas_call(functools.partial(spectrum_kernel, lanes), out_shape=jax.S...  3.25 us
    unnamed x14, local copies, waits for them, and re-layouts  3.2 us
  transfers between devices with their start and end apart: 14, of which 7 were waited for; matrix products, arithmetic and copies ran while one was open for 1% of the time, Pallas kernels for 18%

profile of v8, /device:TPU:0, one launch (start us, length us, event | category | flops | bytes accessed | tf_op | source)
XLA Modules:
  0.0 49.8 jit_solution(6694235162918066961)
XLA Ops:
  0.6 2.3 %shard_map.95 = (bf16[384,256]{1,0:T(8,128)(2,1)}, bf16[384,256]{1,0:T(8,128)(2,1)}, bf16[256,256]{1,0:T(8,128)(2,1)}) custom-call(s32[1,4]{1,0:T(1,128)} %table_hbm.1, bf16[384,4,512]{2,1,0:T(4,128)(2,1)} %x_hbm.3), custom_call_target="tpu_custom_call" | custom-call | flops 201326592 | bytes 1572864 | tf_op jit(solution)/shard_map/pallas_call | solution.py:151
  3.0 2.5 %collective-permute-start.3 = (bf16[384,256]{1,0:T(8,128)(2,1)}, bf16[384,256]{1,0:T(8,128)(2,1)S(1)}, u32[]{:S(2)}, u32[]{:S(2)}) collective-permute-start(bf16[384,256]{1,0:T(8,128)(2,1)} %get-tuple-element.23), channel_id=1, source_target_pairs={{0,24},{8,16},{16,8},{24,0},{1,25},{9,17},{17,9},{25,1},{2,26},{10... | collective-permute-start | bytes 589832 | tf_op jit(solution)/shard_map/ppermute | solution.py:512
  5.4 0.6 %collective-permute-start.4 = (bf16[384,256]{1,0:T(8,128)(2,1)}, bf16[384,256]{1,0:T(8,128)(2,1)S(1)}, u32[]{:S(2)}, u32[]{:S(2)}) collective-permute-start(bf16[384,256]{1,0:T(8,128)(2,1)} %get-tuple-element.24), channel_id=1, source_target_pairs={{0,16},{8,24},{16,0},{24,8},{1,17},{9,25},{17,1},{25,9},{2,18},{10... | collective-permute-start | bytes 589832 | tf_op jit(solution)/shard_map/ppermute | solution.py:512
  6.1 3.0 %shard_map.96 = (bf16[384,256]{1,0:T(8,128)(2,1)}, bf16[384,256]{1,0:T(8,128)(2,1)}, bf16[384,256]{1,0:T(8,128)(2,1)}, bf16[384,256]{1,0:T(8,128)(2,1)}, bf16[38...) custom-call(bf16[256,256]{1,0:T(8,128)(2,1)} %get-tuple-element.17.table_hbm, bf16[384,4,512]{2,1,0:T(4,128)(2,1)} %x_hbm.3), custom_call_target="tpu_custom_call" | custom-call | flops 402653184 | bytes 3145728 | tf_op jit(solution)/shard_map/pallas_call | solution.py:151
  9.1 1.5 %collective-permute-start = (bf16[384,256]{1,0:T(8,128)(2,1)}, bf16[384,256]{1,0:T(8,128)(2,1)S(1)}, u32[]{:S(2)}, u32[]{:S(2)}) collective-permute-start(bf16[384,256]{1,0:T(8,128)(2,1)} %get-tuple-element.19), channel_id=1, source_target_pairs={{0,24},{8,16},{16,8},{24,0},{1,25},{9,17},{17,9},{25,1},{2,26},{10... | collective-permute-start | bytes 589832 | tf_op jit(solution)/shard_map/ppermute | solution.py:512
  10.6 0.2 collective-permute-start.1
  10.9 0.2 collective-permute-start.5
  11.1 0.7 %fusion = (f32[1,256]{1,0:T(1,128)S(1)}, f32[1,256]{1,0:T(1,128)S(1)}) fusion(f32[1,512]{1,0:T(1,128)} %bitcast.7), kind=kLoop, calls=%fused_computation.3 | loop fusion | bytes 4096 | tf_op jit(solution)/shard_map/slice | solution.py:542
  11.8 0.0 collective-permute-done.3.refs_1_
  11.8 0.3 collective-permute-start.2
  12.1 4.1 %collective-permute-done.4.refs_2_ = bf16[384,256]{1,0:T(8,128)(2,1)S(1)} collective-permute-done((bf16[384,256]{1,0:T(8,128)(2,1)}, bf16[384,256]{1,0:T(8,128)(2,1)S(1)}, u32[]{:S(2)}, u32[]{:S(2)}) %collective-permute-start.4) | collective-permute-done | bytes 196640 | tf_op jit(solution)/shard_map/ppermute | solution.py:512
  16.1 0.0 collective-permute-done.5.refs_3_
  16.2 0.0 copy-start.2
  16.2 0.9 %copy-done.2 = bf16[384,256]{1,0:T(8,128)(2,1)S(1)} copy-done((bf16[384,256]{1,0:T(8,128)(2,1)S(1)}, bf16[384,256]{1,0:T(8,128)(2,1)}, u32[]{:S(2)}) %copy-start.2) | copy-done | bytes 196632
  17.1 0.0 copy-start.3
  17.1 0.7 %copy-done.3 = s32[4]{0:T(128)S(1)} copy-done((s32[4]{0:T(128)S(1)}, s32[4]{0:T(128)}, u32[]{:S(2)}) %copy-start.3) | copy-done | bytes 40
  17.7 0.0 copy-start.4
  17.7 0.7 %copy-done.4 = s32[11]{0:T(128)S(1)} copy-done((s32[11]{0:T(128)S(1)}, s32[11]{0:T(128)}, u32[]{:S(2)}) %copy-start.4) | copy-done | bytes 68
  18.4 0.0 copy-start.6
  18.4 0.9 %copy-done.6 = bf16[512,256]{1,0:T(8,128)(2,1)S(1)} copy-done((bf16[512,256]{1,0:T(8,128)(2,1)S(1)}, bf16[512,256]{1,0:T(8,128)(2,1)}, u32[]{:S(2)}) %copy-start.6) | copy-done | bytes 262168
  19.3 0.0 copy-start.5
  19.3 1.6 %shard_map.98.refs_5_.refs_0_ = f32[22,128,256]{2,1,0:T(8,128)S(1)} custom-call(s32[4]{0:T(128)S(1)} %copy-done.3, s32[11]{0:T(128)S(1)} %copy-done.4, bf16[512,256]{1,0:T(8,128)(2,1)S(1)} %copy-done.6, bf16[384,256]{1,0:T(8,128)(2,1)S(1)} %copy-done.2, bf16[384,256]{1,0:T(8,128)(2,1)S(1)} %collective-permute-done.3.refs_1_, ...), custom_call_target="tpu_custom_call" | custom-call | flops 2560000000 | bytes 3000000 | tf_op jit(solution)/shard_map/pallas_call | solution.py:277
  21.0 0.0 copy-done.5
  21.0 0.0 copy-start.1
  21.0 2.8 %shard_map.97.refs_4_ = f32[128,128]{1,0:T(8,128)S(1)} custom-call(s32[4]{0:T(128)S(1)} %copy-done.3, s32[11]{0:T(128)S(1)} %copy-done.4, f32[1,256]{1,0:T(1,128)S(1)} %get-tuple-element.34.w_ref, bf16[512,256]{1,0:T(8,128)(2,1)S(1)} %copy-done.6, bf16[2816,128]{1,0:T(8,128)(2,1)S(1)} %copy-done.5, bf16[384,256]{1,0:T(8,128)(2,1)S(1)} %copy-done.2, ...), custom_call_target="tpu_custom_call" | custom-call | flops 2560000000 | bytes 3000000 | tf_op jit(solution)/shard_map/pallas_call | solution.py:248
  23.8 0.0 collective-permute-done.refs_1_
  23.8 0.0 collective-permute-done.1.refs_2_
  23.8 0.0 collective-permute-done.2.refs_3_
  23.8 0.0 copy-done.1
  23.8 2.4 %shard_map.99 = (bf16[64,128]{1,0:T(8,128)(2,1)S(1)}, bf16[64,128]{1,0:T(8,128)(2,1)S(1)}) custom-call(s32[4]{0:T(128)S(1)} %copy-done.3, s32[11]{0:T(128)S(1)} %copy-done.4, f32[1,256]{1,0:T(1,128)S(1)} %get-tuple-element.35.w_ref, bf16[512,256]{1,0:T(8,128)(2,1)S(1)} %copy-done.6, bf16[2816,128]{1,0:T(8,128)(2,1)S(1)} %copy-done.5, ...), custom_call_target="tpu_custom_call" | custom-call | flops 2560000000 | bytes 3000000 | tf_op jit(solution)/shard_map/pallas_call | solution.py:248
  26.3 0.1 collective-permute-start.6
  26.3 1.2 %collective-permute-done.6 = bf16[64,128]{1,0:T(8,128)(2,1)S(1)} collective-permute-done((bf16[64,128]{1,0:T(8,128)(2,1)S(1)}, bf16[64,128]{1,0:T(8,128)(2,1)S(1)}, u32[]{:S(2)}, u32[]{:S(2)}) %collective-permute-start.6) | collective-permute-done | bytes 16416 | tf_op jit(solution)/shard_map/ppermute | solution.py:512
  27.5 3.2 %collective-permute-start.9 = (bf16[64,128]{1,0:T(8,128)(2,1)S(1)}, bf16[64,128]{1,0:T(8,128)(2,1)S(1)}, u32[]{:S(2)}, u32[]{:S(2)}) collective-permute-start(bf16[64,128]{1,0:T(8,128)(2,1)S(1)} %add_convert_fusion.1), channel_id=1, source_target_pairs={{0,17},{1,16},{2,19},{3,18},{4,21},{5,20},{6,23},{7,22},{8,25},{9,... | collective-permute-start | bytes 49160 | tf_op jit(solution)/shard_map/ppermute | solution.py:512
  30.7 0.5 %collective-permute-start.8 = (bf16[64,128]{1,0:T(8,128)(2,1)S(1)}, bf16[64,128]{1,0:T(8,128)(2,1)S(1)}, u32[]{:S(2)}, u32[]{:S(2)}) collective-permute-start(bf16[64,128]{1,0:T(8,128)(2,1)S(1)} %add_convert_fusion.1), channel_id=1, source_target_pairs={{0,1},{1,0},{2,3},{3,2},{4,5},{5,4},{6,7},{7,6},{8,9},{9,8},{10,11... | collective-permute-start | bytes 49160 | tf_op jit(solution)/shard_map/ppermute | solution.py:512
  31.3 0.1 collective-permute-start.7
  31.4 1.1 %collective-permute-done.9 = bf16[64,128]{1,0:T(8,128)(2,1)S(1)} collective-permute-done((bf16[64,128]{1,0:T(8,128)(2,1)S(1)}, bf16[64,128]{1,0:T(8,128)(2,1)S(1)}, u32[]{:S(2)}, u32[]{:S(2)}) %collective-permute-start.9) | collective-permute-done | bytes 16416 | tf_op jit(solution)/shard_map/ppermute | solution.py:512
  32.5 2.0 %collective-permute-done.8 = bf16[64,128]{1,0:T(8,128)(2,1)S(1)} collective-permute-done((bf16[64,128]{1,0:T(8,128)(2,1)S(1)}, bf16[64,128]{1,0:T(8,128)(2,1)S(1)}, u32[]{:S(2)}, u32[]{:S(2)}) %collective-permute-start.8) | collective-permute-done | bytes 16416 | tf_op jit(solution)/shard_map/ppermute | solution.py:512
  34.5 0.5 %collective-permute-done.7 = bf16[64,128]{1,0:T(8,128)(2,1)S(1)} collective-permute-done((bf16[64,128]{1,0:T(8,128)(2,1)S(1)}, bf16[64,128]{1,0:T(8,128)(2,1)S(1)}, u32[]{:S(2)}, u32[]{:S(2)}) %collective-permute-start.7) | collective-permute-done | bytes 16416 | tf_op jit(solution)/shard_map/ppermute | solution.py:512
  35.0 0.0 copy-start
  35.0 3.7 %collective-permute-start.12 = (bf16[64,128]{1,0:T(8,128)(2,1)S(1)}, bf16[64,128]{1,0:T(8,128)(2,1)S(1)}, u32[]{:S(2)}, u32[]{:S(2)}) collective-permute-start(bf16[64,128]{1,0:T(8,128)(2,1)S(1)} %add_convert_fusion), channel_id=1, source_target_pairs={{0,6},{1,7},{2,4},{3,5},{4,2},{5,3},{6,0},{7,1},{8,14},{9,15},{10,... | collective-permute-start | bytes 49160 | tf_op jit(solution)/shard_map/ppermute | solution.py:512
  38.7 0.0 collective-permute-start.11
  38.7 0.8 %collective-permute-start.10 = (bf16[64,128]{1,0:T(8,128)(2,1)S(1)}, bf16[64,128]{1,0:T(8,128)(2,1)S(1)}, u32[]{:S(2)}, u32[]{:S(2)}) collective-permute-start(bf16[64,128]{1,0:T(8,128)(2,1)S(1)} %add_convert_fusion), channel_id=1, source_target_pairs={{0,2},{1,3},{2,0},{3,1},{4,6},{5,7},{6,4},{7,5},{8,10},{9,11},{10,... | collective-permute-start | bytes 49160 | tf_op jit(solution)/shard_map/ppermute | solution.py:512
  39.5 1.6 %shard_map.100.refs_1_ = f32[22,128,256]{2,1,0:T(8,128)S(1)} custom-call(s32[4]{0:T(128)S(1)} %copy-done.3, s32[11]{0:T(128)S(1)} %copy-done.4, bf16[512,256]{1,0:T(8,128)(2,1)S(1)} %copy-done.6, bf16[384,256]{1,0:T(8,128)(2,1)S(1)} %copy-done.1, bf16[384,256]{1,0:T(8,128)(2,1)S(1)} %collective-permute-done.refs_1_, ...), custom_call_target="tpu_custom_call" | custom-call | flops 2560000000 | bytes 3000000 | tf_op jit(solution)/shard_map/pallas_call | solution.py:277
  41.1 0.0 collective-permute-done.12
  41.1 2.2 %collective-permute-done.11 = bf16[64,128]{1,0:T(8,128)(2,1)S(1)} collective-permute-done((bf16[64,128]{1,0:T(8,128)(2,1)S(1)}, bf16[64,128]{1,0:T(8,128)(2,1)S(1)}, u32[]{:S(2)}, u32[]{:S(2)}) %collective-permute-start.11) | collective-permute-done | bytes 16416 | tf_op jit(solution)/shard_map/ppermute | solution.py:512
  43.3 0.0 collective-permute-done.10
  43.4 0.1 collective-permute-start.13
  43.4 1.2 %collective-permute-done.13.other_ref = f32[64,128]{1,0:T(8,128)S(1)} collective-permute-done((f32[64,128]{1,0:T(8,128)S(1)}, f32[64,128]{1,0:T(8,128)S(1)}, u32[]{:S(2)}, u32[]{:S(2)}) %collective-permute-start.13) | collective-permute-done | bytes 32800 | tf_op jit(solution)/shard_map/ppermute | solution.py:512
  44.6 0.0 copy-done
  44.6 5.2 %shard_map.101 = (bf16[2,11,128,512]{3,2,1,0:T(8,128)(2,1)}, f32[11,11,2,16]{3,2,1,0:T(2,128)}) custom-call(f32[64,128]{1,0:T(8,128)S(1)} %add_add_fusion.half_ref, f32[64,128]{1,0:T(8,128)S(1)} %collective-permute-done.13.other_ref, bf16[2,128,256]{2,1,0:T(8,128)(2,1)S(1)} %copy-done, f32[22,128,256]{2,1,0:T(8,128)S(1)} %shard_map.98.refs_5_.refs_0_, ...), custom_call_target="tpu_custom_call" | custom-call | tf_op jit(solution)/shard_map/pallas_call | solution.py:484
  (3 shorter events, 0.0 us)
Async XLA Ops:
  3.0 8.8 %collective-permute-start.3 = (bf16[384,256]{1,0:T(8,128)(2,1)}, bf16[384,256]{1,0:T(8,128)(2,1)S(1)}, u32[]{:S(2)}, u32[]{:S(2)}) collective-permute-start(bf16[384,256]{1,0:T(8,128)(2,1)} %get-tuple-element.23), channel_id=1, source_target_pairs={{0,24},{8,16},{16,8},{24,0},{1,25},{9,17},{17,9},{25,1},{2,26},{10... | collective-permute-start | bytes 589832 | tf_op jit(solution)/shard_map/ppermute | solution.py:512
  5.4 10.7 %collective-permute-start.4 = (bf16[384,256]{1,0:T(8,128)(2,1)}, bf16[384,256]{1,0:T(8,128)(2,1)S(1)}, u32[]{:S(2)}, u32[]{:S(2)}) collective-permute-start(bf16[384,256]{1,0:T(8,128)(2,1)} %get-tuple-element.24), channel_id=1, source_target_pairs={{0,16},{8,24},{16,0},{24,8},{1,17},{9,25},{17,1},{25,9},{2,18},{10... | collective-permute-start | bytes 589832 | tf_op jit(solution)/shard_map/ppermute | solution.py:512
  9.1 14.7 %collective-permute-start = (bf16[384,256]{1,0:T(8,128)(2,1)}, bf16[384,256]{1,0:T(8,128)(2,1)S(1)}, u32[]{:S(2)}, u32[]{:S(2)}) collective-permute-start(bf16[384,256]{1,0:T(8,128)(2,1)} %get-tuple-element.19), channel_id=1, source_target_pairs={{0,24},{8,16},{16,8},{24,0},{1,25},{9,17},{17,9},{25,1},{2,26},{10... | collective-permute-start | bytes 589832 | tf_op jit(solution)/shard_map/ppermute | solution.py:512
  10.6 13.2 %collective-permute-start.1 = (bf16[384,256]{1,0:T(8,128)(2,1)}, bf16[384,256]{1,0:T(8,128)(2,1)S(1)}, u32[]{:S(2)}, u32[]{:S(2)}) collective-permute-start(bf16[384,256]{1,0:T(8,128)(2,1)} %get-tuple-element.20), channel_id=1, source_target_pairs={{0,16},{8,24},{16,0},{24,8},{1,17},{9,25},{17,1},{25,9},{2,18},{10... | collective-permute-start | bytes 589832 | tf_op jit(solution)/shard_map/ppermute | solution.py:512
  10.9 5.3 %collective-permute-start.5 = (bf16[384,256]{1,0:T(8,128)(2,1)}, bf16[384,256]{1,0:T(8,128)(2,1)S(1)}, u32[]{:S(2)}, u32[]{:S(2)}) collective-permute-start(bf16[384,256]{1,0:T(8,128)(2,1)} %get-tuple-element.25), channel_id=1, source_target_pairs={{0,8},{8,0},{16,24},{24,16},{1,9},{9,1},{17,25},{25,17},{2,10},{10... | collective-permute-start | bytes 589832 | tf_op jit(solution)/shard_map/ppermute | solution.py:512
  11.8 12.0 %collective-permute-start.2 = (bf16[384,256]{1,0:T(8,128)(2,1)}, bf16[384,256]{1,0:T(8,128)(2,1)S(1)}, u32[]{:S(2)}, u32[]{:S(2)}) collective-permute-start(bf16[384,256]{1,0:T(8,128)(2,1)} %get-tuple-element.21), channel_id=1, source_target_pairs={{0,8},{8,0},{16,24},{24,16},{1,9},{9,1},{17,25},{25,17},{2,10},{10... | collective-permute-start | bytes 589832 | tf_op jit(solution)/shard_map/ppermute | solution.py:512
  16.2 0.9 %copy-start.2 = (bf16[384,256]{1,0:T(8,128)(2,1)S(1)}, bf16[384,256]{1,0:T(8,128)(2,1)}, u32[]{:S(2)}) copy-start(bf16[384,256]{1,0:T(8,128)(2,1)} %get-tuple-element.22.refs_0_) | copy-start | bytes 589828
  17.1 0.7 %copy-start.3 = (s32[4]{0:T(128)S(1)}, s32[4]{0:T(128)}, u32[]{:S(2)}) copy-start(s32[4]{0:T(128)} %order_ref.7) | copy-start | bytes 52
  17.7 0.7 %copy-start.4 = (s32[11]{0:T(128)S(1)}, s32[11]{0:T(128)}, u32[]{:S(2)}) copy-start(s32[11]{0:T(128)} %offsets_ref.7) | copy-start | bytes 136
  18.4 0.9 %copy-start.6 = (bf16[512,256]{1,0:T(8,128)(2,1)S(1)}, bf16[512,256]{1,0:T(8,128)(2,1)}, u32[]{:S(2)}) copy-start(bf16[512,256]{1,0:T(8,128)(2,1)} %constant.6.clone.f_ref) | copy-start | bytes 786436
  19.3 1.6 %copy-start.5 = (bf16[2816,128]{1,0:T(8,128)(2,1)S(1)}, bf16[2816,128]{1,0:T(8,128)(2,1)}, u32[]{:S(2)}) copy-start(bf16[2816,128]{1,0:T(8,128)(2,1)} %constant.7.clone.pick_ref) | copy-start | bytes 2162692
  21.0 2.8 %copy-start.1 = (bf16[384,256]{1,0:T(8,128)(2,1)S(1)}, bf16[384,256]{1,0:T(8,128)(2,1)}, u32[]{:S(2)}) copy-start(bf16[384,256]{1,0:T(8,128)(2,1)} %get-tuple-element.18.refs_0_) | copy-start | bytes 589828
  26.3 1.2 %collective-permute-start.6 = (bf16[64,128]{1,0:T(8,128)(2,1)S(1)}, bf16[64,128]{1,0:T(8,128)(2,1)S(1)}, u32[]{:S(2)}, u32[]{:S(2)}) collective-permute-start(bf16[64,128]{1,0:T(8,128)(2,1)S(1)} %get-tuple-element.27.refs_5_), channel_id=1, source_target_pairs={{0,8},{1,9},{2,10},{3,11},{4,12},{5,13},{6,14},{7,15},{8,0},{9,1},... | collective-permute-start | bytes 49160 | tf_op jit(solution)/shard_map/ppermute | solution.py:512
  27.5 4.9 %collective-permute-start.9 = (bf16[64,128]{1,0:T(8,128)(2,1)S(1)}, bf16[64,128]{1,0:T(8,128)(2,1)S(1)}, u32[]{:S(2)}, u32[]{:S(2)}) collective-permute-start(bf16[64,128]{1,0:T(8,128)(2,1)S(1)} %add_convert_fusion.1), channel_id=1, source_target_pairs={{0,17},{1,16},{2,19},{3,18},{4,21},{5,20},{6,23},{7,22},{8,25},{9,... | collective-permute-start | bytes 49160 | tf_op jit(solution)/shard_map/ppermute | solution.py:512
  30.7 3.7 %collective-permute-start.8 = (bf16[64,128]{1,0:T(8,128)(2,1)S(1)}, bf16[64,128]{1,0:T(8,128)(2,1)S(1)}, u32[]{:S(2)}, u32[]{:S(2)}) collective-permute-start(bf16[64,128]{1,0:T(8,128)(2,1)S(1)} %add_convert_fusion.1), channel_id=1, source_target_pairs={{0,1},{1,0},{2,3},{3,2},{4,5},{5,4},{6,7},{7,6},{8,9},{9,8},{10,11... | collective-permute-start | bytes 49160 | tf_op jit(solution)/shard_map/ppermute | solution.py:512
  31.3 3.7 %collective-permute-start.7 = (bf16[64,128]{1,0:T(8,128)(2,1)S(1)}, bf16[64,128]{1,0:T(8,128)(2,1)S(1)}, u32[]{:S(2)}, u32[]{:S(2)}) collective-permute-start(bf16[64,128]{1,0:T(8,128)(2,1)S(1)} %add_convert_fusion.1), channel_id=1, source_target_pairs={{0,16},{1,17},{2,18},{3,19},{4,20},{5,21},{6,22},{7,23},{8,24},{9,... | collective-permute-start | bytes 49160 | tf_op jit(solution)/shard_map/ppermute | solution.py:512
  35.0 9.6 %copy-start = (bf16[2,128,256]{2,1,0:T(8,128)(2,1)S(1)}, bf16[2,128,256]{2,1,0:T(8,128)(2,1)}, u32[]{:S(2)}) copy-start(bf16[2,128,256]{2,1,0:T(8,128)(2,1)} %constant.8.clone.spread_ref) | copy-start | bytes 393220
  35.0 6.1 %collective-permute-start.12 = (bf16[64,128]{1,0:T(8,128)(2,1)S(1)}, bf16[64,128]{1,0:T(8,128)(2,1)S(1)}, u32[]{:S(2)}, u32[]{:S(2)}) collective-permute-start(bf16[64,128]{1,0:T(8,128)(2,1)S(1)} %add_convert_fusion), channel_id=1, source_target_pairs={{0,6},{1,7},{2,4},{3,5},{4,2},{5,3},{6,0},{7,1},{8,14},{9,15},{10,... | collective-permute-start | bytes 49160 | tf_op jit(solution)/shard_map/ppermute | solution.py:512
  38.7 4.6 %collective-permute-start.11 = (bf16[64,128]{1,0:T(8,128)(2,1)S(1)}, bf16[64,128]{1,0:T(8,128)(2,1)S(1)}, u32[]{:S(2)}, u32[]{:S(2)}) collective-permute-start(bf16[64,128]{1,0:T(8,128)(2,1)S(1)} %add_convert_fusion), channel_id=1, source_target_pairs={{0,4},{1,5},{2,6},{3,7},{4,0},{5,1},{6,2},{7,3},{8,12},{9,13},{10,... | collective-permute-start | bytes 49160 | tf_op jit(solution)/shard_map/ppermute | solution.py:512
  38.7 4.6 %collective-permute-start.10 = (bf16[64,128]{1,0:T(8,128)(2,1)S(1)}, bf16[64,128]{1,0:T(8,128)(2,1)S(1)}, u32[]{:S(2)}, u32[]{:S(2)}) collective-permute-start(bf16[64,128]{1,0:T(8,128)(2,1)S(1)} %add_convert_fusion), channel_id=1, source_target_pairs={{0,2},{1,3},{2,0},{3,1},{4,6},{5,7},{6,4},{7,5},{8,10},{9,11},{10,... | collective-permute-start | bytes 49160 | tf_op jit(solution)/shard_map/ppermute | solution.py:512
  43.4 1.3 %collective-permute-start.13 = (f32[64,128]{1,0:T(8,128)S(1)}, f32[64,128]{1,0:T(8,128)S(1)}, u32[]{:S(2)}, u32[]{:S(2)}) collective-permute-start(f32[64,128]{1,0:T(8,128)S(1)} %add_add_fusion.half_ref), channel_id=1, source_target_pairs={{0,8},{1,9},{2,10},{3,11},{4,12},{5,13},{6,14},{7,15},{8,0},{9,1},... | collective-permute-start | bytes 98312 | tf_op jit(solution)/shard_map/ppermute | solution.py:512

commit v9 on v8

--- a/solution.py
+++ b/solution.py
@@ -16,7 +16,6 @@
 SUB = 8
 HALF_ROWS = NBLK * SUB
 GROUPS = NFREQ // SUB
-STEP_GROUPS = 4
 MATS = 7
 PACKED = 128
 HALF = PACKED // 2
@@ -205,63 +204,87 @@
     return jnp.concatenate([real, pad, imag, pad], axis=0)
 
 
-def gram_kernel(lanes, scale, first, last, order_ref, offsets_ref, w_ref, f_ref, pick_ref, *refs):
-    pieces = refs[:lanes]
-    rest = refs[lanes:]
-    if not first:
-        before_ref, _, *rest = rest
-    *packed_refs, record, s_ref, masked = rest
-    fill_record(order_ref, pieces, record, jnp.sqrt(w_ref[...]))
-    transform(offsets_ref, f_ref[:NFFT] if last else f_ref[...], record, s_ref)
+def gram_rows(base, groups, s_ref, pick_ref, masked):
     row = lax.broadcasted_iota(jnp.int32, (HALF_ROWS, LANE), 0)
     col = lax.broadcasted_iota(jnp.int32, (HALF_ROWS, LANE), 1)
     same = row % SUB == col % SUB
-    for g in range(GROUPS):
-        at = slice(g * SUB, (g + 1) * SUB)
-        s = s_ref[:, at, :]
-        full = dot_nt(s.reshape(2 * HALF_ROWS, -1).astype(BF16), padded(s).astype(BF16))
-        real = full[:HALF_ROWS, :LANE] + full[HALF_ROWS:, LANE:]
-        imag = full[:HALF_ROWS, LANE:] - full[HALF_ROWS:, :LANE]
-        real = jnp.where(same, real, 0.0)
-        imag = jnp.where(same, imag, 0.0)
+    for pair in range(0, groups, 2):
+        blocks = []
+        for g in (pair, pair + 1):
+            s = s_ref[:, pl.ds(pl.multiple_of(base + g * SUB, SUB), SUB), :]
+            full = dot_nt(s.reshape(2 * HALF_ROWS, -1).astype(BF16), padded(s).astype(BF16))
+            real = full[:HALF_ROWS, :LANE] + full[HALF_ROWS:, LANE:]
+            imag = full[:HALF_ROWS, LANE:] - full[HALF_ROWS:, :LANE]
+            blocks.append([jnp.where(same, part, 0.0) for part in (real, imag)])
+        at = slice(pair * SUB, (pair + 2) * SUB)
         for a in range(NBLK):
             rows = slice(a * SUB, (a + 1) * SUB)
-            masked[at, a * WIDE : a * WIDE + LANE] = real[rows]
-            masked[at, a * WIDE + LANE : (a + 1) * WIDE] = imag[rows]
-    total = dot(masked[...].astype(BF16), pick_ref[...]).T * scale
-    if not first:
-        total = total + before_ref[...]
+            for part in range(2):
+                both = jnp.concatenate([block[part][rows] for block in blocks], axis=0)
+                cols = slice(a * WIDE + part * LANE, a * WIDE + (part + 1) * LANE)
+                masked[at, cols] = both.astype(BF16)
+    return dot(masked[...], pick_ref[...])
+
+
+def gram_kernel(lanes, scale, last, order_ref, offsets_ref, w_ref, f_ref, pick_ref, *refs):
+    pieces = refs[:lanes]
     if not last:
-        packed_refs[0][...] = total
+        gram_ref, record, s_ref, masked = refs[lanes:]
+    else:
+        before_ref, _, gram_ref, s_ref, record, masked = refs[lanes:]
+    fill_record(order_ref, pieces, record, jnp.sqrt(w_ref[...]))
+    transform(offsets_ref, f_ref[:NFFT] if last else f_ref[...], record, s_ref)
+    if not last:
+        gram_ref[...] = gram_rows(0, GROUPS, s_ref, pick_ref, masked) * scale
         return
-    keep_ref, send_ref = packed_refs
-    other = lax.axis_index("tm") % 2 == 1
-    keep_ref[...] = jnp.where(other, total[HALF:], total[:HALF]).astype(BF16)
-    send_ref[...] = jnp.where(other, total[:HALF], total[HALF:]).astype(BF16)
-
-
-def gram_part(order, offsets, weights, tables, pieces, before, last, scale):
+    base = pl.multiple_of((1 - lax.axis_index("tm") % 2) * HALF, HALF)
+    total = gram_rows(base, GROUPS // 2, s_ref, pick_ref, masked) * scale
+    gram_ref[...] = (total + before_ref[pl.ds(base, HALF), :]).astype(BF16)
+
+
+def gram_part(order, offsets, weights, tables, pieces, before, scale):
     lanes = len(pieces)
     steps, width = pieces[0].shape
-    first = not before
+    last = bool(before)
     args = [order, offsets, weights, *tables, *pieces, *before]
+    spectrum_shape = (2 * NBLK, NFREQ, width)
+    scratch = [pltpu.VMEM((width // LANE, lanes * steps, LANE), F32)]
+    if last:
+        outs = [jax.ShapeDtypeStruct((HALF, PACKED), BF16)]
+        outs.append(jax.ShapeDtypeStruct(spectrum_shape, F32))
+    else:
+        outs = [jax.ShapeDtypeStruct((NFREQ, PACKED), F32)]
+        scratch.append(pltpu.VMEM(spectrum_shape, F32))
+    scratch.append(pltpu.VMEM((HALF if last else NFREQ, NBLK * WIDE), BF16))
     return pl.pallas_call(
-        functools.partial(gram_kernel, lanes, scale, first, last),
-        out_shape=[jax.ShapeDtypeStruct((HALF, NFREQ), BF16)] * 2
-        if last
-        else [jax.ShapeDtypeStruct((PACKED, NFREQ), F32)],
+        functools.partial(gram_kernel, lanes, scale, last),
+        out_shape=outs,
         in_specs=[SMEM, SMEM] + [VMEM] * (len(args) - 2),
-        out_specs=[VMEM] * (2 if last else 1),
-        scratch_shapes=[
-            pltpu.VMEM((width // LANE, lanes * steps, LANE), F32),
-            pltpu.VMEM((2 * NBLK, NFREQ, width), F32),
-            pltpu.VMEM((NFREQ, NBLK * WIDE), F32),
-        ],
+        out_specs=[VMEM] * len(outs),
+        scratch_shapes=scratch,
         compiler_params=pltpu.CompilerParams(vmem_limit_bytes=32 * 2**20),
         cost_estimate=pl.CostEstimate(
             flops=width * 10**7, bytes_accessed=3 * 10**6, transcendentals=0
         ),
     )(*args)
+
+
+def own_kernel(scale, s_ref, pick_ref, before_ref, gram_ref, masked):
+    base = pl.multiple_of(lax.axis_index("tm") % 2 * HALF, HALF)
+    total = gram_rows(base, GROUPS // 2, s_ref, pick_ref, masked) * scale
+    gram_ref[...] = (total + before_ref[pl.ds(base, HALF), :]).astype(BF16)
+
+
+def own_part(scaled, pick, before, scale):
+    return pl.pallas_call(
+        functools.partial(own_kernel, scale),
+        out_shape=jax.ShapeDtypeStruct((HALF, PACKED), BF16),
+        in_specs=[VMEM] * 3,
+        out_specs=VMEM,
+        scratch_shapes=[pltpu.VMEM((HALF, NBLK * WIDE), BF16)],
+        compiler_params=pltpu.CompilerParams(vmem_limit_bytes=32 * 2**20),
+        cost_estimate=pl.CostEstimate(flops=10**9, bytes_accessed=3 * 10**6, transcendentals=0),
+    )(scaled, pick, before)
 
 
 def spectrum_kernel(lanes, order_ref, offsets_ref, f_ref, *refs):
@@ -393,6 +416,7 @@
     core = lax.axis_index("tm") % 2
     packed[pl.ds(pl.multiple_of(core * HALF, HALF), HALF), :] = half_ref[...]
     packed[pl.ds(pl.multiple_of((1 - core) * HALF, HALF), HALF), :] = other_ref[...]
+    packed[...] = packed[...].T
     at = lax.axis_index("sx") * lax.axis_size("sy") + lax.axis_index("sy")
     rolled[...] = pltpu.roll(packed[...], (NFREQ - at * share) % NFREQ, 1)
     y, *free = [Hermitian(mats[2 * i], mats[2 * i + 1]) for i in range(MATS)]
@@ -448,56 +472,58 @@
 
 def mode_kernel(chunks, share, half_ref, other_ref, spread_ref, *refs):
     s_refs = refs[:chunks]
-    out_ref, gram_ref, v, mean, packed, rolled, *mats = refs[chunks:]
-    step = pl.program_id(0)
-
-    @pl.when(step == 0)
-    def _():
-        stacks = make_roots(share, half_ref, other_ref, gram_ref, packed, rolled, mats)
-        mean[...] = jnp.broadcast_to(stacks[0][:, NBLK : NBLK + 1], (NFREQ, LANE))
-        row = lax.broadcasted_iota(jnp.int32, (NFREQ, 2 * HALF_ROWS), 0)
-        col = lax.broadcasted_iota(jnp.int32, (NFREQ, 2 * HALF_ROWS), 1)
-        same = row % SUB == col % SUB
-        place = lax.broadcasted_iota(jnp.int32, (NFREQ, LANE), 1) // 32
-        rows = [jnp.where(place == m % STACK, stacks[m // STACK], 0.0) for m in range(NBLK)]
-        rows = jnp.concatenate(rows, axis=0).astype(BF16)
-        for c in range(2):
-            wide = dot(rows, spread_ref[c])[:, : 2 * HALF_ROWS]
-            for m in range(NBLK):
-                here = wide[m * NFREQ : (m + 1) * NFREQ]
-                v[c * NBLK + m] = jnp.where(same, here, 0.0)
-
-    fields = []
-    for h in range(STEP_GROUPS):
-        at = pl.ds(pl.multiple_of((step * STEP_GROUPS + h) * SUB, SUB), SUB)
-        s = jnp.concatenate([r[:, at, :] for r in s_refs], axis=2)
-        flat = s.reshape(2 * HALF_ROWS, -1).astype(BF16)
-        field = dot(v[:, at, :].reshape(2 * HALF_ROWS, 2 * HALF_ROWS).astype(BF16), flat)
-        scale = jnp.concatenate([mean[at, :]] * (s.shape[2] // LANE), axis=1)
-        fields.append(field.reshape(s.shape) + s * scale[None])
-    both = jnp.concatenate(fields, axis=1).astype(BF16)
-    out_ref[...] = both.reshape(out_ref.shape)
+    out_hbm, gram_ref, out, v, mean, packed, rolled, sem, *mats = refs[chunks:]
+    stacks = make_roots(share, half_ref, other_ref, gram_ref, packed, rolled, mats)
+    mean[...] = jnp.broadcast_to(stacks[0][:, NBLK : NBLK + 1], (NFREQ, LANE))
+    row = lax.broadcasted_iota(jnp.int32, (NFREQ, 2 * HALF_ROWS), 0)
+    col = lax.broadcasted_iota(jnp.int32, (NFREQ, 2 * HALF_ROWS), 1)
+    same = row % SUB == col % SUB
+    place = lax.broadcasted_iota(jnp.int32, (NFREQ, LANE), 1) // 32
+    rows = [jnp.where(place == m % STACK, stacks[m // STACK], 0.0) for m in range(NBLK)]
+    rows = jnp.concatenate(rows, axis=0).astype(BF16)
+    for c in range(2):
+        wide = dot(rows, spread_ref[c])[:, : 2 * HALF_ROWS]
+        for m in range(NBLK):
+            v[c * NBLK + m] = jnp.where(same, wide[m * NFREQ : (m + 1) * NFREQ], 0.0)
+
+    copies = []
+    for pair in range(GROUPS // 2):
+        fields = []
+        for g in (2 * pair, 2 * pair + 1):
+            at = slice(g * SUB, (g + 1) * SUB)
+            s = jnp.concatenate([r[:, at, :] for r in s_refs], axis=2)
+            flat = s.reshape(2 * HALF_ROWS, -1).astype(BF16)
+            field = dot(v[:, at, :].reshape(2 * HALF_ROWS, 2 * HALF_ROWS).astype(BF16), flat)
+            scale = jnp.concatenate([mean[at, :]] * (s.shape[2] // LANE), axis=1)
+            fields.append(field.reshape(s.shape) + s * scale[None])
+        both = jnp.concatenate(fields, axis=1).astype(BF16)
+        at = slice(pair * 2 * SUB, (pair + 1) * 2 * SUB)
+        out[:, :, at, :] = both.reshape(2, NBLK, 2 * SUB, -1)
+        copies.append(
+            pltpu.make_async_copy(out.at[:, :, at, :], out_hbm.at[:, :, at, :], sem.at[pair])
+        )
+        copies[-1].start()
+    for copy in copies:
+        copy.wait()
 
 
 def mode_fields(half, other, spread, spectra, share):
-    width = sum(s.shape[2] for s in spectra)
+    shape = (2, NBLK, NFREQ, sum(s.shape[2] for s in spectra))
     return pl.pallas_call(
         functools.partial(mode_kernel, len(spectra), share),
-        grid=(GROUPS // STEP_GROUPS,),
         out_shape=[
-            jax.ShapeDtypeStruct((2, NBLK, NFREQ, width), BF16),
+            jax.ShapeDtypeStruct(shape, BF16),
             jax.ShapeDtypeStruct((NBLK, NBLK, 2, share), F32),
         ],
         in_specs=[VMEM] * (3 + len(spectra)),
-        out_specs=[
-            pl.BlockSpec((2, NBLK, STEP_GROUPS * SUB, width), lambda i: (0, 0, i, 0)),
-            spec((NBLK, NBLK, 2, share)),
-        ],
+        out_specs=[HBM, VMEM],
         scratch_shapes=[
+            pltpu.VMEM(shape, BF16),
             pltpu.VMEM((2 * NBLK, NFREQ, 2 * HALF_ROWS), F32),
             pltpu.VMEM((NFREQ, LANE), F32),
             pltpu.VMEM((PACKED, NFREQ), F32),
             pltpu.VMEM((PACKED, NFREQ), F32),
+            pltpu.SemaphoreType.DMA((GROUPS // 2,)),
         ]
         + [
             pltpu.VMEM((2, NBLK, SUB, NFREQ), F32),
@@ -535,22 +561,20 @@
         moved = [swap(packed[d], "tm", d, lanes) for d in reversed(range(1, lanes))]
         arrived.append([packed[0]] + moved)
 
-    spectra = []
-    before = []
-    for at, pieces in enumerate(arrived):
-        base, width = chunks[at]
-        here = weights[:, base : base + width]
-        last = at == len(arrived) - 1
-        total = gram_part(block_order, offsets, here, tables, pieces, before, last, scale)
-        after = total if last else []
-        spectra.append(spectrum(block_order, offsets, tables[0], pieces, after))
-        before = [total[0], spectra[-1]]
-
     axes = ("tm", "sx", "sy")
     size = lanes * groups
     bits = [b * groups for b in powers(lanes)] + powers(groups)
-    keep, send = total
-    half = keep.astype(F32) + swap(send, axes, bits[0], size).astype(F32)
+    parts = [weights[:, base : base + width] for base, width in chunks]
+    (before,) = gram_part(block_order, offsets, parts[0], tables, arrived[0], [], scale)
+    spectra = [spectrum(block_order, offsets, tables[0], arrived[0], [])]
+    send, scaled = gram_part(
+        block_order, offsets, parts[1], tables, arrived[1], [before, spectra[0]], scale
+    )
+
+    other = swap(send, axes, bits[0], size)
+    keep = own_part(scaled, tables[1], before, scale)
+    spectra.append(spectrum(block_order, offsets, tables[0], arrived[1], [keep]))
+    half = keep.astype(F32) + other.astype(F32)
     for at in range(1, len(bits), 2):
         masks = bits[at : at + 2]
         if len(masks) == 2:

time: 50 us -> 49.6 us (level)
  waiting for transfers between devices: 12.3 us -> 11.6 us
    ppermute x14, waiting for transfers between devices: 12.3 us -> 11.6 us  [swap(): return lax.ppermute(x, axes, [(i, i ^ mask) for i in range(size)])]
    pallas_call x3 -> x4, Pallas kernels: 10.3 us -> 10.5 us  [the longest x1 5.04 us: mode_fields(): pl.pallas_call(functools.partial(mode_kernel, len(spectra), share), out_s...]
    unnamed x14 -> x20, local copies, waits for them, and re-layouts: 3.2 us -> 3.22 us
  transfers between devices with their start and end apart: 14 -> 14, of which waited for: 7 -> 7; matrix products, arithmetic and copies ran while one was open for 1% -> 1% of each run, Pallas kernels for 18% -> 20%
where the time goes in v9:
time: 49.6 us; the launch traced here: 49.4 us
  Pallas kernels  19.1 us (39%)
  starting transfers between devices  13.9 us (28%)
  waiting for transfers between devices  11.6 us (23%)
  local copies, waits for them, and re-layouts  3.92 us (8%)
  between operations  0.78 us (2%)
    ppermute x14, starting transfers between devices, swap(): return lax.ppermute(x, axes, [(i, i ^ mask) for i in range(size)])  13.9 us
    ppermute x14, waiting for transfers between devices, swap(): return lax.ppermute(x, axes, [(i, i ^ mask) for i in range(size)])  11.6 us
    pallas_call x2, Pallas kernels, pack(): pl.pallas_call(functools.partial(pack_kernel, jobs, parts, first), out_sh...  5.38 us
    pallas_call x1, Pallas kernels, mode_fields(): pl.pallas_call(functools.partial(mode_kernel, len(spectra), share), out_s...  5.04 us
    pallas_call x2, Pallas kernels, gram_part(): pl.pallas_call(functools.partial(gram_kernel, lanes, scale, last), out_sh...  4.79 us
    pallas_call x2, Pallas kernels, spectrum(): pl.pallas_call(functools.partial(spectrum_kernel, lanes), out_shape=jax.S...  3.23 us
    unnamed x20, local copies, waits for them, and re-layouts  3.22 us
  transfers between devices with their start and end apart: 14, of which 7 were waited for; matrix products, arithmetic and copies ran while one was open for 1% of the time, Pallas kernels for 20%

profile of v9, /device:TPU:0, one launch (start us, length us, event | category | flops | bytes accessed | tf_op | source)
XLA Modules:
  0.0 49.4 jit_solution(9868031569756876288)
XLA Ops:
  0.6 2.3 %shard_map.95 = (bf16[384,256]{1,0:T(8,128)(2,1)}, bf16[384,256]{1,0:T(8,128)(2,1)}, bf16[256,256]{1,0:T(8,128)(2,1)}) custom-call(s32[1,4]{1,0:T(1,128)} %table_hbm.1, bf16[384,4,512]{2,1,0:T(4,128)(2,1)} %x_hbm.3), custom_call_target="tpu_custom_call" | custom-call | flops 201326592 | bytes 1572864 | tf_op jit(solution)/shard_map/pallas_call | solution.py:150
  3.0 2.5 %collective-permute-start.3 = (bf16[384,256]{1,0:T(8,128)(2,1)}, bf16[384,256]{1,0:T(8,128)(2,1)S(1)}, u32[]{:S(2)}, u32[]{:S(2)}) collective-permute-start(bf16[384,256]{1,0:T(8,128)(2,1)} %get-tuple-element.23), channel_id=1, source_target_pairs={{0,24},{8,16},{16,8},{24,0},{1,25},{9,17},{17,9},{25,1},{2,26},{10... | collective-permute-start | bytes 589832 | tf_op jit(solution)/shard_map/ppermute | solution.py:538
  5.4 0.6 %collective-permute-start.4 = (bf16[384,256]{1,0:T(8,128)(2,1)}, bf16[384,256]{1,0:T(8,128)(2,1)S(1)}, u32[]{:S(2)}, u32[]{:S(2)}) collective-permute-start(bf16[384,256]{1,0:T(8,128)(2,1)} %get-tuple-element.24), channel_id=1, source_target_pairs={{0,16},{8,24},{16,0},{24,8},{1,17},{9,25},{17,1},{25,9},{2,18},{10... | collective-permute-start | bytes 589832 | tf_op jit(solution)/shard_map/ppermute | solution.py:538
  6.1 3.0 %shard_map.96 = (bf16[384,256]{1,0:T(8,128)(2,1)}, bf16[384,256]{1,0:T(8,128)(2,1)}, bf16[384,256]{1,0:T(8,128)(2,1)}, bf16[384,256]{1,0:T(8,128)(2,1)}, bf16[38...) custom-call(bf16[256,256]{1,0:T(8,128)(2,1)} %get-tuple-element.17.table_hbm, bf16[384,4,512]{2,1,0:T(4,128)(2,1)} %x_hbm.3), custom_call_target="tpu_custom_call" | custom-call | flops 402653184 | bytes 3145728 | tf_op jit(solution)/shard_map/pallas_call | solution.py:150
  9.1 1.5 %collective-permute-start = (bf16[384,256]{1,0:T(8,128)(2,1)}, bf16[384,256]{1,0:T(8,128)(2,1)S(1)}, u32[]{:S(2)}, u32[]{:S(2)}) collective-permute-start(bf16[384,256]{1,0:T(8,128)(2,1)} %get-tuple-element.19), channel_id=1, source_target_pairs={{0,24},{8,16},{16,8},{24,0},{1,25},{9,17},{17,9},{25,1},{2,26},{10... | collective-permute-start | bytes 589832 | tf_op jit(solution)/shard_map/ppermute | solution.py:538
  10.6 0.2 collective-permute-start.1
  10.9 0.2 collective-permute-start.5
  11.1 0.7 %fusion = (f32[1,256]{1,0:T(1,128)S(1)}, f32[1,256]{1,0:T(1,128)S(1)}) fusion(f32[1,512]{1,0:T(1,128)} %bitcast.7), kind=kLoop, calls=%fused_computation.3 | loop fusion | bytes 4096 | tf_op jit(solution)/shard_map/slice | solution.py:567
  11.8 0.0 collective-permute-done.3.refs_1_
  11.8 0.3 collective-permute-start.2
  12.1 4.1 %collective-permute-done.4.refs_2_ = bf16[384,256]{1,0:T(8,128)(2,1)S(1)} collective-permute-done((bf16[384,256]{1,0:T(8,128)(2,1)}, bf16[384,256]{1,0:T(8,128)(2,1)S(1)}, u32[]{:S(2)}, u32[]{:S(2)}) %collective-permute-start.4) | collective-permute-done | bytes 196640 | tf_op jit(solution)/shard_map/ppermute | solution.py:538
  16.2 0.0 collective-permute-done.5.refs_3_
  16.2 0.0 copy-start.2
  16.2 0.9 %copy-done.2 = bf16[384,256]{1,0:T(8,128)(2,1)S(1)} copy-done((bf16[384,256]{1,0:T(8,128)(2,1)S(1)}, bf16[384,256]{1,0:T(8,128)(2,1)}, u32[]{:S(2)}) %copy-start.2) | copy-done | bytes 196632
  17.1 0.0 copy-start.3
  17.1 0.7 %copy-done.3 = s32[4]{0:T(128)S(1)} copy-done((s32[4]{0:T(128)S(1)}, s32[4]{0:T(128)}, u32[]{:S(2)}) %copy-start.3) | copy-done | bytes 40
  17.7 0.0 copy-start.5
  17.7 0.7 %copy-done.5 = s32[11]{0:T(128)S(1)} copy-done((s32[11]{0:T(128)S(1)}, s32[11]{0:T(128)}, u32[]{:S(2)}) %copy-start.5) | copy-done | bytes 68
  18.4 0.0 copy-start.8
  18.4 0.9 %copy-done.8 = bf16[512,256]{1,0:T(8,128)(2,1)S(1)} copy-done((bf16[512,256]{1,0:T(8,128)(2,1)S(1)}, bf16[512,256]{1,0:T(8,128)(2,1)}, u32[]{:S(2)}) %copy-start.8) | copy-done | bytes 262168
  19.3 0.0 copy-start.7
  19.3 1.6 %shard_map.98.refs_5_.refs_0_ = f32[22,128,256]{2,1,0:T(8,128)S(1)} custom-call(s32[4]{0:T(128)S(1)} %copy-done.3, s32[11]{0:T(128)S(1)} %copy-done.5, bf16[512,256]{1,0:T(8,128)(2,1)S(1)} %copy-done.8, bf16[384,256]{1,0:T(8,128)(2,1)S(1)} %copy-done.2, bf16[384,256]{1,0:T(8,128)(2,1)S(1)} %collective-permute-done.3.refs_1_, ...), custom_call_target="tpu_custom_call" | custom-call | flops 2560000000 | bytes 3000000 | tf_op jit(solution)/shard_map/pallas_call | solution.py:300
  21.0 0.0 copy-done.7
  21.0 0.0 copy-start.1
  21.0 2.7 %shard_map.97.refs_4_.before_ref = f32[128,128]{1,0:T(8,128)S(1)} custom-call(s32[4]{0:T(128)S(1)} %copy-done.3, s32[11]{0:T(128)S(1)} %copy-done.5, f32[1,256]{1,0:T(1,128)S(1)} %get-tuple-element.34.w_ref, bf16[512,256]{1,0:T(8,128)(2,1)S(1)} %copy-done.8, bf16[2816,128]{1,0:T(8,128)(2,1)S(1)} %copy-done.7, bf16[384,256]{1,0:T(8,128)(2,1)S(1)} %copy-done.2, ...), custom_call_target="tpu_custom_call" | custom-call | flops 2560000000 | bytes 3000000 | tf_op jit(solution)/shard_map/pallas_call | solution.py:259
  23.7 0.0 collective-permute-done.refs_1_
  23.7 0.0 collective-permute-done.1.refs_2_
  23.7 0.0 collective-permute-done.2.refs_3_
  23.8 0.0 copy-done.1
  23.8 2.1 %shard_map.99 = (bf16[64,128]{1,0:T(8,128)(2,1)S(1)}, f32[22,128,256]{2,1,0:T(8,128)S(1)}) custom-call(s32[4]{0:T(128)S(1)} %copy-done.3, s32[11]{0:T(128)S(1)} %copy-done.5, f32[1,256]{1,0:T(1,128)S(1)} %get-tuple-element.35.w_ref, bf16[512,256]{1,0:T(8,128)(2,1)S(1)} %copy-done.8, bf16[2816,128]{1,0:T(8,128)(2,1)S(1)} %copy-done.7, ...), custom_call_target="tpu_custom_call" | custom-call | flops 2560000000 | bytes 3000000 | tf_op jit(solution)/shard_map/pallas_call | solution.py:259
  25.8 0.0 copy-start.4
  25.9 0.0 copy-start.6
  25.9 0.0 copy-start.9
  25.9 0.1 collective-permute-start.6
  26.0 0.7 %shard_map.100.refs_4_ = bf16[64,128]{1,0:T(8,128)(2,1)S(1)} custom-call(f32[22,128,256]{2,1,0:T(8,128)S(1)} %get-tuple-element.26.s_ref, bf16[2816,128]{1,0:T(8,128)(2,1)S(1)} %copy-done.7, f32[128,128]{1,0:T(8,128)S(1)} %shard_map.97.refs_4_.before_ref), custom_call_target="tpu_custom_call" | custom-call | flops 1000000000 | bytes 3000000 | tf_op jit(solution)/shard_map/pallas_call | solution.py:279
  26.7 0.5 collective-permute-done.6
  27.1 3.3 %collective-permute-start.9 = (bf16[64,128]{1,0:T(8,128)(2,1)S(1)}, bf16[64,128]{1,0:T(8,128)(2,1)S(1)}, u32[]{:S(2)}, u32[]{:S(2)}) collective-permute-start(bf16[64,128]{1,0:T(8,128)(2,1)S(1)} %add_convert_fusion.1), channel_id=1, source_target_pairs={{0,17},{1,16},{2,19},{3,18},{4,21},{5,20},{6,23},{7,22},{8,25},{9,... | collective-permute-start | bytes 49160 | tf_op jit(solution)/shard_map/ppermute | solution.py:538
  30.4 0.5 %collective-permute-start.8 = (bf16[64,128]{1,0:T(8,128)(2,1)S(1)}, bf16[64,128]{1,0:T(8,128)(2,1)S(1)}, u32[]{:S(2)}, u32[]{:S(2)}) collective-permute-start(bf16[64,128]{1,0:T(8,128)(2,1)S(1)} %add_convert_fusion.1), channel_id=1, source_target_pairs={{0,1},{1,0},{2,3},{3,2},{4,5},{5,4},{6,7},{7,6},{8,9},{9,8},{10,11... | collective-permute-start | bytes 49160 | tf_op jit(solution)/shard_map/ppermute | solution.py:538
  31.0 0.1 collective-permute-start.7
  31.1 1.1 %collective-permute-done.9 = bf16[64,128]{1,0:T(8,128)(2,1)S(1)} collective-permute-done((bf16[64,128]{1,0:T(8,128)(2,1)S(1)}, bf16[64,128]{1,0:T(8,128)(2,1)S(1)}, u32[]{:S(2)}, u32[]{:S(2)}) %collective-permute-start.9) | collective-permute-done | bytes 16416 | tf_op jit(solution)/shard_map/ppermute | solution.py:538
  32.2 2.0 %collective-permute-done.8 = bf16[64,128]{1,0:T(8,128)(2,1)S(1)} collective-permute-done((bf16[64,128]{1,0:T(8,128)(2,1)S(1)}, bf16[64,128]{1,0:T(8,128)(2,1)S(1)}, u32[]{:S(2)}, u32[]{:S(2)}) %collective-permute-start.8) | collective-permute-done | bytes 16416 | tf_op jit(solution)/shard_map/ppermute | solution.py:538
  34.2 0.5 %collective-permute-done.7 = bf16[64,128]{1,0:T(8,128)(2,1)S(1)} collective-permute-done((bf16[64,128]{1,0:T(8,128)(2,1)S(1)}, bf16[64,128]{1,0:T(8,128)(2,1)S(1)}, u32[]{:S(2)}, u32[]{:S(2)}) %collective-permute-start.7) | collective-permute-done | bytes 16416 | tf_op jit(solution)/shard_map/ppermute | solution.py:538
  34.7 0.0 copy-start
  34.7 3.7 %collective-permute-start.12 = (bf16[64,128]{1,0:T(8,128)(2,1)S(1)}, bf16[64,128]{1,0:T(8,128)(2,1)S(1)}, u32[]{:S(2)}, u32[]{:S(2)}) collective-permute-start(bf16[64,128]{1,0:T(8,128)(2,1)S(1)} %add_convert_fusion), channel_id=1, source_target_pairs={{0,6},{1,7},{2,4},{3,5},{4,2},{5,3},{6,0},{7,1},{8,14},{9,15},{10,... | collective-permute-start | bytes 49160 | tf_op jit(solution)/shard_map/ppermute | solution.py:538
  38.4 0.0 collective-permute-start.11
  38.4 0.8 %collective-permute-start.10 = (bf16[64,128]{1,0:T(8,128)(2,1)S(1)}, bf16[64,128]{1,0:T(8,128)(2,1)S(1)}, u32[]{:S(2)}, u32[]{:S(2)}) collective-permute-start(bf16[64,128]{1,0:T(8,128)(2,1)S(1)} %add_convert_fusion), channel_id=1, source_target_pairs={{0,2},{1,3},{2,0},{3,1},{4,6},{5,7},{6,4},{7,5},{8,10},{9,11},{10,... | collective-permute-start | bytes 49160 | tf_op jit(solution)/shard_map/ppermute | solution.py:538
  39.2 0.0 copy-done.4
  39.2 0.0 copy-done.6
  39.2 0.0 copy-done.9
  39.2 1.6 %shard_map.101.refs_1_ = f32[22,128,256]{2,1,0:T(8,128)S(1)} custom-call(s32[4]{0:T(128)S(1)} %copy-done.4, s32[11]{0:T(128)S(1)} %copy-done.6, bf16[512,256]{1,0:T(8,128)(2,1)S(1)} %copy-done.9, bf16[384,256]{1,0:T(8,128)(2,1)S(1)} %copy-done.1, bf16[384,256]{1,0:T(8,128)(2,1)S(1)} %collective-permute-done.refs_1_, ...), custom_call_target="tpu_custom_call" | custom-call | flops 2560000000 | bytes 3000000 | tf_op jit(solution)/shard_map/pallas_call | solution.py:300
  40.8 0.0 collective-permute-done.12
  40.8 2.2 %collective-permute-done.11 = bf16[64,128]{1,0:T(8,128)(2,1)S(1)} collective-permute-done((bf16[64,128]{1,0:T(8,128)(2,1)S(1)}, bf16[64,128]{1,0:T(8,128)(2,1)S(1)}, u32[]{:S(2)}, u32[]{:S(2)}) %collective-permute-start.11) | collective-permute-done | bytes 16416 | tf_op jit(solution)/shard_map/ppermute | solution.py:538
  43.0 0.0 collective-permute-done.10
  43.1 0.1 collective-permute-start.13
  43.1 1.2 %collective-permute-done.13.other_ref = f32[64,128]{1,0:T(8,128)S(1)} collective-permute-done((f32[64,128]{1,0:T(8,128)S(1)}, f32[64,128]{1,0:T(8,128)S(1)}, u32[]{:S(2)}, u32[]{:S(2)}) %collective-permute-start.13) | collective-permute-done | bytes 32800 | tf_op jit(solution)/shard_map/ppermute | solution.py:538
  44.3 0.0 copy-done
  44.3 5.0 %shard_map.102 = (bf16[2,11,128,512]{3,2,1,0:T(8,128)(2,1)}, f32[11,11,2,16]{3,2,1,0:T(2,128)}) custom-call(f32[64,128]{1,0:T(8,128)S(1)} %add_add_fusion.half_ref, f32[64,128]{1,0:T(8,128)S(1)} %collective-permute-done.13.other_ref, bf16[2,128,256]{2,1,0:T(8,128)(2,1)S(1)} %copy-done, f32[22,128,256]{2,1,0:T(8,128)S(1)} %shard_map.98.refs_5_.refs_0_, ...), custom_call_target="tpu_custom_call" | custom-call | tf_op jit(solution)/shard_map/pallas_call | solution.py:512
  (3 shorter events, 0.0 us)
Async XLA Ops:
  3.0 8.8 %collective-permute-start.3 = (bf16[384,256]{1,0:T(8,128)(2,1)}, bf16[384,256]{1,0:T(8,128)(2,1)S(1)}, u32[]{:S(2)}, u32[]{:S(2)}) collective-permute-start(bf16[384,256]{1,0:T(8,128)(2,1)} %get-tuple-element.23), channel_id=1, source_target_pairs={{0,24},{8,16},{16,8},{24,0},{1,25},{9,17},{17,9},{25,1},{2,26},{10... | collective-permute-start | bytes 589832 | tf_op jit(solution)/shard_map/ppermute | solution.py:538
  5.4 10.7 %collective-permute-start.4 = (bf16[384,256]{1,0:T(8,128)(2,1)}, bf16[384,256]{1,0:T(8,128)(2,1)S(1)}, u32[]{:S(2)}, u32[]{:S(2)}) collective-permute-start(bf16[384,256]{1,0:T(8,128)(2,1)} %get-tuple-element.24), channel_id=1, source_target_pairs={{0,16},{8,24},{16,0},{24,8},{1,17},{9,25},{17,1},{25,9},{2,18},{10... | collective-permute-start | bytes 589832 | tf_op jit(solution)/shard_map/ppermute | solution.py:538
  9.1 14.6 %collective-permute-start = (bf16[384,256]{1,0:T(8,128)(2,1)}, bf16[384,256]{1,0:T(8,128)(2,1)S(1)}, u32[]{:S(2)}, u32[]{:S(2)}) collective-permute-start(bf16[384,256]{1,0:T(8,128)(2,1)} %get-tuple-element.19), channel_id=1, source_target_pairs={{0,24},{8,16},{16,8},{24,0},{1,25},{9,17},{17,9},{25,1},{2,26},{10... | collective-permute-start | bytes 589832 | tf_op jit(solution)/shard_map/ppermute | solution.py:538
  10.6 13.1 %collective-permute-start.1 = (bf16[384,256]{1,0:T(8,128)(2,1)}, bf16[384,256]{1,0:T(8,128)(2,1)S(1)}, u32[]{:S(2)}, u32[]{:S(2)}) collective-permute-start(bf16[384,256]{1,0:T(8,128)(2,1)} %get-tuple-element.20), channel_id=1, source_target_pairs={{0,16},{8,24},{16,0},{24,8},{1,17},{9,25},{17,1},{25,9},{2,18},{10... | collective-permute-start | bytes 589832 | tf_op jit(solution)/shard_map/ppermute | solution.py:538
  10.9 5.3 %collective-permute-start.5 = (bf16[384,256]{1,0:T(8,128)(2,1)}, bf16[384,256]{1,0:T(8,128)(2,1)S(1)}, u32[]{:S(2)}, u32[]{:S(2)}) collective-permute-start(bf16[384,256]{1,0:T(8,128)(2,1)} %get-tuple-element.25), channel_id=1, source_target_pairs={{0,8},{8,0},{16,24},{24,16},{1,9},{9,1},{17,25},{25,17},{2,10},{10... | collective-permute-start | bytes 589832 | tf_op jit(solution)/shard_map/ppermute | solution.py:538
  11.8 12.0 %collective-permute-start.2 = (bf16[384,256]{1,0:T(8,128)(2,1)}, bf16[384,256]{1,0:T(8,128)(2,1)S(1)}, u32[]{:S(2)}, u32[]{:S(2)}) collective-permute-start(bf16[384,256]{1,0:T(8,128)(2,1)} %get-tuple-element.21), channel_id=1, source_target_pairs={{0,8},{8,0},{16,24},{24,16},{1,9},{9,1},{17,25},{25,17},{2,10},{10... | collective-permute-start | bytes 589832 | tf_op jit(solution)/shard_map/ppermute | solution.py:538
  16.2 0.9 %copy-start.2 = (bf16[384,256]{1,0:T(8,128)(2,1)S(1)}, bf16[384,256]{1,0:T(8,128)(2,1)}, u32[]{:S(2)}) copy-start(bf16[384,256]{1,0:T(8,128)(2,1)} %get-tuple-element.22.refs_0_) | copy-start | bytes 589828
  17.1 0.7 %copy-start.3 = (s32[4]{0:T(128)S(1)}, s32[4]{0:T(128)}, u32[]{:S(2)}) copy-start(s32[4]{0:T(128)} %order_ref.7) | copy-start | bytes 52
  17.7 0.7 %copy-start.5 = (s32[11]{0:T(128)S(1)}, s32[11]{0:T(128)}, u32[]{:S(2)}) copy-start(s32[11]{0:T(128)} %offsets_ref.7) | copy-start | bytes 136
  18.4 0.9 %copy-start.8 = (bf16[512,256]{1,0:T(8,128)(2,1)S(1)}, bf16[512,256]{1,0:T(8,128)(2,1)}, u32[]{:S(2)}) copy-start(bf16[512,256]{1,0:T(8,128)(2,1)} %constant.6.clone.f_ref) | copy-start | bytes 786436
  19.3 1.6 %copy-start.7 = (bf16[2816,128]{1,0:T(8,128)(2,1)S(1)}, bf16[2816,128]{1,0:T(8,128)(2,1)}, u32[]{:S(2)}) copy-start(bf16[2816,128]{1,0:T(8,128)(2,1)} %constant.7.clone.pick_ref) | copy-start | bytes 2162692
  21.0 2.8 %copy-start.1 = (bf16[384,256]{1,0:T(8,128)(2,1)S(1)}, bf16[384,256]{1,0:T(8,128)(2,1)}, u32[]{:S(2)}) copy-start(bf16[384,256]{1,0:T(8,128)(2,1)} %get-tuple-element.18.refs_0_) | copy-start | bytes 589828
  25.8 13.4 %copy-start.4 = (s32[4]{0:T(128)S(1)}, s32[4]{0:T(128)}, u32[]{:S(2)}) copy-start(s32[4]{0:T(128)} %order_ref.7) | copy-start | bytes 52
  25.9 13.3 %copy-start.6 = (s32[11]{0:T(128)S(1)}, s32[11]{0:T(128)}, u32[]{:S(2)}) copy-start(s32[11]{0:T(128)} %offsets_ref.7) | copy-start | bytes 136
  25.9 13.3 %copy-start.9 = (bf16[512,256]{1,0:T(8,128)(2,1)S(1)}, bf16[512,256]{1,0:T(8,128)(2,1)}, u32[]{:S(2)}) copy-start(bf16[512,256]{1,0:T(8,128)(2,1)} %constant.6.clone.f_ref) | copy-start | bytes 786436
  25.9 1.2 %collective-permute-start.6 = (bf16[64,128]{1,0:T(8,128)(2,1)S(1)}, bf16[64,128]{1,0:T(8,128)(2,1)S(1)}, u32[]{:S(2)}, u32[]{:S(2)}) collective-permute-start(bf16[64,128]{1,0:T(8,128)(2,1)S(1)} %get-tuple-element.27), channel_id=1, source_target_pairs={{0,8},{1,9},{2,10},{3,11},{4,12},{5,13},{6,14},{7,15},{8,0},{9,1},... | collective-permute-start | bytes 49160 | tf_op jit(solution)/shard_map/ppermute | solution.py:538
  27.1 5.0 %collective-permute-start.9 = (bf16[64,128]{1,0:T(8,128)(2,1)S(1)}, bf16[64,128]{1,0:T(8,128)(2,1)S(1)}, u32[]{:S(2)}, u32[]{:S(2)}) collective-permute-start(bf16[64,128]{1,0:T(8,128)(2,1)S(1)} %add_convert_fusion.1), channel_id=1, source_target_pairs={{0,17},{1,16},{2,19},{3,18},{4,21},{5,20},{6,23},{7,22},{8,25},{9,... | collective-permute-start | bytes 49160 | tf_op jit(solution)/shard_map/ppermute | solution.py:538
  30.4 3.7 %collective-permute-start.8 = (bf16[64,128]{1,0:T(8,128)(2,1)S(1)}, bf16[64,128]{1,0:T(8,128)(2,1)S(1)}, u32[]{:S(2)}, u32[]{:S(2)}) collective-permute-start(bf16[64,128]{1,0:T(8,128)(2,1)S(1)} %add_convert_fusion.1), channel_id=1, source_target_pairs={{0,1},{1,0},{2,3},{3,2},{4,5},{5,4},{6,7},{7,6},{8,9},{9,8},{10,11... | collective-permute-start | bytes 49160 | tf_op jit(solution)/shard_map/ppermute | solution.py:538
  31.0 3.7 %collective-permute-start.7 = (bf16[64,128]{1,0:T(8,128)(2,1)S(1)}, bf16[64,128]{1,0:T(8,128)(2,1)S(1)}, u32[]{:S(2)}, u32[]{:S(2)}) collective-permute-start(bf16[64,128]{1,0:T(8,128)(2,1)S(1)} %add_convert_fusion.1), channel_id=1, source_target_pairs={{0,16},{1,17},{2,18},{3,19},{4,20},{5,21},{6,22},{7,23},{8,24},{9,... | collective-permute-start | bytes 49160 | tf_op jit(solution)/shard_map/ppermute | solution.py:538
  34.7 9.6 %copy-start = (bf16[2,128,256]{2,1,0:T(8,128)(2,1)S(1)}, bf16[2,128,256]{2,1,0:T(8,128)(2,1)}, u32[]{:S(2)}) copy-start(bf16[2,128,256]{2,1,0:T(8,128)(2,1)} %constant.8.clone.spread_ref) | copy-start | bytes 393220
  34.7 6.1 %collective-permute-start.12 = (bf16[64,128]{1,0:T(8,128)(2,1)S(1)}, bf16[64,128]{1,0:T(8,128)(2,1)S(1)}, u32[]{:S(2)}, u32[]{:S(2)}) collective-permute-start(bf16[64,128]{1,0:T(8,128)(2,1)S(1)} %add_convert_fusion), channel_id=1, source_target_pairs={{0,6},{1,7},{2,4},{3,5},{4,2},{5,3},{6,0},{7,1},{8,14},{9,15},{10,... | collective-permute-start | bytes 49160 | tf_op jit(solution)/shard_map/ppermute | solution.py:538
  38.4 4.6 %collective-permute-start.11 = (bf16[64,128]{1,0:T(8,128)(2,1)S(1)}, bf16[64,128]{1,0:T(8,128)(2,1)S(1)}, u32[]{:S(2)}, u32[]{:S(2)}) collective-permute-start(bf16[64,128]{1,0:T(8,128)(2,1)S(1)} %add_convert_fusion), channel_id=1, source_target_pairs={{0,4},{1,5},{2,6},{3,7},{4,0},{5,1},{6,2},{7,3},{8,12},{9,13},{10,... | collective-permute-start | bytes 49160 | tf_op jit(solution)/shard_map/ppermute | solution.py:538
  38.4 4.6 %collective-permute-start.10 = (bf16[64,128]{1,0:T(8,128)(2,1)S(1)}, bf16[64,128]{1,0:T(8,128)(2,1)S(1)}, u32[]{:S(2)}, u32[]{:S(2)}) collective-permute-start(bf16[64,128]{1,0:T(8,128)(2,1)S(1)} %add_convert_fusion), channel_id=1, source_target_pairs={{0,2},{1,3},{2,0},{3,1},{4,6},{5,7},{6,4},{7,5},{8,10},{9,11},{10,... | collective-permute-start | bytes 49160 | tf_op jit(solution)/shard_map/ppermute | solution.py:538
  43.1 1.3 %collective-permute-start.13 = (f32[64,128]{1,0:T(8,128)S(1)}, f32[64,128]{1,0:T(8,128)S(1)}, u32[]{:S(2)}, u32[]{:S(2)}) collective-permute-start(f32[64,128]{1,0:T(8,128)S(1)} %add_add_fusion.half_ref), channel_id=1, source_target_pairs={{0,8},{1,9},{2,10},{3,11},{4,12},{5,13},{6,14},{7,15},{8,0},{9,1},... | collective-permute-start | bytes 98312 | tf_op jit(solution)/shard_map/ppermute | solution.py:538

commit v10 on v9

--- a/solution.py
+++ b/solution.py
@@ -14,6 +14,7 @@
 NBLK = 11
 LANE = 128
 SUB = 8
+TILE = 16
 HALF_ROWS = NBLK * SUB
 GROUPS = NFREQ // SUB
 MATS = 7
@@ -36,7 +37,11 @@
     table = np.concatenate([np.cos(angles) * scaled, -np.sin(angles) * scaled], axis=0)
     high = table.astype(jnp.bfloat16)
     low = (table - high.astype(np.float64)).astype(jnp.bfloat16)
-    return np.concatenate([high, low], axis=0)
+    both = np.concatenate([high, low], axis=0)
+    shifted = np.zeros((TILE, 2 * NFFT, NFFT + TILE), jnp.bfloat16)
+    for shift in range(TILE):
+        shifted[shift, :, shift : shift + NFFT] = both
+    return shifted
 
 
 def packed_rows():
@@ -169,31 +174,26 @@
     )(table, snapshots)
 
 
-def fill_record(order_ref, pieces, record, factor):
+def fill_record(order_ref, pieces, record):
     steps, width = pieces[0].shape
     me = lax.axis_index("tm")
     for d, piece in enumerate(pieces):
         partner = me ^ (len(pieces) - d if d else 0)
         start = pl.multiple_of(order_ref[partner] * steps, steps)
-        for c in range(width // LANE):
-            cols = slice(c * LANE, (c + 1) * LANE)
-            part = piece[:, cols].astype(F32)
-            record[c, pl.ds(start, steps), :] = part if factor is None else part * factor[:, cols]
-
-
-def transform(offsets_ref, f, record, s_ref):
-    wanted = [(i, c) for i in range(NBLK) for c in range(record.shape[0])]
-    for first in range(0, len(wanted), 2):
-        pair = wanted[first : first + 2]
-        x = [record[c, pl.ds(offsets_ref[i], NFFT), :].astype(BF16) for i, c in pair]
-        x = jnp.concatenate(x, axis=1) if len(x) > 1 else x[0]
-        y = dot(f, x)
-        if f.shape[0] > NFFT:
+        record[pl.ds(start, steps), :] = piece[...]
+    record[len(pieces) * steps :, :] = jnp.zeros((TILE, width), BF16)
+
+
+def transform(offsets_ref, f_ref, parts, record, s_ref):
+    for i in range(NBLK):
+        shift = offsets_ref[i] % TILE
+        start = pl.multiple_of(offsets_ref[i] - shift, TILE)
+        x = record[pl.ds(start, NFFT + TILE), :]
+        y = dot(f_ref[shift, : parts * NFFT, :], x)
+        if parts == 2:
             y = y[:NFFT] + y[NFFT:]
-        for at, (i, c) in enumerate(pair):
-            cols = slice(c * LANE, (c + 1) * LANE)
-            s_ref[i, :, cols] = y[:NFREQ, at * LANE : (at + 1) * LANE]
-            s_ref[NBLK + i, :, cols] = y[NFREQ:, at * LANE : (at + 1) * LANE]
+        s_ref[i] = y[:NFREQ]
+        s_ref[NBLK + i] = y[NFREQ:]
 
 
 def padded(s):
@@ -204,7 +204,7 @@
     return jnp.concatenate([real, pad, imag, pad], axis=0)
 
 
-def gram_rows(base, groups, s_ref, pick_ref, masked):
+def gram_rows(base, groups, w, s_ref, pick_ref, masked):
     row = lax.broadcasted_iota(jnp.int32, (HALF_ROWS, LANE), 0)
     col = lax.broadcasted_iota(jnp.int32, (HALF_ROWS, LANE), 1)
     same = row % SUB == col % SUB
@@ -212,7 +212,8 @@
         blocks = []
         for g in (pair, pair + 1):
             s = s_ref[:, pl.ds(pl.multiple_of(base + g * SUB, SUB), SUB), :]
-            full = dot_nt(s.reshape(2 * HALF_ROWS, -1).astype(BF16), padded(s).astype(BF16))
+            weighted = s.reshape(2 * HALF_ROWS, -1) * w
+            full = dot_nt(weighted.astype(BF16), padded(s).astype(BF16))
             real = full[:HALF_ROWS, :LANE] + full[HALF_ROWS:, LANE:]
             imag = full[:HALF_ROWS, LANE:] - full[HALF_ROWS:, :LANE]
             blocks.append([jnp.where(same, part, 0.0) for part in (real, imag)])
@@ -232,13 +233,14 @@
         gram_ref, record, s_ref, masked = refs[lanes:]
     else:
         before_ref, _, gram_ref, s_ref, record, masked = refs[lanes:]
-    fill_record(order_ref, pieces, record, jnp.sqrt(w_ref[...]))
-    transform(offsets_ref, f_ref[:NFFT] if last else f_ref[...], record, s_ref)
+    fill_record(order_ref, pieces, record)
+    transform(offsets_ref, f_ref, 1 if last else 2, record, s_ref)
+    w = w_ref[...]
     if not last:
-        gram_ref[...] = gram_rows(0, GROUPS, s_ref, pick_ref, masked) * scale
+        gram_ref[...] = gram_rows(0, GROUPS, w, s_ref, pick_ref, masked) * scale
         return
     base = pl.multiple_of((1 - lax.axis_index("tm") % 2) * HALF, HALF)
-    total = gram_rows(base, GROUPS // 2, s_ref, pick_ref, masked) * scale
+    total = gram_rows(base, GROUPS // 2, w, s_ref, pick_ref, masked) * scale
     gram_ref[...] = (total + before_ref[pl.ds(base, HALF), :]).astype(BF16)
 
 
@@ -248,7 +250,7 @@
     last = bool(before)
     args = [order, offsets, weights, *tables, *pieces, *before]
     spectrum_shape = (2 * NBLK, NFREQ, width)
-    scratch = [pltpu.VMEM((width // LANE, lanes * steps, LANE), F32)]
+    scratch = [pltpu.VMEM((lanes * steps + TILE, width), BF16)]
     if last:
         outs = [jax.ShapeDtypeStruct((HALF, PACKED), BF16)]
         outs.append(jax.ShapeDtypeStruct(spectrum_shape, F32))
@@ -269,28 +271,29 @@
     )(*args)
 
 
-def own_kernel(scale, s_ref, pick_ref, before_ref, gram_ref, masked):
+def own_kernel(scale, w_ref, s_ref, pick_ref, before_ref, gram_ref, masked):
     base = pl.multiple_of(lax.axis_index("tm") % 2 * HALF, HALF)
-    total = gram_rows(base, GROUPS // 2, s_ref, pick_ref, masked) * scale
+    w = w_ref[...]
+    total = gram_rows(base, GROUPS // 2, w, s_ref, pick_ref, masked) * scale
     gram_ref[...] = (total + before_ref[pl.ds(base, HALF), :]).astype(BF16)
 
 
-def own_part(scaled, pick, before, scale):
+def own_part(weights, rough, pick, before, scale):
     return pl.pallas_call(
         functools.partial(own_kernel, scale),
         out_shape=jax.ShapeDtypeStruct((HALF, PACKED), BF16),
-        in_specs=[VMEM] * 3,
+        in_specs=[VMEM] * 4,
         out_specs=VMEM,
         scratch_shapes=[pltpu.VMEM((HALF, NBLK * WIDE), BF16)],
         compiler_params=pltpu.CompilerParams(vmem_limit_bytes=32 * 2**20),
         cost_estimate=pl.CostEstimate(flops=10**9, bytes_accessed=3 * 10**6, transcendentals=0),
-    )(scaled, pick, before)
+    )(weights, rough, pick, before)
 
 
 def spectrum_kernel(lanes, order_ref, offsets_ref, f_ref, *refs):
     s_ref, record = refs[-2:]
-    fill_record(order_ref, refs[:lanes], record, None)
-    transform(offsets_ref, f_ref[...], record, s_ref)
+    fill_record(order_ref, refs[:lanes], record)
+    transform(offsets_ref, f_ref, 2, record, s_ref)
 
 
 def spectrum(order, offsets, fourier, pieces, after):
@@ -302,7 +305,7 @@
         out_shape=jax.ShapeDtypeStruct((2 * NBLK, NFREQ, width), F32),
         in_specs=[SMEM, SMEM] + [VMEM] * (len(args) - 2),
         out_specs=VMEM,
-        scratch_shapes=[pltpu.VMEM((width // LANE, lanes * steps, LANE), F32)],
+        scratch_shapes=[pltpu.VMEM((lanes * steps + TILE, width), BF16)],
         compiler_params=pltpu.CompilerParams(vmem_limit_bytes=32 * 2**20),
         cost_estimate=pl.CostEstimate(
             flops=width * 10**7, bytes_accessed=3 * 10**6, transcendentals=0
@@ -567,12 +570,12 @@
     parts = [weights[:, base : base + width] for base, width in chunks]
     (before,) = gram_part(block_order, offsets, parts[0], tables, arrived[0], [], scale)
     spectra = [spectrum(block_order, offsets, tables[0], arrived[0], [])]
-    send, scaled = gram_part(
+    send, rough = gram_part(
         block_order, offsets, parts[1], tables, arrived[1], [before, spectra[0]], scale
     )
 
     other = swap(send, axes, bits[0], size)
-    keep = own_part(scaled, tables[1], before, scale)
+    keep = own_part(parts[1], rough, tables[1], before, scale)
     spectra.append(spectrum(block_order, offsets, tables[0], arrived[1], [keep]))
     half = keep.astype(F32) + other.astype(F32)
     for at in range(1, len(bits), 2):

time: 49.6 us -> 52.9 us (1.067)
  local copies, waits for them, and re-layouts: 3.92 us -> 6.38 us
  Pallas kernels: 19.1 us -> 21.4 us
  waiting for transfers between devices: 11.6 us -> 10.5 us
    unnamed x20 -> x16, local copies, waits for them, and re-layouts: 3.22 us -> 5.69 us
    pallas_call x2, Pallas kernels: 3.23 us -> 4.53 us  [spectrum(): pl.pallas_call(functools.partial(spectrum_kernel, lanes), out_shape=jax.S...]
    ppermute x14, waiting for transfers between devices: 11.6 us -> 10.5 us  [swap(): return lax.ppermute(x, axes, [(i, i ^ mask) for i in range(size)])]
    pallas_call x2, Pallas kernels: 4.79 us -> 5.79 us  [gram_part(): pl.pallas_call(functools.partial(gram_kernel, lanes, scale, last), out_sh...]
  transfers between devices with their start and end apart: 14 -> 14, of which waited for: 7 -> 7; matrix products, arithmetic and copies ran while one was open for 1% -> 1% of each run, Pallas kernels for 20% -> 22%
where the time goes in v10:
time: 52.9 us; the launch traced here: 52.6 us
  Pallas kernels  21.4 us (40%)
  starting transfers between devices  13.5 us (26%)
  waiting for transfers between devices  10.5 us (20%)
  local copies, waits for them, and re-layouts  6.38 us (12%)
  between operations  0.76 us (1%)
    ppermute x14, starting transfers between devices, swap(): return lax.ppermute(x, axes, [(i, i ^ mask) for i in range(size)])  13.5 us
    ppermute x14, waiting for transfers between devices, swap(): return lax.ppermute(x, axes, [(i, i ^ mask) for i in range(size)])  10.5 us
    pallas_call x2, Pallas kernels, gram_part(): pl.pallas_call(functools.partial(gram_kernel, lanes, scale, last), out_sh...  5.79 us
    unnamed x16, local copies, waits for them, and re-layouts  5.69 us
    pallas_call x2, Pallas kernels, pack(): pl.pallas_call(functools.partial(pack_kernel, jobs, parts, first), out_sh...  5.36 us
    pallas_call x1, Pallas kernels, mode_fields(): pl.pallas_call(functools.partial(mode_kernel, len(spectra), share), out_s...  5.04 us
    pallas_call x2, Pallas kernels, spectrum(): pl.pallas_call(functools.partial(spectrum_kernel, lanes), out_shape=jax.S...  4.53 us
  transfers between devices with their start and end apart: 14, of which 7 were waited for; matrix products, arithmetic and copies ran while one was open for 1% of the time, Pallas kernels for 22%

profile of v10, /device:TPU:0, one launch (start us, length us, event | category | flops | bytes accessed | tf_op | source)
XLA Modules:
  0.0 52.6 jit_solution(16644682371659340600)
XLA Ops:
  0.6 2.3 %shard_map.95 = (bf16[384,256]{1,0:T(8,128)(2,1)}, bf16[384,256]{1,0:T(8,128)(2,1)}, bf16[256,256]{1,0:T(8,128)(2,1)}) custom-call(s32[1,4]{1,0:T(1,128)} %table_hbm.1, bf16[384,4,512]{2,1,0:T(4,128)(2,1)} %x_hbm.3), custom_call_target="tpu_custom_call" | custom-call | flops 201326592 | bytes 1572864 | tf_op jit(solution)/shard_map/pallas_call | solution.py:155
  3.0 2.5 %collective-permute-start.3 = (bf16[384,256]{1,0:T(8,128)(2,1)}, bf16[384,256]{1,0:T(8,128)(2,1)S(1)}, u32[]{:S(2)}, u32[]{:S(2)}) collective-permute-start(bf16[384,256]{1,0:T(8,128)(2,1)} %get-tuple-element.23), channel_id=1, source_target_pairs={{0,24},{8,16},{16,8},{24,0},{1,25},{9,17},{17,9},{25,1},{2,26},{10... | collective-permute-start | bytes 589832 | tf_op jit(solution)/shard_map/ppermute | solution.py:541
  5.4 0.6 %collective-permute-start.4 = (bf16[384,256]{1,0:T(8,128)(2,1)}, bf16[384,256]{1,0:T(8,128)(2,1)S(1)}, u32[]{:S(2)}, u32[]{:S(2)}) collective-permute-start(bf16[384,256]{1,0:T(8,128)(2,1)} %get-tuple-element.24), channel_id=1, source_target_pairs={{0,16},{8,24},{16,0},{24,8},{1,17},{9,25},{17,1},{25,9},{2,18},{10... | collective-permute-start | bytes 589832 | tf_op jit(solution)/shard_map/ppermute | solution.py:541
  6.1 3.0 %shard_map.96 = (bf16[384,256]{1,0:T(8,128)(2,1)}, bf16[384,256]{1,0:T(8,128)(2,1)}, bf16[384,256]{1,0:T(8,128)(2,1)}, bf16[384,256]{1,0:T(8,128)(2,1)}, bf16[38...) custom-call(bf16[256,256]{1,0:T(8,128)(2,1)} %get-tuple-element.17.table_hbm, bf16[384,4,512]{2,1,0:T(4,128)(2,1)} %x_hbm.3), custom_call_target="tpu_custom_call" | custom-call | flops 402653184 | bytes 3145728 | tf_op jit(solution)/shard_map/pallas_call | solution.py:155
  9.1 1.5 %collective-permute-start = (bf16[384,256]{1,0:T(8,128)(2,1)}, bf16[384,256]{1,0:T(8,128)(2,1)S(1)}, u32[]{:S(2)}, u32[]{:S(2)}) collective-permute-start(bf16[384,256]{1,0:T(8,128)(2,1)} %get-tuple-element.19), channel_id=1, source_target_pairs={{0,24},{8,16},{16,8},{24,0},{1,25},{9,17},{17,9},{25,1},{2,26},{10... | collective-permute-start | bytes 589832 | tf_op jit(solution)/shard_map/ppermute | solution.py:541
  10.6 0.3 collective-permute-start.1
  10.9 0.2 collective-permute-start.5
  11.0 0.7 %fusion = (f32[1,256]{1,0:T(1,128)S(1)}, f32[1,256]{1,0:T(1,128)S(1)}) fusion(f32[1,512]{1,0:T(1,128)} %bitcast.7), kind=kLoop, calls=%fused_computation.3 | loop fusion | bytes 4096 | tf_op jit(solution)/shard_map/slice | solution.py:570
  11.7 0.0 collective-permute-done.3.refs_1_
  11.7 0.3 collective-permute-start.2
  12.1 4.1 %collective-permute-done.4.refs_2_ = bf16[384,256]{1,0:T(8,128)(2,1)S(1)} collective-permute-done((bf16[384,256]{1,0:T(8,128)(2,1)}, bf16[384,256]{1,0:T(8,128)(2,1)S(1)}, u32[]{:S(2)}, u32[]{:S(2)}) %collective-permute-start.4) | collective-permute-done | bytes 196640 | tf_op jit(solution)/shard_map/ppermute | solution.py:541
  16.1 0.0 collective-permute-done.5.refs_3_
  16.2 0.0 copy-start
  16.2 2.8 %copy-done = bf16[16,512,272]{2,1,0:T(8,128)(2,1)S(1)} copy-done((bf16[16,512,272]{2,1,0:T(8,128)(2,1)S(1)}, bf16[16,512,272]{2,1,0:T(8,128)(2,1)}, u32[]{:S(2)}) %copy-start) | copy-done | bytes 4456472
  18.9 0.0 copy-start.4
  18.9 0.9 %copy-done.4 = bf16[384,256]{1,0:T(8,128)(2,1)S(1)} copy-done((bf16[384,256]{1,0:T(8,128)(2,1)S(1)}, bf16[384,256]{1,0:T(8,128)(2,1)}, u32[]{:S(2)}) %copy-start.4) | copy-done | bytes 196632
  19.9 0.0 copy-start.6
  19.9 0.7 %copy-done.6 = s32[4]{0:T(128)S(1)} copy-done((s32[4]{0:T(128)S(1)}, s32[4]{0:T(128)}, u32[]{:S(2)}) %copy-start.6) | copy-done | bytes 40
  20.5 0.0 copy-start.7
  20.5 0.7 %copy-done.7 = s32[11]{0:T(128)S(1)} copy-done((s32[11]{0:T(128)S(1)}, s32[11]{0:T(128)}, u32[]{:S(2)}) %copy-start.7) | copy-done | bytes 68
  21.2 0.0 copy-start.1
  21.2 0.0 copy-start.3
  21.2 2.3 %shard_map.98.refs_5_.refs_0_ = f32[22,128,256]{2,1,0:T(8,128)S(1)} custom-call(s32[4]{0:T(128)S(1)} %copy-done.6, s32[11]{0:T(128)S(1)} %copy-done.7, bf16[16,512,272]{2,1,0:T(8,128)(2,1)S(1)} %copy-done, bf16[384,256]{1,0:T(8,128)(2,1)S(1)} %copy-done.4, bf16[384,256]{1,0:T(8,128)(2,1)S(1)} %collective-permute-done.3.refs_1_, ...), custom_call_target="tpu_custom_call" | custom-call | flops 2560000000 | bytes 3000000 | tf_op jit(solution)/shard_map/pallas_call | solution.py:303
  23.4 0.5 copy-done.1
  24.0 0.1 copy-done.3
  24.1 0.0 copy-start.2
  24.1 3.4 %shard_map.97.refs_4_.before_ref = f32[128,128]{1,0:T(8,128)S(1)} custom-call(s32[4]{0:T(128)S(1)} %copy-done.6, s32[11]{0:T(128)S(1)} %copy-done.7, f32[1,256]{1,0:T(1,128)S(1)} %get-tuple-element.34.w_ref, bf16[16,512,272]{2,1,0:T(8,128)(2,1)S(1)} %copy-done.1, bf16[2816,128]{1,0:T(8,128)(2,1)S(1)} %copy-done.3, bf16[384,256]{1,0:T(8,128)(2,1)S(1)} %copy-done.4, ...), custom_call_target="tpu_custom_call" | custom-call | flops 2560000000 | bytes 3000000 | tf_op jit(solution)/shard_map/pallas_call | solution.py:261
  27.5 0.0 collective-permute-done.refs_1_
  27.5 0.0 collective-permute-done.1.refs_2_
  27.6 0.0 collective-permute-done.2.refs_3_
  27.6 0.0 copy-done.2
  27.6 2.4 %shard_map.99 = (bf16[64,128]{1,0:T(8,128)(2,1)S(1)}, f32[22,128,256]{2,1,0:T(8,128)S(1)}) custom-call(s32[4]{0:T(128)S(1)} %copy-done.6, s32[11]{0:T(128)S(1)} %copy-done.7, f32[1,256]{1,0:T(1,128)S(1)} %get-tuple-element.35.w_ref, bf16[16,512,272]{2,1,0:T(8,128)(2,1)S(1)} %copy-done.1, bf16[2816,128]{1,0:T(8,128)(2,1)S(1)} %copy-done.3, ...), custom_call_target="tpu_custom_call" | custom-call | flops 2560000000 | bytes 3000000 | tf_op jit(solution)/shard_map/pallas_call | solution.py:261
  29.9 0.1 collective-permute-start.6
  30.0 0.7 %shard_map.100.refs_4_ = bf16[64,128]{1,0:T(8,128)(2,1)S(1)} custom-call(f32[1,256]{1,0:T(1,128)S(1)} %get-tuple-element.35.w_ref, f32[22,128,256]{2,1,0:T(8,128)S(1)} %get-tuple-element.26.s_ref, bf16[2816,128]{1,0:T(8,128)(2,1)S(1)} %copy-done.3, f32[128,128]{1,0:T(8,128)S(1)} %shard_map.97.refs_4_.before_ref), custom_call_target="tpu_custom_call" | custom-call | flops 1000000000 | bytes 3000000 | tf_op jit(solution)/shard_map/pallas_call | solution.py:282
  30.7 0.5 collective-permute-done.6
  31.2 2.5 %collective-permute-start.9 = (bf16[64,128]{1,0:T(8,128)(2,1)S(1)}, bf16[64,128]{1,0:T(8,128)(2,1)S(1)}, u32[]{:S(2)}, u32[]{:S(2)}) collective-permute-start(bf16[64,128]{1,0:T(8,128)(2,1)S(1)} %add_convert_fusion.1), channel_id=1, source_target_pairs={{0,17},{1,16},{2,19},{3,18},{4,21},{5,20},{6,23},{7,22},{8,25},{9,... | collective-permute-start | bytes 49160 | tf_op jit(solution)/shard_map/ppermute | solution.py:541
  33.7 0.5 %collective-permute-start.8 = (bf16[64,128]{1,0:T(8,128)(2,1)S(1)}, bf16[64,128]{1,0:T(8,128)(2,1)S(1)}, u32[]{:S(2)}, u32[]{:S(2)}) collective-permute-start(bf16[64,128]{1,0:T(8,128)(2,1)S(1)} %add_convert_fusion.1), channel_id=1, source_target_pairs={{0,1},{1,0},{2,3},{3,2},{4,5},{5,4},{6,7},{7,6},{8,9},{9,8},{10,11... | collective-permute-start | bytes 49160 | tf_op jit(solution)/shard_map/ppermute | solution.py:541
  34.2 0.6 %collective-permute-start.7 = (bf16[64,128]{1,0:T(8,128)(2,1)S(1)}, bf16[64,128]{1,0:T(8,128)(2,1)S(1)}, u32[]{:S(2)}, u32[]{:S(2)}) collective-permute-start(bf16[64,128]{1,0:T(8,128)(2,1)S(1)} %add_convert_fusion.1), channel_id=1, source_target_pairs={{0,16},{1,17},{2,18},{3,19},{4,20},{5,21},{6,22},{7,23},{8,24},{9,... | collective-permute-start | bytes 49160 | tf_op jit(solution)/shard_map/ppermute | solution.py:541
  34.8 1.1 %collective-permute-done.9 = bf16[64,128]{1,0:T(8,128)(2,1)S(1)} collective-permute-done((bf16[64,128]{1,0:T(8,128)(2,1)S(1)}, bf16[64,128]{1,0:T(8,128)(2,1)S(1)}, u32[]{:S(2)}, u32[]{:S(2)}) %collective-permute-start.9) | collective-permute-done | bytes 16416 | tf_op jit(solution)/shard_map/ppermute | solution.py:541
  35.9 1.5 %collective-permute-done.8 = bf16[64,128]{1,0:T(8,128)(2,1)S(1)} collective-permute-done((bf16[64,128]{1,0:T(8,128)(2,1)S(1)}, bf16[64,128]{1,0:T(8,128)(2,1)S(1)}, u32[]{:S(2)}, u32[]{:S(2)}) %collective-permute-start.8) | collective-permute-done | bytes 16416 | tf_op jit(solution)/shard_map/ppermute | solution.py:541
  37.4 0.5 %collective-permute-done.7 = bf16[64,128]{1,0:T(8,128)(2,1)S(1)} collective-permute-done((bf16[64,128]{1,0:T(8,128)(2,1)S(1)}, bf16[64,128]{1,0:T(8,128)(2,1)S(1)}, u32[]{:S(2)}, u32[]{:S(2)}) %collective-permute-start.7) | collective-permute-done | bytes 16416 | tf_op jit(solution)/shard_map/ppermute | solution.py:541
  38.0 0.0 copy-start.5
  38.0 3.7 %collective-permute-start.12 = (bf16[64,128]{1,0:T(8,128)(2,1)S(1)}, bf16[64,128]{1,0:T(8,128)(2,1)S(1)}, u32[]{:S(2)}, u32[]{:S(2)}) collective-permute-start(bf16[64,128]{1,0:T(8,128)(2,1)S(1)} %add_convert_fusion), channel_id=1, source_target_pairs={{0,6},{1,7},{2,4},{3,5},{4,2},{5,3},{6,0},{7,1},{8,14},{9,15},{10,... | collective-permute-start | bytes 49160 | tf_op jit(solution)/shard_map/ppermute | solution.py:541
  41.6 0.0 collective-permute-start.11
  41.6 0.8 %collective-permute-start.10 = (bf16[64,128]{1,0:T(8,128)(2,1)S(1)}, bf16[64,128]{1,0:T(8,128)(2,1)S(1)}, u32[]{:S(2)}, u32[]{:S(2)}) collective-permute-start(bf16[64,128]{1,0:T(8,128)(2,1)S(1)} %add_convert_fusion), channel_id=1, source_target_pairs={{0,2},{1,3},{2,0},{3,1},{4,6},{5,7},{6,4},{7,5},{8,10},{9,11},{10,... | collective-permute-start | bytes 49160 | tf_op jit(solution)/shard_map/ppermute | solution.py:541
  42.4 2.3 %shard_map.101.refs_1_ = f32[22,128,256]{2,1,0:T(8,128)S(1)} custom-call(s32[4]{0:T(128)S(1)} %copy-done.6, s32[11]{0:T(128)S(1)} %copy-done.7, bf16[16,512,272]{2,1,0:T(8,128)(2,1)S(1)} %copy-done.1, bf16[384,256]{1,0:T(8,128)(2,1)S(1)} %copy-done.2, bf16[384,256]{1,0:T(8,128)(2,1)S(1)} %collective-permute-done.refs_1_, ...), custom_call_target="tpu_custom_call" | custom-call | flops 2560000000 | bytes 3000000 | tf_op jit(solution)/shard_map/pallas_call | solution.py:303
  44.7 0.0 collective-permute-done.12
  44.7 1.6 %collective-permute-done.11 = bf16[64,128]{1,0:T(8,128)(2,1)S(1)} collective-permute-done((bf16[64,128]{1,0:T(8,128)(2,1)S(1)}, bf16[64,128]{1,0:T(8,128)(2,1)S(1)}, u32[]{:S(2)}, u32[]{:S(2)}) %collective-permute-start.11) | collective-permute-done | bytes 16416 | tf_op jit(solution)/shard_map/ppermute | solution.py:541
  46.3 0.0 collective-permute-done.10
  46.3 0.1 collective-permute-start.13
  46.4 1.2 %collective-permute-done.13.other_ref = f32[64,128]{1,0:T(8,128)S(1)} collective-permute-done((f32[64,128]{1,0:T(8,128)S(1)}, f32[64,128]{1,0:T(8,128)S(1)}, u32[]{:S(2)}, u32[]{:S(2)}) %collective-permute-start.13) | collective-permute-done | bytes 32800 | tf_op jit(solution)/shard_map/ppermute | solution.py:541
  47.6 0.0 copy-done.5
  47.6 5.0 %shard_map.102 = (bf16[2,11,128,512]{3,2,1,0:T(8,128)(2,1)}, f32[11,11,2,16]{3,2,1,0:T(2,128)}) custom-call(f32[64,128]{1,0:T(8,128)S(1)} %add_add_fusion.half_ref, f32[64,128]{1,0:T(8,128)S(1)} %collective-permute-done.13.other_ref, bf16[2,128,256]{2,1,0:T(8,128)(2,1)S(1)} %copy-done.5, f32[22,128,256]{2,1,0:T(8,128)S(1)} %shard_map.98.refs_5_.refs_0_, ...), custom_call_target="tpu_custom_call" | custom-call | tf_op jit(solution)/shard_map/pallas_call | solution.py:515
  (3 shorter events, 0.0 us)
Async XLA Ops:
  3.0 8.8 %collective-permute-start.3 = (bf16[384,256]{1,0:T(8,128)(2,1)}, bf16[384,256]{1,0:T(8,128)(2,1)S(1)}, u32[]{:S(2)}, u32[]{:S(2)}) collective-permute-start(bf16[384,256]{1,0:T(8,128)(2,1)} %get-tuple-element.23), channel_id=1, source_target_pairs={{0,24},{8,16},{16,8},{24,0},{1,25},{9,17},{17,9},{25,1},{2,26},{10... | collective-permute-start | bytes 589832 | tf_op jit(solution)/shard_map/ppermute | solution.py:541
  5.4 10.7 %collective-permute-start.4 = (bf16[384,256]{1,0:T(8,128)(2,1)}, bf16[384,256]{1,0:T(8,128)(2,1)S(1)}, u32[]{:S(2)}, u32[]{:S(2)}) collective-permute-start(bf16[384,256]{1,0:T(8,128)(2,1)} %get-tuple-element.24), channel_id=1, source_target_pairs={{0,16},{8,24},{16,0},{24,8},{1,17},{9,25},{17,1},{25,9},{2,18},{10... | collective-permute-start | bytes 589832 | tf_op jit(solution)/shard_map/ppermute | solution.py:541
  9.1 18.4 %collective-permute-start = (bf16[384,256]{1,0:T(8,128)(2,1)}, bf16[384,256]{1,0:T(8,128)(2,1)S(1)}, u32[]{:S(2)}, u32[]{:S(2)}) collective-permute-start(bf16[384,256]{1,0:T(8,128)(2,1)} %get-tuple-element.19), channel_id=1, source_target_pairs={{0,24},{8,16},{16,8},{24,0},{1,25},{9,17},{17,9},{25,1},{2,26},{10... | collective-permute-start | bytes 589832 | tf_op jit(solution)/shard_map/ppermute | solution.py:541
  10.6 16.9 %collective-permute-start.1 = (bf16[384,256]{1,0:T(8,128)(2,1)}, bf16[384,256]{1,0:T(8,128)(2,1)S(1)}, u32[]{:S(2)}, u32[]{:S(2)}) collective-permute-start(bf16[384,256]{1,0:T(8,128)(2,1)} %get-tuple-element.20), channel_id=1, source_target_pairs={{0,16},{8,24},{16,0},{24,8},{1,17},{9,25},{17,1},{25,9},{2,18},{10... | collective-permute-start | bytes 589832 | tf_op jit(solution)/shard_map/ppermute | solution.py:541
  10.9 5.3 %collective-permute-start.5 = (bf16[384,256]{1,0:T(8,128)(2,1)}, bf16[384,256]{1,0:T(8,128)(2,1)S(1)}, u32[]{:S(2)}, u32[]{:S(2)}) collective-permute-start(bf16[384,256]{1,0:T(8,128)(2,1)} %get-tuple-element.25), channel_id=1, source_target_pairs={{0,8},{8,0},{16,24},{24,16},{1,9},{9,1},{17,25},{25,17},{2,10},{10... | collective-permute-start | bytes 589832 | tf_op jit(solution)/shard_map/ppermute | solution.py:541
  11.7 15.8 %collective-permute-start.2 = (bf16[384,256]{1,0:T(8,128)(2,1)}, bf16[384,256]{1,0:T(8,128)(2,1)S(1)}, u32[]{:S(2)}, u32[]{:S(2)}) collective-permute-start(bf16[384,256]{1,0:T(8,128)(2,1)} %get-tuple-element.21), channel_id=1, source_target_pairs={{0,8},{8,0},{16,24},{24,16},{1,9},{9,1},{17,25},{25,17},{2,10},{10... | collective-permute-start | bytes 589832 | tf_op jit(solution)/shard_map/ppermute | solution.py:541
  16.2 2.8 %copy-start = (bf16[16,512,272]{2,1,0:T(8,128)(2,1)S(1)}, bf16[16,512,272]{2,1,0:T(8,128)(2,1)}, u32[]{:S(2)}) copy-start(bf16[16,512,272]{2,1,0:T(8,128)(2,1)} %constant.6.clone.f_ref) | copy-start | bytes 13369348
  18.9 0.9 %copy-start.4 = (bf16[384,256]{1,0:T(8,128)(2,1)S(1)}, bf16[384,256]{1,0:T(8,128)(2,1)}, u32[]{:S(2)}) copy-start(bf16[384,256]{1,0:T(8,128)(2,1)} %get-tuple-element.22.refs_0_) | copy-start | bytes 589828
  19.9 0.7 %copy-start.6 = (s32[4]{0:T(128)S(1)}, s32[4]{0:T(128)}, u32[]{:S(2)}) copy-start(s32[4]{0:T(128)} %order_ref.7) | copy-start | bytes 52
  20.5 0.7 %copy-start.7 = (s32[11]{0:T(128)S(1)}, s32[11]{0:T(128)}, u32[]{:S(2)}) copy-start(s32[11]{0:T(128)} %offsets_ref.7) | copy-start | bytes 136
  21.2 2.8 %copy-start.1 = (bf16[16,512,272]{2,1,0:T(8,128)(2,1)S(1)}, bf16[16,512,272]{2,1,0:T(8,128)(2,1)}, u32[]{:S(2)}) copy-start(bf16[16,512,272]{2,1,0:T(8,128)(2,1)} %constant.6.clone.f_ref) | copy-start | bytes 13369348
  21.2 2.9 %copy-start.3 = (bf16[2816,128]{1,0:T(8,128)(2,1)S(1)}, bf16[2816,128]{1,0:T(8,128)(2,1)}, u32[]{:S(2)}) copy-start(bf16[2816,128]{1,0:T(8,128)(2,1)} %constant.7.clone.pick_ref) | copy-start | bytes 2162692
  24.1 3.5 %copy-start.2 = (bf16[384,256]{1,0:T(8,128)(2,1)S(1)}, bf16[384,256]{1,0:T(8,128)(2,1)}, u32[]{:S(2)}) copy-start(bf16[384,256]{1,0:T(8,128)(2,1)} %get-tuple-element.18.refs_0_) | copy-start | bytes 589828
  29.9 1.2 %collective-permute-start.6 = (bf16[64,128]{1,0:T(8,128)(2,1)S(1)}, bf16[64,128]{1,0:T(8,128)(2,1)S(1)}, u32[]{:S(2)}, u32[]{:S(2)}) collective-permute-start(bf16[64,128]{1,0:T(8,128)(2,1)S(1)} %get-tuple-element.27), channel_id=1, source_target_pairs={{0,8},{1,9},{2,10},{3,11},{4,12},{5,13},{6,14},{7,15},{8,0},{9,1},... | collective-permute-start | bytes 49160 | tf_op jit(solution)/shard_map/ppermute | solution.py:541
  31.2 4.7 %collective-permute-start.9 = (bf16[64,128]{1,0:T(8,128)(2,1)S(1)}, bf16[64,128]{1,0:T(8,128)(2,1)S(1)}, u32[]{:S(2)}, u32[]{:S(2)}) collective-permute-start(bf16[64,128]{1,0:T(8,128)(2,1)S(1)} %add_convert_fusion.1), channel_id=1, source_target_pairs={{0,17},{1,16},{2,19},{3,18},{4,21},{5,20},{6,23},{7,22},{8,25},{9,... | collective-permute-start | bytes 49160 | tf_op jit(solution)/shard_map/ppermute | solution.py:541
  33.7 3.7 %collective-permute-start.8 = (bf16[64,128]{1,0:T(8,128)(2,1)S(1)}, bf16[64,128]{1,0:T(8,128)(2,1)S(1)}, u32[]{:S(2)}, u32[]{:S(2)}) collective-permute-start(bf16[64,128]{1,0:T(8,128)(2,1)S(1)} %add_convert_fusion.1), channel_id=1, source_target_pairs={{0,1},{1,0},{2,3},{3,2},{4,5},{5,4},{6,7},{7,6},{8,9},{9,8},{10,11... | collective-permute-start | bytes 49160 | tf_op jit(solution)/shard_map/ppermute | solution.py:541
  34.2 3.7 %collective-permute-start.7 = (bf16[64,128]{1,0:T(8,128)(2,1)S(1)}, bf16[64,128]{1,0:T(8,128)(2,1)S(1)}, u32[]{:S(2)}, u32[]{:S(2)}) collective-permute-start(bf16[64,128]{1,0:T(8,128)(2,1)S(1)} %add_convert_fusion.1), channel_id=1, source_target_pairs={{0,16},{1,17},{2,18},{3,19},{4,20},{5,21},{6,22},{7,23},{8,24},{9,... | collective-permute-start | bytes 49160 | tf_op jit(solution)/shard_map/ppermute | solution.py:541
  38.0 9.6 %copy-start.5 = (bf16[2,128,256]{2,1,0:T(8,128)(2,1)S(1)}, bf16[2,128,256]{2,1,0:T(8,128)(2,1)}, u32[]{:S(2)}) copy-start(bf16[2,128,256]{2,1,0:T(8,128)(2,1)} %constant.8.clone.spread_ref) | copy-start | bytes 393220
  38.0 6.7 %collective-permute-start.12 = (bf16[64,128]{1,0:T(8,128)(2,1)S(1)}, bf16[64,128]{1,0:T(8,128)(2,1)S(1)}, u32[]{:S(2)}, u32[]{:S(2)}) collective-permute-start(bf16[64,128]{1,0:T(8,128)(2,1)S(1)} %add_convert_fusion), channel_id=1, source_target_pairs={{0,6},{1,7},{2,4},{3,5},{4,2},{5,3},{6,0},{7,1},{8,14},{9,15},{10,... | collective-permute-start | bytes 49160 | tf_op jit(solution)/shard_map/ppermute | solution.py:541
  41.6 4.6 %collective-permute-start.11 = (bf16[64,128]{1,0:T(8,128)(2,1)S(1)}, bf16[64,128]{1,0:T(8,128)(2,1)S(1)}, u32[]{:S(2)}, u32[]{:S(2)}) collective-permute-start(bf16[64,128]{1,0:T(8,128)(2,1)S(1)} %add_convert_fusion), channel_id=1, source_target_pairs={{0,4},{1,5},{2,6},{3,7},{4,0},{5,1},{6,2},{7,3},{8,12},{9,13},{10,... | collective-permute-start | bytes 49160 | tf_op jit(solution)/shard_map/ppermute | solution.py:541
  41.6 4.6 %collective-permute-start.10 = (bf16[64,128]{1,0:T(8,128)(2,1)S(1)}, bf16[64,128]{1,0:T(8,128)(2,1)S(1)}, u32[]{:S(2)}, u32[]{:S(2)}) collective-permute-start(bf16[64,128]{1,0:T(8,128)(2,1)S(1)} %add_convert_fusion), channel_id=1, source_target_pairs={{0,2},{1,3},{2,0},{3,1},{4,6},{5,7},{6,4},{7,5},{8,10},{9,11},{10,... | collective-permute-start | bytes 49160 | tf_op jit(solution)/shard_map/ppermute | solution.py:541
  46.3 1.3 %collective-permute-start.13 = (f32[64,128]{1,0:T(8,128)S(1)}, f32[64,128]{1,0:T(8,128)S(1)}, u32[]{:S(2)}, u32[]{:S(2)}) collective-permute-start(f32[64,128]{1,0:T(8,128)S(1)} %add_add_fusion.half_ref), channel_id=1, source_target_pairs={{0,8},{1,9},{2,10},{3,11},{4,12},{5,13},{6,14},{7,15},{8,0},{9,1},... | collective-permute-start | bytes 98312 | tf_op jit(solution)/shard_map/ppermute | solution.py:541

commit v11 on v9

--- a/solution.py
+++ b/solution.py
@@ -103,11 +103,11 @@
     return jnp.where(in_row == row_of, 1.0, 0.0).astype(BF16)
 
 
-def pack_kernel(jobs, parts, first, table_hbm, x_hbm, *refs):
+def pack_kernel(jobs, parts, first, follows, table_hbm, x_hbm, *refs):
     steps, lanes, _ = x_hbm.shape
     base = jobs[0][0]
     table, x_ref, table_sem, x_sem = refs[-4:]
-    outs = list(refs[:-4])
+    outs = list(refs[follows:-4])
     part = steps // parts
     table_copy = pltpu.make_async_copy(table_hbm, table, table_sem)
     table_copy.start()
@@ -136,7 +136,7 @@
                     next(out)[at, :] = y[d * rows : (d + 1) * rows]
 
 
-def pack(table, snapshots, jobs, first):
+def pack(table, snapshots, jobs, first, after=()):
     steps, lanes, _ = snapshots.shape
     parts = math.gcd(steps * lanes // WIDE, 3)
     outs = [
@@ -148,9 +148,9 @@
         outs.append(jax.ShapeDtypeStruct((WIDE, WIDE), BF16))
     columns = jobs[-1][0] + jobs[-1][1] - jobs[0][0]
     return pl.pallas_call(
-        functools.partial(pack_kernel, jobs, parts, first),
+        functools.partial(pack_kernel, jobs, parts, first, len(after)),
         out_shape=outs,
-        in_specs=[HBM] * 2,
+        in_specs=[HBM] * (2 + len(after)),
         out_specs=[VMEM] * len(outs),
         scratch_shapes=[
             pltpu.SMEM(table.shape, jnp.int32) if first else pltpu.VMEM(table.shape, BF16),
@@ -159,14 +159,10 @@
             pltpu.SemaphoreType.DMA((parts,)),
         ],
         compiler_params=pltpu.CompilerParams(
-            vmem_limit_bytes=FIRST_LIMIT if first else SECOND_LIMIT
+            vmem_limit_bytes=FIRST_LIMIT if first else 40 * 2**20 if after else SECOND_LIMIT
         ),
-        cost_estimate=pl.CostEstimate(
-            flops=2 * WIDE * steps * lanes * columns,
-            bytes_accessed=4 * steps * lanes * columns,
-            transcendentals=0,
-        ),
-    )(table, snapshots)
+        cost_estimate=pl.CostEstimate(flops=1000, bytes_accessed=1000, transcendentals=0),
+    )(table, snapshots, *after)
 
 
 def fill_record(order_ref, pieces, record, factor):
@@ -228,24 +224,25 @@
 
 def gram_kernel(lanes, scale, last, order_ref, offsets_ref, w_ref, f_ref, pick_ref, *refs):
     pieces = refs[:lanes]
-    if not last:
-        gram_ref, record, s_ref, masked = refs[lanes:]
+    refs = refs[lanes:]
+    if last:
+        before_ref, _, gram_ref, s_ref, record, masked = refs
     else:
-        before_ref, _, gram_ref, s_ref, record, masked = refs[lanes:]
+        *before_refs, gram_ref, record, s_ref, masked = refs
     fill_record(order_ref, pieces, record, jnp.sqrt(w_ref[...]))
     transform(offsets_ref, f_ref[:NFFT] if last else f_ref[...], record, s_ref)
     if not last:
-        gram_ref[...] = gram_rows(0, GROUPS, s_ref, pick_ref, masked) * scale
+        total = gram_rows(0, GROUPS, s_ref, pick_ref, masked) * scale
+        gram_ref[...] = total + before_refs[0][...] if before_refs else total
         return
     base = pl.multiple_of((1 - lax.axis_index("tm") % 2) * HALF, HALF)
     total = gram_rows(base, GROUPS // 2, s_ref, pick_ref, masked) * scale
     gram_ref[...] = (total + before_ref[pl.ds(base, HALF), :]).astype(BF16)
 
 
-def gram_part(order, offsets, weights, tables, pieces, before, scale):
+def gram_part(order, offsets, weights, tables, pieces, before, last, scale):
     lanes = len(pieces)
     steps, width = pieces[0].shape
-    last = bool(before)
     args = [order, offsets, weights, *tables, *pieces, *before]
     spectrum_shape = (2 * NBLK, NFREQ, width)
     scratch = [pltpu.VMEM((width // LANE, lanes * steps, LANE), F32)]
@@ -263,9 +260,7 @@
         out_specs=[VMEM] * len(outs),
         scratch_shapes=scratch,
         compiler_params=pltpu.CompilerParams(vmem_limit_bytes=32 * 2**20),
-        cost_estimate=pl.CostEstimate(
-            flops=width * 10**7, bytes_accessed=3 * 10**6, transcendentals=0
-        ),
+        cost_estimate=pl.CostEstimate(flops=1000, bytes_accessed=1000, transcendentals=0),
     )(*args)
 
 
@@ -304,9 +299,7 @@
         out_specs=VMEM,
         scratch_shapes=[pltpu.VMEM((width // LANE, lanes * steps, LANE), F32)],
         compiler_params=pltpu.CompilerParams(vmem_limit_bytes=32 * 2**20),
-        cost_estimate=pl.CostEstimate(
-            flops=width * 10**7, bytes_accessed=3 * 10**6, transcendentals=0
-        ),
+        cost_estimate=pl.CostEstimate(flops=1000, bytes_accessed=1000, transcendentals=0),
     )(*args)
 
 
@@ -546,34 +539,41 @@
     lanes = lax.axis_size("tm")
     groups = lax.axis_size("sx") * lax.axis_size("sy")
     points = snapshots.shape[2]
-    chunks = [(0, points // 2), (points // 2, points // 2)]
+    half, quarter = points // 2, points // 4
+    chunks = [(0, half), (half, quarter), (half + quarter, quarter)]
     scale = 1.0 / (lanes * groups * points)
     tables = (jnp.asarray(fourier_tables()), jnp.asarray(pick_table()))
     weights = weights.reshape(1, -1)
 
-    near = min(2, lanes)
-    (base, width), (next_base, next_width) = chunks
-    *far, table = pack(owner, snapshots, [(base, width, near, lanes)], True)
-    jobs = [(base, width, 0, near), (next_base, next_width, 0, lanes)]
+    first, table = pack(owner, snapshots, [(*chunks[0], lanes - 1, lanes)], True)
+    moved = [swap(first, "tm", lanes - 1, lanes)]
+    jobs = [(*chunks[0], 0, lanes - 1), (*chunks[1], 0, lanes)]
     rest = list(pack(table, snapshots, jobs, False))
-    arrived = []
-    for packed in (rest[:near] + far, rest[near:]):
-        moved = [swap(packed[d], "tm", d, lanes) for d in reversed(range(1, lanes))]
-        arrived.append([packed[0]] + moved)
+    moved += [swap(rest[d], "tm", d, lanes) for d in reversed(range(1, lanes - 1))]
+    arrived = [[rest[0]] + moved]
+    for packed in (rest[lanes - 1 :], None):
+        if packed is None:
+            packed = pack(table, snapshots, [(*chunks[2], 0, lanes)], False, moved[:1])
+        arrived.append([packed[0]])
+        arrived[-1] += [swap(packed[d], "tm", d, lanes) for d in reversed(range(1, lanes))]
 
     axes = ("tm", "sx", "sy")
     size = lanes * groups
     bits = [b * groups for b in powers(lanes)] + powers(groups)
     parts = [weights[:, base : base + width] for base, width in chunks]
-    (before,) = gram_part(block_order, offsets, parts[0], tables, arrived[0], [], scale)
-    spectra = [spectrum(block_order, offsets, tables[0], arrived[0], [])]
+    spectra = []
+    before = []
+    for pieces, part in zip(arrived[:-1], parts):
+        (total,) = gram_part(block_order, offsets, part, tables, pieces, before, False, scale)
+        spectra.append(spectrum(block_order, offsets, tables[0], pieces, [total]))
+        before = [total, spectra[-1]]
     send, scaled = gram_part(
-        block_order, offsets, parts[1], tables, arrived[1], [before, spectra[0]], scale
+        block_order, offsets, parts[-1], tables, arrived[-1], before, True, scale
     )
 
     other = swap(send, axes, bits[0], size)
-    keep = own_part(scaled, tables[1], before, scale)
-    spectra.append(spectrum(block_order, offsets, tables[0], arrived[1], [keep]))
+    keep = own_part(scaled, tables[1], before[0], scale)
+    spectra.append(spectrum(block_order, offsets, tables[0], arrived[-1], [keep]))
     half = keep.astype(F32) + other.astype(F32)
     for at in range(1, len(bits), 2):
         masks = bits[at : at + 2]

time: 49.6 us -> 50.4 us (1.016)
  Pallas kernels: 19.1 us -> 22.5 us
  local copies, waits for them, and re-layouts: 3.92 us -> 1.45 us
  waiting for transfers between devices: 11.6 us -> 9.89 us
  starting transfers between devices: 13.9 us -> 15.5 us
    pallas_call x2 -> x3, Pallas kernels: 4.79 us -> 6.62 us  [gram_part(): pl.pallas_call(functools.partial(gram_kernel, lanes, scale, last), out_sh...]
    unnamed x20, local copies, waits for them, and re-layouts: 3.22 us -> 1.44 us
    ppermute x14 -> x17, waiting for transfers between devices: 11.6 us -> 9.89 us  [swap(): return lax.ppermute(x, axes, [(i, i ^ mask) for i in range(size)])]
    ppermute x14 -> x17, starting transfers between devices: 13.9 us -> 15.5 us  [swap(): return lax.ppermute(x, axes, [(i, i ^ mask) for i in range(size)])]
    pallas_call x2 -> x3, Pallas kernels: 5.38 us -> 6.19 us  [pack(): pl.pallas_call(functools.partial(pack_kernel, jobs, parts, first, len(aft...]
    pallas_call x2 -> x3, Pallas kernels: 3.23 us -> 4.04 us  [spectrum(): pl.pallas_call(functools.partial(spectrum_kernel, lanes), out_shape=jax.S...]
    slice x1 -> x2, local copies, waits for them, and re-layouts: 0.7 us -> 0.01 us  [body(): parts = [weights[:, base:base + width] for base, width in chunks]]
  transfers between devices with their start and end apart: 14 -> 17, of which waited for: 7 -> 7; matrix products, arithmetic and copies ran while one was open for 1% -> 0% of each run, Pallas kernels for 20% -> 27%
where the time goes in v11:
time: 50.4 us; the launch traced here: 50.2 us
  Pallas kernels  22.5 us (45%)
  starting transfers between devices  15.5 us (31%)
  waiting for transfers between devices  9.89 us (20%)
  local copies, waits for them, and re-layouts  1.45 us (3%)
  between operations  0.86 us (2%)
    ppermute x17, starting transfers between devices, swap(): return lax.ppermute(x, axes, [(i, i ^ mask) for i in range(size)])  15.5 us
    ppermute x17, waiting for transfers between devices, swap(): return lax.ppermute(x, axes, [(i, i ^ mask) for i in range(size)])  9.89 us
    pallas_call x3, Pallas kernels, gram_part(): pl.pallas_call(functools.partial(gram_kernel, lanes, scale, last), out_sh...  6.62 us
    pallas_call x3, Pallas kernels, pack(): pl.pallas_call(functools.partial(pack_kernel, jobs, parts, first, len(aft...  6.19 us
    pallas_call x1, Pallas kernels, mode_fields(): pl.pallas_call(functools.partial(mode_kernel, len(spectra), share), out_s...  5 us
    pallas_call x3, Pallas kernels, spectrum(): pl.pallas_call(functools.partial(spectrum_kernel, lanes), out_shape=jax.S...  4.04 us
    unnamed x20, local copies, waits for them, and re-layouts  1.44 us
  transfers between devices with their start and end apart: 17, of which 7 were waited for; matrix products, arithmetic and copies ran while one was open for 0% of the time, Pallas kernels for 27%

profile of v11, /device:TPU:0, one launch (start us, length us, event | category | flops | bytes accessed | tf_op | source)
XLA Modules:
  0.0 50.2 jit_solution(4966709836468123196)
XLA Ops:
  0.6 2.2 %shard_map.95 = (bf16[384,256]{1,0:T(8,128)(2,1)}, bf16[256,256]{1,0:T(8,128)(2,1)}) custom-call(s32[1,4]{1,0:T(1,128)} %table_hbm.1, bf16[384,4,512]{2,1,0:T(4,128)(2,1)} %x_hbm.5), custom_call_target="tpu_custom_call" | custom-call | flops 1000 | bytes 1000 | tf_op jit(solution)/shard_map/pallas_call | solution.py:150
  2.8 0.0 copy-start.9
  2.8 0.0 copy-start.4
  2.9 2.5 %collective-permute-start = (bf16[384,256]{1,0:T(8,128)(2,1)}, bf16[384,256]{1,0:T(8,128)(2,1)S(1)}, u32[]{:S(2)}, u32[]{:S(2)}) collective-permute-start(bf16[384,256]{1,0:T(8,128)(2,1)} %get-tuple-element.22), channel_id=1, source_target_pairs={{0,24},{8,16},{16,8},{24,0},{1,25},{9,17},{17,9},{25,1},{2,26},{10... | collective-permute-start | bytes 589832 | tf_op jit(solution)/shard_map/ppermute | solution.py:531
  5.3 0.0 copy-start.1
  5.3 0.0 copy-start.2
  5.3 0.0 copy-start.7
  5.3 0.0 copy-start.8
  5.3 3.0 %shard_map.97 = (bf16[384,256]{1,0:T(8,128)(2,1)}, bf16[384,256]{1,0:T(8,128)(2,1)}, bf16[384,256]{1,0:T(8,128)(2,1)}, bf16[384,128]{1,0:T(8,128)(2,1)}, bf16[38...) custom-call(bf16[256,256]{1,0:T(8,128)(2,1)} %get-tuple-element.21.table_hbm, ...), custom_call_target="tpu_custom_call" | custom-call | flops 1000 | bytes 1000 | tf_op jit(solution)/shard_map/pallas_call | solution.py:150
  8.3 0.7 %collective-permute-start.7 = (bf16[384,256]{1,0:T(8,128)(2,1)}, bf16[384,256]{1,0:T(8,128)(2,1)S(1)}, u32[]{:S(2)}, u32[]{:S(2)}) collective-permute-start(bf16[384,256]{1,0:T(8,128)(2,1)} %get-tuple-element.32), channel_id=1, source_target_pairs={{0,16},{8,24},{16,0},{24,8},{1,17},{9,25},{17,1},{25,9},{2,18},{10... | collective-permute-start | bytes 589832 | tf_op jit(solution)/shard_map/ppermute | solution.py:531
  9.0 0.1 collective-permute-start.8
  9.2 1.4 %collective-permute-start.4 = (bf16[384,128]{1,0:T(8,128)(2,1)}, bf16[384,128]{1,0:T(8,128)(2,1)S(1)}, u32[]{:S(2)}, u32[]{:S(2)}) collective-permute-start(bf16[384,128]{1,0:T(8,128)(2,1)} %get-tuple-element.28), channel_id=1, source_target_pairs={{0,24},{8,16},{16,8},{24,0},{1,25},{9,17},{17,9},{25,1},{2,26},{10... | collective-permute-start | bytes 294920 | tf_op jit(solution)/shard_map/ppermute | solution.py:531
  10.6 0.6 %collective-permute-start.5 = (bf16[384,128]{1,0:T(8,128)(2,1)}, bf16[384,128]{1,0:T(8,128)(2,1)S(1)}, u32[]{:S(2)}, u32[]{:S(2)}) collective-permute-start(bf16[384,128]{1,0:T(8,128)(2,1)} %get-tuple-element.29), channel_id=1, source_target_pairs={{0,16},{8,24},{16,0},{24,8},{1,17},{9,25},{17,1},{25,9},{2,18},{10... | collective-permute-start | bytes 294920 | tf_op jit(solution)/shard_map/ppermute | solution.py:531
  11.2 0.0 copy-done.9
  11.2 0.0 collective-permute-done.refs_0_.refs_1_
  11.2 0.1 collective-permute-start.6
  11.2 0.0 copy-done.4
  11.3 0.0 copy-start
  11.3 1.4 %copy-done = bf16[384,4,512]{2,1,0:T(4,128)(2,1)S(1)} copy-done((bf16[384,4,512]{2,1,0:T(4,128)(2,1)S(1)}, bf16[384,4,512]{2,1,0:T(4,128)(2,1)}, u32[]{:S(2)}) %copy-start) | copy-done | bytes 1572888
  12.7 0.0 copy-start.3
  12.7 1.0 %shard_map.96 = (bf16[384,128]{1,0:T(8,128)(2,1)S(1)}, bf16[384,128]{1,0:T(8,128)(2,1)S(1)}, bf16[384,128]{1,0:T(8,128)(2,1)S(1)}, bf16[384,128]{1,0:T(8,128)(2,1)S(1)}) custom-call(bf16[256,256]{1,0:T(8,128)(2,1)S(1)} %copy-done.4, bf16[384,4,512]{2,1,0:T(4,128)(2,1)S(1)} %copy-done, bf16[384,256]{1,0:T(8,128)(2,1)S(1)} %collective-permute-done.refs_0_.refs_1_), custom_call_target="tpu_custom_call" | custom-call | flops 1000 | bytes 1000 | tf_op jit(solution)/shard_map/pallas_call | solution.py:150
  13.7 2.7 %collective-permute-done.7.refs_2_ = bf16[384,256]{1,0:T(8,128)(2,1)S(1)} collective-permute-done((bf16[384,256]{1,0:T(8,128)(2,1)}, bf16[384,256]{1,0:T(8,128)(2,1)S(1)}, u32[]{:S(2)}, u32[]{:S(2)}) %collective-permute-start.7) | collective-permute-done | bytes 196640 | tf_op jit(solution)/shard_map/ppermute | solution.py:531
  16.4 0.8 %collective-permute-start.1 = (bf16[384,128]{1,0:T(8,128)(2,1)S(1)}, bf16[384,128]{1,0:T(8,128)(2,1)S(1)}, u32[]{:S(2)}, u32[]{:S(2)}) collective-permute-start(bf16[384,128]{1,0:T(8,128)(2,1)S(1)} %get-tuple-element.24), channel_id=1, source_target_pairs={{0,24},{8,16},{16,8},{24,0},{1,25},{9,17},{17,9},{25,1},{2,26},{10... | collective-permute-start | bytes 294920 | tf_op jit(solution)/shard_map/ppermute | solution.py:531
  17.2 0.0 collective-permute-done.8.refs_3_
  17.2 0.4 collective-permute-start.2
  17.6 0.0 copy-done.1
  17.6 0.0 copy-done.2
  17.6 0.0 copy-done.7
  17.6 0.0 copy-done.8
  17.6 0.0 copy-done.3
  17.6 2.7 %shard_map.98.refs_4_ = f32[128,128]{1,0:T(8,128)S(1)} custom-call(s32[4]{0:T(128)S(1)} %copy-done.7, s32[11]{0:T(128)S(1)} %copy-done.8, f32[1,256]{1,0:T(1,128)S(1)} %slice.14.w_ref, bf16[512,256]{1,0:T(8,128)(2,1)S(1)} %copy-done.1, bf16[2816,128]{1,0:T(8,128)(2,1)S(1)} %copy-done.2, bf16[384,256]{1,0:T(8,128)(2,1)S(1)} %copy-done.3, ...), custom_call_target="tpu_custom_call" | custom-call | flops 1000 | bytes 1000 | tf_op jit(solution)/shard_map/pallas_call | solution.py:256
  20.3 0.0 collective-permute-done.4.refs_1_
  20.3 0.7 %collective-permute-start.3 = (bf16[384,128]{1,0:T(8,128)(2,1)S(1)}, bf16[384,128]{1,0:T(8,128)(2,1)S(1)}, u32[]{:S(2)}, u32[]{:S(2)}) collective-permute-start(bf16[384,128]{1,0:T(8,128)(2,1)S(1)} %get-tuple-element.26), channel_id=1, source_target_pairs={{0,8},{8,0},{16,24},{24,16},{1,9},{9,1},{17,25},{25,17},{2,10},{10... | collective-permute-start | bytes 294920 | tf_op jit(solution)/shard_map/ppermute | solution.py:531
  21.1 1.6 %shard_map.99.refs_5_.refs_0_ = f32[22,128,256]{2,1,0:T(8,128)S(1)} custom-call(s32[4]{0:T(128)S(1)} %copy-done.7, s32[11]{0:T(128)S(1)} %copy-done.8, bf16[512,256]{1,0:T(8,128)(2,1)S(1)} %copy-done.1, bf16[384,256]{1,0:T(8,128)(2,1)S(1)} %copy-done.3, bf16[384,256]{1,0:T(8,128)(2,1)S(1)} %collective-permute-done.refs_0_.refs_1_, ...), custom_call_target="tpu_custom_call" | custom-call | flops 1000 | bytes 1000 | tf_op jit(solution)/shard_map/pallas_call | solution.py:295
  22.7 0.0 collective-permute-done.5.refs_2_
  22.7 0.0 collective-permute-done.6.refs_3_
  22.7 0.0 copy-done.5
  22.7 2.2 %shard_map.100.refs_4_.before_ref = f32[128,128]{1,0:T(8,128)S(1)} custom-call(s32[4]{0:T(128)S(1)} %copy-done.7, s32[11]{0:T(128)S(1)} %copy-done.8, f32[1,128]{1,0:T(1,128)S(1)} %get-tuple-element.42.w_ref, bf16[512,256]{1,0:T(8,128)(2,1)S(1)} %copy-done.1, bf16[2816,128]{1,0:T(8,128)(2,1)S(1)} %copy-done.2, bf16[384,128]{1,0:T(8,128)(2,1)S(1)} %copy-done.5, ...), custom_call_target="tpu_custom_call" | custom-call | flops 1000 | bytes 1000 | tf_op jit(solution)/shard_map/pallas_call | solution.py:256
  24.9 1.2 %shard_map.101.refs_5_.refs_1_ = f32[22,128,128]{2,1,0:T(8,128)S(1)} custom-call(s32[4]{0:T(128)S(1)} %copy-done.7, s32[11]{0:T(128)S(1)} %copy-done.8, bf16[512,256]{1,0:T(8,128)(2,1)S(1)} %copy-done.1, bf16[384,128]{1,0:T(8,128)(2,1)S(1)} %copy-done.5, bf16[384,128]{1,0:T(8,128)(2,1)S(1)} %collective-permute-done.4.refs_1_, ...), custom_call_target="tpu_custom_call" | custom-call | flops 1000 | bytes 1000 | tf_op jit(solution)/shard_map/pallas_call | solution.py:295
  26.2 0.0 collective-permute-done.1.refs_1_
  26.2 0.0 collective-permute-done.2.refs_2_
  26.2 0.0 collective-permute-done.3.refs_3_
  26.2 1.7 %shard_map.102 = (bf16[64,128]{1,0:T(8,128)(2,1)S(1)}, f32[22,128,128]{2,1,0:T(8,128)S(1)}) custom-call(s32[4]{0:T(128)S(1)} %copy-done.7, s32[11]{0:T(128)S(1)} %copy-done.8, f32[1,128]{1,0:T(1,128)S(1)} %get-tuple-element.43.w_ref, bf16[512,256]{1,0:T(8,128)(2,1)S(1)} %copy-done.1, bf16[2816,128]{1,0:T(8,128)(2,1)S(1)} %copy-done.2, ...), custom_call_target="tpu_custom_call" | custom-call | flops 1000 | bytes 1000 | tf_op jit(solution)/shard_map/pallas_call | solution.py:256
  27.9 0.1 collective-permute-start.9
  28.0 0.7 %shard_map.103.refs_4_ = bf16[64,128]{1,0:T(8,128)(2,1)S(1)} custom-call(f32[22,128,128]{2,1,0:T(8,128)S(1)} %get-tuple-element.34.s_ref, bf16[2816,128]{1,0:T(8,128)(2,1)S(1)} %copy-done.2, f32[128,128]{1,0:T(8,128)S(1)} %shard_map.100.refs_4_.before_ref), custom_call_target="tpu_custom_call" | custom-call | flops 1000000000 | bytes 3000000 | tf_op jit(solution)/shard_map/pallas_call | solution.py:274
  28.7 0.0 copy-start.6
  28.7 0.5 collective-permute-done.9
  29.2 2.1 %collective-permute-start.12 = (bf16[64,128]{1,0:T(8,128)(2,1)S(1)}, bf16[64,128]{1,0:T(8,128)(2,1)S(1)}, u32[]{:S(2)}, u32[]{:S(2)}) collective-permute-start(bf16[64,128]{1,0:T(8,128)(2,1)S(1)} %add_convert_fusion.1), channel_id=1, source_target_pairs={{0,17},{1,16},{2,19},{3,18},{4,21},{5,20},{6,23},{7,22},{8,25},{9,... | collective-permute-start | bytes 49160 | tf_op jit(solution)/shard_map/ppermute | solution.py:531
  31.3 0.5 %collective-permute-start.11 = (bf16[64,128]{1,0:T(8,128)(2,1)S(1)}, bf16[64,128]{1,0:T(8,128)(2,1)S(1)}, u32[]{:S(2)}, u32[]{:S(2)}) collective-permute-start(bf16[64,128]{1,0:T(8,128)(2,1)S(1)} %add_convert_fusion.1), channel_id=1, source_target_pairs={{0,1},{1,0},{2,3},{3,2},{4,5},{5,4},{6,7},{7,6},{8,9},{9,8},{10,11... | collective-permute-start | bytes 49160 | tf_op jit(solution)/shard_map/ppermute | solution.py:531
  31.9 0.9 %collective-permute-start.10 = (bf16[64,128]{1,0:T(8,128)(2,1)S(1)}, bf16[64,128]{1,0:T(8,128)(2,1)S(1)}, u32[]{:S(2)}, u32[]{:S(2)}) collective-permute-start(bf16[64,128]{1,0:T(8,128)(2,1)S(1)} %add_convert_fusion.1), channel_id=1, source_target_pairs={{0,16},{1,17},{2,18},{3,19},{4,20},{5,21},{6,22},{7,23},{8,24},{9,... | collective-permute-start | bytes 49160 | tf_op jit(solution)/shard_map/ppermute | solution.py:531
  32.7 1.1 %collective-permute-done.12 = bf16[64,128]{1,0:T(8,128)(2,1)S(1)} collective-permute-done((bf16[64,128]{1,0:T(8,128)(2,1)S(1)}, bf16[64,128]{1,0:T(8,128)(2,1)S(1)}, u32[]{:S(2)}, u32[]{:S(2)}) %collective-permute-start.12) | collective-permute-done | bytes 16416 | tf_op jit(solution)/shard_map/ppermute | solution.py:531
  33.9 1.2 %collective-permute-done.11 = bf16[64,128]{1,0:T(8,128)(2,1)S(1)} collective-permute-done((bf16[64,128]{1,0:T(8,128)(2,1)S(1)}, bf16[64,128]{1,0:T(8,128)(2,1)S(1)}, u32[]{:S(2)}, u32[]{:S(2)}) %collective-permute-start.11) | collective-permute-done | bytes 16416 | tf_op jit(solution)/shard_map/ppermute | solution.py:531
  35.0 0.5 %collective-permute-done.10 = bf16[64,128]{1,0:T(8,128)(2,1)S(1)} collective-permute-done((bf16[64,128]{1,0:T(8,128)(2,1)S(1)}, bf16[64,128]{1,0:T(8,128)(2,1)S(1)}, u32[]{:S(2)}, u32[]{:S(2)}) %collective-permute-start.10) | collective-permute-done | bytes 16416 | tf_op jit(solution)/shard_map/ppermute | solution.py:531
  35.6 3.7 %collective-permute-start.15 = (bf16[64,128]{1,0:T(8,128)(2,1)S(1)}, bf16[64,128]{1,0:T(8,128)(2,1)S(1)}, u32[]{:S(2)}, u32[]{:S(2)}) collective-permute-start(bf16[64,128]{1,0:T(8,128)(2,1)S(1)} %add_convert_fusion), channel_id=1, source_target_pairs={{0,6},{1,7},{2,4},{3,5},{4,2},{5,3},{6,0},{7,1},{8,14},{9,15},{10,... | collective-permute-start | bytes 49160 | tf_op jit(solution)/shard_map/ppermute | solution.py:531
  39.3 0.0 collective-permute-start.14
  39.3 0.8 %collective-permute-start.13 = (bf16[64,128]{1,0:T(8,128)(2,1)S(1)}, bf16[64,128]{1,0:T(8,128)(2,1)S(1)}, u32[]{:S(2)}, u32[]{:S(2)}) collective-permute-start(bf16[64,128]{1,0:T(8,128)(2,1)S(1)} %add_convert_fusion), channel_id=1, source_target_pairs={{0,2},{1,3},{2,0},{3,1},{4,6},{5,7},{6,4},{7,5},{8,10},{9,11},{10,... | collective-permute-start | bytes 49160 | tf_op jit(solution)/shard_map/ppermute | solution.py:531
  40.1 1.2 %shard_map.104.refs_2_ = f32[22,128,128]{2,1,0:T(8,128)S(1)} custom-call(s32[4]{0:T(128)S(1)} %copy-done.7, s32[11]{0:T(128)S(1)} %copy-done.8, bf16[512,256]{1,0:T(8,128)(2,1)S(1)} %copy-done.1, bf16[384,128]{1,0:T(8,128)(2,1)S(1)} %get-tuple-element.23.refs_0_, bf16[384,128]{1,0:T(8,128)(2,1)S(1)} %collective-permute-done.1.refs_1_, ...), custom_call_target="tpu_custom_call" | custom-call | flops 1000 | bytes 1000 | tf_op jit(solution)/shard_map/pallas_call | solution.py:295
  41.3 0.0 collective-permute-done.15
  41.3 2.6 %collective-permute-done.14 = bf16[64,128]{1,0:T(8,128)(2,1)S(1)} collective-permute-done((bf16[64,128]{1,0:T(8,128)(2,1)S(1)}, bf16[64,128]{1,0:T(8,128)(2,1)S(1)}, u32[]{:S(2)}, u32[]{:S(2)}) %collective-permute-start.14) | collective-permute-done | bytes 16416 | tf_op jit(solution)/shard_map/ppermute | solution.py:531
  43.9 0.0 collective-permute-done.13
  43.9 0.1 collective-permute-start.16
  44.0 1.2 %collective-permute-done.16.other_ref = f32[64,128]{1,0:T(8,128)S(1)} collective-permute-done((f32[64,128]{1,0:T(8,128)S(1)}, f32[64,128]{1,0:T(8,128)S(1)}, u32[]{:S(2)}, u32[]{:S(2)}) %collective-permute-start.16) | collective-permute-done | bytes 32800 | tf_op jit(solution)/shard_map/ppermute | solution.py:531
  45.2 0.0 copy-done.6
  45.2 5.0 %shard_map.105 = (bf16[2,11,128,512]{3,2,1,0:T(8,128)(2,1)}, f32[11,11,2,16]{3,2,1,0:T(2,128)}) custom-call(f32[64,128]{1,0:T(8,128)S(1)} %add_add_fusion.half_ref, f32[64,128]{1,0:T(8,128)S(1)} %collective-permute-done.16.other_ref, bf16[2,128,256]{2,1,0:T(8,128)(2,1)S(1)} %copy-done.6, f32[22,128,256]{2,1,0:T(8,128)S(1)} %shard_map.99.refs_5_.refs_0_, ...), custom_call_target="tpu_custom_call" | custom-call | tf_op jit(solution)/shard_map/pallas_call | solution.py:505
  (6 shorter events, 0.0 us)
Async XLA Ops:
  2.8 8.3 %copy-start.9 = (f32[512]{0:T(512)S(1)}, f32[512]{0:T(512)}, u32[]{:S(2)}) copy-start(f32[512]{0:T(512)} %param.9) | copy-start | bytes 6148
  2.8 8.4 %copy-start.4 = (bf16[256,256]{1,0:T(8,128)(2,1)S(1)}, bf16[256,256]{1,0:T(8,128)(2,1)}, u32[]{:S(2)}) copy-start(bf16[256,256]{1,0:T(8,128)(2,1)} %get-tuple-element.21.table_hbm) | copy-start | bytes 393220
  2.9 8.3 %collective-permute-start = (bf16[384,256]{1,0:T(8,128)(2,1)}, bf16[384,256]{1,0:T(8,128)(2,1)S(1)}, u32[]{:S(2)}, u32[]{:S(2)}) collective-permute-start(bf16[384,256]{1,0:T(8,128)(2,1)} %get-tuple-element.22), channel_id=1, source_target_pairs={{0,24},{8,16},{16,8},{24,0},{1,25},{9,17},{17,9},{25,1},{2,26},{10... | collective-permute-start | bytes 589832 | tf_op jit(solution)/shard_map/ppermute | solution.py:531
  5.3 12.3 %copy-start.1 = (bf16[512,256]{1,0:T(8,128)(2,1)S(1)}, bf16[512,256]{1,0:T(8,128)(2,1)}, u32[]{:S(2)}) copy-start(bf16[512,256]{1,0:T(8,128)(2,1)} %constant.6.clone.f_ref) | copy-start | bytes 786436
  5.3 12.3 %copy-start.2 = (bf16[2816,128]{1,0:T(8,128)(2,1)S(1)}, bf16[2816,128]{1,0:T(8,128)(2,1)}, u32[]{:S(2)}) copy-start(bf16[2816,128]{1,0:T(8,128)(2,1)} %constant.7.clone.pick_ref) | copy-start | bytes 2162692
  5.3 12.3 %copy-start.7 = (s32[4]{0:T(128)S(1)}, s32[4]{0:T(128)}, u32[]{:S(2)}) copy-start(s32[4]{0:T(128)} %order_ref.11) | copy-start | bytes 52
  5.3 12.3 %copy-start.8 = (s32[11]{0:T(128)S(1)}, s32[11]{0:T(128)}, u32[]{:S(2)}) copy-start(s32[11]{0:T(128)} %offsets_ref.11) | copy-start | bytes 136
  8.3 8.1 %collective-permute-start.7 = (bf16[384,256]{1,0:T(8,128)(2,1)}, bf16[384,256]{1,0:T(8,128)(2,1)S(1)}, u32[]{:S(2)}, u32[]{:S(2)}) collective-permute-start(bf16[384,256]{1,0:T(8,128)(2,1)} %get-tuple-element.32), channel_id=1, source_target_pairs={{0,16},{8,24},{16,0},{24,8},{1,17},{9,25},{17,1},{25,9},{2,18},{10... | collective-permute-start | bytes 589832 | tf_op jit(solution)/shard_map/ppermute | solution.py:531
  9.0 8.2 %collective-permute-start.8 = (bf16[384,256]{1,0:T(8,128)(2,1)}, bf16[384,256]{1,0:T(8,128)(2,1)S(1)}, u32[]{:S(2)}, u32[]{:S(2)}) collective-permute-start(bf16[384,256]{1,0:T(8,128)(2,1)} %get-tuple-element.33), channel_id=1, source_target_pairs={{0,8},{8,0},{16,24},{24,16},{1,9},{9,1},{17,25},{25,17},{2,10},{10... | collective-permute-start | bytes 589832 | tf_op jit(solution)/shard_map/ppermute | solution.py:531
  9.2 11.1 %collective-permute-start.4 = (bf16[384,128]{1,0:T(8,128)(2,1)}, bf16[384,128]{1,0:T(8,128)(2,1)S(1)}, u32[]{:S(2)}, u32[]{:S(2)}) collective-permute-start(bf16[384,128]{1,0:T(8,128)(2,1)} %get-tuple-element.28), channel_id=1, source_target_pairs={{0,24},{8,16},{16,8},{24,0},{1,25},{9,17},{17,9},{25,1},{2,26},{10... | collective-permute-start | bytes 294920 | tf_op jit(solution)/shard_map/ppermute | solution.py:531
  10.6 12.1 %collective-permute-start.5 = (bf16[384,128]{1,0:T(8,128)(2,1)}, bf16[384,128]{1,0:T(8,128)(2,1)S(1)}, u32[]{:S(2)}, u32[]{:S(2)}) collective-permute-start(bf16[384,128]{1,0:T(8,128)(2,1)} %get-tuple-element.29), channel_id=1, source_target_pairs={{0,16},{8,24},{16,0},{24,8},{1,17},{9,25},{17,1},{25,9},{2,18},{10... | collective-permute-start | bytes 294920 | tf_op jit(solution)/shard_map/ppermute | solution.py:531
  11.2 11.5 %collective-permute-start.6 = (bf16[384,128]{1,0:T(8,128)(2,1)}, bf16[384,128]{1,0:T(8,128)(2,1)S(1)}, u32[]{:S(2)}, u32[]{:S(2)}) collective-permute-start(bf16[384,128]{1,0:T(8,128)(2,1)} %get-tuple-element.30), channel_id=1, source_target_pairs={{0,8},{8,0},{16,24},{24,16},{1,9},{9,1},{17,25},{25,17},{2,10},{10... | collective-permute-start | bytes 294920 | tf_op jit(solution)/shard_map/ppermute | solution.py:531
  11.3 1.4 %copy-start = (bf16[384,4,512]{2,1,0:T(4,128)(2,1)S(1)}, bf16[384,4,512]{2,1,0:T(4,128)(2,1)}, u32[]{:S(2)}) copy-start(bf16[384,4,512]{2,1,0:T(4,128)(2,1)} %x_hbm.5) | copy-start | bytes 4718596
  12.7 4.9 %copy-start.3 = (bf16[384,256]{1,0:T(8,128)(2,1)S(1)}, bf16[384,256]{1,0:T(8,128)(2,1)}, u32[]{:S(2)}) copy-start(bf16[384,256]{1,0:T(8,128)(2,1)} %get-tuple-element.31.refs_0_) | copy-start | bytes 589828
  16.4 9.8 %collective-permute-start.1 = (bf16[384,128]{1,0:T(8,128)(2,1)S(1)}, bf16[384,128]{1,0:T(8,128)(2,1)S(1)}, u32[]{:S(2)}, u32[]{:S(2)}) collective-permute-start(bf16[384,128]{1,0:T(8,128)(2,1)S(1)} %get-tuple-element.24), channel_id=1, source_target_pairs={{0,24},{8,16},{16,8},{24,0},{1,25},{9,17},{17,9},{25,1},{2,26},{10... | collective-permute-start | bytes 294920 | tf_op jit(solution)/shard_map/ppermute | solution.py:531
  17.2 9.0 %collective-permute-start.2 = (bf16[384,128]{1,0:T(8,128)(2,1)S(1)}, bf16[384,128]{1,0:T(8,128)(2,1)S(1)}, u32[]{:S(2)}, u32[]{:S(2)}) collective-permute-start(bf16[384,128]{1,0:T(8,128)(2,1)S(1)} %get-tuple-element.25), channel_id=1, source_target_pairs={{0,16},{8,24},{16,0},{24,8},{1,17},{9,25},{17,1},{25,9},{2,18},{10... | collective-permute-start | bytes 294920 | tf_op jit(solution)/shard_map/ppermute | solution.py:531
  20.3 5.9 %collective-permute-start.3 = (bf16[384,128]{1,0:T(8,128)(2,1)S(1)}, bf16[384,128]{1,0:T(8,128)(2,1)S(1)}, u32[]{:S(2)}, u32[]{:S(2)}) collective-permute-start(bf16[384,128]{1,0:T(8,128)(2,1)S(1)} %get-tuple-element.26), channel_id=1, source_target_pairs={{0,8},{8,0},{16,24},{24,16},{1,9},{9,1},{17,25},{25,17},{2,10},{10... | collective-permute-start | bytes 294920 | tf_op jit(solution)/shard_map/ppermute | solution.py:531
  21.1 1.6 %copy-start.5 = (bf16[384,128]{1,0:T(8,128)(2,1)S(1)}, bf16[384,128]{1,0:T(8,128)(2,1)}, u32[]{:S(2)}) copy-start(bf16[384,128]{1,0:T(8,128)(2,1)} %get-tuple-element.27.refs_0_) | copy-start | bytes 294916
  27.9 1.2 %collective-permute-start.9 = (bf16[64,128]{1,0:T(8,128)(2,1)S(1)}, bf16[64,128]{1,0:T(8,128)(2,1)S(1)}, u32[]{:S(2)}, u32[]{:S(2)}) collective-permute-start(bf16[64,128]{1,0:T(8,128)(2,1)S(1)} %get-tuple-element.35), channel_id=1, source_target_pairs={{0,8},{1,9},{2,10},{3,11},{4,12},{5,13},{6,14},{7,15},{8,0},{9,1},... | collective-permute-start | bytes 49160 | tf_op jit(solution)/shard_map/ppermute | solution.py:531
  28.7 16.5 %copy-start.6 = (bf16[2,128,256]{2,1,0:T(8,128)(2,1)S(1)}, bf16[2,128,256]{2,1,0:T(8,128)(2,1)}, u32[]{:S(2)}) copy-start(bf16[2,128,256]{2,1,0:T(8,128)(2,1)} %constant.8.clone.spread_ref) | copy-start | bytes 393220
  29.2 4.7 %collective-permute-start.12 = (bf16[64,128]{1,0:T(8,128)(2,1)S(1)}, bf16[64,128]{1,0:T(8,128)(2,1)S(1)}, u32[]{:S(2)}, u32[]{:S(2)}) collective-permute-start(bf16[64,128]{1,0:T(8,128)(2,1)S(1)} %add_convert_fusion.1), channel_id=1, source_target_pairs={{0,17},{1,16},{2,19},{3,18},{4,21},{5,20},{6,23},{7,22},{8,25},{9,... | collective-permute-start | bytes 49160 | tf_op jit(solution)/shard_map/ppermute | solution.py:531
  31.3 3.7 %collective-permute-start.11 = (bf16[64,128]{1,0:T(8,128)(2,1)S(1)}, bf16[64,128]{1,0:T(8,128)(2,1)S(1)}, u32[]{:S(2)}, u32[]{:S(2)}) collective-permute-start(bf16[64,128]{1,0:T(8,128)(2,1)S(1)} %add_convert_fusion.1), channel_id=1, source_target_pairs={{0,1},{1,0},{2,3},{3,2},{4,5},{5,4},{6,7},{7,6},{8,9},{9,8},{10,11... | collective-permute-start | bytes 49160 | tf_op jit(solution)/shard_map/ppermute | solution.py:531
  31.9 3.7 %collective-permute-start.10 = (bf16[64,128]{1,0:T(8,128)(2,1)S(1)}, bf16[64,128]{1,0:T(8,128)(2,1)S(1)}, u32[]{:S(2)}, u32[]{:S(2)}) collective-permute-start(bf16[64,128]{1,0:T(8,128)(2,1)S(1)} %add_convert_fusion.1), channel_id=1, source_target_pairs={{0,16},{1,17},{2,18},{3,19},{4,20},{5,21},{6,22},{7,23},{8,24},{9,... | collective-permute-start | bytes 49160 | tf_op jit(solution)/shard_map/ppermute | solution.py:531
  35.6 5.7 %collective-permute-start.15 = (bf16[64,128]{1,0:T(8,128)(2,1)S(1)}, bf16[64,128]{1,0:T(8,128)(2,1)S(1)}, u32[]{:S(2)}, u32[]{:S(2)}) collective-permute-start(bf16[64,128]{1,0:T(8,128)(2,1)S(1)} %add_convert_fusion), channel_id=1, source_target_pairs={{0,6},{1,7},{2,4},{3,5},{4,2},{5,3},{6,0},{7,1},{8,14},{9,15},{10,... | collective-permute-start | bytes 49160 | tf_op jit(solution)/shard_map/ppermute | solution.py:531
  39.3 4.6 %collective-permute-start.14 = (bf16[64,128]{1,0:T(8,128)(2,1)S(1)}, bf16[64,128]{1,0:T(8,128)(2,1)S(1)}, u32[]{:S(2)}, u32[]{:S(2)}) collective-permute-start(bf16[64,128]{1,0:T(8,128)(2,1)S(1)} %add_convert_fusion), channel_id=1, source_target_pairs={{0,4},{1,5},{2,6},{3,7},{4,0},{5,1},{6,2},{7,3},{8,12},{9,13},{10,... | collective-permute-start | bytes 49160 | tf_op jit(solution)/shard_map/ppermute | solution.py:531
  39.3 4.6 %collective-permute-start.13 = (bf16[64,128]{1,0:T(8,128)(2,1)S(1)}, bf16[64,128]{1,0:T(8,128)(2,1)S(1)}, u32[]{:S(2)}, u32[]{:S(2)}) collective-permute-start(bf16[64,128]{1,0:T(8,128)(2,1)S(1)} %add_convert_fusion), channel_id=1, source_target_pairs={{0,2},{1,3},{2,0},{3,1},{4,6},{5,7},{6,4},{7,5},{8,10},{9,11},{10,... | collective-permute-start | bytes 49160 | tf_op jit(solution)/shard_map/ppermute | solution.py:531
  43.9 1.3 %collective-permute-start.16 = (f32[64,128]{1,0:T(8,128)S(1)}, f32[64,128]{1,0:T(8,128)S(1)}, u32[]{:S(2)}, u32[]{:S(2)}) collective-permute-start(f32[64,128]{1,0:T(8,128)S(1)} %add_add_fusion.half_ref), channel_id=1, source_target_pairs={{0,8},{1,9},{2,10},{3,11},{4,12},{5,13},{6,14},{7,15},{8,0},{9,1},... | collective-permute-start | bytes 98312 | tf_op jit(solution)/shard_map/ppermute | solution.py:531

commit v12 on v11

--- a/solution.py
+++ b/solution.py
@@ -561,31 +561,32 @@
     size = lanes * groups
     bits = [b * groups for b in powers(lanes)] + powers(groups)
     parts = [weights[:, base : base + width] for base, width in chunks]
-    spectra = []
-    before = []
-    for pieces, part in zip(arrived[:-1], parts):
-        (total,) = gram_part(block_order, offsets, part, tables, pieces, before, False, scale)
-        spectra.append(spectrum(block_order, offsets, tables[0], pieces, [total]))
-        before = [total, spectra[-1]]
+    (total,) = gram_part(block_order, offsets, parts[0], tables, arrived[0], [], False, scale)
+    spectra = [spectrum(block_order, offsets, tables[0], arrived[0], [total])]
+    before = [total, spectra[0]]
+    before = gram_part(block_order, offsets, parts[1], tables, arrived[1], before, False, scale)
     send, scaled = gram_part(
-        block_order, offsets, parts[-1], tables, arrived[-1], before, True, scale
+        block_order, offsets, parts[2], tables, arrived[2], [*before, spectra[0]], True, scale
     )
 
     other = swap(send, axes, bits[0], size)
     keep = own_part(scaled, tables[1], before[0], scale)
-    spectra.append(spectrum(block_order, offsets, tables[0], arrived[-1], [keep]))
+    spectra += [spectrum(block_order, offsets, tables[0], a, [keep]) for a in arrived[1:]]
     half = keep.astype(F32) + other.astype(F32)
     for at in range(1, len(bits), 2):
         masks = bits[at : at + 2]
         if len(masks) == 2:
             masks.append(masks[0] ^ masks[1])
+            masks = masks[1:] + masks[:1] if at > 1 else masks
         half = half.astype(BF16)
         terms = [half] + [swap(half, axes, mask, size) for mask in masks]
         terms = [t.astype(F32) for t in terms]
         while len(terms) > 1:
             terms = [a + b for a, b in zip(terms[::2], terms[1::2])]
         half = terms[0]
-    half, spectra[-1] = lax.optimization_barrier((half, spectra[-1]))
+        if at == 1:
+            half, spectra[1] = lax.optimization_barrier((half, spectra[1]))
+    half, spectra[2] = lax.optimization_barrier((half, spectra[2]))
     other = swap(half, axes, bits[0], size)
 
     spread = jnp.asarray(spread_table())

time: 50.4 us -> 49.3 us (0.978)
  waiting for transfers between devices: 9.89 us -> 8.66 us
    ppermute x17, waiting for transfers between devices: 9.89 us -> 8.66 us  [swap(): return lax.ppermute(x, axes, [(i, i ^ mask) for i in range(size)])]
  transfers between devices with their start and end apart: 17 -> 17, of which waited for: 7 -> 6; matrix products, arithmetic and copies ran while one was open for 0% -> 0% of each run, Pallas kernels for 27% -> 28%
where the time goes in v12:
time: 49.3 us; the launch traced here: 49.1 us
  Pallas kernels  22.6 us (46%)
  starting transfers between devices  15.5 us (31%)
  waiting for transfers between devices  8.66 us (18%)
  local copies, waits for them, and re-layouts  1.45 us (3%)
  between operations  0.87 us (2%)
    ppermute x17, starting transfers between devices, swap(): return lax.ppermute(x, axes, [(i, i ^ mask) for i in range(size)])  15.5 us
    ppermute x17, waiting for transfers between devices, swap(): return lax.ppermute(x, axes, [(i, i ^ mask) for i in range(size)])  8.66 us
    pallas_call x3, Pallas kernels, gram_part(): pl.pallas_call(functools.partial(gram_kernel, lanes, scale, last), out_sh...  6.62 us
    pallas_call x3, Pallas kernels, pack(): pl.pallas_call(functools.partial(pack_kernel, jobs, parts, first, len(aft...  6.19 us
    pallas_call x1, Pallas kernels, mode_fields(): pl.pallas_call(functools.partial(mode_kernel, len(spectra), share), out_s...  5.1 us
    pallas_call x3, Pallas kernels, spectrum(): pl.pallas_call(functools.partial(spectrum_kernel, lanes), out_shape=jax.S...  4.02 us
    unnamed x20, local copies, waits for them, and re-layouts  1.44 us
  transfers between devices with their start and end apart: 17, of which 6 were waited for; matrix products, arithmetic and copies ran while one was open for 0% of the time, Pallas kernels for 28%

profile of v12, /device:TPU:0, one launch (start us, length us, event | category | flops | bytes accessed | tf_op | source)
XLA Modules:
  0.0 49.1 jit_solution(12123227484047906409)
XLA Ops:
  0.6 2.2 %shard_map.95 = (bf16[384,256]{1,0:T(8,128)(2,1)}, bf16[256,256]{1,0:T(8,128)(2,1)}) custom-call(s32[1,4]{1,0:T(1,128)} %table_hbm.1, bf16[384,4,512]{2,1,0:T(4,128)(2,1)} %x_hbm.5), custom_call_target="tpu_custom_call" | custom-call | flops 1000 | bytes 1000 | tf_op jit(solution)/shard_map/pallas_call | solution.py:150
  2.8 0.0 copy-start.9
  2.8 0.0 copy-start.4
  2.9 2.5 %collective-permute-start = (bf16[384,256]{1,0:T(8,128)(2,1)}, bf16[384,256]{1,0:T(8,128)(2,1)S(1)}, u32[]{:S(2)}, u32[]{:S(2)}) collective-permute-start(bf16[384,256]{1,0:T(8,128)(2,1)} %get-tuple-element.24), channel_id=1, source_target_pairs={{0,24},{8,16},{16,8},{24,0},{1,25},{9,17},{17,9},{25,1},{2,26},{10... | collective-permute-start | bytes 589832 | tf_op jit(solution)/shard_map/ppermute | solution.py:531
  5.3 0.0 copy-start.1
  5.3 0.0 copy-start.7
  5.3 0.0 copy-start.8
  5.3 3.0 %shard_map.97 = (bf16[384,256]{1,0:T(8,128)(2,1)}, bf16[384,256]{1,0:T(8,128)(2,1)}, bf16[384,256]{1,0:T(8,128)(2,1)}, bf16[384,128]{1,0:T(8,128)(2,1)}, bf16[38...) custom-call(bf16[256,256]{1,0:T(8,128)(2,1)} %get-tuple-element.23.table_hbm, ...), custom_call_target="tpu_custom_call" | custom-call | flops 1000 | bytes 1000 | tf_op jit(solution)/shard_map/pallas_call | solution.py:150
  8.3 0.7 %collective-permute-start.7 = (bf16[384,256]{1,0:T(8,128)(2,1)}, bf16[384,256]{1,0:T(8,128)(2,1)S(1)}, u32[]{:S(2)}, u32[]{:S(2)}) collective-permute-start(bf16[384,256]{1,0:T(8,128)(2,1)} %get-tuple-element.34), channel_id=1, source_target_pairs={{0,16},{8,24},{16,0},{24,8},{1,17},{9,25},{17,1},{25,9},{2,18},{10... | collective-permute-start | bytes 589832 | tf_op jit(solution)/shard_map/ppermute | solution.py:531
  9.0 0.1 collective-permute-start.8
  9.2 1.4 %collective-permute-start.4 = (bf16[384,128]{1,0:T(8,128)(2,1)}, bf16[384,128]{1,0:T(8,128)(2,1)S(1)}, u32[]{:S(2)}, u32[]{:S(2)}) collective-permute-start(bf16[384,128]{1,0:T(8,128)(2,1)} %get-tuple-element.30), channel_id=1, source_target_pairs={{0,24},{8,16},{16,8},{24,0},{1,25},{9,17},{17,9},{25,1},{2,26},{10... | collective-permute-start | bytes 294920 | tf_op jit(solution)/shard_map/ppermute | solution.py:531
  10.6 0.6 %collective-permute-start.5 = (bf16[384,128]{1,0:T(8,128)(2,1)}, bf16[384,128]{1,0:T(8,128)(2,1)S(1)}, u32[]{:S(2)}, u32[]{:S(2)}) collective-permute-start(bf16[384,128]{1,0:T(8,128)(2,1)} %get-tuple-element.31), channel_id=1, source_target_pairs={{0,16},{8,24},{16,0},{24,8},{1,17},{9,25},{17,1},{25,9},{2,18},{10... | collective-permute-start | bytes 294920 | tf_op jit(solution)/shard_map/ppermute | solution.py:531
  11.2 0.0 copy-done.9
  11.2 0.0 collective-permute-done.refs_0_.refs_1_
  11.2 0.1 collective-permute-start.6
  11.2 0.0 copy-done.4
  11.3 0.0 copy-start
  11.3 1.4 %copy-done = bf16[384,4,512]{2,1,0:T(4,128)(2,1)S(1)} copy-done((bf16[384,4,512]{2,1,0:T(4,128)(2,1)S(1)}, bf16[384,4,512]{2,1,0:T(4,128)(2,1)}, u32[]{:S(2)}) %copy-start) | copy-done | bytes 1572888
  12.7 0.0 copy-start.3
  12.7 1.0 %shard_map.96 = (bf16[384,128]{1,0:T(8,128)(2,1)S(1)}, bf16[384,128]{1,0:T(8,128)(2,1)S(1)}, bf16[384,128]{1,0:T(8,128)(2,1)S(1)}, bf16[384,128]{1,0:T(8,128)(2,1)S(1)}) custom-call(bf16[256,256]{1,0:T(8,128)(2,1)S(1)} %copy-done.4, bf16[384,4,512]{2,1,0:T(4,128)(2,1)S(1)} %copy-done, bf16[384,256]{1,0:T(8,128)(2,1)S(1)} %collective-permute-done.refs_0_.refs_1_), custom_call_target="tpu_custom_call" | custom-call | flops 1000 | bytes 1000 | tf_op jit(solution)/shard_map/pallas_call | solution.py:150
  13.7 2.7 %collective-permute-done.7.refs_2_ = bf16[384,256]{1,0:T(8,128)(2,1)S(1)} collective-permute-done((bf16[384,256]{1,0:T(8,128)(2,1)}, bf16[384,256]{1,0:T(8,128)(2,1)S(1)}, u32[]{:S(2)}, u32[]{:S(2)}) %collective-permute-start.7) | collective-permute-done | bytes 196640 | tf_op jit(solution)/shard_map/ppermute | solution.py:531
  16.4 0.8 %collective-permute-start.1 = (bf16[384,128]{1,0:T(8,128)(2,1)S(1)}, bf16[384,128]{1,0:T(8,128)(2,1)S(1)}, u32[]{:S(2)}, u32[]{:S(2)}) collective-permute-start(bf16[384,128]{1,0:T(8,128)(2,1)S(1)} %get-tuple-element.26), channel_id=1, source_target_pairs={{0,24},{8,16},{16,8},{24,0},{1,25},{9,17},{17,9},{25,1},{2,26},{10... | collective-permute-start | bytes 294920 | tf_op jit(solution)/shard_map/ppermute | solution.py:531
  17.2 0.0 collective-permute-done.8.refs_3_
  17.2 0.4 collective-permute-start.2
  17.6 0.0 copy-done.1
  17.6 0.0 copy-done.2
  17.6 0.0 copy-done.7
  17.6 0.0 copy-done.8
  17.6 0.0 copy-done.3
  17.6 2.7 %shard_map.98.refs_4_ = f32[128,128]{1,0:T(8,128)S(1)} custom-call(s32[4]{0:T(128)S(1)} %copy-done.7, s32[11]{0:T(128)S(1)} %copy-done.8, f32[1,256]{1,0:T(1,128)S(1)} %slice.14.w_ref, bf16[512,256]{1,0:T(8,128)(2,1)S(1)} %copy-done.1, bf16[2816,128]{1,0:T(8,128)(2,1)S(1)} %copy-done.2, bf16[384,256]{1,0:T(8,128)(2,1)S(1)} %copy-done.3, ...), custom_call_target="tpu_custom_call" | custom-call | flops 1000 | bytes 1000 | tf_op jit(solution)/shard_map/pallas_call | solution.py:256
  20.3 0.0 collective-permute-done.4.refs_1_
  20.3 0.8 %collective-permute-start.3 = (bf16[384,128]{1,0:T(8,128)(2,1)S(1)}, bf16[384,128]{1,0:T(8,128)(2,1)S(1)}, u32[]{:S(2)}, u32[]{:S(2)}) collective-permute-start(bf16[384,128]{1,0:T(8,128)(2,1)S(1)} %get-tuple-element.28), channel_id=1, source_target_pairs={{0,8},{8,0},{16,24},{24,16},{1,9},{9,1},{17,25},{25,17},{2,10},{10... | collective-permute-start | bytes 294920 | tf_op jit(solution)/shard_map/ppermute | solution.py:531
  21.1 0.0 copy-start.5
  21.1 1.6 %shard_map.99.refs_5_.refs_0_ = f32[22,128,256]{2,1,0:T(8,128)S(1)} custom-call(s32[4]{0:T(128)S(1)} %copy-done.7, s32[11]{0:T(128)S(1)} %copy-done.8, bf16[512,256]{1,0:T(8,128)(2,1)S(1)} %copy-done.1, bf16[384,256]{1,0:T(8,128)(2,1)S(1)} %copy-done.3, bf16[384,256]{1,0:T(8,128)(2,1)S(1)} %collective-permute-done.refs_0_.refs_1_, ...), custom_call_target="tpu_custom_call" | custom-call | flops 1000 | bytes 1000 | tf_op jit(solution)/shard_map/pallas_call | solution.py:295
  22.7 0.0 collective-permute-done.5.refs_2_
  22.7 0.0 collective-permute-done.6.refs_3_
  22.7 0.0 copy-done.5
  22.7 2.2 %shard_map.100.refs_4_.before_ref = f32[128,128]{1,0:T(8,128)S(1)} custom-call(s32[4]{0:T(128)S(1)} %copy-done.7, s32[11]{0:T(128)S(1)} %copy-done.8, f32[1,128]{1,0:T(1,128)S(1)} %get-tuple-element.46.w_ref, bf16[512,256]{1,0:T(8,128)(2,1)S(1)} %copy-done.1, bf16[2816,128]{1,0:T(8,128)(2,1)S(1)} %copy-done.2, bf16[384,128]{1,0:T(8,128)(2,1)S(1)} %copy-done.5, ...), custom_call_target="tpu_custom_call" | custom-call | flops 1000 | bytes 1000 | tf_op jit(solution)/shard_map/pallas_call | solution.py:256
  24.9 0.0 collective-permute-done.1.refs_1_
  24.9 0.0 collective-permute-done.2.refs_2_
  25.0 0.0 collective-permute-done.3.refs_3_
  25.0 1.7 %shard_map.101 = (bf16[64,128]{1,0:T(8,128)(2,1)S(1)}, f32[22,128,128]{2,1,0:T(8,128)S(1)}) custom-call(s32[4]{0:T(128)S(1)} %copy-done.7, s32[11]{0:T(128)S(1)} %copy-done.8, f32[1,128]{1,0:T(1,128)S(1)} %get-tuple-element.47.w_ref, bf16[512,256]{1,0:T(8,128)(2,1)S(1)} %copy-done.1, bf16[2816,128]{1,0:T(8,128)(2,1)S(1)} %copy-done.2, ...), custom_call_target="tpu_custom_call" | custom-call | flops 1000 | bytes 1000 | tf_op jit(solution)/shard_map/pallas_call | solution.py:256
  26.7 0.1 collective-permute-start.9
  26.8 0.7 %shard_map.102.refs_4_ = bf16[64,128]{1,0:T(8,128)(2,1)S(1)} custom-call(f32[22,128,128]{2,1,0:T(8,128)S(1)} %get-tuple-element.36.s_ref, bf16[2816,128]{1,0:T(8,128)(2,1)S(1)} %copy-done.2, f32[128,128]{1,0:T(8,128)S(1)} %shard_map.100.refs_4_.before_ref), custom_call_target="tpu_custom_call" | custom-call | flops 1000000000 | bytes 3000000 | tf_op jit(solution)/shard_map/pallas_call | solution.py:274
  27.5 0.5 collective-permute-done.9
  28.0 2.1 %collective-permute-start.12 = (bf16[64,128]{1,0:T(8,128)(2,1)S(1)}, bf16[64,128]{1,0:T(8,128)(2,1)S(1)}, u32[]{:S(2)}, u32[]{:S(2)}) collective-permute-start(bf16[64,128]{1,0:T(8,128)(2,1)S(1)} %add_convert_fusion), channel_id=1, source_target_pairs={{0,17},{1,16},{2,19},{3,18},{4,21},{5,20},{6,23},{7,22},{8,25},{9,... | collective-permute-start | bytes 49160 | tf_op jit(solution)/shard_map/ppermute | solution.py:531
  30.1 0.5 %collective-permute-start.11 = (bf16[64,128]{1,0:T(8,128)(2,1)S(1)}, bf16[64,128]{1,0:T(8,128)(2,1)S(1)}, u32[]{:S(2)}, u32[]{:S(2)}) collective-permute-start(bf16[64,128]{1,0:T(8,128)(2,1)S(1)} %add_convert_fusion), channel_id=1, source_target_pairs={{0,1},{1,0},{2,3},{3,2},{4,5},{5,4},{6,7},{7,6},{8,9},{9,8},{10,11... | collective-permute-start | bytes 49160 | tf_op jit(solution)/shard_map/ppermute | solution.py:531
  30.6 0.9 %collective-permute-start.10 = (bf16[64,128]{1,0:T(8,128)(2,1)S(1)}, bf16[64,128]{1,0:T(8,128)(2,1)S(1)}, u32[]{:S(2)}, u32[]{:S(2)}) collective-permute-start(bf16[64,128]{1,0:T(8,128)(2,1)S(1)} %add_convert_fusion), channel_id=1, source_target_pairs={{0,16},{1,17},{2,18},{3,19},{4,20},{5,21},{6,22},{7,23},{8,24},{9,... | collective-permute-start | bytes 49160 | tf_op jit(solution)/shard_map/ppermute | solution.py:531
  31.5 1.2 %shard_map.103.refs_1_ = f32[22,128,128]{2,1,0:T(8,128)S(1)} custom-call(s32[4]{0:T(128)S(1)} %copy-done.7, s32[11]{0:T(128)S(1)} %copy-done.8, bf16[512,256]{1,0:T(8,128)(2,1)S(1)} %copy-done.1, bf16[384,128]{1,0:T(8,128)(2,1)S(1)} %copy-done.5, bf16[384,128]{1,0:T(8,128)(2,1)S(1)} %collective-permute-done.4.refs_1_, ...), custom_call_target="tpu_custom_call" | custom-call | flops 1000 | bytes 1000 | tf_op jit(solution)/shard_map/pallas_call | solution.py:295
  32.7 0.0 copy-start.6
  32.7 0.0 collective-permute-done.12
  32.7 1.1 %collective-permute-done.11 = bf16[64,128]{1,0:T(8,128)(2,1)S(1)} collective-permute-done((bf16[64,128]{1,0:T(8,128)(2,1)S(1)}, bf16[64,128]{1,0:T(8,128)(2,1)S(1)}, u32[]{:S(2)}, u32[]{:S(2)}) %collective-permute-start.11) | collective-permute-done | bytes 16416 | tf_op jit(solution)/shard_map/ppermute | solution.py:531
  33.8 0.5 %collective-permute-done.10 = bf16[64,128]{1,0:T(8,128)(2,1)S(1)} collective-permute-done((bf16[64,128]{1,0:T(8,128)(2,1)S(1)}, bf16[64,128]{1,0:T(8,128)(2,1)S(1)}, u32[]{:S(2)}, u32[]{:S(2)}) %collective-permute-start.10) | collective-permute-done | bytes 16416 | tf_op jit(solution)/shard_map/ppermute | solution.py:531
  34.4 3.7 %collective-permute-start.14 = (bf16[64,128]{1,0:T(8,128)(2,1)S(1)}, bf16[64,128]{1,0:T(8,128)(2,1)S(1)}, u32[]{:S(2)}, u32[]{:S(2)}) collective-permute-start(bf16[64,128]{1,0:T(8,128)(2,1)S(1)} %add_add_fusion.1), channel_id=1, source_target_pairs={{0,6},{1,7},{2,4},{3,5},{4,2},{5,3},{6,0},{7,1},{8,14},{9,15},{10,... | collective-permute-start | bytes 49160 | tf_op jit(solution)/shard_map/ppermute | solution.py:531
  38.0 0.0 collective-permute-start.13
  38.0 0.8 %collective-permute-start.15 = (bf16[64,128]{1,0:T(8,128)(2,1)S(1)}, bf16[64,128]{1,0:T(8,128)(2,1)S(1)}, u32[]{:S(2)}, u32[]{:S(2)}) collective-permute-start(bf16[64,128]{1,0:T(8,128)(2,1)S(1)} %add_add_fusion.1), channel_id=1, source_target_pairs={{0,2},{1,3},{2,0},{3,1},{4,6},{5,7},{6,4},{7,5},{8,10},{9,11},{10,... | collective-permute-start | bytes 49160 | tf_op jit(solution)/shard_map/ppermute | solution.py:531
  38.8 1.2 %shard_map.104.refs_2_ = f32[22,128,128]{2,1,0:T(8,128)S(1)} custom-call(s32[4]{0:T(128)S(1)} %copy-done.7, s32[11]{0:T(128)S(1)} %copy-done.8, bf16[512,256]{1,0:T(8,128)(2,1)S(1)} %copy-done.1, bf16[384,128]{1,0:T(8,128)(2,1)S(1)} %get-tuple-element.25.refs_0_, bf16[384,128]{1,0:T(8,128)(2,1)S(1)} %collective-permute-done.1.refs_1_, ...), custom_call_target="tpu_custom_call" | custom-call | flops 1000 | bytes 1000 | tf_op jit(solution)/shard_map/pallas_call | solution.py:295
  40.0 0.0 collective-permute-done.14
  40.0 2.6 %collective-permute-done.13 = bf16[64,128]{1,0:T(8,128)(2,1)S(1)} collective-permute-done((bf16[64,128]{1,0:T(8,128)(2,1)S(1)}, bf16[64,128]{1,0:T(8,128)(2,1)S(1)}, u32[]{:S(2)}, u32[]{:S(2)}) %collective-permute-start.13) | collective-permute-done | bytes 16416 | tf_op jit(solution)/shard_map/ppermute | solution.py:531
  42.7 0.0 collective-permute-done.15
  42.7 0.1 collective-permute-start.16
  42.8 1.2 %collective-permute-done.16.other_ref = f32[64,128]{1,0:T(8,128)S(1)} collective-permute-done((f32[64,128]{1,0:T(8,128)S(1)}, f32[64,128]{1,0:T(8,128)S(1)}, u32[]{:S(2)}, u32[]{:S(2)}) %collective-permute-start.16) | collective-permute-done | bytes 32800 | tf_op jit(solution)/shard_map/ppermute | solution.py:531
  44.0 0.0 copy-done.6
  44.0 5.1 %shard_map.105 = (bf16[2,11,128,512]{3,2,1,0:T(8,128)(2,1)}, f32[11,11,2,16]{3,2,1,0:T(2,128)}) custom-call(f32[64,128]{1,0:T(8,128)S(1)} %add_add_fusion.half_ref, f32[64,128]{1,0:T(8,128)S(1)} %collective-permute-done.16.other_ref, bf16[2,128,256]{2,1,0:T(8,128)(2,1)S(1)} %copy-done.6, f32[22,128,256]{2,1,0:T(8,128)S(1)} %shard_map.99.refs_5_.refs_0_, ...), custom_call_target="tpu_custom_call" | custom-call | tf_op jit(solution)/shard_map/pallas_call | solution.py:505
  (6 shorter events, 0.0 us)
Async XLA Ops:
  2.8 8.3 %copy-start.9 = (f32[512]{0:T(512)S(1)}, f32[512]{0:T(512)}, u32[]{:S(2)}) copy-start(f32[512]{0:T(512)} %param.9) | copy-start | bytes 6148
  2.8 8.4 %copy-start.4 = (bf16[256,256]{1,0:T(8,128)(2,1)S(1)}, bf16[256,256]{1,0:T(8,128)(2,1)}, u32[]{:S(2)}) copy-start(bf16[256,256]{1,0:T(8,128)(2,1)} %get-tuple-element.23.table_hbm) | copy-start | bytes 393220
  2.9 8.3 %collective-permute-start = (bf16[384,256]{1,0:T(8,128)(2,1)}, bf16[384,256]{1,0:T(8,128)(2,1)S(1)}, u32[]{:S(2)}, u32[]{:S(2)}) collective-permute-start(bf16[384,256]{1,0:T(8,128)(2,1)} %get-tuple-element.24), channel_id=1, source_target_pairs={{0,24},{8,16},{16,8},{24,0},{1,25},{9,17},{17,9},{25,1},{2,26},{10... | collective-permute-start | bytes 589832 | tf_op jit(solution)/shard_map/ppermute | solution.py:531
  5.3 12.3 %copy-start.1 = (bf16[512,256]{1,0:T(8,128)(2,1)S(1)}, bf16[512,256]{1,0:T(8,128)(2,1)}, u32[]{:S(2)}) copy-start(bf16[512,256]{1,0:T(8,128)(2,1)} %constant.6.clone.f_ref) | copy-start | bytes 786436
  5.3 12.3 %copy-start.2 = (bf16[2816,128]{1,0:T(8,128)(2,1)S(1)}, bf16[2816,128]{1,0:T(8,128)(2,1)}, u32[]{:S(2)}) copy-start(bf16[2816,128]{1,0:T(8,128)(2,1)} %constant.7.clone.pick_ref) | copy-start | bytes 2162692
  5.3 12.3 %copy-start.7 = (s32[4]{0:T(128)S(1)}, s32[4]{0:T(128)}, u32[]{:S(2)}) copy-start(s32[4]{0:T(128)} %order_ref.11) | copy-start | bytes 52
  5.3 12.3 %copy-start.8 = (s32[11]{0:T(128)S(1)}, s32[11]{0:T(128)}, u32[]{:S(2)}) copy-start(s32[11]{0:T(128)} %offsets_ref.11) | copy-start | bytes 136
  8.3 8.1 %collective-permute-start.7 = (bf16[384,256]{1,0:T(8,128)(2,1)}, bf16[384,256]{1,0:T(8,128)(2,1)S(1)}, u32[]{:S(2)}, u32[]{:S(2)}) collective-permute-start(bf16[384,256]{1,0:T(8,128)(2,1)} %get-tuple-element.34), channel_id=1, source_target_pairs={{0,16},{8,24},{16,0},{24,8},{1,17},{9,25},{17,1},{25,9},{2,18},{10... | collective-permute-start | bytes 589832 | tf_op jit(solution)/shard_map/ppermute | solution.py:531
  9.0 8.2 %collective-permute-start.8 = (bf16[384,256]{1,0:T(8,128)(2,1)}, bf16[384,256]{1,0:T(8,128)(2,1)S(1)}, u32[]{:S(2)}, u32[]{:S(2)}) collective-permute-start(bf16[384,256]{1,0:T(8,128)(2,1)} %get-tuple-element.35), channel_id=1, source_target_pairs={{0,8},{8,0},{16,24},{24,16},{1,9},{9,1},{17,25},{25,17},{2,10},{10... | collective-permute-start | bytes 589832 | tf_op jit(solution)/shard_map/ppermute | solution.py:531
  9.2 11.1 %collective-permute-start.4 = (bf16[384,128]{1,0:T(8,128)(2,1)}, bf16[384,128]{1,0:T(8,128)(2,1)S(1)}, u32[]{:S(2)}, u32[]{:S(2)}) collective-permute-start(bf16[384,128]{1,0:T(8,128)(2,1)} %get-tuple-element.30), channel_id=1, source_target_pairs={{0,24},{8,16},{16,8},{24,0},{1,25},{9,17},{17,9},{25,1},{2,26},{10... | collective-permute-start | bytes 294920 | tf_op jit(solution)/shard_map/ppermute | solution.py:531
  10.6 12.1 %collective-permute-start.5 = (bf16[384,128]{1,0:T(8,128)(2,1)}, bf16[384,128]{1,0:T(8,128)(2,1)S(1)}, u32[]{:S(2)}, u32[]{:S(2)}) collective-permute-start(bf16[384,128]{1,0:T(8,128)(2,1)} %get-tuple-element.31), channel_id=1, source_target_pairs={{0,16},{8,24},{16,0},{24,8},{1,17},{9,25},{17,1},{25,9},{2,18},{10... | collective-permute-start | bytes 294920 | tf_op jit(solution)/shard_map/ppermute | solution.py:531
  11.2 11.5 %collective-permute-start.6 = (bf16[384,128]{1,0:T(8,128)(2,1)}, bf16[384,128]{1,0:T(8,128)(2,1)S(1)}, u32[]{:S(2)}, u32[]{:S(2)}) collective-permute-start(bf16[384,128]{1,0:T(8,128)(2,1)} %get-tuple-element.32), channel_id=1, source_target_pairs={{0,8},{8,0},{16,24},{24,16},{1,9},{9,1},{17,25},{25,17},{2,10},{10... | collective-permute-start | bytes 294920 | tf_op jit(solution)/shard_map/ppermute | solution.py:531
  11.3 1.4 %copy-start = (bf16[384,4,512]{2,1,0:T(4,128)(2,1)S(1)}, bf16[384,4,512]{2,1,0:T(4,128)(2,1)}, u32[]{:S(2)}) copy-start(bf16[384,4,512]{2,1,0:T(4,128)(2,1)} %x_hbm.5) | copy-start | bytes 4718596
  12.7 4.9 %copy-start.3 = (bf16[384,256]{1,0:T(8,128)(2,1)S(1)}, bf16[384,256]{1,0:T(8,128)(2,1)}, u32[]{:S(2)}) copy-start(bf16[384,256]{1,0:T(8,128)(2,1)} %get-tuple-element.33.refs_0_) | copy-start | bytes 589828
  16.4 8.5 %collective-permute-start.1 = (bf16[384,128]{1,0:T(8,128)(2,1)S(1)}, bf16[384,128]{1,0:T(8,128)(2,1)S(1)}, u32[]{:S(2)}, u32[]{:S(2)}) collective-permute-start(bf16[384,128]{1,0:T(8,128)(2,1)S(1)} %get-tuple-element.26), channel_id=1, source_target_pairs={{0,24},{8,16},{16,8},{24,0},{1,25},{9,17},{17,9},{25,1},{2,26},{10... | collective-permute-start | bytes 294920 | tf_op jit(solution)/shard_map/ppermute | solution.py:531
  17.2 7.7 %collective-permute-start.2 = (bf16[384,128]{1,0:T(8,128)(2,1)S(1)}, bf16[384,128]{1,0:T(8,128)(2,1)S(1)}, u32[]{:S(2)}, u32[]{:S(2)}) collective-permute-start(bf16[384,128]{1,0:T(8,128)(2,1)S(1)} %get-tuple-element.27), channel_id=1, source_target_pairs={{0,16},{8,24},{16,0},{24,8},{1,17},{9,25},{17,1},{25,9},{2,18},{10... | collective-permute-start | bytes 294920 | tf_op jit(solution)/shard_map/ppermute | solution.py:531
  20.3 4.7 %collective-permute-start.3 = (bf16[384,128]{1,0:T(8,128)(2,1)S(1)}, bf16[384,128]{1,0:T(8,128)(2,1)S(1)}, u32[]{:S(2)}, u32[]{:S(2)}) collective-permute-start(bf16[384,128]{1,0:T(8,128)(2,1)S(1)} %get-tuple-element.28), channel_id=1, source_target_pairs={{0,8},{8,0},{16,24},{24,16},{1,9},{9,1},{17,25},{25,17},{2,10},{10... | collective-permute-start | bytes 294920 | tf_op jit(solution)/shard_map/ppermute | solution.py:531
  21.1 1.6 %copy-start.5 = (bf16[384,128]{1,0:T(8,128)(2,1)S(1)}, bf16[384,128]{1,0:T(8,128)(2,1)}, u32[]{:S(2)}) copy-start(bf16[384,128]{1,0:T(8,128)(2,1)} %get-tuple-element.29.refs_0_) | copy-start | bytes 294916
  26.7 1.2 %collective-permute-start.9 = (bf16[64,128]{1,0:T(8,128)(2,1)S(1)}, bf16[64,128]{1,0:T(8,128)(2,1)S(1)}, u32[]{:S(2)}, u32[]{:S(2)}) collective-permute-start(bf16[64,128]{1,0:T(8,128)(2,1)S(1)} %get-tuple-element.37), channel_id=1, source_target_pairs={{0,8},{1,9},{2,10},{3,11},{4,12},{5,13},{6,14},{7,15},{8,0},{9,1},... | collective-permute-start | bytes 49160 | tf_op jit(solution)/shard_map/ppermute | solution.py:531
  28.0 4.8 %collective-permute-start.12 = (bf16[64,128]{1,0:T(8,128)(2,1)S(1)}, bf16[64,128]{1,0:T(8,128)(2,1)S(1)}, u32[]{:S(2)}, u32[]{:S(2)}) collective-permute-start(bf16[64,128]{1,0:T(8,128)(2,1)S(1)} %add_convert_fusion), channel_id=1, source_target_pairs={{0,17},{1,16},{2,19},{3,18},{4,21},{5,20},{6,23},{7,22},{8,25},{9,... | collective-permute-start | bytes 49160 | tf_op jit(solution)/shard_map/ppermute | solution.py:531
  30.1 3.7 %collective-permute-start.11 = (bf16[64,128]{1,0:T(8,128)(2,1)S(1)}, bf16[64,128]{1,0:T(8,128)(2,1)S(1)}, u32[]{:S(2)}, u32[]{:S(2)}) collective-permute-start(bf16[64,128]{1,0:T(8,128)(2,1)S(1)} %add_convert_fusion), channel_id=1, source_target_pairs={{0,1},{1,0},{2,3},{3,2},{4,5},{5,4},{6,7},{7,6},{8,9},{9,8},{10,11... | collective-permute-start | bytes 49160 | tf_op jit(solution)/shard_map/ppermute | solution.py:531
  30.6 3.7 %collective-permute-start.10 = (bf16[64,128]{1,0:T(8,128)(2,1)S(1)}, bf16[64,128]{1,0:T(8,128)(2,1)S(1)}, u32[]{:S(2)}, u32[]{:S(2)}) collective-permute-start(bf16[64,128]{1,0:T(8,128)(2,1)S(1)} %add_convert_fusion), channel_id=1, source_target_pairs={{0,16},{1,17},{2,18},{3,19},{4,20},{5,21},{6,22},{7,23},{8,24},{9,... | collective-permute-start | bytes 49160 | tf_op jit(solution)/shard_map/ppermute | solution.py:531
  32.7 11.2 %copy-start.6 = (bf16[2,128,256]{2,1,0:T(8,128)(2,1)S(1)}, bf16[2,128,256]{2,1,0:T(8,128)(2,1)}, u32[]{:S(2)}) copy-start(bf16[2,128,256]{2,1,0:T(8,128)(2,1)} %constant.8.clone.spread_ref) | copy-start | bytes 393220
  34.4 5.7 %collective-permute-start.14 = (bf16[64,128]{1,0:T(8,128)(2,1)S(1)}, bf16[64,128]{1,0:T(8,128)(2,1)S(1)}, u32[]{:S(2)}, u32[]{:S(2)}) collective-permute-start(bf16[64,128]{1,0:T(8,128)(2,1)S(1)} %add_add_fusion.1), channel_id=1, source_target_pairs={{0,6},{1,7},{2,4},{3,5},{4,2},{5,3},{6,0},{7,1},{8,14},{9,15},{10,... | collective-permute-start | bytes 49160 | tf_op jit(solution)/shard_map/ppermute | solution.py:531
  38.0 4.6 %collective-permute-start.13 = (bf16[64,128]{1,0:T(8,128)(2,1)S(1)}, bf16[64,128]{1,0:T(8,128)(2,1)S(1)}, u32[]{:S(2)}, u32[]{:S(2)}) collective-permute-start(bf16[64,128]{1,0:T(8,128)(2,1)S(1)} %add_add_fusion.1), channel_id=1, source_target_pairs={{0,4},{1,5},{2,6},{3,7},{4,0},{5,1},{6,2},{7,3},{8,12},{9,13},{10,... | collective-permute-start | bytes 49160 | tf_op jit(solution)/shard_map/ppermute | solution.py:531
  38.0 4.6 %collective-permute-start.15 = (bf16[64,128]{1,0:T(8,128)(2,1)S(1)}, bf16[64,128]{1,0:T(8,128)(2,1)S(1)}, u32[]{:S(2)}, u32[]{:S(2)}) collective-permute-start(bf16[64,128]{1,0:T(8,128)(2,1)S(1)} %add_add_fusion.1), channel_id=1, source_target_pairs={{0,2},{1,3},{2,0},{3,1},{4,6},{5,7},{6,4},{7,5},{8,10},{9,11},{10,... | collective-permute-start | bytes 49160 | tf_op jit(solution)/shard_map/ppermute | solution.py:531
  42.7 1.3 %collective-permute-start.16 = (f32[64,128]{1,0:T(8,128)S(1)}, f32[64,128]{1,0:T(8,128)S(1)}, u32[]{:S(2)}, u32[]{:S(2)}) collective-permute-start(f32[64,128]{1,0:T(8,128)S(1)} %add_add_fusion.half_ref), channel_id=1, source_target_pairs={{0,8},{1,9},{2,10},{3,11},{4,12},{5,13},{6,14},{7,15},{8,0},{9,1},... | collective-permute-start | bytes 98312 | tf_op jit(solution)/shard_map/ppermute | solution.py:531

commit v13 on v12

--- a/solution.py
+++ b/solution.py
@@ -17,6 +17,7 @@
 HALF_ROWS = NBLK * SUB
 GROUPS = NFREQ // SUB
 MATS = 7
+NEAR = 2
 PACKED = 128
 HALF = PACKED // 2
 STACK = 4
@@ -165,16 +166,17 @@
     )(table, snapshots, *after)
 
 
-def fill_record(order_ref, pieces, record, factor):
-    steps, width = pieces[0].shape
+def fill_record(base, order_ref, pieces, record, factor):
+    steps = pieces[0].shape[0]
     me = lax.axis_index("tm")
     for d, piece in enumerate(pieces):
-        partner = me ^ (len(pieces) - d if d else 0)
-        start = pl.multiple_of(order_ref[partner] * steps, steps)
-        for c in range(width // LANE):
-            cols = slice(c * LANE, (c + 1) * LANE)
-            part = piece[:, cols].astype(F32)
-            record[c, pl.ds(start, steps), :] = part if factor is None else part * factor[:, cols]
+        start = pl.multiple_of(order_ref[me ^ d] * steps, steps)
+        for c in range(record.shape[0]):
+            at = c * LANE + (base if d < NEAR else 0)
+            part = piece[:, at : at + LANE].astype(F32)
+            if factor is not None:
+                part = part * factor[:, c * LANE : (c + 1) * LANE]
+            record[c, pl.ds(start, steps), :] = part
 
 
 def transform(offsets_ref, f, record, s_ref):
@@ -222,27 +224,27 @@
     return dot(masked[...], pick_ref[...])
 
 
-def gram_kernel(lanes, scale, last, order_ref, offsets_ref, w_ref, f_ref, pick_ref, *refs):
+def gram_kernel(lanes, base, scale, last, order_ref, offsets_ref, w_ref, f_ref, pick_ref, *refs):
     pieces = refs[:lanes]
     refs = refs[lanes:]
     if last:
-        before_ref, _, gram_ref, s_ref, record, masked = refs
+        before_ref, gram_ref, s_ref, record, masked = refs
     else:
         *before_refs, gram_ref, record, s_ref, masked = refs
-    fill_record(order_ref, pieces, record, jnp.sqrt(w_ref[...]))
+    fill_record(base, order_ref, pieces, record, jnp.sqrt(w_ref[...]))
     transform(offsets_ref, f_ref[:NFFT] if last else f_ref[...], record, s_ref)
     if not last:
         total = gram_rows(0, GROUPS, s_ref, pick_ref, masked) * scale
         gram_ref[...] = total + before_refs[0][...] if before_refs else total
         return
-    base = pl.multiple_of((1 - lax.axis_index("tm") % 2) * HALF, HALF)
-    total = gram_rows(base, GROUPS // 2, s_ref, pick_ref, masked) * scale
-    gram_ref[...] = (total + before_ref[pl.ds(base, HALF), :]).astype(BF16)
-
-
-def gram_part(order, offsets, weights, tables, pieces, before, last, scale):
+    half = pl.multiple_of((1 - lax.axis_index("tm") % 2) * HALF, HALF)
+    total = gram_rows(half, GROUPS // 2, s_ref, pick_ref, masked) * scale
+    gram_ref[...] = (total + before_ref[pl.ds(half, HALF), :]).astype(BF16)
+
+
+def gram_part(order, offsets, weights, tables, pieces, before, base, last, scale):
     lanes = len(pieces)
-    steps, width = pieces[0].shape
+    steps, width = pieces[-1].shape
     args = [order, offsets, weights, *tables, *pieces, *before]
     spectrum_shape = (2 * NBLK, NFREQ, width)
     scratch = [pltpu.VMEM((width // LANE, lanes * steps, LANE), F32)]
@@ -254,7 +256,7 @@
         scratch.append(pltpu.VMEM(spectrum_shape, F32))
     scratch.append(pltpu.VMEM((HALF if last else NFREQ, NBLK * WIDE), BF16))
     return pl.pallas_call(
-        functools.partial(gram_kernel, lanes, scale, last),
+        functools.partial(gram_kernel, lanes, base, scale, last),
         out_shape=outs,
         in_specs=[SMEM, SMEM] + [VMEM] * (len(args) - 2),
         out_specs=[VMEM] * len(outs),
@@ -282,18 +284,18 @@
     )(scaled, pick, before)
 
 
-def spectrum_kernel(lanes, order_ref, offsets_ref, f_ref, *refs):
+def spectrum_kernel(lanes, base, order_ref, offsets_ref, f_ref, *refs):
     s_ref, record = refs[-2:]
-    fill_record(order_ref, refs[:lanes], record, None)
+    fill_record(base, order_ref, refs[:lanes], record, None)
     transform(offsets_ref, f_ref[...], record, s_ref)
 
 
-def spectrum(order, offsets, fourier, pieces, after):
+def spectrum(order, offsets, fourier, pieces, base, after):
     lanes = len(pieces)
-    steps, width = pieces[0].shape
+    steps, width = pieces[-1].shape
     args = [order, offsets, fourier, *pieces, *after]
     return pl.pallas_call(
-        functools.partial(spectrum_kernel, lanes),
+        functools.partial(spectrum_kernel, lanes, base),
         out_shape=jax.ShapeDtypeStruct((2 * NBLK, NFREQ, width), F32),
         in_specs=[SMEM, SMEM] + [VMEM] * (len(args) - 2),
         out_specs=VMEM,
@@ -545,33 +547,40 @@
     tables = (jnp.asarray(fourier_tables()), jnp.asarray(pick_table()))
     weights = weights.reshape(1, -1)
 
-    first, table = pack(owner, snapshots, [(*chunks[0], lanes - 1, lanes)], True)
-    moved = [swap(first, "tm", lanes - 1, lanes)]
-    jobs = [(*chunks[0], 0, lanes - 1), (*chunks[1], 0, lanes)]
-    rest = list(pack(table, snapshots, jobs, False))
-    moved += [swap(rest[d], "tm", d, lanes) for d in reversed(range(1, lanes - 1))]
-    arrived = [[rest[0]] + moved]
-    for packed in (rest[lanes - 1 :], None):
-        if packed is None:
-            packed = pack(table, snapshots, [(*chunks[2], 0, lanes)], False, moved[:1])
-        arrived.append([packed[0]])
-        arrived[-1] += [swap(packed[d], "tm", d, lanes) for d in reversed(range(1, lanes))]
+    def send(packed, begin, end):
+        return [swap(p, "tm", d, lanes) for d, p in zip(range(begin, end), packed)]
+
+    c0, c1, c2 = chunks
+    first, table = pack(owner, snapshots, [(*c0, lanes - 1, lanes)], True)
+    first = send([first], lanes - 1, lanes)
+    middle = pack(table, snapshots, [(*c0, 0, lanes - 1), (*c1, NEAR, lanes)], False)
+    jobs = [(c1[0], c1[1] + c2[1], 0, NEAR), (*c2, NEAR, lanes)]
+    rest = pack(table, snapshots, jobs, False, first)
+    near = [rest[0], *send(rest[1:], 1, NEAR)]
+    arrived = [
+        [middle[0], *send(middle[1:], 1, lanes - 1), *first],
+        [*near, *send(middle[lanes - 1 :], NEAR, lanes)],
+        [*near, *send(rest[NEAR:], NEAR, lanes)],
+    ]
+    starts = (0, 0, c1[1])
 
     axes = ("tm", "sx", "sy")
     size = lanes * groups
     bits = [b * groups for b in powers(lanes)] + powers(groups)
     parts = [weights[:, base : base + width] for base, width in chunks]
-    (total,) = gram_part(block_order, offsets, parts[0], tables, arrived[0], [], False, scale)
-    spectra = [spectrum(block_order, offsets, tables[0], arrived[0], [total])]
-    before = [total, spectra[0]]
-    before = gram_part(block_order, offsets, parts[1], tables, arrived[1], before, False, scale)
-    send, scaled = gram_part(
-        block_order, offsets, parts[2], tables, arrived[2], [*before, spectra[0]], True, scale
-    )
-
-    other = swap(send, axes, bits[0], size)
+    before = []
+    for at, base in enumerate(starts):
+        last = at == len(chunks) - 1
+        args = (block_order, offsets, parts[at], tables, arrived[at], before, base, last, scale)
+        before, before_last = gram_part(*args), before
+    before, (given, scaled) = before_last, before
+
+    other = swap(given, axes, bits[0], size)
     keep = own_part(scaled, tables[1], before[0], scale)
-    spectra += [spectrum(block_order, offsets, tables[0], a, [keep]) for a in arrived[1:]]
+    spectra = [
+        spectrum(block_order, offsets, tables[0], pieces, base, [keep])
+        for base, pieces in zip(starts, arrived)
+    ]
     half = keep.astype(F32) + other.astype(F32)
     for at in range(1, len(bits), 2):
         masks = bits[at : at + 2]
@@ -585,8 +594,8 @@
             terms = [a + b for a, b in zip(terms[::2], terms[1::2])]
         half = terms[0]
         if at == 1:
-            half, spectra[1] = lax.optimization_barrier((half, spectra[1]))
-    half, spectra[2] = lax.optimization_barrier((half, spectra[2]))
+            half, *spectra[1:] = lax.optimization_barrier((half, *spectra[1:]))
+    half, spectra[0] = lax.optimization_barrier((half, spectra[0]))
     other = swap(half, axes, bits[0], size)
 
     spread = jnp.asarray(spread_table())

time: 49.3 us -> 49 us (level)
  waiting for transfers between devices: 8.66 us -> 7.53 us
  starting transfers between devices: 15.5 us -> 16.5 us
    ppermute x17 -> x16, waiting for transfers between devices: 8.66 us -> 7.53 us  [swap(): return lax.ppermute(x, axes, [(i, i ^ mask) for i in range(size)])]
    ppermute x17 -> x16, starting transfers between devices: 15.5 us -> 16.5 us  [swap(): return lax.ppermute(x, axes, [(i, i ^ mask) for i in range(size)])]
    unnamed x20 -> x18, local copies, waits for them, and re-layouts: 1.44 us -> 1.44 us
  transfers between devices with their start and end apart: 17 -> 16, of which waited for: 6 -> 8; matrix products, arithmetic and copies ran while one was open for 0% -> 0% of each run, Pallas kernels for 28% -> 28%
where the time goes in v13:
time: 49 us; the launch traced here: 48.8 us
  Pallas kernels  22.4 us (46%)
  starting transfers between devices  16.5 us (34%)
  waiting for transfers between devices  7.53 us (15%)
  local copies, waits for them, and re-layouts  1.44 us (3%)
  between operations  0.86 us (2%)
    ppermute x16, starting transfers between devices, swap(): return lax.ppermute(x, axes, [(i, i ^ mask) for i in range(size)])  16.5 us
    ppermute x16, waiting for transfers between devices, swap(): return lax.ppermute(x, axes, [(i, i ^ mask) for i in range(size)])  7.53 us
    pallas_call x3, Pallas kernels, gram_part(): pl.pallas_call(functools.partial(gram_kernel, lanes, base, scale, last),...  6.63 us
    pallas_call x3, Pallas kernels, pack(): pl.pallas_call(functools.partial(pack_kernel, jobs, parts, first, len(aft...  6.04 us
    pallas_call x1, Pallas kernels, mode_fields(): pl.pallas_call(functools.partial(mode_kernel, len(spectra), share), out_s...  5.01 us
    pallas_call x3, Pallas kernels, spectrum(): pl.pallas_call(functools.partial(spectrum_kernel, lanes, base), out_shape...  4.06 us
    unnamed x18, local copies, waits for them, and re-layouts  1.44 us
  transfers between devices with their start and end apart: 16, of which 8 were waited for; matrix products, arithmetic and copies ran while one was open for 0% of the time, Pallas kernels for 28%

profile of v13, /device:TPU:0, one launch (start us, length us, event | category | flops | bytes accessed | tf_op | source)
XLA Modules:
  0.0 48.8 jit_solution(12523621786962805903)
XLA Ops:
  0.6 2.2 %shard_map.95 = (bf16[384,256]{1,0:T(8,128)(2,1)}, bf16[256,256]{1,0:T(8,128)(2,1)}) custom-call(s32[1,4]{1,0:T(1,128)} %table_hbm.1, bf16[384,4,512]{2,1,0:T(4,128)(2,1)} %x_hbm.5), custom_call_target="tpu_custom_call" | custom-call | flops 1000 | bytes 1000 | tf_op jit(solution)/shard_map/pallas_call | solution.py:151
  2.8 0.0 copy-start.4
  2.8 2.5 %collective-permute-start = (bf16[384,256]{1,0:T(8,128)(2,1)}, bf16[384,256]{1,0:T(8,128)(2,1)S(1)}, u32[]{:S(2)}, u32[]{:S(2)}) collective-permute-start(bf16[384,256]{1,0:T(8,128)(2,1)} %get-tuple-element.23), channel_id=1, source_target_pairs={{0,24},{8,16},{16,8},{24,0},{1,25},{9,17},{17,9},{25,1},{2,26},{10... | collective-permute-start | bytes 589832 | tf_op jit(solution)/shard_map/ppermute | solution.py:533
  5.3 0.0 copy-start.8
  5.3 0.0 copy-start.1
  5.3 0.0 copy-start.2
  5.3 0.0 copy-start.6
  5.3 0.0 copy-start.7
  5.3 2.8 %shard_map.97 = (bf16[384,256]{1,0:T(8,128)(2,1)}, bf16[384,256]{1,0:T(8,128)(2,1)}, bf16[384,256]{1,0:T(8,128)(2,1)}, bf16[384,128]{1,0:T(8,128)(2,1)}, bf16[384,128]{1,0:T(8,128)(2,1)}) custom-call(bf16[256,256]{1,0:T(8,128)(2,1)} %get-tuple-element.22.table_hbm, bf16[384,4,512]{2,1,0:T(4,128)(2,1)} %x_hbm.5), custom_call_target="tpu_custom_call" | custom-call | flops 1000 | bytes 1000 | tf_op jit(solution)/shard_map/pallas_call | solution.py:151
  8.2 0.7 %collective-permute-start.6 = (bf16[384,256]{1,0:T(8,128)(2,1)}, bf16[384,256]{1,0:T(8,128)(2,1)S(1)}, u32[]{:S(2)}, u32[]{:S(2)}) collective-permute-start(bf16[384,256]{1,0:T(8,128)(2,1)} %get-tuple-element.31), channel_id=1, source_target_pairs={{0,8},{8,0},{16,24},{24,16},{1,9},{9,1},{17,25},{25,17},{2,10},{10... | collective-permute-start | bytes 589832 | tf_op jit(solution)/shard_map/ppermute | solution.py:533
  8.9 0.0 collective-permute-start.7
  8.9 2.0 %collective-permute-start.4 = (bf16[384,128]{1,0:T(8,128)(2,1)}, bf16[384,128]{1,0:T(8,128)(2,1)S(1)}, u32[]{:S(2)}, u32[]{:S(2)}) collective-permute-start(bf16[384,128]{1,0:T(8,128)(2,1)} %get-tuple-element.28), channel_id=1, source_target_pairs={{0,16},{8,24},{16,0},{24,8},{1,17},{9,25},{17,1},{25,9},{2,18},{10... | collective-permute-start | bytes 294920 | tf_op jit(solution)/shard_map/ppermute | solution.py:533
  11.0 0.0 collective-permute-start.5
  11.0 0.0 collective-permute-done.refs_0_.refs_3_
  11.0 0.0 copy-done.4
  11.0 0.0 copy-start
  11.0 1.4 %copy-done = bf16[384,4,512]{2,1,0:T(4,128)(2,1)S(1)} copy-done((bf16[384,4,512]{2,1,0:T(4,128)(2,1)S(1)}, bf16[384,4,512]{2,1,0:T(4,128)(2,1)}, u32[]{:S(2)}) %copy-start) | copy-done | bytes 1572888
  12.4 0.0 copy-start.3
  12.4 1.0 %shard_map.96 = (bf16[384,256]{1,0:T(8,128)(2,1)S(1)}, bf16[384,256]{1,0:T(8,128)(2,1)S(1)}, bf16[384,128]{1,0:T(8,128)(2,1)S(1)}, bf16[384,128]{1,0:T(8,128)(2,1)S(1)}) custom-call(bf16[256,256]{1,0:T(8,128)(2,1)S(1)} %copy-done.4, bf16[384,4,512]{2,1,0:T(4,128)(2,1)S(1)} %copy-done, bf16[384,256]{1,0:T(8,128)(2,1)S(1)} %collective-permute-done.refs_0_.refs_3_), custom_call_target="tpu_custom_call" | custom-call | flops 1000 | bytes 1000 | tf_op jit(solution)/shard_map/pallas_call | solution.py:151
  13.4 2.4 %collective-permute-start.2 = (bf16[384,128]{1,0:T(8,128)(2,1)S(1)}, bf16[384,128]{1,0:T(8,128)(2,1)S(1)}, u32[]{:S(2)}, u32[]{:S(2)}) collective-permute-start(bf16[384,128]{1,0:T(8,128)(2,1)S(1)} %get-tuple-element.26), channel_id=1, source_target_pairs={{0,16},{8,24},{16,0},{24,8},{1,17},{9,25},{17,1},{25,9},{2,18},{10... | collective-permute-start | bytes 294920 | tf_op jit(solution)/shard_map/ppermute | solution.py:533
  15.8 0.0 collective-permute-done.6.refs_1_
  15.8 0.0 collective-permute-start.3
  15.8 1.1 %collective-permute-done.7.refs_2_ = bf16[384,256]{1,0:T(8,128)(2,1)S(1)} collective-permute-done((bf16[384,256]{1,0:T(8,128)(2,1)}, bf16[384,256]{1,0:T(8,128)(2,1)S(1)}, u32[]{:S(2)}, u32[]{:S(2)}) %collective-permute-start.7) | collective-permute-done | bytes 196640 | tf_op jit(solution)/shard_map/ppermute | solution.py:533
  16.9 0.0 collective-permute-start.1
  16.9 0.0 copy-done.8
  16.9 0.0 copy-done.1
  16.9 0.0 copy-done.2
  16.9 0.0 copy-done.6
  16.9 0.0 copy-done.7
  17.0 0.0 copy-done.3
  17.0 2.7 %shard_map.98.refs_4_ = f32[128,128]{1,0:T(8,128)S(1)} custom-call(s32[4]{0:T(128)S(1)} %copy-done.6, s32[11]{0:T(128)S(1)} %copy-done.7, f32[1,256]{1,0:T(1,128)S(1)} %slice.14.w_ref, bf16[512,256]{1,0:T(8,128)(2,1)S(1)} %copy-done.1, bf16[2816,128]{1,0:T(8,128)(2,1)S(1)} %copy-done.2, bf16[384,256]{1,0:T(8,128)(2,1)S(1)} %copy-done.3, ...), custom_call_target="tpu_custom_call" | custom-call | flops 1000 | bytes 1000 | tf_op jit(solution)/shard_map/pallas_call | solution.py:258
  19.7 0.0 collective-permute-done.4.refs_2_
  19.7 0.0 collective-permute-done.5.refs_3_
  19.7 0.0 collective-permute-done.1.refs_1_
  19.7 2.2 %shard_map.99.refs_4_.before_ref = f32[128,128]{1,0:T(8,128)S(1)} custom-call(s32[4]{0:T(128)S(1)} %copy-done.6, s32[11]{0:T(128)S(1)} %copy-done.7, f32[1,128]{1,0:T(1,128)S(1)} %get-tuple-element.44.w_ref, bf16[512,256]{1,0:T(8,128)(2,1)S(1)} %copy-done.1, bf16[2816,128]{1,0:T(8,128)(2,1)S(1)} %copy-done.2, ...), custom_call_target="tpu_custom_call" | custom-call | flops 1000 | bytes 1000 | tf_op jit(solution)/shard_map/pallas_call | solution.py:258
  21.9 1.3 %collective-permute-done.2.refs_2_ = bf16[384,128]{1,0:T(8,128)(2,1)S(1)} collective-permute-done((bf16[384,128]{1,0:T(8,128)(2,1)S(1)}, bf16[384,128]{1,0:T(8,128)(2,1)S(1)}, u32[]{:S(2)}, u32[]{:S(2)}) %collective-permute-start.2) | collective-permute-done | bytes 98336 | tf_op jit(solution)/shard_map/ppermute | solution.py:533
  23.2 0.4 collective-permute-done.3.refs_3_
  23.6 1.7 %shard_map.100 = (bf16[64,128]{1,0:T(8,128)(2,1)S(1)}, f32[22,128,128]{2,1,0:T(8,128)S(1)}) custom-call(s32[4]{0:T(128)S(1)} %copy-done.6, s32[11]{0:T(128)S(1)} %copy-done.7, f32[1,128]{1,0:T(1,128)S(1)} %get-tuple-element.45.w_ref, bf16[512,256]{1,0:T(8,128)(2,1)S(1)} %copy-done.1, bf16[2816,128]{1,0:T(8,128)(2,1)S(1)} %copy-done.2, ...), custom_call_target="tpu_custom_call" | custom-call | flops 1000 | bytes 1000 | tf_op jit(solution)/shard_map/pallas_call | solution.py:258
  25.3 0.8 %collective-permute-start.8 = (bf16[64,128]{1,0:T(8,128)(2,1)S(1)}, bf16[64,128]{1,0:T(8,128)(2,1)S(1)}, u32[]{:S(2)}, u32[]{:S(2)}) collective-permute-start(bf16[64,128]{1,0:T(8,128)(2,1)S(1)} %get-tuple-element.34), channel_id=1, source_target_pairs={{0,8},{1,9},{2,10},{3,11},{4,12},{5,13},{6,14},{7,15},{8,0},{9,1},... | collective-permute-start | bytes 49160 | tf_op jit(solution)/shard_map/ppermute | solution.py:533
  26.0 0.7 %shard_map.101.refs_4_ = bf16[64,128]{1,0:T(8,128)(2,1)S(1)} custom-call(f32[22,128,128]{2,1,0:T(8,128)S(1)} %get-tuple-element.33.s_ref, bf16[2816,128]{1,0:T(8,128)(2,1)S(1)} %copy-done.2, f32[128,128]{1,0:T(8,128)S(1)} %shard_map.99.refs_4_.before_ref), custom_call_target="tpu_custom_call" | custom-call | flops 1000000000 | bytes 3000000 | tf_op jit(solution)/shard_map/pallas_call | solution.py:276
  26.7 0.2 collective-permute-done.8
  26.9 3.0 %collective-permute-start.11 = (bf16[64,128]{1,0:T(8,128)(2,1)S(1)}, bf16[64,128]{1,0:T(8,128)(2,1)S(1)}, u32[]{:S(2)}, u32[]{:S(2)}) collective-permute-start(bf16[64,128]{1,0:T(8,128)(2,1)S(1)} %add_convert_fusion), channel_id=1, source_target_pairs={{0,17},{1,16},{2,19},{3,18},{4,21},{5,20},{6,23},{7,22},{8,25},{9,... | collective-permute-start | bytes 49160 | tf_op jit(solution)/shard_map/ppermute | solution.py:533
  29.9 0.5 %collective-permute-start.10 = (bf16[64,128]{1,0:T(8,128)(2,1)S(1)}, bf16[64,128]{1,0:T(8,128)(2,1)S(1)}, u32[]{:S(2)}, u32[]{:S(2)}) collective-permute-start(bf16[64,128]{1,0:T(8,128)(2,1)S(1)} %add_convert_fusion), channel_id=1, source_target_pairs={{0,1},{1,0},{2,3},{3,2},{4,5},{5,4},{6,7},{7,6},{8,9},{9,8},{10,11... | collective-permute-start | bytes 49160 | tf_op jit(solution)/shard_map/ppermute | solution.py:533
  30.4 0.1 collective-permute-start.9
  30.5 1.2 %shard_map.103.refs_2_ = f32[22,128,128]{2,1,0:T(8,128)S(1)} custom-call(s32[4]{0:T(128)S(1)} %copy-done.6, s32[11]{0:T(128)S(1)} %copy-done.7, bf16[512,256]{1,0:T(8,128)(2,1)S(1)} %copy-done.1, bf16[384,256]{1,0:T(8,128)(2,1)S(1)} %get-tuple-element.24.refs_0_, bf16[384,256]{1,0:T(8,128)(2,1)S(1)} %collective-permute-done.1.refs_1_, ...), custom_call_target="tpu_custom_call" | custom-call | flops 1000 | bytes 1000 | tf_op jit(solution)/shard_map/pallas_call | solution.py:297
  31.8 1.2 %shard_map.102.refs_1_ = f32[22,128,128]{2,1,0:T(8,128)S(1)} custom-call(s32[4]{0:T(128)S(1)} %copy-done.6, s32[11]{0:T(128)S(1)} %copy-done.7, bf16[512,256]{1,0:T(8,128)(2,1)S(1)} %copy-done.1, bf16[384,256]{1,0:T(8,128)(2,1)S(1)} %get-tuple-element.24.refs_0_, bf16[384,256]{1,0:T(8,128)(2,1)S(1)} %collective-permute-done.1.refs_1_, ...), custom_call_target="tpu_custom_call" | custom-call | flops 1000 | bytes 1000 | tf_op jit(solution)/shard_map/pallas_call | solution.py:297
  33.0 0.0 collective-permute-done.11
  33.0 0.6 %collective-permute-done.10 = bf16[64,128]{1,0:T(8,128)(2,1)S(1)} collective-permute-done((bf16[64,128]{1,0:T(8,128)(2,1)S(1)}, bf16[64,128]{1,0:T(8,128)(2,1)S(1)}, u32[]{:S(2)}, u32[]{:S(2)}) %collective-permute-start.10) | collective-permute-done | bytes 16416 | tf_op jit(solution)/shard_map/ppermute | solution.py:533
  33.6 0.5 %collective-permute-done.9 = bf16[64,128]{1,0:T(8,128)(2,1)S(1)} collective-permute-done((bf16[64,128]{1,0:T(8,128)(2,1)S(1)}, bf16[64,128]{1,0:T(8,128)(2,1)S(1)}, u32[]{:S(2)}, u32[]{:S(2)}) %collective-permute-start.9) | collective-permute-done | bytes 16416 | tf_op jit(solution)/shard_map/ppermute | solution.py:533
  34.2 0.0 copy-start.5
  34.2 3.7 %collective-permute-start.13 = (bf16[64,128]{1,0:T(8,128)(2,1)S(1)}, bf16[64,128]{1,0:T(8,128)(2,1)S(1)}, u32[]{:S(2)}, u32[]{:S(2)}) collective-permute-start(bf16[64,128]{1,0:T(8,128)(2,1)S(1)} %add_add_fusion.1), channel_id=1, source_target_pairs={{0,6},{1,7},{2,4},{3,5},{4,2},{5,3},{6,0},{7,1},{8,14},{9,15},{10,... | collective-permute-start | bytes 49160 | tf_op jit(solution)/shard_map/ppermute | solution.py:533
  37.9 0.0 collective-permute-start.12
  37.9 0.8 %collective-permute-start.14 = (bf16[64,128]{1,0:T(8,128)(2,1)S(1)}, bf16[64,128]{1,0:T(8,128)(2,1)S(1)}, u32[]{:S(2)}, u32[]{:S(2)}) collective-permute-start(bf16[64,128]{1,0:T(8,128)(2,1)S(1)} %add_add_fusion.1), channel_id=1, source_target_pairs={{0,2},{1,3},{2,0},{3,1},{4,6},{5,7},{6,4},{7,5},{8,10},{9,11},{10,... | collective-permute-start | bytes 49160 | tf_op jit(solution)/shard_map/ppermute | solution.py:533
  38.6 1.6 %shard_map.104.refs_0_ = f32[22,128,256]{2,1,0:T(8,128)S(1)} custom-call(s32[4]{0:T(128)S(1)} %copy-done.6, s32[11]{0:T(128)S(1)} %copy-done.7, bf16[512,256]{1,0:T(8,128)(2,1)S(1)} %copy-done.1, bf16[384,256]{1,0:T(8,128)(2,1)S(1)} %copy-done.3, bf16[384,256]{1,0:T(8,128)(2,1)S(1)} %collective-permute-done.6.refs_1_, ...), custom_call_target="tpu_custom_call" | custom-call | flops 1000 | bytes 1000 | tf_op jit(solution)/shard_map/pallas_call | solution.py:297
  40.3 0.0 collective-permute-done.13
  40.3 2.2 %collective-permute-done.12 = bf16[64,128]{1,0:T(8,128)(2,1)S(1)} collective-permute-done((bf16[64,128]{1,0:T(8,128)(2,1)S(1)}, bf16[64,128]{1,0:T(8,128)(2,1)S(1)}, u32[]{:S(2)}, u32[]{:S(2)}) %collective-permute-start.12) | collective-permute-done | bytes 16416 | tf_op jit(solution)/shard_map/ppermute | solution.py:533
  42.5 0.0 collective-permute-done.14
  42.5 0.1 collective-permute-start.15
  42.6 1.2 %collective-permute-done.15.other_ref = f32[64,128]{1,0:T(8,128)S(1)} collective-permute-done((f32[64,128]{1,0:T(8,128)S(1)}, f32[64,128]{1,0:T(8,128)S(1)}, u32[]{:S(2)}, u32[]{:S(2)}) %collective-permute-start.15) | collective-permute-done | bytes 32800 | tf_op jit(solution)/shard_map/ppermute | solution.py:533
  43.8 0.0 copy-done.5
  43.8 5.0 %shard_map.105 = (bf16[2,11,128,512]{3,2,1,0:T(8,128)(2,1)}, f32[11,11,2,16]{3,2,1,0:T(2,128)}) custom-call(f32[64,128]{1,0:T(8,128)S(1)} %add_add_fusion.half_ref, f32[64,128]{1,0:T(8,128)S(1)} %collective-permute-done.15.other_ref, bf16[2,128,256]{2,1,0:T(8,128)(2,1)S(1)} %copy-done.5, f32[22,128,256]{2,1,0:T(8,128)S(1)} %shard_map.104.refs_0_, ...), custom_call_target="tpu_custom_call" | custom-call | tf_op jit(solution)/shard_map/pallas_call | solution.py:507
  (5 shorter events, 0.0 us)
Async XLA Ops:
  2.8 8.1 %copy-start.4 = (bf16[256,256]{1,0:T(8,128)(2,1)S(1)}, bf16[256,256]{1,0:T(8,128)(2,1)}, u32[]{:S(2)}) copy-start(bf16[256,256]{1,0:T(8,128)(2,1)} %get-tuple-element.22.table_hbm) | copy-start | bytes 393220
  2.8 8.1 %collective-permute-start = (bf16[384,256]{1,0:T(8,128)(2,1)}, bf16[384,256]{1,0:T(8,128)(2,1)S(1)}, u32[]{:S(2)}, u32[]{:S(2)}) collective-permute-start(bf16[384,256]{1,0:T(8,128)(2,1)} %get-tuple-element.23), channel_id=1, source_target_pairs={{0,24},{8,16},{16,8},{24,0},{1,25},{9,17},{17,9},{25,1},{2,26},{10... | collective-permute-start | bytes 589832 | tf_op jit(solution)/shard_map/ppermute | solution.py:533
  5.3 11.6 %copy-start.8 = (f32[512]{0:T(512)S(1)}, f32[512]{0:T(512)}, u32[]{:S(2)}) copy-start(f32[512]{0:T(512)} %param.9) | copy-start | bytes 6148
  5.3 11.6 %copy-start.1 = (bf16[512,256]{1,0:T(8,128)(2,1)S(1)}, bf16[512,256]{1,0:T(8,128)(2,1)}, u32[]{:S(2)}) copy-start(bf16[512,256]{1,0:T(8,128)(2,1)} %constant.6.clone.f_ref) | copy-start | bytes 786436
  5.3 11.6 %copy-start.2 = (bf16[2816,128]{1,0:T(8,128)(2,1)S(1)}, bf16[2816,128]{1,0:T(8,128)(2,1)}, u32[]{:S(2)}) copy-start(bf16[2816,128]{1,0:T(8,128)(2,1)} %constant.7.clone.pick_ref) | copy-start | bytes 2162692
  5.3 11.6 %copy-start.6 = (s32[4]{0:T(128)S(1)}, s32[4]{0:T(128)}, u32[]{:S(2)}) copy-start(s32[4]{0:T(128)} %order_ref.11) | copy-start | bytes 52
  5.3 11.6 %copy-start.7 = (s32[11]{0:T(128)S(1)}, s32[11]{0:T(128)}, u32[]{:S(2)}) copy-start(s32[11]{0:T(128)} %offsets_ref.11) | copy-start | bytes 136
  8.2 7.6 %collective-permute-start.6 = (bf16[384,256]{1,0:T(8,128)(2,1)}, bf16[384,256]{1,0:T(8,128)(2,1)S(1)}, u32[]{:S(2)}, u32[]{:S(2)}) collective-permute-start(bf16[384,256]{1,0:T(8,128)(2,1)} %get-tuple-element.31), channel_id=1, source_target_pairs={{0,8},{8,0},{16,24},{24,16},{1,9},{9,1},{17,25},{25,17},{2,10},{10... | collective-permute-start | bytes 589832 | tf_op jit(solution)/shard_map/ppermute | solution.py:533
  8.9 8.0 %collective-permute-start.7 = (bf16[384,256]{1,0:T(8,128)(2,1)}, bf16[384,256]{1,0:T(8,128)(2,1)S(1)}, u32[]{:S(2)}, u32[]{:S(2)}) collective-permute-start(bf16[384,256]{1,0:T(8,128)(2,1)} %get-tuple-element.32), channel_id=1, source_target_pairs={{0,16},{8,24},{16,0},{24,8},{1,17},{9,25},{17,1},{25,9},{2,18},{10... | collective-permute-start | bytes 589832 | tf_op jit(solution)/shard_map/ppermute | solution.py:533
  8.9 10.7 %collective-permute-start.4 = (bf16[384,128]{1,0:T(8,128)(2,1)}, bf16[384,128]{1,0:T(8,128)(2,1)S(1)}, u32[]{:S(2)}, u32[]{:S(2)}) collective-permute-start(bf16[384,128]{1,0:T(8,128)(2,1)} %get-tuple-element.28), channel_id=1, source_target_pairs={{0,16},{8,24},{16,0},{24,8},{1,17},{9,25},{17,1},{25,9},{2,18},{10... | collective-permute-start | bytes 294920 | tf_op jit(solution)/shard_map/ppermute | solution.py:533
  11.0 8.7 %collective-permute-start.5 = (bf16[384,128]{1,0:T(8,128)(2,1)}, bf16[384,128]{1,0:T(8,128)(2,1)S(1)}, u32[]{:S(2)}, u32[]{:S(2)}) collective-permute-start(bf16[384,128]{1,0:T(8,128)(2,1)} %get-tuple-element.29), channel_id=1, source_target_pairs={{0,24},{8,16},{16,8},{24,0},{1,25},{9,17},{17,9},{25,1},{2,26},{10... | collective-permute-start | bytes 294920 | tf_op jit(solution)/shard_map/ppermute | solution.py:533
  11.0 1.4 %copy-start = (bf16[384,4,512]{2,1,0:T(4,128)(2,1)S(1)}, bf16[384,4,512]{2,1,0:T(4,128)(2,1)}, u32[]{:S(2)}) copy-start(bf16[384,4,512]{2,1,0:T(4,128)(2,1)} %x_hbm.5) | copy-start | bytes 4718596
  12.4 4.6 %copy-start.3 = (bf16[384,256]{1,0:T(8,128)(2,1)S(1)}, bf16[384,256]{1,0:T(8,128)(2,1)}, u32[]{:S(2)}) copy-start(bf16[384,256]{1,0:T(8,128)(2,1)} %get-tuple-element.30.refs_0_) | copy-start | bytes 589828
  13.4 9.8 %collective-permute-start.2 = (bf16[384,128]{1,0:T(8,128)(2,1)S(1)}, bf16[384,128]{1,0:T(8,128)(2,1)S(1)}, u32[]{:S(2)}, u32[]{:S(2)}) collective-permute-start(bf16[384,128]{1,0:T(8,128)(2,1)S(1)} %get-tuple-element.26), channel_id=1, source_target_pairs={{0,16},{8,24},{16,0},{24,8},{1,17},{9,25},{17,1},{25,9},{2,18},{10... | collective-permute-start | bytes 294920 | tf_op jit(solution)/shard_map/ppermute | solution.py:533
  15.8 7.8 %collective-permute-start.3 = (bf16[384,128]{1,0:T(8,128)(2,1)S(1)}, bf16[384,128]{1,0:T(8,128)(2,1)S(1)}, u32[]{:S(2)}, u32[]{:S(2)}) collective-permute-start(bf16[384,128]{1,0:T(8,128)(2,1)S(1)} %get-tuple-element.27), channel_id=1, source_target_pairs={{0,24},{8,16},{16,8},{24,0},{1,25},{9,17},{17,9},{25,1},{2,26},{10... | collective-permute-start | bytes 294920 | tf_op jit(solution)/shard_map/ppermute | solution.py:533
  16.9 2.8 %collective-permute-start.1 = (bf16[384,256]{1,0:T(8,128)(2,1)S(1)}, bf16[384,256]{1,0:T(8,128)(2,1)S(1)}, u32[]{:S(2)}, u32[]{:S(2)}) collective-permute-start(bf16[384,256]{1,0:T(8,128)(2,1)S(1)} %get-tuple-element.25), channel_id=1, source_target_pairs={{0,8},{8,0},{16,24},{24,16},{1,9},{9,1},{17,25},{25,17},{2,10},{10... | collective-permute-start | bytes 589832 | tf_op jit(solution)/shard_map/ppermute | solution.py:533
  25.3 1.6 %collective-permute-start.8 = (bf16[64,128]{1,0:T(8,128)(2,1)S(1)}, bf16[64,128]{1,0:T(8,128)(2,1)S(1)}, u32[]{:S(2)}, u32[]{:S(2)}) collective-permute-start(bf16[64,128]{1,0:T(8,128)(2,1)S(1)} %get-tuple-element.34), channel_id=1, source_target_pairs={{0,8},{1,9},{2,10},{3,11},{4,12},{5,13},{6,14},{7,15},{8,0},{9,1},... | collective-permute-start | bytes 49160 | tf_op jit(solution)/shard_map/ppermute | solution.py:533
  26.9 6.1 %collective-permute-start.11 = (bf16[64,128]{1,0:T(8,128)(2,1)S(1)}, bf16[64,128]{1,0:T(8,128)(2,1)S(1)}, u32[]{:S(2)}, u32[]{:S(2)}) collective-permute-start(bf16[64,128]{1,0:T(8,128)(2,1)S(1)} %add_convert_fusion), channel_id=1, source_target_pairs={{0,17},{1,16},{2,19},{3,18},{4,21},{5,20},{6,23},{7,22},{8,25},{9,... | collective-permute-start | bytes 49160 | tf_op jit(solution)/shard_map/ppermute | solution.py:533
  29.9 3.7 %collective-permute-start.10 = (bf16[64,128]{1,0:T(8,128)(2,1)S(1)}, bf16[64,128]{1,0:T(8,128)(2,1)S(1)}, u32[]{:S(2)}, u32[]{:S(2)}) collective-permute-start(bf16[64,128]{1,0:T(8,128)(2,1)S(1)} %add_convert_fusion), channel_id=1, source_target_pairs={{0,1},{1,0},{2,3},{3,2},{4,5},{5,4},{6,7},{7,6},{8,9},{9,8},{10,11... | collective-permute-start | bytes 49160 | tf_op jit(solution)/shard_map/ppermute | solution.py:533
  30.4 3.7 %collective-permute-start.9 = (bf16[64,128]{1,0:T(8,128)(2,1)S(1)}, bf16[64,128]{1,0:T(8,128)(2,1)S(1)}, u32[]{:S(2)}, u32[]{:S(2)}) collective-permute-start(bf16[64,128]{1,0:T(8,128)(2,1)S(1)} %add_convert_fusion), channel_id=1, source_target_pairs={{0,16},{1,17},{2,18},{3,19},{4,20},{5,21},{6,22},{7,23},{8,24},{9,... | collective-permute-start | bytes 49160 | tf_op jit(solution)/shard_map/ppermute | solution.py:533
  34.2 9.6 %copy-start.5 = (bf16[2,128,256]{2,1,0:T(8,128)(2,1)S(1)}, bf16[2,128,256]{2,1,0:T(8,128)(2,1)}, u32[]{:S(2)}) copy-start(bf16[2,128,256]{2,1,0:T(8,128)(2,1)} %constant.8.clone.spread_ref) | copy-start | bytes 393220
  34.2 6.1 %collective-permute-start.13 = (bf16[64,128]{1,0:T(8,128)(2,1)S(1)}, bf16[64,128]{1,0:T(8,128)(2,1)S(1)}, u32[]{:S(2)}, u32[]{:S(2)}) collective-permute-start(bf16[64,128]{1,0:T(8,128)(2,1)S(1)} %add_add_fusion.1), channel_id=1, source_target_pairs={{0,6},{1,7},{2,4},{3,5},{4,2},{5,3},{6,0},{7,1},{8,14},{9,15},{10,... | collective-permute-start | bytes 49160 | tf_op jit(solution)/shard_map/ppermute | solution.py:533
  37.9 4.6 %collective-permute-start.12 = (bf16[64,128]{1,0:T(8,128)(2,1)S(1)}, bf16[64,128]{1,0:T(8,128)(2,1)S(1)}, u32[]{:S(2)}, u32[]{:S(2)}) collective-permute-start(bf16[64,128]{1,0:T(8,128)(2,1)S(1)} %add_add_fusion.1), channel_id=1, source_target_pairs={{0,4},{1,5},{2,6},{3,7},{4,0},{5,1},{6,2},{7,3},{8,12},{9,13},{10,... | collective-permute-start | bytes 49160 | tf_op jit(solution)/shard_map/ppermute | solution.py:533
  37.9 4.6 %collective-permute-start.14 = (bf16[64,128]{1,0:T(8,128)(2,1)S(1)}, bf16[64,128]{1,0:T(8,128)(2,1)S(1)}, u32[]{:S(2)}, u32[]{:S(2)}) collective-permute-start(bf16[64,128]{1,0:T(8,128)(2,1)S(1)} %add_add_fusion.1), channel_id=1, source_target_pairs={{0,2},{1,3},{2,0},{3,1},{4,6},{5,7},{6,4},{7,5},{8,10},{9,11},{10,... | collective-permute-start | bytes 49160 | tf_op jit(solution)/shard_map/ppermute | solution.py:533
  42.5 1.3 %collective-permute-start.15 = (f32[64,128]{1,0:T(8,128)S(1)}, f32[64,128]{1,0:T(8,128)S(1)}, u32[]{:S(2)}, u32[]{:S(2)}) collective-permute-start(f32[64,128]{1,0:T(8,128)S(1)} %add_add_fusion.half_ref), channel_id=1, source_target_pairs={{0,8},{1,9},{2,10},{3,11},{4,12},{5,13},{6,14},{7,15},{8,0},{9,1},... | collective-permute-start | bytes 98312 | tf_op jit(solution)/shard_map/ppermute | solution.py:533

commit v14 on v13

--- a/solution.py
+++ b/solution.py
@@ -25,6 +25,7 @@
 WIDE = 2 * LANE
 FIRST_LIMIT = 64 * 2**20
 SECOND_LIMIT = FIRST_LIMIT - 1450 * 2**10
+LAST_LIMIT = 40 * 2**20
 BF16 = jnp.bfloat16
 F32 = jnp.float32
 
@@ -89,40 +90,38 @@
 HBM = pl.BlockSpec(memory_space=pltpu.HBM)
 
 
-def lane_pick(owner, lanes):
+def lane_pick(owner, lanes, begin, end):
     me = lax.axis_index("tm")
     rows = WIDE // lanes
-    out_row = lax.broadcasted_iota(jnp.int32, (WIDE, WIDE), 0)
-    in_row = lax.broadcasted_iota(jnp.int32, (WIDE, WIDE), 1)
+    shape = ((end - begin) * rows, WIDE)
+    out_row = lax.broadcasted_iota(jnp.int32, shape, 0)
+    in_row = lax.broadcasted_iota(jnp.int32, shape, 1)
     row_of = (out_row % rows) * lanes
-    for d in range(lanes):
+    for d in range(begin, end):
         slot = me ^ d
         source = jnp.int32(0)
         for lane in range(lanes):
             source = source + jnp.where(owner[0, lane] == slot, lane, 0)
-        row_of = jnp.where(out_row // rows == d, row_of + source, row_of)
+        row_of = jnp.where(out_row // rows == d - begin, row_of + source, row_of)
     return jnp.where(in_row == row_of, 1.0, 0.0).astype(BF16)
 
 
-def pack_kernel(jobs, parts, first, follows, table_hbm, x_hbm, *refs):
+def pack_kernel(jobs, parts, follows, owner_hbm, x_hbm, *refs):
     steps, lanes, _ = x_hbm.shape
     base = jobs[0][0]
-    table, x_ref, table_sem, x_sem = refs[-4:]
-    outs = list(refs[follows:-4])
+    *outs, owner, pick, x_ref, owner_sem, x_sem = refs[follows:]
     part = steps // parts
-    table_copy = pltpu.make_async_copy(table_hbm, table, table_sem)
-    table_copy.start()
+    owner_copy = pltpu.make_async_copy(owner_hbm, owner, owner_sem)
+    owner_copy.start()
     copies = []
     for i in range(parts):
         at = slice(i * part, (i + 1) * part)
         source = x_hbm.at[at, :, base : base + x_ref.shape[2]]
         copies.append(pltpu.make_async_copy(source, x_ref.at[at], x_sem.at[i]))
         copies[-1].start()
-    table_copy.wait()
-    pick = table
-    if first:
-        pick = outs.pop()
-        pick[...] = lane_pick(table, lanes)
+    owner_copy.wait()
+    lowest = min(begin for _, _, begin, _ in jobs)
+    pick[...] = lane_pick(owner, lanes, lowest, max(end for _, _, _, end in jobs))
     rows = WIDE // lanes
     for i in range(parts):
         copies[i].wait()
@@ -132,12 +131,13 @@
             out = iter(outs)
             for job, width, begin, end in jobs:
                 here = x[:, job - base : job - base + width]
-                y = dot(pick[begin * rows : end * rows, :], here).astype(BF16)
+                chosen = pick[(begin - lowest) * rows : (end - lowest) * rows, :]
+                y = dot(chosen, here).astype(BF16)
                 for d in range(end - begin):
                     next(out)[at, :] = y[d * rows : (d + 1) * rows]
 
 
-def pack(table, snapshots, jobs, first, after=()):
+def pack(owner, snapshots, jobs, limit, after=()):
     steps, lanes, _ = snapshots.shape
     parts = math.gcd(steps * lanes // WIDE, 3)
     outs = [
@@ -145,25 +145,23 @@
         for _, width, begin, end in jobs
         for _ in range(begin, end)
     ]
-    if first:
-        outs.append(jax.ShapeDtypeStruct((WIDE, WIDE), BF16))
     columns = jobs[-1][0] + jobs[-1][1] - jobs[0][0]
+    partners = max(end for _, _, _, end in jobs) - min(begin for _, _, begin, _ in jobs)
     return pl.pallas_call(
-        functools.partial(pack_kernel, jobs, parts, first, len(after)),
+        functools.partial(pack_kernel, jobs, parts, len(after)),
         out_shape=outs,
         in_specs=[HBM] * (2 + len(after)),
         out_specs=[VMEM] * len(outs),
         scratch_shapes=[
-            pltpu.SMEM(table.shape, jnp.int32) if first else pltpu.VMEM(table.shape, BF16),
+            pltpu.SMEM(owner.shape, jnp.int32),
+            pltpu.VMEM((partners * (WIDE // lanes), WIDE), BF16),
             pltpu.VMEM((steps, lanes, columns), BF16),
             pltpu.SemaphoreType.DMA,
             pltpu.SemaphoreType.DMA((parts,)),
         ],
-        compiler_params=pltpu.CompilerParams(
-            vmem_limit_bytes=FIRST_LIMIT if first else 40 * 2**20 if after else SECOND_LIMIT
-        ),
+        compiler_params=pltpu.CompilerParams(vmem_limit_bytes=limit),
         cost_estimate=pl.CostEstimate(flops=1000, bytes_accessed=1000, transcendentals=0),
-    )(table, snapshots, *after)
+    )(owner, snapshots, *after)
 
 
 def fill_record(base, order_ref, pieces, record, factor):
@@ -328,21 +326,32 @@
             self.corner[1, a - SUB, at, :] = imag
 
 
-def product(x, y, out, diagonal=0.0, terms=()):
+def product(x, y, out, sums, diagonal=0.0, terms=()):
     sub = lax.broadcasted_iota(jnp.int32, (SUB, NFREQ), 0)
     yr = [y.main[0, b] for b in range(NBLK)]
     yi = [y.main[1, b] for b in range(NBLK)]
+    minus = [yi[b] - yr[b] for b in range(NBLK)]
+    plus = [yi[b] + yr[b] for b in range(NBLK)]
     for a in range(NBLK):
-        real = imag = None
+        sums[a] = x.main[0, a] + x.main[1, a]
+    for a in range(CORNER):
+        sums[NBLK + a] = x.corner[0, a] + x.corner[1, a]
+        sums[NBLK + CORNER + a] = x.main[0, SUB + a] - x.main[1, SUB + a]
+    for a in range(NBLK):
+        k1 = k2 = k3 = None
         for b in range(NBLK):
             pr, pi, sign = x.entry(a, b)
-            tr, ti = pi * yi[b], pi * yr[b]
-            if sign > 0:
-                tr, ti = pr * yr[b] - tr, pr * yi[b] + ti
+            if b < SUB:
+                both = sums[a, pl.ds(b, 1), :]
+            elif a < SUB:
+                both = sums[NBLK + CORNER + b - SUB, pl.ds(a, 1), :]
             else:
-                tr, ti = pr * yr[b] + tr, pr * yi[b] - ti
-            real = tr if real is None else real + tr
-            imag = ti if imag is None else imag + ti
+                both = sums[NBLK + a - SUB, pl.ds(b - SUB, 1), :]
+            t1, t2, t3 = both * yr[b], pr * minus[b], pi * plus[b]
+            k1 = t1 if k1 is None else k1 + t1
+            k2 = t2 if k2 is None else k2 + t2
+            k3 = t3 if k3 is None else k3 + t3 if sign > 0 else k3 - t3
+        real, imag = k1 - k3, k1 + k2
         for factor, term in terms:
             real = real + factor * term.main[0, a]
             imag = imag + factor * term.main[1, a]
@@ -388,26 +397,26 @@
 TWO_STEPS = (2.25, -2.4375, 1.6875, -0.5625, 0.0625)
 
 
-def inverse_root(w, mats):
+def inverse_root(w, mats, sums):
     q, u, r, t, w2, z = mats
     c0, c1, c2, c3, c4 = TWO_STEPS
-    product(w, w, q)
+    product(w, w, q, sums)
     combine(u, 0.0, [(c3, w), (c4, q)])
-    product(q, u, z, c0, [(c1, w), (c2, q)])
-    product(z, z, t)
-    product(w, t, w2)
-    product(w2, w2, q)
+    product(q, u, z, sums, c0, [(c1, w), (c2, q)])
+    product(z, z, t, sums)
+    product(w, t, w2, sums)
+    product(w2, w2, q, sums)
     combine(u, 0.0, [(c3, w2), (c4, q)])
-    product(q, u, r, c0, [(c1, w2), (c2, q)])
-    product(r, r, t)
-    product(z, r, u)
-    product(w2, t, q)
+    product(q, u, r, sums, c0, [(c1, w2), (c2, q)])
+    product(r, r, t, sums)
+    product(z, r, u, sums)
+    product(w2, t, q, sums)
     combine(q, 1.5, [(-0.5, q)])
-    product(u, q, z)
+    product(u, q, z, sums)
     return z
 
 
-def make_roots(share, half_ref, other_ref, gram_ref, packed, rolled, mats):
+def make_roots(share, half_ref, other_ref, gram_ref, packed, rolled, sums, mats):
     core = lax.axis_index("tm") % 2
     packed[pl.ds(pl.multiple_of(core * HALF, HALF), HALF), :] = half_ref[...]
     packed[pl.ds(pl.multiple_of((1 - core) * HALF, HALF), HALF), :] = other_ref[...]
@@ -438,7 +447,7 @@
             gram_ref[e, a, 0:1, :] = real
             gram_ref[a, e, 1:2, :] = imag
             gram_ref[e, a, 1:2, :] = -imag
-    z = inverse_root(y, free)
+    z = inverse_root(y, free, sums)
     mean = sum(z.entry(a, a)[0] for a in range(NBLK)) * (1.0 / NBLK)
     sub = lax.broadcasted_iota(jnp.int32, (SUB, NFREQ), 0)
     none = jnp.zeros((SUB - CORNER, NFREQ), F32)
@@ -467,8 +476,8 @@
 
 def mode_kernel(chunks, share, half_ref, other_ref, spread_ref, *refs):
     s_refs = refs[:chunks]
-    out_hbm, gram_ref, out, v, mean, packed, rolled, sem, *mats = refs[chunks:]
-    stacks = make_roots(share, half_ref, other_ref, gram_ref, packed, rolled, mats)
+    out_hbm, gram_ref, out, v, mean, packed, rolled, sums, sem, *mats = refs[chunks:]
+    stacks = make_roots(share, half_ref, other_ref, gram_ref, packed, rolled, sums, mats)
     mean[...] = jnp.broadcast_to(stacks[0][:, NBLK : NBLK + 1], (NFREQ, LANE))
     row = lax.broadcasted_iota(jnp.int32, (NFREQ, 2 * HALF_ROWS), 0)
     col = lax.broadcasted_iota(jnp.int32, (NFREQ, 2 * HALF_ROWS), 1)
@@ -518,6 +527,7 @@
             pltpu.VMEM((NFREQ, LANE), F32),
             pltpu.VMEM((PACKED, NFREQ), F32),
             pltpu.VMEM((PACKED, NFREQ), F32),
+            pltpu.VMEM((NBLK + 2 * CORNER, SUB, NFREQ), F32),
             pltpu.SemaphoreType.DMA((GROUPS // 2,)),
         ]
         + [
@@ -551,11 +561,12 @@
         return [swap(p, "tm", d, lanes) for d, p in zip(range(begin, end), packed)]
 
     c0, c1, c2 = chunks
-    first, table = pack(owner, snapshots, [(*c0, lanes - 1, lanes)], True)
-    first = send([first], lanes - 1, lanes)
-    middle = pack(table, snapshots, [(*c0, 0, lanes - 1), (*c1, NEAR, lanes)], False)
+    packed = pack(owner, snapshots, [(*c0, lanes - 1, lanes)], FIRST_LIMIT)
+    first = send(packed, lanes - 1, lanes)
+    jobs = [(*c0, 0, lanes - 1), (*c1, NEAR, lanes)]
+    middle = pack(owner, snapshots, jobs, SECOND_LIMIT, packed)
     jobs = [(c1[0], c1[1] + c2[1], 0, NEAR), (*c2, NEAR, lanes)]
-    rest = pack(table, snapshots, jobs, False, first)
+    rest = pack(owner, snapshots, jobs, LAST_LIMIT, [*first, middle[0]])
     near = [rest[0], *send(rest[1:], 1, NEAR)]
     arrived = [
         [middle[0], *send(middle[1:], 1, lanes - 1), *first],

time: 49 us -> 48.8 us (level)
  waiting for transfers between devices: 7.53 us -> 6.26 us
  local copies, waits for them, and re-layouts: 1.44 us -> 2.38 us
    ppermute x16, waiting for transfers between devices: 7.53 us -> 6.26 us  [swap(): return lax.ppermute(x, axes, [(i, i ^ mask) for i in range(size)])]
    unnamed x18, local copies, waits for them, and re-layouts: 1.44 us -> 2.38 us
where the time goes in v14:
time: 48.8 us; the launch traced here: 48.6 us
  Pallas kernels  22.2 us (45%)
  starting transfers between devices  16.9 us (35%)
  waiting for transfers between devices  6.26 us (13%)
  local copies, waits for them, and re-layouts  2.38 us (5%)
  between operations  0.86 us (2%)
    ppermute x16, starting transfers between devices, swap(): return lax.ppermute(x, axes, [(i, i ^ mask) for i in range(size)])  16.9 us
    pallas_call x3, Pallas kernels, gram_part(): pl.pallas_call(functools.partial(gram_kernel, lanes, base, scale, last),...  6.6 us
    ppermute x16, waiting for transfers between devices, swap(): return lax.ppermute(x, axes, [(i, i ^ mask) for i in range(size)])  6.26 us
    pallas_call x3, Pallas kernels, pack(): pl.pallas_call(functools.partial(pack_kernel, jobs, parts, len(after)), o...  6.1 us
    pallas_call x1, Pallas kernels, mode_fields(): pl.pallas_call(functools.partial(mode_kernel, len(spectra), share), out_s...  4.77 us
    pallas_call x3, Pallas kernels, spectrum(): pl.pallas_call(functools.partial(spectrum_kernel, lanes, base), out_shape...  4.06 us
    unnamed x18, local copies, waits for them, and re-layouts  2.38 us
  transfers between devices with their start and end apart: 16, of which 8 were waited for; matrix products, arithmetic and copies ran while one was open for 0% of the time, Pallas kernels for 28%

profile of v14, /device:TPU:0, one launch (start us, length us, event | category | flops | bytes accessed | tf_op | source)
XLA Modules:
  0.0 48.6 jit_solution(7851984082553006143)
XLA Ops:
  0.6 2.2 %shard_map.95.refs_0_ = bf16[384,256]{1,0:T(8,128)(2,1)} custom-call(s32[1,4]{1,0:T(1,128)} %owner_hbm.5, bf16[384,4,512]{2,1,0:T(4,128)(2,1)} %x_hbm.5), custom_call_target="tpu_custom_call" | custom-call | flops 1000 | bytes 1000 | tf_op jit(solution)/shard_map/pallas_call | solution.py:150
  2.8 0.0 copy-start.7
  2.8 0.0 copy-start.8
  2.9 0.0 copy-start.1
  2.9 0.0 copy-start.2
  2.9 0.0 copy-start.5
  2.9 0.0 copy-start.6
  2.9 2.5 %collective-permute-start = (bf16[384,256]{1,0:T(8,128)(2,1)}, bf16[384,256]{1,0:T(8,128)(2,1)S(1)}, u32[]{:S(2)}, u32[]{:S(2)}) collective-permute-start(bf16[384,256]{1,0:T(8,128)(2,1)} %shard_map.95.refs_0_), channel_id=1, source_target_pairs={{0,24},{8,16},{16,8},{24,0},{1,25},{9,17},{17,9},{25,1},{2,26},{10... | collective-permute-start | bytes 589832 | tf_op jit(solution)/shard_map/ppermute | solution.py:543
  5.4 2.6 %shard_map.96 = (bf16[384,256]{1,0:T(8,128)(2,1)}, bf16[384,256]{1,0:T(8,128)(2,1)}, bf16[384,256]{1,0:T(8,128)(2,1)}, bf16[384,128]{1,0:T(8,128)(2,1)}, bf16[384,128]{1,0:T(8,128)(2,1)}) custom-call(s32[1,4]{1,0:T(1,128)} %owner_hbm.5, bf16[384,4,512]{2,1,0:T(4,128)(2,1)} %x_hbm.5, bf16[384,256]{1,0:T(8,128)(2,1)} %shard_map.95.refs_0_), custom_call_target="tpu_custom_call" | custom-call | flops 1000 | bytes 1000 | tf_op jit(solution)/shard_map/pallas_call | solution.py:150
  8.0 0.7 %collective-permute-start.6 = (bf16[384,256]{1,0:T(8,128)(2,1)}, bf16[384,256]{1,0:T(8,128)(2,1)S(1)}, u32[]{:S(2)}, u32[]{:S(2)}) collective-permute-start(bf16[384,256]{1,0:T(8,128)(2,1)} %get-tuple-element.27), channel_id=1, source_target_pairs={{0,8},{8,0},{16,24},{24,16},{1,9},{9,1},{17,25},{25,17},{2,10},{10... | collective-permute-start | bytes 589832 | tf_op jit(solution)/shard_map/ppermute | solution.py:543
  8.7 0.1 collective-permute-start.7
  8.8 2.0 %collective-permute-start.4 = (bf16[384,128]{1,0:T(8,128)(2,1)}, bf16[384,128]{1,0:T(8,128)(2,1)S(1)}, u32[]{:S(2)}, u32[]{:S(2)}) collective-permute-start(bf16[384,128]{1,0:T(8,128)(2,1)} %get-tuple-element.25), channel_id=1, source_target_pairs={{0,16},{8,24},{16,0},{24,8},{1,17},{9,25},{17,1},{25,9},{2,18},{10... | collective-permute-start | bytes 294920 | tf_op jit(solution)/shard_map/ppermute | solution.py:543
  10.8 0.0 collective-permute-start.5
  10.8 0.2 collective-permute-done.refs_0_.refs_3_
  11.0 0.0 copy-done.7
  11.0 0.0 copy-start
  11.0 1.4 %copy-done = bf16[384,4,512]{2,1,0:T(4,128)(2,1)S(1)} copy-done((bf16[384,4,512]{2,1,0:T(4,128)(2,1)S(1)}, bf16[384,4,512]{2,1,0:T(4,128)(2,1)}, u32[]{:S(2)}) %copy-start) | copy-done | bytes 1572888
  12.4 0.0 copy-start.3
  12.4 0.9 %copy-done.3 = bf16[384,256]{1,0:T(8,128)(2,1)S(1)} copy-done((bf16[384,256]{1,0:T(8,128)(2,1)S(1)}, bf16[384,256]{1,0:T(8,128)(2,1)}, u32[]{:S(2)}) %copy-start.3) | copy-done | bytes 196632
  13.3 1.3 %shard_map.97 = (bf16[384,256]{1,0:T(8,128)(2,1)S(1)}, bf16[384,256]{1,0:T(8,128)(2,1)S(1)}, bf16[384,128]{1,0:T(8,128)(2,1)S(1)}, bf16[384,128]{1,0:T(8,128)(2,1)S(1)}) custom-call(s32[1,4]{1,0:T(1,128)S(1)} %copy-done.7, bf16[384,4,512]{2,1,0:T(4,128)(2,1)S(1)} %copy-done, bf16[384,256]{1,0:T(8,128)(2,1)S(1)} %collective-permute-done.refs_0_.refs_3_, ...), custom_call_target="tpu_custom_call" | custom-call | flops 1000 | bytes 1000 | tf_op jit(solution)/shard_map/pallas_call | solution.py:150
  14.6 2.4 %collective-permute-start.2 = (bf16[384,128]{1,0:T(8,128)(2,1)S(1)}, bf16[384,128]{1,0:T(8,128)(2,1)S(1)}, u32[]{:S(2)}, u32[]{:S(2)}) collective-permute-start(bf16[384,128]{1,0:T(8,128)(2,1)S(1)} %get-tuple-element.23), channel_id=1, source_target_pairs={{0,16},{8,24},{16,0},{24,8},{1,17},{9,25},{17,1},{25,9},{2,18},{10... | collective-permute-start | bytes 294920 | tf_op jit(solution)/shard_map/ppermute | solution.py:543
  17.1 0.0 collective-permute-done.6.refs_1_
  17.1 0.0 collective-permute-start.3
  17.1 0.0 collective-permute-done.7.refs_2_
  17.1 0.2 collective-permute-start.1
  17.3 0.0 copy-done.8
  17.3 0.0 copy-done.1
  17.3 0.0 copy-done.2
  17.3 0.0 copy-done.5
  17.3 0.0 copy-done.6
  17.3 2.7 %shard_map.98.refs_4_ = f32[128,128]{1,0:T(8,128)S(1)} custom-call(s32[4]{0:T(128)S(1)} %copy-done.5, s32[11]{0:T(128)S(1)} %copy-done.6, f32[1,256]{1,0:T(1,128)S(1)} %slice.14.w_ref, bf16[512,256]{1,0:T(8,128)(2,1)S(1)} %copy-done.1, bf16[2816,128]{1,0:T(8,128)(2,1)S(1)} %copy-done.2, bf16[384,256]{1,0:T(8,128)(2,1)S(1)} %copy-done.3, ...), custom_call_target="tpu_custom_call" | custom-call | flops 1000 | bytes 1000 | tf_op jit(solution)/shard_map/pallas_call | solution.py:256
  20.0 0.0 collective-permute-done.4.refs_2_
  20.0 0.0 collective-permute-done.5.refs_3_
  20.0 0.0 collective-permute-done.1.refs_1_
  20.0 2.2 %shard_map.99.refs_4_.before_ref = f32[128,128]{1,0:T(8,128)S(1)} custom-call(s32[4]{0:T(128)S(1)} %copy-done.5, s32[11]{0:T(128)S(1)} %copy-done.6, f32[1,128]{1,0:T(1,128)S(1)} %get-tuple-element.40.w_ref, bf16[512,256]{1,0:T(8,128)(2,1)S(1)} %copy-done.1, bf16[2816,128]{1,0:T(8,128)(2,1)S(1)} %copy-done.2, ...), custom_call_target="tpu_custom_call" | custom-call | flops 1000 | bytes 1000 | tf_op jit(solution)/shard_map/pallas_call | solution.py:256
  22.2 0.8 %collective-permute-done.2.refs_2_ = bf16[384,128]{1,0:T(8,128)(2,1)S(1)} collective-permute-done((bf16[384,128]{1,0:T(8,128)(2,1)S(1)}, bf16[384,128]{1,0:T(8,128)(2,1)S(1)}, u32[]{:S(2)}, u32[]{:S(2)}) %collective-permute-start.2) | collective-permute-done | bytes 98336 | tf_op jit(solution)/shard_map/ppermute | solution.py:543
  23.0 0.5 %collective-permute-done.3.refs_3_ = bf16[384,128]{1,0:T(8,128)(2,1)S(1)} collective-permute-done((bf16[384,128]{1,0:T(8,128)(2,1)S(1)}, bf16[384,128]{1,0:T(8,128)(2,1)S(1)}, u32[]{:S(2)}, u32[]{:S(2)}) %collective-permute-start.3) | collective-permute-done | bytes 98336 | tf_op jit(solution)/shard_map/ppermute | solution.py:543
  23.5 1.7 %shard_map.100 = (bf16[64,128]{1,0:T(8,128)(2,1)S(1)}, f32[22,128,128]{2,1,0:T(8,128)S(1)}) custom-call(s32[4]{0:T(128)S(1)} %copy-done.5, s32[11]{0:T(128)S(1)} %copy-done.6, f32[1,128]{1,0:T(1,128)S(1)} %get-tuple-element.41.w_ref, bf16[512,256]{1,0:T(8,128)(2,1)S(1)} %copy-done.1, bf16[2816,128]{1,0:T(8,128)(2,1)S(1)} %copy-done.2, ...), custom_call_target="tpu_custom_call" | custom-call | flops 1000 | bytes 1000 | tf_op jit(solution)/shard_map/pallas_call | solution.py:256
  25.2 0.6 %collective-permute-start.8 = (bf16[64,128]{1,0:T(8,128)(2,1)S(1)}, bf16[64,128]{1,0:T(8,128)(2,1)S(1)}, u32[]{:S(2)}, u32[]{:S(2)}) collective-permute-start(bf16[64,128]{1,0:T(8,128)(2,1)S(1)} %get-tuple-element.30), channel_id=1, source_target_pairs={{0,8},{1,9},{2,10},{3,11},{4,12},{5,13},{6,14},{7,15},{8,0},{9,1},... | collective-permute-start | bytes 49160 | tf_op jit(solution)/shard_map/ppermute | solution.py:543
  25.8 0.7 %shard_map.101.refs_4_ = bf16[64,128]{1,0:T(8,128)(2,1)S(1)} custom-call(f32[22,128,128]{2,1,0:T(8,128)S(1)} %get-tuple-element.29.s_ref, bf16[2816,128]{1,0:T(8,128)(2,1)S(1)} %copy-done.2, f32[128,128]{1,0:T(8,128)S(1)} %shard_map.99.refs_4_.before_ref), custom_call_target="tpu_custom_call" | custom-call | flops 1000000000 | bytes 3000000 | tf_op jit(solution)/shard_map/pallas_call | solution.py:274
  26.5 0.2 collective-permute-done.8
  26.7 3.3 %collective-permute-start.11 = (bf16[64,128]{1,0:T(8,128)(2,1)S(1)}, bf16[64,128]{1,0:T(8,128)(2,1)S(1)}, u32[]{:S(2)}, u32[]{:S(2)}) collective-permute-start(bf16[64,128]{1,0:T(8,128)(2,1)S(1)} %add_convert_fusion), channel_id=1, source_target_pairs={{0,17},{1,16},{2,19},{3,18},{4,21},{5,20},{6,23},{7,22},{8,25},{9,... | collective-permute-start | bytes 49160 | tf_op jit(solution)/shard_map/ppermute | solution.py:543
  29.9 0.5 %collective-permute-start.10 = (bf16[64,128]{1,0:T(8,128)(2,1)S(1)}, bf16[64,128]{1,0:T(8,128)(2,1)S(1)}, u32[]{:S(2)}, u32[]{:S(2)}) collective-permute-start(bf16[64,128]{1,0:T(8,128)(2,1)S(1)} %add_convert_fusion), channel_id=1, source_target_pairs={{0,1},{1,0},{2,3},{3,2},{4,5},{5,4},{6,7},{7,6},{8,9},{9,8},{10,11... | collective-permute-start | bytes 49160 | tf_op jit(solution)/shard_map/ppermute | solution.py:543
  30.5 0.1 collective-permute-start.9
  30.6 1.2 %shard_map.103.refs_2_ = f32[22,128,128]{2,1,0:T(8,128)S(1)} custom-call(s32[4]{0:T(128)S(1)} %copy-done.5, s32[11]{0:T(128)S(1)} %copy-done.6, bf16[512,256]{1,0:T(8,128)(2,1)S(1)} %copy-done.1, bf16[384,256]{1,0:T(8,128)(2,1)S(1)} %get-tuple-element.21.refs_0_, bf16[384,256]{1,0:T(8,128)(2,1)S(1)} %collective-permute-done.1.refs_1_, ...), custom_call_target="tpu_custom_call" | custom-call | flops 1000 | bytes 1000 | tf_op jit(solution)/shard_map/pallas_call | solution.py:295
  31.8 1.2 %shard_map.102.refs_1_ = f32[22,128,128]{2,1,0:T(8,128)S(1)} custom-call(s32[4]{0:T(128)S(1)} %copy-done.5, s32[11]{0:T(128)S(1)} %copy-done.6, bf16[512,256]{1,0:T(8,128)(2,1)S(1)} %copy-done.1, bf16[384,256]{1,0:T(8,128)(2,1)S(1)} %get-tuple-element.21.refs_0_, bf16[384,256]{1,0:T(8,128)(2,1)S(1)} %collective-permute-done.1.refs_1_, ...), custom_call_target="tpu_custom_call" | custom-call | flops 1000 | bytes 1000 | tf_op jit(solution)/shard_map/pallas_call | solution.py:295
  33.0 0.0 collective-permute-done.11
  33.1 0.6 %collective-permute-done.10 = bf16[64,128]{1,0:T(8,128)(2,1)S(1)} collective-permute-done((bf16[64,128]{1,0:T(8,128)(2,1)S(1)}, bf16[64,128]{1,0:T(8,128)(2,1)S(1)}, u32[]{:S(2)}, u32[]{:S(2)}) %collective-permute-start.10) | collective-permute-done | bytes 16416 | tf_op jit(solution)/shard_map/ppermute | solution.py:543
  33.7 0.5 %collective-permute-done.9 = bf16[64,128]{1,0:T(8,128)(2,1)S(1)} collective-permute-done((bf16[64,128]{1,0:T(8,128)(2,1)S(1)}, bf16[64,128]{1,0:T(8,128)(2,1)S(1)}, u32[]{:S(2)}, u32[]{:S(2)}) %collective-permute-start.9) | collective-permute-done | bytes 16416 | tf_op jit(solution)/shard_map/ppermute | solution.py:543
  34.2 0.0 copy-start.4
  34.3 3.7 %collective-permute-start.13 = (bf16[64,128]{1,0:T(8,128)(2,1)S(1)}, bf16[64,128]{1,0:T(8,128)(2,1)S(1)}, u32[]{:S(2)}, u32[]{:S(2)}) collective-permute-start(bf16[64,128]{1,0:T(8,128)(2,1)S(1)} %add_add_fusion.1), channel_id=1, source_target_pairs={{0,6},{1,7},{2,4},{3,5},{4,2},{5,3},{6,0},{7,1},{8,14},{9,15},{10,... | collective-permute-start | bytes 49160 | tf_op jit(solution)/shard_map/ppermute | solution.py:543
  37.9 0.0 collective-permute-start.12
  37.9 0.8 %collective-permute-start.14 = (bf16[64,128]{1,0:T(8,128)(2,1)S(1)}, bf16[64,128]{1,0:T(8,128)(2,1)S(1)}, u32[]{:S(2)}, u32[]{:S(2)}) collective-permute-start(bf16[64,128]{1,0:T(8,128)(2,1)S(1)} %add_add_fusion.1), channel_id=1, source_target_pairs={{0,2},{1,3},{2,0},{3,1},{4,6},{5,7},{6,4},{7,5},{8,10},{9,11},{10,... | collective-permute-start | bytes 49160 | tf_op jit(solution)/shard_map/ppermute | solution.py:543
  38.7 1.6 %shard_map.104.refs_0_ = f32[22,128,256]{2,1,0:T(8,128)S(1)} custom-call(s32[4]{0:T(128)S(1)} %copy-done.5, s32[11]{0:T(128)S(1)} %copy-done.6, bf16[512,256]{1,0:T(8,128)(2,1)S(1)} %copy-done.1, bf16[384,256]{1,0:T(8,128)(2,1)S(1)} %copy-done.3, bf16[384,256]{1,0:T(8,128)(2,1)S(1)} %collective-permute-done.6.refs_1_, ...), custom_call_target="tpu_custom_call" | custom-call | flops 1000 | bytes 1000 | tf_op jit(solution)/shard_map/pallas_call | solution.py:295
  40.3 0.0 collective-permute-done.13
  40.3 2.2 %collective-permute-done.12 = bf16[64,128]{1,0:T(8,128)(2,1)S(1)} collective-permute-done((bf16[64,128]{1,0:T(8,128)(2,1)S(1)}, bf16[64,128]{1,0:T(8,128)(2,1)S(1)}, u32[]{:S(2)}, u32[]{:S(2)}) %collective-permute-start.12) | collective-permute-done | bytes 16416 | tf_op jit(solution)/shard_map/ppermute | solution.py:543
  42.6 0.0 collective-permute-done.14
  42.6 0.1 collective-permute-start.15
  42.6 1.2 %collective-permute-done.15.other_ref = f32[64,128]{1,0:T(8,128)S(1)} collective-permute-done((f32[64,128]{1,0:T(8,128)S(1)}, f32[64,128]{1,0:T(8,128)S(1)}, u32[]{:S(2)}, u32[]{:S(2)}) %collective-permute-start.15) | collective-permute-done | bytes 32800 | tf_op jit(solution)/shard_map/ppermute | solution.py:543
  43.8 0.0 copy-done.4
  43.8 4.8 %shard_map.105 = (bf16[2,11,128,512]{3,2,1,0:T(8,128)(2,1)}, f32[11,11,2,16]{3,2,1,0:T(2,128)}) custom-call(f32[64,128]{1,0:T(8,128)S(1)} %add_add_fusion.half_ref, f32[64,128]{1,0:T(8,128)S(1)} %collective-permute-done.15.other_ref, bf16[2,128,256]{2,1,0:T(8,128)(2,1)S(1)} %copy-done.4, f32[22,128,256]{2,1,0:T(8,128)S(1)} %shard_map.104.refs_0_, ...), custom_call_target="tpu_custom_call" | custom-call | tf_op jit(solution)/shard_map/pallas_call | solution.py:516
  (5 shorter events, 0.0 us)
Async XLA Ops:
  2.8 8.2 %copy-start.7 = (s32[1,4]{1,0:T(1,128)S(1)}, s32[1,4]{1,0:T(1,128)}, u32[]{:S(2)}) copy-start(s32[1,4]{1,0:T(1,128)} %owner_hbm.5) | copy-start | bytes 52
  2.8 14.4 %copy-start.8 = (f32[512]{0:T(512)S(1)}, f32[512]{0:T(512)}, u32[]{:S(2)}) copy-start(f32[512]{0:T(512)} %param.9) | copy-start | bytes 6148
  2.9 14.4 %copy-start.1 = (bf16[512,256]{1,0:T(8,128)(2,1)S(1)}, bf16[512,256]{1,0:T(8,128)(2,1)}, u32[]{:S(2)}) copy-start(bf16[512,256]{1,0:T(8,128)(2,1)} %constant.6.clone.f_ref) | copy-start | bytes 786436
  2.9 14.4 %copy-start.2 = (bf16[2816,128]{1,0:T(8,128)(2,1)S(1)}, bf16[2816,128]{1,0:T(8,128)(2,1)}, u32[]{:S(2)}) copy-start(bf16[2816,128]{1,0:T(8,128)(2,1)} %constant.7.clone.pick_ref) | copy-start | bytes 2162692
  2.9 14.4 %copy-start.5 = (s32[4]{0:T(128)S(1)}, s32[4]{0:T(128)}, u32[]{:S(2)}) copy-start(s32[4]{0:T(128)} %order_ref.11) | copy-start | bytes 52
  2.9 14.4 %copy-start.6 = (s32[11]{0:T(128)S(1)}, s32[11]{0:T(128)}, u32[]{:S(2)}) copy-start(s32[11]{0:T(128)} %offsets_ref.11) | copy-start | bytes 136
  2.9 8.1 %collective-permute-start = (bf16[384,256]{1,0:T(8,128)(2,1)}, bf16[384,256]{1,0:T(8,128)(2,1)S(1)}, u32[]{:S(2)}, u32[]{:S(2)}) collective-permute-start(bf16[384,256]{1,0:T(8,128)(2,1)} %shard_map.95.refs_0_), channel_id=1, source_target_pairs={{0,24},{8,16},{16,8},{24,0},{1,25},{9,17},{17,9},{25,1},{2,26},{10... | collective-permute-start | bytes 589832 | tf_op jit(solution)/shard_map/ppermute | solution.py:543
  8.0 9.1 %collective-permute-start.6 = (bf16[384,256]{1,0:T(8,128)(2,1)}, bf16[384,256]{1,0:T(8,128)(2,1)S(1)}, u32[]{:S(2)}, u32[]{:S(2)}) collective-permute-start(bf16[384,256]{1,0:T(8,128)(2,1)} %get-tuple-element.27), channel_id=1, source_target_pairs={{0,8},{8,0},{16,24},{24,16},{1,9},{9,1},{17,25},{25,17},{2,10},{10... | collective-permute-start | bytes 589832 | tf_op jit(solution)/shard_map/ppermute | solution.py:543
  8.7 8.3 %collective-permute-start.7 = (bf16[384,256]{1,0:T(8,128)(2,1)}, bf16[384,256]{1,0:T(8,128)(2,1)S(1)}, u32[]{:S(2)}, u32[]{:S(2)}) collective-permute-start(bf16[384,256]{1,0:T(8,128)(2,1)} %get-tuple-element.28), channel_id=1, source_target_pairs={{0,16},{8,24},{16,0},{24,8},{1,17},{9,25},{17,1},{25,9},{2,18},{10... | collective-permute-start | bytes 589832 | tf_op jit(solution)/shard_map/ppermute | solution.py:543
  8.8 11.2 %collective-permute-start.4 = (bf16[384,128]{1,0:T(8,128)(2,1)}, bf16[384,128]{1,0:T(8,128)(2,1)S(1)}, u32[]{:S(2)}, u32[]{:S(2)}) collective-permute-start(bf16[384,128]{1,0:T(8,128)(2,1)} %get-tuple-element.25), channel_id=1, source_target_pairs={{0,16},{8,24},{16,0},{24,8},{1,17},{9,25},{17,1},{25,9},{2,18},{10... | collective-permute-start | bytes 294920 | tf_op jit(solution)/shard_map/ppermute | solution.py:543
  10.8 9.3 %collective-permute-start.5 = (bf16[384,128]{1,0:T(8,128)(2,1)}, bf16[384,128]{1,0:T(8,128)(2,1)S(1)}, u32[]{:S(2)}, u32[]{:S(2)}) collective-permute-start(bf16[384,128]{1,0:T(8,128)(2,1)} %get-tuple-element.26), channel_id=1, source_target_pairs={{0,24},{8,16},{16,8},{24,0},{1,25},{9,17},{17,9},{25,1},{2,26},{10... | collective-permute-start | bytes 294920 | tf_op jit(solution)/shard_map/ppermute | solution.py:543
  11.0 1.4 %copy-start = (bf16[384,4,512]{2,1,0:T(4,128)(2,1)S(1)}, bf16[384,4,512]{2,1,0:T(4,128)(2,1)}, u32[]{:S(2)}) copy-start(bf16[384,4,512]{2,1,0:T(4,128)(2,1)} %x_hbm.5) | copy-start | bytes 4718596
  12.4 0.9 %copy-start.3 = (bf16[384,256]{1,0:T(8,128)(2,1)S(1)}, bf16[384,256]{1,0:T(8,128)(2,1)}, u32[]{:S(2)}) copy-start(bf16[384,256]{1,0:T(8,128)(2,1)} %get-tuple-element.20.refs_1_.refs_0_) | copy-start | bytes 589828
  14.6 8.4 %collective-permute-start.2 = (bf16[384,128]{1,0:T(8,128)(2,1)S(1)}, bf16[384,128]{1,0:T(8,128)(2,1)S(1)}, u32[]{:S(2)}, u32[]{:S(2)}) collective-permute-start(bf16[384,128]{1,0:T(8,128)(2,1)S(1)} %get-tuple-element.23), channel_id=1, source_target_pairs={{0,16},{8,24},{16,0},{24,8},{1,17},{9,25},{17,1},{25,9},{2,18},{10... | collective-permute-start | bytes 294920 | tf_op jit(solution)/shard_map/ppermute | solution.py:543
  17.1 6.5 %collective-permute-start.3 = (bf16[384,128]{1,0:T(8,128)(2,1)S(1)}, bf16[384,128]{1,0:T(8,128)(2,1)S(1)}, u32[]{:S(2)}, u32[]{:S(2)}) collective-permute-start(bf16[384,128]{1,0:T(8,128)(2,1)S(1)} %get-tuple-element.24), channel_id=1, source_target_pairs={{0,24},{8,16},{16,8},{24,0},{1,25},{9,17},{17,9},{25,1},{2,26},{10... | collective-permute-start | bytes 294920 | tf_op jit(solution)/shard_map/ppermute | solution.py:543
  17.1 3.0 %collective-permute-start.1 = (bf16[384,256]{1,0:T(8,128)(2,1)S(1)}, bf16[384,256]{1,0:T(8,128)(2,1)S(1)}, u32[]{:S(2)}, u32[]{:S(2)}) collective-permute-start(bf16[384,256]{1,0:T(8,128)(2,1)S(1)} %get-tuple-element.22), channel_id=1, source_target_pairs={{0,8},{8,0},{16,24},{24,16},{1,9},{9,1},{17,25},{25,17},{2,10},{10... | collective-permute-start | bytes 589832 | tf_op jit(solution)/shard_map/ppermute | solution.py:543
  25.2 1.4 %collective-permute-start.8 = (bf16[64,128]{1,0:T(8,128)(2,1)S(1)}, bf16[64,128]{1,0:T(8,128)(2,1)S(1)}, u32[]{:S(2)}, u32[]{:S(2)}) collective-permute-start(bf16[64,128]{1,0:T(8,128)(2,1)S(1)} %get-tuple-element.30), channel_id=1, source_target_pairs={{0,8},{1,9},{2,10},{3,11},{4,12},{5,13},{6,14},{7,15},{8,0},{9,1},... | collective-permute-start | bytes 49160 | tf_op jit(solution)/shard_map/ppermute | solution.py:543
  26.7 6.4 %collective-permute-start.11 = (bf16[64,128]{1,0:T(8,128)(2,1)S(1)}, bf16[64,128]{1,0:T(8,128)(2,1)S(1)}, u32[]{:S(2)}, u32[]{:S(2)}) collective-permute-start(bf16[64,128]{1,0:T(8,128)(2,1)S(1)} %add_convert_fusion), channel_id=1, source_target_pairs={{0,17},{1,16},{2,19},{3,18},{4,21},{5,20},{6,23},{7,22},{8,25},{9,... | collective-permute-start | bytes 49160 | tf_op jit(solution)/shard_map/ppermute | solution.py:543
  29.9 3.7 %collective-permute-start.10 = (bf16[64,128]{1,0:T(8,128)(2,1)S(1)}, bf16[64,128]{1,0:T(8,128)(2,1)S(1)}, u32[]{:S(2)}, u32[]{:S(2)}) collective-permute-start(bf16[64,128]{1,0:T(8,128)(2,1)S(1)} %add_convert_fusion), channel_id=1, source_target_pairs={{0,1},{1,0},{2,3},{3,2},{4,5},{5,4},{6,7},{7,6},{8,9},{9,8},{10,11... | collective-permute-start | bytes 49160 | tf_op jit(solution)/shard_map/ppermute | solution.py:543
  30.5 3.7 %collective-permute-start.9 = (bf16[64,128]{1,0:T(8,128)(2,1)S(1)}, bf16[64,128]{1,0:T(8,128)(2,1)S(1)}, u32[]{:S(2)}, u32[]{:S(2)}) collective-permute-start(bf16[64,128]{1,0:T(8,128)(2,1)S(1)} %add_convert_fusion), channel_id=1, source_target_pairs={{0,16},{1,17},{2,18},{3,19},{4,20},{5,21},{6,22},{7,23},{8,24},{9,... | collective-permute-start | bytes 49160 | tf_op jit(solution)/shard_map/ppermute | solution.py:543
  34.2 9.6 %copy-start.4 = (bf16[2,128,256]{2,1,0:T(8,128)(2,1)S(1)}, bf16[2,128,256]{2,1,0:T(8,128)(2,1)}, u32[]{:S(2)}) copy-start(bf16[2,128,256]{2,1,0:T(8,128)(2,1)} %constant.8.clone.spread_ref) | copy-start | bytes 393220
  34.3 6.1 %collective-permute-start.13 = (bf16[64,128]{1,0:T(8,128)(2,1)S(1)}, bf16[64,128]{1,0:T(8,128)(2,1)S(1)}, u32[]{:S(2)}, u32[]{:S(2)}) collective-permute-start(bf16[64,128]{1,0:T(8,128)(2,1)S(1)} %add_add_fusion.1), channel_id=1, source_target_pairs={{0,6},{1,7},{2,4},{3,5},{4,2},{5,3},{6,0},{7,1},{8,14},{9,15},{10,... | collective-permute-start | bytes 49160 | tf_op jit(solution)/shard_map/ppermute | solution.py:543
  37.9 4.6 %collective-permute-start.12 = (bf16[64,128]{1,0:T(8,128)(2,1)S(1)}, bf16[64,128]{1,0:T(8,128)(2,1)S(1)}, u32[]{:S(2)}, u32[]{:S(2)}) collective-permute-start(bf16[64,128]{1,0:T(8,128)(2,1)S(1)} %add_add_fusion.1), channel_id=1, source_target_pairs={{0,4},{1,5},{2,6},{3,7},{4,0},{5,1},{6,2},{7,3},{8,12},{9,13},{10,... | collective-permute-start | bytes 49160 | tf_op jit(solution)/shard_map/ppermute | solution.py:543
  37.9 4.6 %collective-permute-start.14 = (bf16[64,128]{1,0:T(8,128)(2,1)S(1)}, bf16[64,128]{1,0:T(8,128)(2,1)S(1)}, u32[]{:S(2)}, u32[]{:S(2)}) collective-permute-start(bf16[64,128]{1,0:T(8,128)(2,1)S(1)} %add_add_fusion.1), channel_id=1, source_target_pairs={{0,2},{1,3},{2,0},{3,1},{4,6},{5,7},{6,4},{7,5},{8,10},{9,11},{10,... | collective-permute-start | bytes 49160 | tf_op jit(solution)/shard_map/ppermute | solution.py:543
  42.6 1.3 %collective-permute-start.15 = (f32[64,128]{1,0:T(8,128)S(1)}, f32[64,128]{1,0:T(8,128)S(1)}, u32[]{:S(2)}, u32[]{:S(2)}) collective-permute-start(f32[64,128]{1,0:T(8,128)S(1)} %add_add_fusion.half_ref), channel_id=1, source_target_pairs={{0,8},{1,9},{2,10},{3,11},{4,12},{5,13},{6,14},{7,15},{8,0},{9,1},... | collective-permute-start | bytes 98312 | tf_op jit(solution)/shard_map/ppermute | solution.py:543

commit v15 on v14

--- a/solution.py
+++ b/solution.py
@@ -226,7 +226,7 @@
     pieces = refs[:lanes]
     refs = refs[lanes:]
     if last:
-        before_ref, gram_ref, s_ref, record, masked = refs
+        before_ref, _, gram_ref, s_ref, record, masked = refs
     else:
         *before_refs, gram_ref, record, s_ref, masked = refs
     fill_record(base, order_ref, pieces, record, jnp.sqrt(w_ref[...]))
@@ -579,18 +579,20 @@
     size = lanes * groups
     bits = [b * groups for b in powers(lanes)] + powers(groups)
     parts = [weights[:, base : base + width] for base, width in chunks]
+    head = (block_order, offsets)
     before = []
-    for at, base in enumerate(starts):
-        last = at == len(chunks) - 1
-        args = (block_order, offsets, parts[at], tables, arrived[at], before, base, last, scale)
-        before, before_last = gram_part(*args), before
-    before, (given, scaled) = before_last, before
+    for at in range(2):
+        args = (*head, parts[at], tables, arrived[at], before, starts[at], False, scale)
+        before = gram_part(*args)
+    spectra = [spectrum(*head, tables[0], arrived[0], starts[0], before)]
+    args = (*head, parts[2], tables, arrived[2], [*before, spectra[0]], starts[2], True, scale)
+    given, scaled = gram_part(*args)
 
     other = swap(given, axes, bits[0], size)
     keep = own_part(scaled, tables[1], before[0], scale)
-    spectra = [
-        spectrum(block_order, offsets, tables[0], pieces, base, [keep])
-        for base, pieces in zip(starts, arrived)
+    spectra += [
+        spectrum(*head, tables[0], pieces, base, [keep])
+        for base, pieces in zip(starts[1:], arrived[1:])
     ]
     half = keep.astype(F32) + other.astype(F32)
     for at in range(1, len(bits), 2):
@@ -605,8 +607,8 @@
             terms = [a + b for a, b in zip(terms[::2], terms[1::2])]
         half = terms[0]
         if at == 1:
-            half, *spectra[1:] = lax.optimization_barrier((half, *spectra[1:]))
-    half, spectra[0] = lax.optimization_barrier((half, spectra[0]))
+            half, spectra[1] = lax.optimization_barrier((half, spectra[1]))
+    half, spectra[2] = lax.optimization_barrier((half, spectra[2]))
     other = swap(half, axes, bits[0], size)
 
     spread = jnp.asarray(spread_table())

time: 48.8 us -> 49 us (level)
  transfers between devices with their start and end apart: 16 -> 16, of which waited for: 8 -> 6; matrix products, arithmetic and copies ran while one was open for 0% -> 0% of each run, Pallas kernels for 28% -> 28%
where the time goes in v15:
time: 49 us; the launch traced here: 48.8 us
  Pallas kernels  22.3 us (46%)
  starting transfers between devices  16.7 us (34%)
  waiting for transfers between devices  6.46 us (13%)
  local copies, waits for them, and re-layouts  2.38 us (5%)
  between operations  0.87 us (2%)
    ppermute x16, starting transfers between devices, swap(): return lax.ppermute(x, axes, [(i, i ^ mask) for i in range(size)])  16.7 us
    pallas_call x3, Pallas kernels, gram_part(): pl.pallas_call(functools.partial(gram_kernel, lanes, base, scale, last),...  6.61 us
    ppermute x16, waiting for transfers between devices, swap(): return lax.ppermute(x, axes, [(i, i ^ mask) for i in range(size)])  6.46 us
    pallas_call x3, Pallas kernels, pack(): pl.pallas_call(functools.partial(pack_kernel, jobs, parts, len(after)), o...  6.1 us
    pallas_call x1, Pallas kernels, mode_fields(): pl.pallas_call(functools.partial(mode_kernel, len(spectra), share), out_s...  4.94 us
    pallas_call x3, Pallas kernels, spectrum(): pl.pallas_call(functools.partial(spectrum_kernel, lanes, base), out_shape...  4.03 us
    unnamed x18, local copies, waits for them, and re-layouts  2.38 us
  transfers between devices with their start and end apart: 16, of which 6 were waited for; matrix products, arithmetic and copies ran while one was open for 0% of the time, Pallas kernels for 28%

profile of v15, /device:TPU:0, one launch (start us, length us, event | category | flops | bytes accessed | tf_op | source)
XLA Modules:
  0.0 48.8 jit_solution(16276548838843823153)
XLA Ops:
  0.6 2.2 %shard_map.95.refs_0_ = bf16[384,256]{1,0:T(8,128)(2,1)} custom-call(s32[1,4]{1,0:T(1,128)} %owner_hbm.5, bf16[384,4,512]{2,1,0:T(4,128)(2,1)} %x_hbm.5), custom_call_target="tpu_custom_call" | custom-call | flops 1000 | bytes 1000 | tf_op jit(solution)/shard_map/pallas_call | solution.py:150
  2.8 0.0 copy-start.7
  2.8 0.0 copy-start.8
  2.9 0.0 copy-start.1
  2.9 0.0 copy-start.2
  2.9 0.0 copy-start.5
  2.9 0.0 copy-start.6
  2.9 2.5 %collective-permute-start = (bf16[384,256]{1,0:T(8,128)(2,1)}, bf16[384,256]{1,0:T(8,128)(2,1)S(1)}, u32[]{:S(2)}, u32[]{:S(2)}) collective-permute-start(bf16[384,256]{1,0:T(8,128)(2,1)} %shard_map.95.refs_0_), channel_id=1, source_target_pairs={{0,24},{8,16},{16,8},{24,0},{1,25},{9,17},{17,9},{25,1},{2,26},{10... | collective-permute-start | bytes 589832 | tf_op jit(solution)/shard_map/ppermute | solution.py:543
  5.4 2.6 %shard_map.96 = (bf16[384,256]{1,0:T(8,128)(2,1)}, bf16[384,256]{1,0:T(8,128)(2,1)}, bf16[384,256]{1,0:T(8,128)(2,1)}, bf16[384,128]{1,0:T(8,128)(2,1)}, bf16[384,128]{1,0:T(8,128)(2,1)}) custom-call(s32[1,4]{1,0:T(1,128)} %owner_hbm.5, bf16[384,4,512]{2,1,0:T(4,128)(2,1)} %x_hbm.5, bf16[384,256]{1,0:T(8,128)(2,1)} %shard_map.95.refs_0_), custom_call_target="tpu_custom_call" | custom-call | flops 1000 | bytes 1000 | tf_op jit(solution)/shard_map/pallas_call | solution.py:150
  8.0 0.7 %collective-permute-start.6 = (bf16[384,256]{1,0:T(8,128)(2,1)}, bf16[384,256]{1,0:T(8,128)(2,1)S(1)}, u32[]{:S(2)}, u32[]{:S(2)}) collective-permute-start(bf16[384,256]{1,0:T(8,128)(2,1)} %get-tuple-element.26), channel_id=1, source_target_pairs={{0,8},{8,0},{16,24},{24,16},{1,9},{9,1},{17,25},{25,17},{2,10},{10... | collective-permute-start | bytes 589832 | tf_op jit(solution)/shard_map/ppermute | solution.py:543
  8.7 0.1 collective-permute-start.7
  8.8 2.0 %collective-permute-start.4 = (bf16[384,128]{1,0:T(8,128)(2,1)}, bf16[384,128]{1,0:T(8,128)(2,1)S(1)}, u32[]{:S(2)}, u32[]{:S(2)}) collective-permute-start(bf16[384,128]{1,0:T(8,128)(2,1)} %get-tuple-element.24), channel_id=1, source_target_pairs={{0,16},{8,24},{16,0},{24,8},{1,17},{9,25},{17,1},{25,9},{2,18},{10... | collective-permute-start | bytes 294920 | tf_op jit(solution)/shard_map/ppermute | solution.py:543
  10.8 0.0 collective-permute-start.5
  10.8 0.2 collective-permute-done.refs_0_.refs_3_
  11.0 0.0 copy-done.7
  11.0 0.0 copy-start
  11.0 1.4 %copy-done = bf16[384,4,512]{2,1,0:T(4,128)(2,1)S(1)} copy-done((bf16[384,4,512]{2,1,0:T(4,128)(2,1)S(1)}, bf16[384,4,512]{2,1,0:T(4,128)(2,1)}, u32[]{:S(2)}) %copy-start) | copy-done | bytes 1572888
  12.4 0.0 copy-start.3
  12.4 0.9 %copy-done.3 = bf16[384,256]{1,0:T(8,128)(2,1)S(1)} copy-done((bf16[384,256]{1,0:T(8,128)(2,1)S(1)}, bf16[384,256]{1,0:T(8,128)(2,1)}, u32[]{:S(2)}) %copy-start.3) | copy-done | bytes 196632
  13.3 1.3 %shard_map.97 = (bf16[384,256]{1,0:T(8,128)(2,1)S(1)}, bf16[384,256]{1,0:T(8,128)(2,1)S(1)}, bf16[384,128]{1,0:T(8,128)(2,1)S(1)}, bf16[384,128]{1,0:T(8,128)(2,1)S(1)}) custom-call(s32[1,4]{1,0:T(1,128)S(1)} %copy-done.7, bf16[384,4,512]{2,1,0:T(4,128)(2,1)S(1)} %copy-done, bf16[384,256]{1,0:T(8,128)(2,1)S(1)} %collective-permute-done.refs_0_.refs_3_, ...), custom_call_target="tpu_custom_call" | custom-call | flops 1000 | bytes 1000 | tf_op jit(solution)/shard_map/pallas_call | solution.py:150
  14.6 2.4 %collective-permute-start.2 = (bf16[384,128]{1,0:T(8,128)(2,1)S(1)}, bf16[384,128]{1,0:T(8,128)(2,1)S(1)}, u32[]{:S(2)}, u32[]{:S(2)}) collective-permute-start(bf16[384,128]{1,0:T(8,128)(2,1)S(1)} %get-tuple-element.22), channel_id=1, source_target_pairs={{0,16},{8,24},{16,0},{24,8},{1,17},{9,25},{17,1},{25,9},{2,18},{10... | collective-permute-start | bytes 294920 | tf_op jit(solution)/shard_map/ppermute | solution.py:543
  17.1 0.0 collective-permute-done.6.refs_1_
  17.1 0.0 collective-permute-start.3
  17.1 0.0 collective-permute-done.7.refs_2_
  17.1 0.2 collective-permute-start.1
  17.3 0.0 copy-done.8
  17.3 0.0 copy-done.1
  17.3 0.0 copy-done.2
  17.3 0.0 copy-done.5
  17.3 0.0 copy-done.6
  17.3 2.7 %shard_map.98.refs_4_ = f32[128,128]{1,0:T(8,128)S(1)} custom-call(s32[4]{0:T(128)S(1)} %copy-done.5, s32[11]{0:T(128)S(1)} %copy-done.6, f32[1,256]{1,0:T(1,128)S(1)} %slice.14.w_ref, bf16[512,256]{1,0:T(8,128)(2,1)S(1)} %copy-done.1, bf16[2816,128]{1,0:T(8,128)(2,1)S(1)} %copy-done.2, bf16[384,256]{1,0:T(8,128)(2,1)S(1)} %copy-done.3, ...), custom_call_target="tpu_custom_call" | custom-call | flops 1000 | bytes 1000 | tf_op jit(solution)/shard_map/pallas_call | solution.py:256
  20.0 0.0 collective-permute-done.4.refs_2_
  20.0 0.0 collective-permute-done.5.refs_3_
  20.0 0.0 collective-permute-done.1.refs_1_
  20.0 2.2 %shard_map.99.refs_4_.before_ref = f32[128,128]{1,0:T(8,128)S(1)} custom-call(s32[4]{0:T(128)S(1)} %copy-done.5, s32[11]{0:T(128)S(1)} %copy-done.6, f32[1,128]{1,0:T(1,128)S(1)} %get-tuple-element.38.w_ref, bf16[512,256]{1,0:T(8,128)(2,1)S(1)} %copy-done.1, bf16[2816,128]{1,0:T(8,128)(2,1)S(1)} %copy-done.2, ...), custom_call_target="tpu_custom_call" | custom-call | flops 1000 | bytes 1000 | tf_op jit(solution)/shard_map/pallas_call | solution.py:256
  22.2 1.6 %shard_map.100.refs_5_.refs_0_ = f32[22,128,256]{2,1,0:T(8,128)S(1)} custom-call(s32[4]{0:T(128)S(1)} %copy-done.5, s32[11]{0:T(128)S(1)} %copy-done.6, bf16[512,256]{1,0:T(8,128)(2,1)S(1)} %copy-done.1, bf16[384,256]{1,0:T(8,128)(2,1)S(1)} %copy-done.3, bf16[384,256]{1,0:T(8,128)(2,1)S(1)} %collective-permute-done.6.refs_1_, ...), custom_call_target="tpu_custom_call" | custom-call | flops 1000 | bytes 1000 | tf_op jit(solution)/shard_map/pallas_call | solution.py:295
  23.9 0.0 collective-permute-done.2.refs_2_
  23.9 0.0 collective-permute-done.3.refs_3_
  23.9 1.7 %shard_map.101 = (bf16[64,128]{1,0:T(8,128)(2,1)S(1)}, f32[22,128,128]{2,1,0:T(8,128)S(1)}) custom-call(s32[4]{0:T(128)S(1)} %copy-done.5, s32[11]{0:T(128)S(1)} %copy-done.6, f32[1,128]{1,0:T(1,128)S(1)} %get-tuple-element.39.w_ref, bf16[512,256]{1,0:T(8,128)(2,1)S(1)} %copy-done.1, bf16[2816,128]{1,0:T(8,128)(2,1)S(1)} %copy-done.2, ...), custom_call_target="tpu_custom_call" | custom-call | flops 1000 | bytes 1000 | tf_op jit(solution)/shard_map/pallas_call | solution.py:256
  25.6 0.8 %collective-permute-start.8 = (bf16[64,128]{1,0:T(8,128)(2,1)S(1)}, bf16[64,128]{1,0:T(8,128)(2,1)S(1)}, u32[]{:S(2)}, u32[]{:S(2)}) collective-permute-start(bf16[64,128]{1,0:T(8,128)(2,1)S(1)} %get-tuple-element.29), channel_id=1, source_target_pairs={{0,8},{1,9},{2,10},{3,11},{4,12},{5,13},{6,14},{7,15},{8,0},{9,1},... | collective-permute-start | bytes 49160 | tf_op jit(solution)/shard_map/ppermute | solution.py:543
  26.4 0.7 %shard_map.102.refs_4_ = bf16[64,128]{1,0:T(8,128)(2,1)S(1)} custom-call(f32[22,128,128]{2,1,0:T(8,128)S(1)} %get-tuple-element.28.s_ref, bf16[2816,128]{1,0:T(8,128)(2,1)S(1)} %copy-done.2, f32[128,128]{1,0:T(8,128)S(1)} %shard_map.99.refs_4_.before_ref), custom_call_target="tpu_custom_call" | custom-call | flops 1000000000 | bytes 3000000 | tf_op jit(solution)/shard_map/pallas_call | solution.py:274
  27.0 0.2 collective-permute-done.8
  27.2 2.7 %collective-permute-start.11 = (bf16[64,128]{1,0:T(8,128)(2,1)S(1)}, bf16[64,128]{1,0:T(8,128)(2,1)S(1)}, u32[]{:S(2)}, u32[]{:S(2)}) collective-permute-start(bf16[64,128]{1,0:T(8,128)(2,1)S(1)} %add_convert_fusion), channel_id=1, source_target_pairs={{0,17},{1,16},{2,19},{3,18},{4,21},{5,20},{6,23},{7,22},{8,25},{9,... | collective-permute-start | bytes 49160 | tf_op jit(solution)/shard_map/ppermute | solution.py:543
  29.9 0.5 %collective-permute-start.10 = (bf16[64,128]{1,0:T(8,128)(2,1)S(1)}, bf16[64,128]{1,0:T(8,128)(2,1)S(1)}, u32[]{:S(2)}, u32[]{:S(2)}) collective-permute-start(bf16[64,128]{1,0:T(8,128)(2,1)S(1)} %add_convert_fusion), channel_id=1, source_target_pairs={{0,1},{1,0},{2,3},{3,2},{4,5},{5,4},{6,7},{7,6},{8,9},{9,8},{10,11... | collective-permute-start | bytes 49160 | tf_op jit(solution)/shard_map/ppermute | solution.py:543
  30.5 0.3 collective-permute-start.9
  30.8 1.2 %shard_map.103.refs_1_ = f32[22,128,128]{2,1,0:T(8,128)S(1)} custom-call(s32[4]{0:T(128)S(1)} %copy-done.5, s32[11]{0:T(128)S(1)} %copy-done.6, bf16[512,256]{1,0:T(8,128)(2,1)S(1)} %copy-done.1, bf16[384,256]{1,0:T(8,128)(2,1)S(1)} %get-tuple-element.20.refs_0_, bf16[384,256]{1,0:T(8,128)(2,1)S(1)} %collective-permute-done.1.refs_1_, ...), custom_call_target="tpu_custom_call" | custom-call | flops 1000 | bytes 1000 | tf_op jit(solution)/shard_map/pallas_call | solution.py:295
  32.0 0.0 copy-start.4
  32.0 0.0 collective-permute-done.11
  32.0 1.7 %collective-permute-done.10 = bf16[64,128]{1,0:T(8,128)(2,1)S(1)} collective-permute-done((bf16[64,128]{1,0:T(8,128)(2,1)S(1)}, bf16[64,128]{1,0:T(8,128)(2,1)S(1)}, u32[]{:S(2)}, u32[]{:S(2)}) %collective-permute-start.10) | collective-permute-done | bytes 16416 | tf_op jit(solution)/shard_map/ppermute | solution.py:543
  33.7 0.5 %collective-permute-done.9 = bf16[64,128]{1,0:T(8,128)(2,1)S(1)} collective-permute-done((bf16[64,128]{1,0:T(8,128)(2,1)S(1)}, bf16[64,128]{1,0:T(8,128)(2,1)S(1)}, u32[]{:S(2)}, u32[]{:S(2)}) %collective-permute-start.9) | collective-permute-done | bytes 16416 | tf_op jit(solution)/shard_map/ppermute | solution.py:543
  34.2 3.7 %collective-permute-start.13 = (bf16[64,128]{1,0:T(8,128)(2,1)S(1)}, bf16[64,128]{1,0:T(8,128)(2,1)S(1)}, u32[]{:S(2)}, u32[]{:S(2)}) collective-permute-start(bf16[64,128]{1,0:T(8,128)(2,1)S(1)} %add_add_fusion.1), channel_id=1, source_target_pairs={{0,6},{1,7},{2,4},{3,5},{4,2},{5,3},{6,0},{7,1},{8,14},{9,15},{10,... | collective-permute-start | bytes 49160 | tf_op jit(solution)/shard_map/ppermute | solution.py:543
  37.9 0.0 collective-permute-start.12
  37.9 0.8 %collective-permute-start.14 = (bf16[64,128]{1,0:T(8,128)(2,1)S(1)}, bf16[64,128]{1,0:T(8,128)(2,1)S(1)}, u32[]{:S(2)}, u32[]{:S(2)}) collective-permute-start(bf16[64,128]{1,0:T(8,128)(2,1)S(1)} %add_add_fusion.1), channel_id=1, source_target_pairs={{0,2},{1,3},{2,0},{3,1},{4,6},{5,7},{6,4},{7,5},{8,10},{9,11},{10,... | collective-permute-start | bytes 49160 | tf_op jit(solution)/shard_map/ppermute | solution.py:543
  38.7 1.2 %shard_map.104.refs_2_ = f32[22,128,128]{2,1,0:T(8,128)S(1)} custom-call(s32[4]{0:T(128)S(1)} %copy-done.5, s32[11]{0:T(128)S(1)} %copy-done.6, bf16[512,256]{1,0:T(8,128)(2,1)S(1)} %copy-done.1, bf16[384,256]{1,0:T(8,128)(2,1)S(1)} %get-tuple-element.20.refs_0_, bf16[384,256]{1,0:T(8,128)(2,1)S(1)} %collective-permute-done.1.refs_1_, ...), custom_call_target="tpu_custom_call" | custom-call | flops 1000 | bytes 1000 | tf_op jit(solution)/shard_map/pallas_call | solution.py:295
  39.9 0.0 collective-permute-done.13
  39.9 2.6 %collective-permute-done.12 = bf16[64,128]{1,0:T(8,128)(2,1)S(1)} collective-permute-done((bf16[64,128]{1,0:T(8,128)(2,1)S(1)}, bf16[64,128]{1,0:T(8,128)(2,1)S(1)}, u32[]{:S(2)}, u32[]{:S(2)}) %collective-permute-start.12) | collective-permute-done | bytes 16416 | tf_op jit(solution)/shard_map/ppermute | solution.py:543
  42.5 0.0 collective-permute-done.14
  42.5 0.1 collective-permute-start.15
  42.6 1.2 %collective-permute-done.15.other_ref = f32[64,128]{1,0:T(8,128)S(1)} collective-permute-done((f32[64,128]{1,0:T(8,128)S(1)}, f32[64,128]{1,0:T(8,128)S(1)}, u32[]{:S(2)}, u32[]{:S(2)}) %collective-permute-start.15) | collective-permute-done | bytes 32800 | tf_op jit(solution)/shard_map/ppermute | solution.py:543
  43.8 0.0 copy-done.4
  43.8 4.9 %shard_map.105 = (bf16[2,11,128,512]{3,2,1,0:T(8,128)(2,1)}, f32[11,11,2,16]{3,2,1,0:T(2,128)}) custom-call(f32[64,128]{1,0:T(8,128)S(1)} %add_add_fusion.half_ref, f32[64,128]{1,0:T(8,128)S(1)} %collective-permute-done.15.other_ref, bf16[2,128,256]{2,1,0:T(8,128)(2,1)S(1)} %copy-done.4, f32[22,128,256]{2,1,0:T(8,128)S(1)} %shard_map.100.refs_5_.refs_0_, ...), custom_call_target="tpu_custom_call" | custom-call | tf_op jit(solution)/shard_map/pallas_call | solution.py:516
  (5 shorter events, 0.0 us)
Async XLA Ops:
  2.8 8.2 %copy-start.7 = (s32[1,4]{1,0:T(1,128)S(1)}, s32[1,4]{1,0:T(1,128)}, u32[]{:S(2)}) copy-start(s32[1,4]{1,0:T(1,128)} %owner_hbm.5) | copy-start | bytes 52
  2.8 14.4 %copy-start.8 = (f32[512]{0:T(512)S(1)}, f32[512]{0:T(512)}, u32[]{:S(2)}) copy-start(f32[512]{0:T(512)} %param.9) | copy-start | bytes 6148
  2.9 14.4 %copy-start.1 = (bf16[512,256]{1,0:T(8,128)(2,1)S(1)}, bf16[512,256]{1,0:T(8,128)(2,1)}, u32[]{:S(2)}) copy-start(bf16[512,256]{1,0:T(8,128)(2,1)} %constant.6.clone.f_ref) | copy-start | bytes 786436
  2.9 14.4 %copy-start.2 = (bf16[2816,128]{1,0:T(8,128)(2,1)S(1)}, bf16[2816,128]{1,0:T(8,128)(2,1)}, u32[]{:S(2)}) copy-start(bf16[2816,128]{1,0:T(8,128)(2,1)} %constant.7.clone.pick_ref) | copy-start | bytes 2162692
  2.9 14.4 %copy-start.5 = (s32[4]{0:T(128)S(1)}, s32[4]{0:T(128)}, u32[]{:S(2)}) copy-start(s32[4]{0:T(128)} %order_ref.11) | copy-start | bytes 52
  2.9 14.4 %copy-start.6 = (s32[11]{0:T(128)S(1)}, s32[11]{0:T(128)}, u32[]{:S(2)}) copy-start(s32[11]{0:T(128)} %offsets_ref.11) | copy-start | bytes 136
  2.9 8.1 %collective-permute-start = (bf16[384,256]{1,0:T(8,128)(2,1)}, bf16[384,256]{1,0:T(8,128)(2,1)S(1)}, u32[]{:S(2)}, u32[]{:S(2)}) collective-permute-start(bf16[384,256]{1,0:T(8,128)(2,1)} %shard_map.95.refs_0_), channel_id=1, source_target_pairs={{0,24},{8,16},{16,8},{24,0},{1,25},{9,17},{17,9},{25,1},{2,26},{10... | collective-permute-start | bytes 589832 | tf_op jit(solution)/shard_map/ppermute | solution.py:543
  8.0 9.1 %collective-permute-start.6 = (bf16[384,256]{1,0:T(8,128)(2,1)}, bf16[384,256]{1,0:T(8,128)(2,1)S(1)}, u32[]{:S(2)}, u32[]{:S(2)}) collective-permute-start(bf16[384,256]{1,0:T(8,128)(2,1)} %get-tuple-element.26), channel_id=1, source_target_pairs={{0,8},{8,0},{16,24},{24,16},{1,9},{9,1},{17,25},{25,17},{2,10},{10... | collective-permute-start | bytes 589832 | tf_op jit(solution)/shard_map/ppermute | solution.py:543
  8.7 8.3 %collective-permute-start.7 = (bf16[384,256]{1,0:T(8,128)(2,1)}, bf16[384,256]{1,0:T(8,128)(2,1)S(1)}, u32[]{:S(2)}, u32[]{:S(2)}) collective-permute-start(bf16[384,256]{1,0:T(8,128)(2,1)} %get-tuple-element.27), channel_id=1, source_target_pairs={{0,16},{8,24},{16,0},{24,8},{1,17},{9,25},{17,1},{25,9},{2,18},{10... | collective-permute-start | bytes 589832 | tf_op jit(solution)/shard_map/ppermute | solution.py:543
  8.8 11.2 %collective-permute-start.4 = (bf16[384,128]{1,0:T(8,128)(2,1)}, bf16[384,128]{1,0:T(8,128)(2,1)S(1)}, u32[]{:S(2)}, u32[]{:S(2)}) collective-permute-start(bf16[384,128]{1,0:T(8,128)(2,1)} %get-tuple-element.24), channel_id=1, source_target_pairs={{0,16},{8,24},{16,0},{24,8},{1,17},{9,25},{17,1},{25,9},{2,18},{10... | collective-permute-start | bytes 294920 | tf_op jit(solution)/shard_map/ppermute | solution.py:543
  10.8 9.3 %collective-permute-start.5 = (bf16[384,128]{1,0:T(8,128)(2,1)}, bf16[384,128]{1,0:T(8,128)(2,1)S(1)}, u32[]{:S(2)}, u32[]{:S(2)}) collective-permute-start(bf16[384,128]{1,0:T(8,128)(2,1)} %get-tuple-element.25), channel_id=1, source_target_pairs={{0,24},{8,16},{16,8},{24,0},{1,25},{9,17},{17,9},{25,1},{2,26},{10... | collective-permute-start | bytes 294920 | tf_op jit(solution)/shard_map/ppermute | solution.py:543
  11.0 1.4 %copy-start = (bf16[384,4,512]{2,1,0:T(4,128)(2,1)S(1)}, bf16[384,4,512]{2,1,0:T(4,128)(2,1)}, u32[]{:S(2)}) copy-start(bf16[384,4,512]{2,1,0:T(4,128)(2,1)} %x_hbm.5) | copy-start | bytes 4718596
  12.4 0.9 %copy-start.3 = (bf16[384,256]{1,0:T(8,128)(2,1)S(1)}, bf16[384,256]{1,0:T(8,128)(2,1)}, u32[]{:S(2)}) copy-start(bf16[384,256]{1,0:T(8,128)(2,1)} %get-tuple-element.19.refs_1_.refs_0_) | copy-start | bytes 589828
  14.6 9.3 %collective-permute-start.2 = (bf16[384,128]{1,0:T(8,128)(2,1)S(1)}, bf16[384,128]{1,0:T(8,128)(2,1)S(1)}, u32[]{:S(2)}, u32[]{:S(2)}) collective-permute-start(bf16[384,128]{1,0:T(8,128)(2,1)S(1)} %get-tuple-element.22), channel_id=1, source_target_pairs={{0,16},{8,24},{16,0},{24,8},{1,17},{9,25},{17,1},{25,9},{2,18},{10... | collective-permute-start | bytes 294920 | tf_op jit(solution)/shard_map/ppermute | solution.py:543
  17.1 6.8 %collective-permute-start.3 = (bf16[384,128]{1,0:T(8,128)(2,1)S(1)}, bf16[384,128]{1,0:T(8,128)(2,1)S(1)}, u32[]{:S(2)}, u32[]{:S(2)}) collective-permute-start(bf16[384,128]{1,0:T(8,128)(2,1)S(1)} %get-tuple-element.23), channel_id=1, source_target_pairs={{0,24},{8,16},{16,8},{24,0},{1,25},{9,17},{17,9},{25,1},{2,26},{10... | collective-permute-start | bytes 294920 | tf_op jit(solution)/shard_map/ppermute | solution.py:543
  17.1 3.0 %collective-permute-start.1 = (bf16[384,256]{1,0:T(8,128)(2,1)S(1)}, bf16[384,256]{1,0:T(8,128)(2,1)S(1)}, u32[]{:S(2)}, u32[]{:S(2)}) collective-permute-start(bf16[384,256]{1,0:T(8,128)(2,1)S(1)} %get-tuple-element.21), channel_id=1, source_target_pairs={{0,8},{8,0},{16,24},{24,16},{1,9},{9,1},{17,25},{25,17},{2,10},{10... | collective-permute-start | bytes 589832 | tf_op jit(solution)/shard_map/ppermute | solution.py:543
  25.6 1.6 %collective-permute-start.8 = (bf16[64,128]{1,0:T(8,128)(2,1)S(1)}, bf16[64,128]{1,0:T(8,128)(2,1)S(1)}, u32[]{:S(2)}, u32[]{:S(2)}) collective-permute-start(bf16[64,128]{1,0:T(8,128)(2,1)S(1)} %get-tuple-element.29), channel_id=1, source_target_pairs={{0,8},{1,9},{2,10},{3,11},{4,12},{5,13},{6,14},{7,15},{8,0},{9,1},... | collective-permute-start | bytes 49160 | tf_op jit(solution)/shard_map/ppermute | solution.py:543
  27.2 4.8 %collective-permute-start.11 = (bf16[64,128]{1,0:T(8,128)(2,1)S(1)}, bf16[64,128]{1,0:T(8,128)(2,1)S(1)}, u32[]{:S(2)}, u32[]{:S(2)}) collective-permute-start(bf16[64,128]{1,0:T(8,128)(2,1)S(1)} %add_convert_fusion), channel_id=1, source_target_pairs={{0,17},{1,16},{2,19},{3,18},{4,21},{5,20},{6,23},{7,22},{8,25},{9,... | collective-permute-start | bytes 49160 | tf_op jit(solution)/shard_map/ppermute | solution.py:543
  29.9 3.7 %collective-permute-start.10 = (bf16[64,128]{1,0:T(8,128)(2,1)S(1)}, bf16[64,128]{1,0:T(8,128)(2,1)S(1)}, u32[]{:S(2)}, u32[]{:S(2)}) collective-permute-start(bf16[64,128]{1,0:T(8,128)(2,1)S(1)} %add_convert_fusion), channel_id=1, source_target_pairs={{0,1},{1,0},{2,3},{3,2},{4,5},{5,4},{6,7},{7,6},{8,9},{9,8},{10,11... | collective-permute-start | bytes 49160 | tf_op jit(solution)/shard_map/ppermute | solution.py:543
  30.5 3.7 %collective-permute-start.9 = (bf16[64,128]{1,0:T(8,128)(2,1)S(1)}, bf16[64,128]{1,0:T(8,128)(2,1)S(1)}, u32[]{:S(2)}, u32[]{:S(2)}) collective-permute-start(bf16[64,128]{1,0:T(8,128)(2,1)S(1)} %add_convert_fusion), channel_id=1, source_target_pairs={{0,16},{1,17},{2,18},{3,19},{4,20},{5,21},{6,22},{7,23},{8,24},{9,... | collective-permute-start | bytes 49160 | tf_op jit(solution)/shard_map/ppermute | solution.py:543
  32.0 11.8 %copy-start.4 = (bf16[2,128,256]{2,1,0:T(8,128)(2,1)S(1)}, bf16[2,128,256]{2,1,0:T(8,128)(2,1)}, u32[]{:S(2)}) copy-start(bf16[2,128,256]{2,1,0:T(8,128)(2,1)} %constant.8.clone.spread_ref) | copy-start | bytes 393220
  34.2 5.7 %collective-permute-start.13 = (bf16[64,128]{1,0:T(8,128)(2,1)S(1)}, bf16[64,128]{1,0:T(8,128)(2,1)S(1)}, u32[]{:S(2)}, u32[]{:S(2)}) collective-permute-start(bf16[64,128]{1,0:T(8,128)(2,1)S(1)} %add_add_fusion.1), channel_id=1, source_target_pairs={{0,6},{1,7},{2,4},{3,5},{4,2},{5,3},{6,0},{7,1},{8,14},{9,15},{10,... | collective-permute-start | bytes 49160 | tf_op jit(solution)/shard_map/ppermute | solution.py:543
  37.9 4.6 %collective-permute-start.12 = (bf16[64,128]{1,0:T(8,128)(2,1)S(1)}, bf16[64,128]{1,0:T(8,128)(2,1)S(1)}, u32[]{:S(2)}, u32[]{:S(2)}) collective-permute-start(bf16[64,128]{1,0:T(8,128)(2,1)S(1)} %add_add_fusion.1), channel_id=1, source_target_pairs={{0,4},{1,5},{2,6},{3,7},{4,0},{5,1},{6,2},{7,3},{8,12},{9,13},{10,... | collective-permute-start | bytes 49160 | tf_op jit(solution)/shard_map/ppermute | solution.py:543
  37.9 4.6 %collective-permute-start.14 = (bf16[64,128]{1,0:T(8,128)(2,1)S(1)}, bf16[64,128]{1,0:T(8,128)(2,1)S(1)}, u32[]{:S(2)}, u32[]{:S(2)}) collective-permute-start(bf16[64,128]{1,0:T(8,128)(2,1)S(1)} %add_add_fusion.1), channel_id=1, source_target_pairs={{0,2},{1,3},{2,0},{3,1},{4,6},{5,7},{6,4},{7,5},{8,10},{9,11},{10,... | collective-permute-start | bytes 49160 | tf_op jit(solution)/shard_map/ppermute | solution.py:543
  42.5 1.3 %collective-permute-start.15 = (f32[64,128]{1,0:T(8,128)S(1)}, f32[64,128]{1,0:T(8,128)S(1)}, u32[]{:S(2)}, u32[]{:S(2)}) collective-permute-start(f32[64,128]{1,0:T(8,128)S(1)} %add_add_fusion.half_ref), channel_id=1, source_target_pairs={{0,8},{1,9},{2,10},{3,11},{4,12},{5,13},{6,14},{7,15},{8,0},{9,1},... | collective-permute-start | bytes 98312 | tf_op jit(solution)/shard_map/ppermute | solution.py:543

commit v16 on v14

--- a/solution.py
+++ b/solution.py
@@ -561,15 +561,15 @@
         return [swap(p, "tm", d, lanes) for d, p in zip(range(begin, end), packed)]
 
     c0, c1, c2 = chunks
-    packed = pack(owner, snapshots, [(*c0, lanes - 1, lanes)], FIRST_LIMIT)
-    first = send(packed, lanes - 1, lanes)
-    jobs = [(*c0, 0, lanes - 1), (*c1, NEAR, lanes)]
+    packed = pack(owner, snapshots, [(*c0, NEAR, NEAR + 1)], FIRST_LIMIT)
+    first = send(packed, NEAR, NEAR + 1)
+    jobs = [(*c0, 0, NEAR), (*c0, NEAR + 1, lanes), (*c1, NEAR, lanes)]
     middle = pack(owner, snapshots, jobs, SECOND_LIMIT, packed)
     jobs = [(c1[0], c1[1] + c2[1], 0, NEAR), (*c2, NEAR, lanes)]
     rest = pack(owner, snapshots, jobs, LAST_LIMIT, [*first, middle[0]])
     near = [rest[0], *send(rest[1:], 1, NEAR)]
     arrived = [
-        [middle[0], *send(middle[1:], 1, lanes - 1), *first],
+        [middle[0], *send(middle[1:], 1, NEAR), *first, *send(middle[NEAR:], NEAR + 1, lanes)],
         [*near, *send(middle[lanes - 1 :], NEAR, lanes)],
         [*near, *send(rest[NEAR:], NEAR, lanes)],
     ]

time: 48.8 us -> 48 us (0.984)
  starting transfers between devices: 16.9 us -> 16.3 us
    ppermute x16, starting transfers between devices: 16.9 us -> 16.3 us  [swap(): return lax.ppermute(x, axes, [(i, i ^ mask) for i in range(size)])]
  transfers between devices with their start and end apart: 16 -> 16, of which waited for: 8 -> 7; matrix products, arithmetic and copies ran while one was open for 0% -> 0% of each run, Pallas kernels for 28% -> 28%
where the time goes in v16:
time: 48 us; the launch traced here: 47.8 us
  Pallas kernels  22.2 us (46%)
  starting transfers between devices  16.3 us (34%)
  waiting for transfers between devices  5.99 us (12%)
  local copies, waits for them, and re-layouts  2.38 us (5%)
  between operations  0.87 us (2%)
    ppermute x16, starting transfers between devices, swap(): return lax.ppermute(x, axes, [(i, i ^ mask) for i in range(size)])  16.3 us
    pallas_call x3, Pallas kernels, gram_part(): pl.pallas_call(functools.partial(gram_kernel, lanes, base, scale, last),...  6.6 us
    pallas_call x3, Pallas kernels, pack(): pl.pallas_call(functools.partial(pack_kernel, jobs, parts, len(after)), o...  6.15 us
    ppermute x16, waiting for transfers between devices, swap(): return lax.ppermute(x, axes, [(i, i ^ mask) for i in range(size)])  5.99 us
    pallas_call x1, Pallas kernels, mode_fields(): pl.pallas_call(functools.partial(mode_kernel, len(spectra), share), out_s...  4.77 us
    pallas_call x3, Pallas kernels, spectrum(): pl.pallas_call(functools.partial(spectrum_kernel, lanes, base), out_shape...  4.05 us
    unnamed x18, local copies, waits for them, and re-layouts  2.38 us
  transfers between devices with their start and end apart: 16, of which 7 were waited for; matrix products, arithmetic and copies ran while one was open for 0% of the time, Pallas kernels for 28%

profile of v16, /device:TPU:0, one launch (start us, length us, event | category | flops | bytes accessed | tf_op | source)
XLA Modules:
  0.0 47.8 jit_solution(16202727519935697004)
XLA Ops:
  0.6 2.2 %shard_map.95.refs_0_ = bf16[384,256]{1,0:T(8,128)(2,1)} custom-call(s32[1,4]{1,0:T(1,128)} %owner_hbm.5, bf16[384,4,512]{2,1,0:T(4,128)(2,1)} %x_hbm.5), custom_call_target="tpu_custom_call" | custom-call | flops 1000 | bytes 1000 | tf_op jit(solution)/shard_map/pallas_call | solution.py:150
  2.8 0.0 copy-start.7
  2.8 0.0 copy-start.8
  2.9 0.0 copy-start.1
  2.9 0.0 copy-start.2
  2.9 0.0 copy-start.5
  2.9 0.0 copy-start.6
  2.9 3.0 %collective-permute-start = (bf16[384,256]{1,0:T(8,128)(2,1)}, bf16[384,256]{1,0:T(8,128)(2,1)S(1)}, u32[]{:S(2)}, u32[]{:S(2)}) collective-permute-start(bf16[384,256]{1,0:T(8,128)(2,1)} %shard_map.95.refs_0_), channel_id=1, source_target_pairs={{0,16},{8,24},{16,0},{24,8},{1,17},{9,25},{17,1},{25,9},{2,18},{10... | collective-permute-start | bytes 589832 | tf_op jit(solution)/shard_map/ppermute | solution.py:543
  5.9 2.7 %shard_map.96 = (bf16[384,256]{1,0:T(8,128)(2,1)}, bf16[384,256]{1,0:T(8,128)(2,1)}, bf16[384,256]{1,0:T(8,128)(2,1)}, bf16[384,128]{1,0:T(8,128)(2,1)}, bf16[384,128]{1,0:T(8,128)(2,1)}) custom-call(s32[1,4]{1,0:T(1,128)} %owner_hbm.5, bf16[384,4,512]{2,1,0:T(4,128)(2,1)} %x_hbm.5, bf16[384,256]{1,0:T(8,128)(2,1)} %shard_map.95.refs_0_), custom_call_target="tpu_custom_call" | custom-call | flops 1000 | bytes 1000 | tf_op jit(solution)/shard_map/pallas_call | solution.py:150
  8.6 0.1 collective-permute-start.6
  8.7 0.2 collective-permute-start.7
  8.9 1.9 %collective-permute-start.4 = (bf16[384,128]{1,0:T(8,128)(2,1)}, bf16[384,128]{1,0:T(8,128)(2,1)S(1)}, u32[]{:S(2)}, u32[]{:S(2)}) collective-permute-start(bf16[384,128]{1,0:T(8,128)(2,1)} %get-tuple-element.25), channel_id=1, source_target_pairs={{0,16},{8,24},{16,0},{24,8},{1,17},{9,25},{17,1},{25,9},{2,18},{10... | collective-permute-start | bytes 294920 | tf_op jit(solution)/shard_map/ppermute | solution.py:543
  10.8 0.0 collective-permute-start.5
  10.8 0.2 collective-permute-done.refs_0_.refs_2_
  11.0 0.0 copy-done.7
  11.0 0.0 copy-start
  11.0 1.4 %copy-done = bf16[384,4,512]{2,1,0:T(4,128)(2,1)S(1)} copy-done((bf16[384,4,512]{2,1,0:T(4,128)(2,1)S(1)}, bf16[384,4,512]{2,1,0:T(4,128)(2,1)}, u32[]{:S(2)}) %copy-start) | copy-done | bytes 1572888
  12.5 0.0 copy-start.3
  12.5 0.9 %copy-done.3 = bf16[384,256]{1,0:T(8,128)(2,1)S(1)} copy-done((bf16[384,256]{1,0:T(8,128)(2,1)S(1)}, bf16[384,256]{1,0:T(8,128)(2,1)}, u32[]{:S(2)}) %copy-start.3) | copy-done | bytes 196632
  13.4 1.3 %shard_map.97 = (bf16[384,256]{1,0:T(8,128)(2,1)S(1)}, bf16[384,256]{1,0:T(8,128)(2,1)S(1)}, bf16[384,128]{1,0:T(8,128)(2,1)S(1)}, bf16[384,128]{1,0:T(8,128)(2,1)S(1)}) custom-call(s32[1,4]{1,0:T(1,128)S(1)} %copy-done.7, bf16[384,4,512]{2,1,0:T(4,128)(2,1)S(1)} %copy-done, bf16[384,256]{1,0:T(8,128)(2,1)S(1)} %collective-permute-done.refs_0_.refs_2_, ...), custom_call_target="tpu_custom_call" | custom-call | flops 1000 | bytes 1000 | tf_op jit(solution)/shard_map/pallas_call | solution.py:150
  14.7 2.3 %collective-permute-start.2 = (bf16[384,128]{1,0:T(8,128)(2,1)S(1)}, bf16[384,128]{1,0:T(8,128)(2,1)S(1)}, u32[]{:S(2)}, u32[]{:S(2)}) collective-permute-start(bf16[384,128]{1,0:T(8,128)(2,1)S(1)} %get-tuple-element.23), channel_id=1, source_target_pairs={{0,16},{8,24},{16,0},{24,8},{1,17},{9,25},{17,1},{25,9},{2,18},{10... | collective-permute-start | bytes 294920 | tf_op jit(solution)/shard_map/ppermute | solution.py:543
  17.0 0.0 collective-permute-done.6.refs_1_
  17.0 0.0 collective-permute-start.3
  17.0 0.0 collective-permute-done.7.refs_3_
  17.0 0.2 collective-permute-start.1
  17.2 0.0 copy-done.8
  17.2 0.0 copy-done.1
  17.2 0.0 copy-done.2
  17.2 0.0 copy-done.5
  17.2 0.0 copy-done.6
  17.2 2.7 %shard_map.98.refs_4_ = f32[128,128]{1,0:T(8,128)S(1)} custom-call(s32[4]{0:T(128)S(1)} %copy-done.5, s32[11]{0:T(128)S(1)} %copy-done.6, f32[1,256]{1,0:T(1,128)S(1)} %slice.14.w_ref, bf16[512,256]{1,0:T(8,128)(2,1)S(1)} %copy-done.1, bf16[2816,128]{1,0:T(8,128)(2,1)S(1)} %copy-done.2, bf16[384,256]{1,0:T(8,128)(2,1)S(1)} %copy-done.3, ...), custom_call_target="tpu_custom_call" | custom-call | flops 1000 | bytes 1000 | tf_op jit(solution)/shard_map/pallas_call | solution.py:256
  19.9 0.0 collective-permute-done.4.refs_2_
  19.9 0.0 collective-permute-done.5.refs_3_
  19.9 0.0 collective-permute-done.1.refs_1_
  19.9 2.2 %shard_map.99.refs_4_.before_ref = f32[128,128]{1,0:T(8,128)S(1)} custom-call(s32[4]{0:T(128)S(1)} %copy-done.5, s32[11]{0:T(128)S(1)} %copy-done.6, f32[1,128]{1,0:T(1,128)S(1)} %get-tuple-element.40.w_ref, bf16[512,256]{1,0:T(8,128)(2,1)S(1)} %copy-done.1, bf16[2816,128]{1,0:T(8,128)(2,1)S(1)} %copy-done.2, ...), custom_call_target="tpu_custom_call" | custom-call | flops 1000 | bytes 1000 | tf_op jit(solution)/shard_map/pallas_call | solution.py:256
  22.1 0.9 %collective-permute-done.2.refs_2_ = bf16[384,128]{1,0:T(8,128)(2,1)S(1)} collective-permute-done((bf16[384,128]{1,0:T(8,128)(2,1)S(1)}, bf16[384,128]{1,0:T(8,128)(2,1)S(1)}, u32[]{:S(2)}, u32[]{:S(2)}) %collective-permute-start.2) | collective-permute-done | bytes 98336 | tf_op jit(solution)/shard_map/ppermute | solution.py:543
  23.0 1.0 %collective-permute-done.3.refs_3_ = bf16[384,128]{1,0:T(8,128)(2,1)S(1)} collective-permute-done((bf16[384,128]{1,0:T(8,128)(2,1)S(1)}, bf16[384,128]{1,0:T(8,128)(2,1)S(1)}, u32[]{:S(2)}, u32[]{:S(2)}) %collective-permute-start.3) | collective-permute-done | bytes 98336 | tf_op jit(solution)/shard_map/ppermute | solution.py:543
  24.0 1.7 %shard_map.100 = (bf16[64,128]{1,0:T(8,128)(2,1)S(1)}, f32[22,128,128]{2,1,0:T(8,128)S(1)}) custom-call(s32[4]{0:T(128)S(1)} %copy-done.5, s32[11]{0:T(128)S(1)} %copy-done.6, f32[1,128]{1,0:T(1,128)S(1)} %get-tuple-element.41.w_ref, bf16[512,256]{1,0:T(8,128)(2,1)S(1)} %copy-done.1, bf16[2816,128]{1,0:T(8,128)(2,1)S(1)} %copy-done.2, ...), custom_call_target="tpu_custom_call" | custom-call | flops 1000 | bytes 1000 | tf_op jit(solution)/shard_map/pallas_call | solution.py:256
  25.7 0.5 collective-permute-start.8
  26.2 0.7 %shard_map.101.refs_4_ = bf16[64,128]{1,0:T(8,128)(2,1)S(1)} custom-call(f32[22,128,128]{2,1,0:T(8,128)S(1)} %get-tuple-element.29.s_ref, bf16[2816,128]{1,0:T(8,128)(2,1)S(1)} %copy-done.2, f32[128,128]{1,0:T(8,128)S(1)} %shard_map.99.refs_4_.before_ref), custom_call_target="tpu_custom_call" | custom-call | flops 1000000000 | bytes 3000000 | tf_op jit(solution)/shard_map/pallas_call | solution.py:274
  26.8 0.2 collective-permute-done.8
  27.0 2.1 %collective-permute-start.11 = (bf16[64,128]{1,0:T(8,128)(2,1)S(1)}, bf16[64,128]{1,0:T(8,128)(2,1)S(1)}, u32[]{:S(2)}, u32[]{:S(2)}) collective-permute-start(bf16[64,128]{1,0:T(8,128)(2,1)S(1)} %add_convert_fusion), channel_id=1, source_target_pairs={{0,17},{1,16},{2,19},{3,18},{4,21},{5,20},{6,23},{7,22},{8,25},{9,... | collective-permute-start | bytes 49160 | tf_op jit(solution)/shard_map/ppermute | solution.py:543
  29.1 0.4 collective-permute-start.10
  29.5 1.1 %collective-permute-start.9 = (bf16[64,128]{1,0:T(8,128)(2,1)S(1)}, bf16[64,128]{1,0:T(8,128)(2,1)S(1)}, u32[]{:S(2)}, u32[]{:S(2)}) collective-permute-start(bf16[64,128]{1,0:T(8,128)(2,1)S(1)} %add_convert_fusion), channel_id=1, source_target_pairs={{0,16},{1,17},{2,18},{3,19},{4,20},{5,21},{6,22},{7,23},{8,24},{9,... | collective-permute-start | bytes 49160 | tf_op jit(solution)/shard_map/ppermute | solution.py:543
  30.6 1.2 %shard_map.103.refs_2_ = f32[22,128,128]{2,1,0:T(8,128)S(1)} custom-call(s32[4]{0:T(128)S(1)} %copy-done.5, s32[11]{0:T(128)S(1)} %copy-done.6, bf16[512,256]{1,0:T(8,128)(2,1)S(1)} %copy-done.1, bf16[384,256]{1,0:T(8,128)(2,1)S(1)} %get-tuple-element.21.refs_0_, bf16[384,256]{1,0:T(8,128)(2,1)S(1)} %collective-permute-done.1.refs_1_, ...), custom_call_target="tpu_custom_call" | custom-call | flops 1000 | bytes 1000 | tf_op jit(solution)/shard_map/pallas_call | solution.py:295
  31.8 1.2 %shard_map.102.refs_1_ = f32[22,128,128]{2,1,0:T(8,128)S(1)} custom-call(s32[4]{0:T(128)S(1)} %copy-done.5, s32[11]{0:T(128)S(1)} %copy-done.6, bf16[512,256]{1,0:T(8,128)(2,1)S(1)} %copy-done.1, bf16[384,256]{1,0:T(8,128)(2,1)S(1)} %get-tuple-element.21.refs_0_, bf16[384,256]{1,0:T(8,128)(2,1)S(1)} %collective-permute-done.1.refs_1_, ...), custom_call_target="tpu_custom_call" | custom-call | flops 1000 | bytes 1000 | tf_op jit(solution)/shard_map/pallas_call | solution.py:295
  33.0 0.0 collective-permute-done.11
  33.0 0.0 collective-permute-done.10
  33.0 0.2 collective-permute-done.9
  33.2 0.0 copy-start.4
  33.2 3.8 %collective-permute-start.13 = (bf16[64,128]{1,0:T(8,128)(2,1)S(1)}, bf16[64,128]{1,0:T(8,128)(2,1)S(1)}, u32[]{:S(2)}, u32[]{:S(2)}) collective-permute-start(bf16[64,128]{1,0:T(8,128)(2,1)S(1)} %add_add_fusion.1), channel_id=1, source_target_pairs={{0,6},{1,7},{2,4},{3,5},{4,2},{5,3},{6,0},{7,1},{8,14},{9,15},{10,... | collective-permute-start | bytes 49160 | tf_op jit(solution)/shard_map/ppermute | solution.py:543
  37.1 0.0 collective-permute-start.12
  37.1 0.6 %collective-permute-start.14 = (bf16[64,128]{1,0:T(8,128)(2,1)S(1)}, bf16[64,128]{1,0:T(8,128)(2,1)S(1)}, u32[]{:S(2)}, u32[]{:S(2)}) collective-permute-start(bf16[64,128]{1,0:T(8,128)(2,1)S(1)} %add_add_fusion.1), channel_id=1, source_target_pairs={{0,2},{1,3},{2,0},{3,1},{4,6},{5,7},{6,4},{7,5},{8,10},{9,11},{10,... | collective-permute-start | bytes 49160 | tf_op jit(solution)/shard_map/ppermute | solution.py:543
  37.7 1.6 %shard_map.104.refs_0_ = f32[22,128,256]{2,1,0:T(8,128)S(1)} custom-call(s32[4]{0:T(128)S(1)} %copy-done.5, s32[11]{0:T(128)S(1)} %copy-done.6, bf16[512,256]{1,0:T(8,128)(2,1)S(1)} %copy-done.1, bf16[384,256]{1,0:T(8,128)(2,1)S(1)} %copy-done.3, bf16[384,256]{1,0:T(8,128)(2,1)S(1)} %collective-permute-done.6.refs_1_, ...), custom_call_target="tpu_custom_call" | custom-call | flops 1000 | bytes 1000 | tf_op jit(solution)/shard_map/pallas_call | solution.py:295
  39.3 0.0 collective-permute-done.13
  39.4 2.4 %collective-permute-done.12 = bf16[64,128]{1,0:T(8,128)(2,1)S(1)} collective-permute-done((bf16[64,128]{1,0:T(8,128)(2,1)S(1)}, bf16[64,128]{1,0:T(8,128)(2,1)S(1)}, u32[]{:S(2)}, u32[]{:S(2)}) %collective-permute-start.12) | collective-permute-done | bytes 16416 | tf_op jit(solution)/shard_map/ppermute | solution.py:543
  41.7 0.0 collective-permute-done.14
  41.7 0.1 collective-permute-start.15
  41.8 1.2 %collective-permute-done.15.other_ref = f32[64,128]{1,0:T(8,128)S(1)} collective-permute-done((f32[64,128]{1,0:T(8,128)S(1)}, f32[64,128]{1,0:T(8,128)S(1)}, u32[]{:S(2)}, u32[]{:S(2)}) %collective-permute-start.15) | collective-permute-done | bytes 32800 | tf_op jit(solution)/shard_map/ppermute | solution.py:543
  43.0 0.0 copy-done.4
  43.0 4.8 %shard_map.105 = (bf16[2,11,128,512]{3,2,1,0:T(8,128)(2,1)}, f32[11,11,2,16]{3,2,1,0:T(2,128)}) custom-call(f32[64,128]{1,0:T(8,128)S(1)} %add_add_fusion.half_ref, f32[64,128]{1,0:T(8,128)S(1)} %collective-permute-done.15.other_ref, bf16[2,128,256]{2,1,0:T(8,128)(2,1)S(1)} %copy-done.4, f32[22,128,256]{2,1,0:T(8,128)S(1)} %shard_map.104.refs_0_, ...), custom_call_target="tpu_custom_call" | custom-call | tf_op jit(solution)/shard_map/pallas_call | solution.py:516
  (5 shorter events, 0.0 us)
Async XLA Ops:
  2.8 8.2 %copy-start.7 = (s32[1,4]{1,0:T(1,128)S(1)}, s32[1,4]{1,0:T(1,128)}, u32[]{:S(2)}) copy-start(s32[1,4]{1,0:T(1,128)} %owner_hbm.5) | copy-start | bytes 52
  2.8 14.3 %copy-start.8 = (f32[512]{0:T(512)S(1)}, f32[512]{0:T(512)}, u32[]{:S(2)}) copy-start(f32[512]{0:T(512)} %param.9) | copy-start | bytes 6148
  2.9 14.3 %copy-start.1 = (bf16[512,256]{1,0:T(8,128)(2,1)S(1)}, bf16[512,256]{1,0:T(8,128)(2,1)}, u32[]{:S(2)}) copy-start(bf16[512,256]{1,0:T(8,128)(2,1)} %constant.6.clone.f_ref) | copy-start | bytes 786436
  2.9 14.3 %copy-start.2 = (bf16[2816,128]{1,0:T(8,128)(2,1)S(1)}, bf16[2816,128]{1,0:T(8,128)(2,1)}, u32[]{:S(2)}) copy-start(bf16[2816,128]{1,0:T(8,128)(2,1)} %constant.7.clone.pick_ref) | copy-start | bytes 2162692
  2.9 14.3 %copy-start.5 = (s32[4]{0:T(128)S(1)}, s32[4]{0:T(128)}, u32[]{:S(2)}) copy-start(s32[4]{0:T(128)} %order_ref.11) | copy-start | bytes 52
  2.9 14.3 %copy-start.6 = (s32[11]{0:T(128)S(1)}, s32[11]{0:T(128)}, u32[]{:S(2)}) copy-start(s32[11]{0:T(128)} %offsets_ref.11) | copy-start | bytes 136
  2.9 8.1 %collective-permute-start = (bf16[384,256]{1,0:T(8,128)(2,1)}, bf16[384,256]{1,0:T(8,128)(2,1)S(1)}, u32[]{:S(2)}, u32[]{:S(2)}) collective-permute-start(bf16[384,256]{1,0:T(8,128)(2,1)} %shard_map.95.refs_0_), channel_id=1, source_target_pairs={{0,16},{8,24},{16,0},{24,8},{1,17},{9,25},{17,1},{25,9},{2,18},{10... | collective-permute-start | bytes 589832 | tf_op jit(solution)/shard_map/ppermute | solution.py:543
  8.6 8.4 %collective-permute-start.6 = (bf16[384,256]{1,0:T(8,128)(2,1)}, bf16[384,256]{1,0:T(8,128)(2,1)S(1)}, u32[]{:S(2)}, u32[]{:S(2)}) collective-permute-start(bf16[384,256]{1,0:T(8,128)(2,1)} %get-tuple-element.27), channel_id=1, source_target_pairs={{0,8},{8,0},{16,24},{24,16},{1,9},{9,1},{17,25},{25,17},{2,10},{10... | collective-permute-start | bytes 589832 | tf_op jit(solution)/shard_map/ppermute | solution.py:543
  8.7 8.3 %collective-permute-start.7 = (bf16[384,256]{1,0:T(8,128)(2,1)}, bf16[384,256]{1,0:T(8,128)(2,1)S(1)}, u32[]{:S(2)}, u32[]{:S(2)}) collective-permute-start(bf16[384,256]{1,0:T(8,128)(2,1)} %get-tuple-element.28), channel_id=1, source_target_pairs={{0,24},{8,16},{16,8},{24,0},{1,25},{9,17},{17,9},{25,1},{2,26},{10... | collective-permute-start | bytes 589832 | tf_op jit(solution)/shard_map/ppermute | solution.py:543
  8.9 11.0 %collective-permute-start.4 = (bf16[384,128]{1,0:T(8,128)(2,1)}, bf16[384,128]{1,0:T(8,128)(2,1)S(1)}, u32[]{:S(2)}, u32[]{:S(2)}) collective-permute-start(bf16[384,128]{1,0:T(8,128)(2,1)} %get-tuple-element.25), channel_id=1, source_target_pairs={{0,16},{8,24},{16,0},{24,8},{1,17},{9,25},{17,1},{25,9},{2,18},{10... | collective-permute-start | bytes 294920 | tf_op jit(solution)/shard_map/ppermute | solution.py:543
  10.8 9.1 %collective-permute-start.5 = (bf16[384,128]{1,0:T(8,128)(2,1)}, bf16[384,128]{1,0:T(8,128)(2,1)S(1)}, u32[]{:S(2)}, u32[]{:S(2)}) collective-permute-start(bf16[384,128]{1,0:T(8,128)(2,1)} %get-tuple-element.26), channel_id=1, source_target_pairs={{0,24},{8,16},{16,8},{24,0},{1,25},{9,17},{17,9},{25,1},{2,26},{10... | collective-permute-start | bytes 294920 | tf_op jit(solution)/shard_map/ppermute | solution.py:543
  11.0 1.4 %copy-start = (bf16[384,4,512]{2,1,0:T(4,128)(2,1)S(1)}, bf16[384,4,512]{2,1,0:T(4,128)(2,1)}, u32[]{:S(2)}) copy-start(bf16[384,4,512]{2,1,0:T(4,128)(2,1)} %x_hbm.5) | copy-start | bytes 4718596
  12.5 0.9 %copy-start.3 = (bf16[384,256]{1,0:T(8,128)(2,1)S(1)}, bf16[384,256]{1,0:T(8,128)(2,1)}, u32[]{:S(2)}) copy-start(bf16[384,256]{1,0:T(8,128)(2,1)} %get-tuple-element.20.refs_1_.refs_0_) | copy-start | bytes 589828
  14.7 8.4 %collective-permute-start.2 = (bf16[384,128]{1,0:T(8,128)(2,1)S(1)}, bf16[384,128]{1,0:T(8,128)(2,1)S(1)}, u32[]{:S(2)}, u32[]{:S(2)}) collective-permute-start(bf16[384,128]{1,0:T(8,128)(2,1)S(1)} %get-tuple-element.23), channel_id=1, source_target_pairs={{0,16},{8,24},{16,0},{24,8},{1,17},{9,25},{17,1},{25,9},{2,18},{10... | collective-permute-start | bytes 294920 | tf_op jit(solution)/shard_map/ppermute | solution.py:543
  17.0 7.0 %collective-permute-start.3 = (bf16[384,128]{1,0:T(8,128)(2,1)S(1)}, bf16[384,128]{1,0:T(8,128)(2,1)S(1)}, u32[]{:S(2)}, u32[]{:S(2)}) collective-permute-start(bf16[384,128]{1,0:T(8,128)(2,1)S(1)} %get-tuple-element.24), channel_id=1, source_target_pairs={{0,24},{8,16},{16,8},{24,0},{1,25},{9,17},{17,9},{25,1},{2,26},{10... | collective-permute-start | bytes 294920 | tf_op jit(solution)/shard_map/ppermute | solution.py:543
  17.0 3.0 %collective-permute-start.1 = (bf16[384,256]{1,0:T(8,128)(2,1)S(1)}, bf16[384,256]{1,0:T(8,128)(2,1)S(1)}, u32[]{:S(2)}, u32[]{:S(2)}) collective-permute-start(bf16[384,256]{1,0:T(8,128)(2,1)S(1)} %get-tuple-element.22), channel_id=1, source_target_pairs={{0,8},{8,0},{16,24},{24,16},{1,9},{9,1},{17,25},{25,17},{2,10},{10... | collective-permute-start | bytes 589832 | tf_op jit(solution)/shard_map/ppermute | solution.py:543
  25.7 1.3 %collective-permute-start.8 = (bf16[64,128]{1,0:T(8,128)(2,1)S(1)}, bf16[64,128]{1,0:T(8,128)(2,1)S(1)}, u32[]{:S(2)}, u32[]{:S(2)}) collective-permute-start(bf16[64,128]{1,0:T(8,128)(2,1)S(1)} %get-tuple-element.30), channel_id=1, source_target_pairs={{0,8},{1,9},{2,10},{3,11},{4,12},{5,13},{6,14},{7,15},{8,0},{9,1},... | collective-permute-start | bytes 49160 | tf_op jit(solution)/shard_map/ppermute | solution.py:543
  27.0 6.0 %collective-permute-start.11 = (bf16[64,128]{1,0:T(8,128)(2,1)S(1)}, bf16[64,128]{1,0:T(8,128)(2,1)S(1)}, u32[]{:S(2)}, u32[]{:S(2)}) collective-permute-start(bf16[64,128]{1,0:T(8,128)(2,1)S(1)} %add_convert_fusion), channel_id=1, source_target_pairs={{0,17},{1,16},{2,19},{3,18},{4,21},{5,20},{6,23},{7,22},{8,25},{9,... | collective-permute-start | bytes 49160 | tf_op jit(solution)/shard_map/ppermute | solution.py:543
  29.1 3.9 %collective-permute-start.10 = (bf16[64,128]{1,0:T(8,128)(2,1)S(1)}, bf16[64,128]{1,0:T(8,128)(2,1)S(1)}, u32[]{:S(2)}, u32[]{:S(2)}) collective-permute-start(bf16[64,128]{1,0:T(8,128)(2,1)S(1)} %add_convert_fusion), channel_id=1, source_target_pairs={{0,1},{1,0},{2,3},{3,2},{4,5},{5,4},{6,7},{7,6},{8,9},{9,8},{10,11... | collective-permute-start | bytes 49160 | tf_op jit(solution)/shard_map/ppermute | solution.py:543
  29.5 3.7 %collective-permute-start.9 = (bf16[64,128]{1,0:T(8,128)(2,1)S(1)}, bf16[64,128]{1,0:T(8,128)(2,1)S(1)}, u32[]{:S(2)}, u32[]{:S(2)}) collective-permute-start(bf16[64,128]{1,0:T(8,128)(2,1)S(1)} %add_convert_fusion), channel_id=1, source_target_pairs={{0,16},{1,17},{2,18},{3,19},{4,20},{5,21},{6,22},{7,23},{8,24},{9,... | collective-permute-start | bytes 49160 | tf_op jit(solution)/shard_map/ppermute | solution.py:543
  33.2 9.8 %copy-start.4 = (bf16[2,128,256]{2,1,0:T(8,128)(2,1)S(1)}, bf16[2,128,256]{2,1,0:T(8,128)(2,1)}, u32[]{:S(2)}) copy-start(bf16[2,128,256]{2,1,0:T(8,128)(2,1)} %constant.8.clone.spread_ref) | copy-start | bytes 393220
  33.2 6.1 %collective-permute-start.13 = (bf16[64,128]{1,0:T(8,128)(2,1)S(1)}, bf16[64,128]{1,0:T(8,128)(2,1)S(1)}, u32[]{:S(2)}, u32[]{:S(2)}) collective-permute-start(bf16[64,128]{1,0:T(8,128)(2,1)S(1)} %add_add_fusion.1), channel_id=1, source_target_pairs={{0,6},{1,7},{2,4},{3,5},{4,2},{5,3},{6,0},{7,1},{8,14},{9,15},{10,... | collective-permute-start | bytes 49160 | tf_op jit(solution)/shard_map/ppermute | solution.py:543
  37.1 4.6 %collective-permute-start.12 = (bf16[64,128]{1,0:T(8,128)(2,1)S(1)}, bf16[64,128]{1,0:T(8,128)(2,1)S(1)}, u32[]{:S(2)}, u32[]{:S(2)}) collective-permute-start(bf16[64,128]{1,0:T(8,128)(2,1)S(1)} %add_add_fusion.1), channel_id=1, source_target_pairs={{0,4},{1,5},{2,6},{3,7},{4,0},{5,1},{6,2},{7,3},{8,12},{9,13},{10,... | collective-permute-start | bytes 49160 | tf_op jit(solution)/shard_map/ppermute | solution.py:543
  37.1 4.6 %collective-permute-start.14 = (bf16[64,128]{1,0:T(8,128)(2,1)S(1)}, bf16[64,128]{1,0:T(8,128)(2,1)S(1)}, u32[]{:S(2)}, u32[]{:S(2)}) collective-permute-start(bf16[64,128]{1,0:T(8,128)(2,1)S(1)} %add_add_fusion.1), channel_id=1, source_target_pairs={{0,2},{1,3},{2,0},{3,1},{4,6},{5,7},{6,4},{7,5},{8,10},{9,11},{10,... | collective-permute-start | bytes 49160 | tf_op jit(solution)/shard_map/ppermute | solution.py:543
  41.7 1.3 %collective-permute-start.15 = (f32[64,128]{1,0:T(8,128)S(1)}, f32[64,128]{1,0:T(8,128)S(1)}, u32[]{:S(2)}, u32[]{:S(2)}) collective-permute-start(f32[64,128]{1,0:T(8,128)S(1)} %add_add_fusion.half_ref), channel_id=1, source_target_pairs={{0,8},{1,9},{2,10},{3,11},{4,12},{5,13},{6,14},{7,15},{8,0},{9,1},... | collective-permute-start | bytes 98312 | tf_op jit(solution)/shard_map/ppermute | solution.py:543

commit v17 on v16

--- a/solution.py
+++ b/solution.py
@@ -164,10 +164,11 @@
     )(owner, snapshots, *after)
 
 
-def fill_record(base, order_ref, pieces, record, factor):
+def fill_record(place, order_ref, pieces, record, factor):
     steps = pieces[0].shape[0]
     me = lax.axis_index("tm")
-    for d, piece in enumerate(pieces):
+    base, partners = place
+    for d, piece in zip(partners, pieces):
         start = pl.multiple_of(order_ref[me ^ d] * steps, steps)
         for c in range(record.shape[0]):
             at = c * LANE + (base if d < NEAR else 0)
@@ -222,14 +223,14 @@
     return dot(masked[...], pick_ref[...])
 
 
-def gram_kernel(lanes, base, scale, last, order_ref, offsets_ref, w_ref, f_ref, pick_ref, *refs):
+def gram_kernel(lanes, place, scale, last, order_ref, offsets_ref, w_ref, f_ref, pick_ref, *refs):
     pieces = refs[:lanes]
     refs = refs[lanes:]
     if last:
         before_ref, gram_ref, s_ref, record, masked = refs
     else:
         *before_refs, gram_ref, record, s_ref, masked = refs
-    fill_record(base, order_ref, pieces, record, jnp.sqrt(w_ref[...]))
+    fill_record(place, order_ref, pieces, record, jnp.sqrt(w_ref[...]))
     transform(offsets_ref, f_ref[:NFFT] if last else f_ref[...], record, s_ref)
     if not last:
         total = gram_rows(0, GROUPS, s_ref, pick_ref, masked) * scale
@@ -240,7 +241,7 @@
     gram_ref[...] = (total + before_ref[pl.ds(half, HALF), :]).astype(BF16)
 
 
-def gram_part(order, offsets, weights, tables, pieces, before, base, last, scale):
+def gram_part(order, offsets, weights, tables, pieces, before, place, last, scale):
     lanes = len(pieces)
     steps, width = pieces[-1].shape
     args = [order, offsets, weights, *tables, *pieces, *before]
@@ -254,7 +255,7 @@
         scratch.append(pltpu.VMEM(spectrum_shape, F32))
     scratch.append(pltpu.VMEM((HALF if last else NFREQ, NBLK * WIDE), BF16))
     return pl.pallas_call(
-        functools.partial(gram_kernel, lanes, base, scale, last),
+        functools.partial(gram_kernel, lanes, place, scale, last),
         out_shape=outs,
         in_specs=[SMEM, SMEM] + [VMEM] * (len(args) - 2),
         out_specs=[VMEM] * len(outs),
@@ -282,18 +283,18 @@
     )(scaled, pick, before)
 
 
-def spectrum_kernel(lanes, base, order_ref, offsets_ref, f_ref, *refs):
+def spectrum_kernel(lanes, place, order_ref, offsets_ref, f_ref, *refs):
     s_ref, record = refs[-2:]
-    fill_record(base, order_ref, refs[:lanes], record, None)
+    fill_record(place, order_ref, refs[:lanes], record, None)
     transform(offsets_ref, f_ref[...], record, s_ref)
 
 
-def spectrum(order, offsets, fourier, pieces, base, after):
+def spectrum(order, offsets, fourier, pieces, place, after):
     lanes = len(pieces)
     steps, width = pieces[-1].shape
     args = [order, offsets, fourier, *pieces, *after]
     return pl.pallas_call(
-        functools.partial(spectrum_kernel, lanes, base),
+        functools.partial(spectrum_kernel, lanes, place),
         out_shape=jax.ShapeDtypeStruct((2 * NBLK, NFREQ, width), F32),
         in_specs=[SMEM, SMEM] + [VMEM] * (len(args) - 2),
         out_specs=VMEM,
@@ -571,26 +572,28 @@
     arrived = [
         [middle[0], *send(middle[1:], 1, NEAR), *first, *send(middle[NEAR:], NEAR + 1, lanes)],
         [*near, *send(middle[lanes - 1 :], NEAR, lanes)],
-        [*near, *send(rest[NEAR:], NEAR, lanes)],
+        [*near, *send(rest[NEAR:], NEAR, lanes)[::-1]],
     ]
-    starts = (0, 0, c1[1])
+    natural = tuple(range(lanes))
+    turned = natural[:NEAR] + natural[NEAR:][::-1]
+    places = ((0, natural), (0, natural), (c1[1], turned))
 
     axes = ("tm", "sx", "sy")
     size = lanes * groups
     bits = [b * groups for b in powers(lanes)] + powers(groups)
     parts = [weights[:, base : base + width] for base, width in chunks]
     before = []
-    for at, base in enumerate(starts):
+    for at, place in enumerate(places):
         last = at == len(chunks) - 1
-        args = (block_order, offsets, parts[at], tables, arrived[at], before, base, last, scale)
+        args = (block_order, offsets, parts[at], tables, arrived[at], before, place, last, scale)
         before, before_last = gram_part(*args), before
     before, (given, scaled) = before_last, before
 
     other = swap(given, axes, bits[0], size)
     keep = own_part(scaled, tables[1], before[0], scale)
     spectra = [
-        spectrum(block_order, offsets, tables[0], pieces, base, [keep])
-        for base, pieces in zip(starts, arrived)
+        spectrum(block_order, offsets, tables[0], pieces, place, [keep])
+        for place, pieces in zip(places, arrived)
     ]
     half = keep.astype(F32) + other.astype(F32)
     for at in range(1, len(bits), 2):

time: 48 us -> 48.3 us (level)
  waiting for transfers between devices: 5.99 us -> 6.69 us
  starting transfers between devices: 16.3 us -> 15.8 us
    ppermute x16, waiting for transfers between devices: 5.99 us -> 6.69 us  [swap(): return lax.ppermute(x, axes, [(i, i ^ mask) for i in range(size)])]
  transfers between devices with their start and end apart: 16 -> 16, of which waited for: 7 -> 6; matrix products, arithmetic and copies ran while one was open for 0% -> 0% of each run, Pallas kernels for 28% -> 28%
where the time goes in v17:
time: 48.3 us; the launch traced here: 48.1 us
  Pallas kernels  22.2 us (46%)
  starting transfers between devices  15.8 us (33%)
  waiting for transfers between devices  6.69 us (14%)
  local copies, waits for them, and re-layouts  2.38 us (5%)
  between operations  0.89 us (2%)
    ppermute x16, starting transfers between devices, swap(): return lax.ppermute(x, axes, [(i, i ^ mask) for i in range(size)])  15.8 us
    ppermute x16, waiting for transfers between devices, swap(): return lax.ppermute(x, axes, [(i, i ^ mask) for i in range(size)])  6.69 us
    pallas_call x3, Pallas kernels, gram_part(): pl.pallas_call(functools.partial(gram_kernel, lanes, place, scale, last),...  6.59 us
    pallas_call x3, Pallas kernels, pack(): pl.pallas_call(functools.partial(pack_kernel, jobs, parts, len(after)), o...  6.15 us
    pallas_call x1, Pallas kernels, mode_fields(): pl.pallas_call(functools.partial(mode_kernel, len(spectra), share), out_s...  4.77 us
    pallas_call x3, Pallas kernels, spectrum(): pl.pallas_call(functools.partial(spectrum_kernel, lanes, place), out_shap...  4.04 us
    unnamed x18, local copies, waits for them, and re-layouts  2.38 us
  transfers between devices with their start and end apart: 16, of which 6 were waited for; matrix products, arithmetic and copies ran while one was open for 0% of the time, Pallas kernels for 28%

profile of v17, /device:TPU:0, one launch (start us, length us, event | category | flops | bytes accessed | tf_op | source)
XLA Modules:
  0.0 48.1 jit_solution(15122297876990410088)
XLA Ops:
  0.6 2.2 %shard_map.95.refs_0_ = bf16[384,256]{1,0:T(8,128)(2,1)} custom-call(s32[1,4]{1,0:T(1,128)} %owner_hbm.5, bf16[384,4,512]{2,1,0:T(4,128)(2,1)} %x_hbm.5), custom_call_target="tpu_custom_call" | custom-call | flops 1000 | bytes 1000 | tf_op jit(solution)/shard_map/pallas_call | solution.py:150
  2.8 0.0 copy-start.7
  2.8 0.0 copy-start.8
  2.9 0.0 copy-start.1
  2.9 0.0 copy-start.2
  2.9 0.0 copy-start.5
  2.9 0.0 copy-start.6
  2.9 3.0 %collective-permute-start = (bf16[384,256]{1,0:T(8,128)(2,1)}, bf16[384,256]{1,0:T(8,128)(2,1)S(1)}, u32[]{:S(2)}, u32[]{:S(2)}) collective-permute-start(bf16[384,256]{1,0:T(8,128)(2,1)} %shard_map.95.refs_0_), channel_id=1, source_target_pairs={{0,16},{8,24},{16,0},{24,8},{1,17},{9,25},{17,1},{25,9},{2,18},{10... | collective-permute-start | bytes 589832 | tf_op jit(solution)/shard_map/ppermute | solution.py:544
  5.9 2.7 %shard_map.96 = (bf16[384,256]{1,0:T(8,128)(2,1)}, bf16[384,256]{1,0:T(8,128)(2,1)}, bf16[384,256]{1,0:T(8,128)(2,1)}, bf16[384,128]{1,0:T(8,128)(2,1)}, bf16[384,128]{1,0:T(8,128)(2,1)}) custom-call(s32[1,4]{1,0:T(1,128)} %owner_hbm.5, bf16[384,4,512]{2,1,0:T(4,128)(2,1)} %x_hbm.5, bf16[384,256]{1,0:T(8,128)(2,1)} %shard_map.95.refs_0_), custom_call_target="tpu_custom_call" | custom-call | flops 1000 | bytes 1000 | tf_op jit(solution)/shard_map/pallas_call | solution.py:150
  8.6 0.1 collective-permute-start.6
  8.7 0.2 collective-permute-start.7
  8.9 1.9 %collective-permute-start.4 = (bf16[384,128]{1,0:T(8,128)(2,1)}, bf16[384,128]{1,0:T(8,128)(2,1)S(1)}, u32[]{:S(2)}, u32[]{:S(2)}) collective-permute-start(bf16[384,128]{1,0:T(8,128)(2,1)} %get-tuple-element.25), channel_id=1, source_target_pairs={{0,16},{8,24},{16,0},{24,8},{1,17},{9,25},{17,1},{25,9},{2,18},{10... | collective-permute-start | bytes 294920 | tf_op jit(solution)/shard_map/ppermute | solution.py:544
  10.8 0.0 collective-permute-start.5
  10.8 0.2 collective-permute-done.refs_0_.refs_2_
  11.0 0.0 copy-done.7
  11.0 0.0 copy-start
  11.0 1.4 %copy-done = bf16[384,4,512]{2,1,0:T(4,128)(2,1)S(1)} copy-done((bf16[384,4,512]{2,1,0:T(4,128)(2,1)S(1)}, bf16[384,4,512]{2,1,0:T(4,128)(2,1)}, u32[]{:S(2)}) %copy-start) | copy-done | bytes 1572888
  12.5 0.0 copy-start.3
  12.5 0.9 %copy-done.3 = bf16[384,256]{1,0:T(8,128)(2,1)S(1)} copy-done((bf16[384,256]{1,0:T(8,128)(2,1)S(1)}, bf16[384,256]{1,0:T(8,128)(2,1)}, u32[]{:S(2)}) %copy-start.3) | copy-done | bytes 196632
  13.4 1.3 %shard_map.97 = (bf16[384,256]{1,0:T(8,128)(2,1)S(1)}, bf16[384,256]{1,0:T(8,128)(2,1)S(1)}, bf16[384,128]{1,0:T(8,128)(2,1)S(1)}, bf16[384,128]{1,0:T(8,128)(2,1)S(1)}) custom-call(s32[1,4]{1,0:T(1,128)S(1)} %copy-done.7, bf16[384,4,512]{2,1,0:T(4,128)(2,1)S(1)} %copy-done, bf16[384,256]{1,0:T(8,128)(2,1)S(1)} %collective-permute-done.refs_0_.refs_2_, ...), custom_call_target="tpu_custom_call" | custom-call | flops 1000 | bytes 1000 | tf_op jit(solution)/shard_map/pallas_call | solution.py:150
  14.7 1.6 %collective-permute-start.2 = (bf16[384,128]{1,0:T(8,128)(2,1)S(1)}, bf16[384,128]{1,0:T(8,128)(2,1)S(1)}, u32[]{:S(2)}, u32[]{:S(2)}) collective-permute-start(bf16[384,128]{1,0:T(8,128)(2,1)S(1)} %get-tuple-element.23), channel_id=1, source_target_pairs={{0,24},{8,16},{16,8},{24,0},{1,25},{9,17},{17,9},{25,1},{2,26},{10... | collective-permute-start | bytes 294920 | tf_op jit(solution)/shard_map/ppermute | solution.py:544
  16.3 0.0 collective-permute-done.6.refs_1_
  16.3 0.8 %collective-permute-start.3 = (bf16[384,128]{1,0:T(8,128)(2,1)S(1)}, bf16[384,128]{1,0:T(8,128)(2,1)S(1)}, u32[]{:S(2)}, u32[]{:S(2)}) collective-permute-start(bf16[384,128]{1,0:T(8,128)(2,1)S(1)} %get-tuple-element.24), channel_id=1, source_target_pairs={{0,16},{8,24},{16,0},{24,8},{1,17},{9,25},{17,1},{25,9},{2,18},{10... | collective-permute-start | bytes 294920 | tf_op jit(solution)/shard_map/ppermute | solution.py:544
  17.0 0.0 collective-permute-done.7.refs_3_
  17.0 0.1 collective-permute-start.1
  17.1 0.0 copy-done.8
  17.2 0.0 copy-done.1
  17.2 0.0 copy-done.2
  17.2 0.0 copy-done.5
  17.2 0.0 copy-done.6
  17.2 2.7 %shard_map.98.refs_4_ = f32[128,128]{1,0:T(8,128)S(1)} custom-call(s32[4]{0:T(128)S(1)} %copy-done.5, s32[11]{0:T(128)S(1)} %copy-done.6, f32[1,256]{1,0:T(1,128)S(1)} %slice.14.w_ref, bf16[512,256]{1,0:T(8,128)(2,1)S(1)} %copy-done.1, bf16[2816,128]{1,0:T(8,128)(2,1)S(1)} %copy-done.2, bf16[384,256]{1,0:T(8,128)(2,1)S(1)} %copy-done.3, ...), custom_call_target="tpu_custom_call" | custom-call | flops 1000 | bytes 1000 | tf_op jit(solution)/shard_map/pallas_call | solution.py:257
  19.9 0.0 collective-permute-done.4.refs_2_
  19.9 0.0 collective-permute-done.5.refs_3_
  19.9 0.0 collective-permute-done.1.refs_1_
  19.9 2.2 %shard_map.99.refs_4_.before_ref = f32[128,128]{1,0:T(8,128)S(1)} custom-call(s32[4]{0:T(128)S(1)} %copy-done.5, s32[11]{0:T(128)S(1)} %copy-done.6, f32[1,128]{1,0:T(1,128)S(1)} %get-tuple-element.40.w_ref, bf16[512,256]{1,0:T(8,128)(2,1)S(1)} %copy-done.1, bf16[2816,128]{1,0:T(8,128)(2,1)S(1)} %copy-done.2, ...), custom_call_target="tpu_custom_call" | custom-call | flops 1000 | bytes 1000 | tf_op jit(solution)/shard_map/pallas_call | solution.py:257
  22.1 0.0 collective-permute-done.2.refs_2_
  22.1 2.5 %collective-permute-done.3.refs_3_ = bf16[384,128]{1,0:T(8,128)(2,1)S(1)} collective-permute-done((bf16[384,128]{1,0:T(8,128)(2,1)S(1)}, bf16[384,128]{1,0:T(8,128)(2,1)S(1)}, u32[]{:S(2)}, u32[]{:S(2)}) %collective-permute-start.3) | collective-permute-done | bytes 98336 | tf_op jit(solution)/shard_map/ppermute | solution.py:544
  24.6 1.7 %shard_map.100 = (bf16[64,128]{1,0:T(8,128)(2,1)S(1)}, f32[22,128,128]{2,1,0:T(8,128)S(1)}) custom-call(s32[4]{0:T(128)S(1)} %copy-done.5, s32[11]{0:T(128)S(1)} %copy-done.6, f32[1,128]{1,0:T(1,128)S(1)} %get-tuple-element.41.w_ref, bf16[512,256]{1,0:T(8,128)(2,1)S(1)} %copy-done.1, bf16[2816,128]{1,0:T(8,128)(2,1)S(1)} %copy-done.2, ...), custom_call_target="tpu_custom_call" | custom-call | flops 1000 | bytes 1000 | tf_op jit(solution)/shard_map/pallas_call | solution.py:257
  26.3 0.1 collective-permute-start.8
  26.4 0.7 %shard_map.101.refs_4_ = bf16[64,128]{1,0:T(8,128)(2,1)S(1)} custom-call(f32[22,128,128]{2,1,0:T(8,128)S(1)} %get-tuple-element.29.s_ref, bf16[2816,128]{1,0:T(8,128)(2,1)S(1)} %copy-done.2, f32[128,128]{1,0:T(8,128)S(1)} %shard_map.99.refs_4_.before_ref), custom_call_target="tpu_custom_call" | custom-call | flops 1000000000 | bytes 3000000 | tf_op jit(solution)/shard_map/pallas_call | solution.py:275
  27.1 0.5 %collective-permute-done.8 = bf16[64,128]{1,0:T(8,128)(2,1)S(1)} collective-permute-done((bf16[64,128]{1,0:T(8,128)(2,1)S(1)}, bf16[64,128]{1,0:T(8,128)(2,1)S(1)}, u32[]{:S(2)}, u32[]{:S(2)}) %collective-permute-start.8) | collective-permute-done | bytes 16416 | tf_op jit(solution)/shard_map/ppermute | solution.py:544
  27.6 1.8 %collective-permute-start.11 = (bf16[64,128]{1,0:T(8,128)(2,1)S(1)}, bf16[64,128]{1,0:T(8,128)(2,1)S(1)}, u32[]{:S(2)}, u32[]{:S(2)}) collective-permute-start(bf16[64,128]{1,0:T(8,128)(2,1)S(1)} %add_convert_fusion), channel_id=1, source_target_pairs={{0,17},{1,16},{2,19},{3,18},{4,21},{5,20},{6,23},{7,22},{8,25},{9,... | collective-permute-start | bytes 49160 | tf_op jit(solution)/shard_map/ppermute | solution.py:544
  29.4 0.5 %collective-permute-start.10 = (bf16[64,128]{1,0:T(8,128)(2,1)S(1)}, bf16[64,128]{1,0:T(8,128)(2,1)S(1)}, u32[]{:S(2)}, u32[]{:S(2)}) collective-permute-start(bf16[64,128]{1,0:T(8,128)(2,1)S(1)} %add_convert_fusion), channel_id=1, source_target_pairs={{0,1},{1,0},{2,3},{3,2},{4,5},{5,4},{6,7},{7,6},{8,9},{9,8},{10,11... | collective-permute-start | bytes 49160 | tf_op jit(solution)/shard_map/ppermute | solution.py:544
  29.9 1.2 %collective-permute-start.9 = (bf16[64,128]{1,0:T(8,128)(2,1)S(1)}, bf16[64,128]{1,0:T(8,128)(2,1)S(1)}, u32[]{:S(2)}, u32[]{:S(2)}) collective-permute-start(bf16[64,128]{1,0:T(8,128)(2,1)S(1)} %add_convert_fusion), channel_id=1, source_target_pairs={{0,16},{1,17},{2,18},{3,19},{4,20},{5,21},{6,22},{7,23},{8,24},{9,... | collective-permute-start | bytes 49160 | tf_op jit(solution)/shard_map/ppermute | solution.py:544
  31.1 1.2 %shard_map.103.refs_2_ = f32[22,128,128]{2,1,0:T(8,128)S(1)} custom-call(s32[4]{0:T(128)S(1)} %copy-done.5, s32[11]{0:T(128)S(1)} %copy-done.6, bf16[512,256]{1,0:T(8,128)(2,1)S(1)} %copy-done.1, bf16[384,256]{1,0:T(8,128)(2,1)S(1)} %get-tuple-element.21.refs_0_, bf16[384,256]{1,0:T(8,128)(2,1)S(1)} %collective-permute-done.1.refs_1_, ...), custom_call_target="tpu_custom_call" | custom-call | flops 1000 | bytes 1000 | tf_op jit(solution)/shard_map/pallas_call | solution.py:296
  32.3 1.2 %shard_map.102.refs_1_ = f32[22,128,128]{2,1,0:T(8,128)S(1)} custom-call(s32[4]{0:T(128)S(1)} %copy-done.5, s32[11]{0:T(128)S(1)} %copy-done.6, bf16[512,256]{1,0:T(8,128)(2,1)S(1)} %copy-done.1, bf16[384,256]{1,0:T(8,128)(2,1)S(1)} %get-tuple-element.21.refs_0_, bf16[384,256]{1,0:T(8,128)(2,1)S(1)} %collective-permute-done.1.refs_1_, ...), custom_call_target="tpu_custom_call" | custom-call | flops 1000 | bytes 1000 | tf_op jit(solution)/shard_map/pallas_call | solution.py:296
  33.5 0.0 collective-permute-done.11
  33.5 0.0 collective-permute-done.10
  33.5 0.1 collective-permute-done.9
  33.7 0.0 copy-start.4
  33.7 3.7 %collective-permute-start.13 = (bf16[64,128]{1,0:T(8,128)(2,1)S(1)}, bf16[64,128]{1,0:T(8,128)(2,1)S(1)}, u32[]{:S(2)}, u32[]{:S(2)}) collective-permute-start(bf16[64,128]{1,0:T(8,128)(2,1)S(1)} %add_add_fusion.1), channel_id=1, source_target_pairs={{0,6},{1,7},{2,4},{3,5},{4,2},{5,3},{6,0},{7,1},{8,14},{9,15},{10,... | collective-permute-start | bytes 49160 | tf_op jit(solution)/shard_map/ppermute | solution.py:544
  37.4 0.0 collective-permute-start.12
  37.4 0.8 %collective-permute-start.14 = (bf16[64,128]{1,0:T(8,128)(2,1)S(1)}, bf16[64,128]{1,0:T(8,128)(2,1)S(1)}, u32[]{:S(2)}, u32[]{:S(2)}) collective-permute-start(bf16[64,128]{1,0:T(8,128)(2,1)S(1)} %add_add_fusion.1), channel_id=1, source_target_pairs={{0,2},{1,3},{2,0},{3,1},{4,6},{5,7},{6,4},{7,5},{8,10},{9,11},{10,... | collective-permute-start | bytes 49160 | tf_op jit(solution)/shard_map/ppermute | solution.py:544
  38.1 1.6 %shard_map.104.refs_0_ = f32[22,128,256]{2,1,0:T(8,128)S(1)} custom-call(s32[4]{0:T(128)S(1)} %copy-done.5, s32[11]{0:T(128)S(1)} %copy-done.6, bf16[512,256]{1,0:T(8,128)(2,1)S(1)} %copy-done.1, bf16[384,256]{1,0:T(8,128)(2,1)S(1)} %copy-done.3, bf16[384,256]{1,0:T(8,128)(2,1)S(1)} %collective-permute-done.6.refs_1_, ...), custom_call_target="tpu_custom_call" | custom-call | flops 1000 | bytes 1000 | tf_op jit(solution)/shard_map/pallas_call | solution.py:296
  39.8 0.0 collective-permute-done.13
  39.8 2.2 %collective-permute-done.12 = bf16[64,128]{1,0:T(8,128)(2,1)S(1)} collective-permute-done((bf16[64,128]{1,0:T(8,128)(2,1)S(1)}, bf16[64,128]{1,0:T(8,128)(2,1)S(1)}, u32[]{:S(2)}, u32[]{:S(2)}) %collective-permute-start.12) | collective-permute-done | bytes 16416 | tf_op jit(solution)/shard_map/ppermute | solution.py:544
  42.0 0.0 collective-permute-done.14
  42.0 0.1 collective-permute-start.15
  42.1 1.2 %collective-permute-done.15.other_ref = f32[64,128]{1,0:T(8,128)S(1)} collective-permute-done((f32[64,128]{1,0:T(8,128)S(1)}, f32[64,128]{1,0:T(8,128)S(1)}, u32[]{:S(2)}, u32[]{:S(2)}) %collective-permute-start.15) | collective-permute-done | bytes 32800 | tf_op jit(solution)/shard_map/ppermute | solution.py:544
  43.3 0.0 copy-done.4
  43.3 4.8 %shard_map.105 = (bf16[2,11,128,512]{3,2,1,0:T(8,128)(2,1)}, f32[11,11,2,16]{3,2,1,0:T(2,128)}) custom-call(f32[64,128]{1,0:T(8,128)S(1)} %add_add_fusion.half_ref, f32[64,128]{1,0:T(8,128)S(1)} %collective-permute-done.15.other_ref, bf16[2,128,256]{2,1,0:T(8,128)(2,1)S(1)} %copy-done.4, f32[22,128,256]{2,1,0:T(8,128)S(1)} %shard_map.104.refs_0_, ...), custom_call_target="tpu_custom_call" | custom-call | tf_op jit(solution)/shard_map/pallas_call | solution.py:517
  (5 shorter events, 0.0 us)
Async XLA Ops:
  2.8 8.2 %copy-start.7 = (s32[1,4]{1,0:T(1,128)S(1)}, s32[1,4]{1,0:T(1,128)}, u32[]{:S(2)}) copy-start(s32[1,4]{1,0:T(1,128)} %owner_hbm.5) | copy-start | bytes 52
  2.8 14.3 %copy-start.8 = (f32[512]{0:T(512)S(1)}, f32[512]{0:T(512)}, u32[]{:S(2)}) copy-start(f32[512]{0:T(512)} %param.9) | copy-start | bytes 6148
  2.9 14.3 %copy-start.1 = (bf16[512,256]{1,0:T(8,128)(2,1)S(1)}, bf16[512,256]{1,0:T(8,128)(2,1)}, u32[]{:S(2)}) copy-start(bf16[512,256]{1,0:T(8,128)(2,1)} %constant.6.clone.f_ref) | copy-start | bytes 786436
  2.9 14.3 %copy-start.2 = (bf16[2816,128]{1,0:T(8,128)(2,1)S(1)}, bf16[2816,128]{1,0:T(8,128)(2,1)}, u32[]{:S(2)}) copy-start(bf16[2816,128]{1,0:T(8,128)(2,1)} %constant.7.clone.pick_ref) | copy-start | bytes 2162692
  2.9 14.3 %copy-start.5 = (s32[4]{0:T(128)S(1)}, s32[4]{0:T(128)}, u32[]{:S(2)}) copy-start(s32[4]{0:T(128)} %order_ref.11) | copy-start | bytes 52
  2.9 14.3 %copy-start.6 = (s32[11]{0:T(128)S(1)}, s32[11]{0:T(128)}, u32[]{:S(2)}) copy-start(s32[11]{0:T(128)} %offsets_ref.11) | copy-start | bytes 136
  2.9 8.1 %collective-permute-start = (bf16[384,256]{1,0:T(8,128)(2,1)}, bf16[384,256]{1,0:T(8,128)(2,1)S(1)}, u32[]{:S(2)}, u32[]{:S(2)}) collective-permute-start(bf16[384,256]{1,0:T(8,128)(2,1)} %shard_map.95.refs_0_), channel_id=1, source_target_pairs={{0,16},{8,24},{16,0},{24,8},{1,17},{9,25},{17,1},{25,9},{2,18},{10... | collective-permute-start | bytes 589832 | tf_op jit(solution)/shard_map/ppermute | solution.py:544
  8.6 7.7 %collective-permute-start.6 = (bf16[384,256]{1,0:T(8,128)(2,1)}, bf16[384,256]{1,0:T(8,128)(2,1)S(1)}, u32[]{:S(2)}, u32[]{:S(2)}) collective-permute-start(bf16[384,256]{1,0:T(8,128)(2,1)} %get-tuple-element.27), channel_id=1, source_target_pairs={{0,8},{8,0},{16,24},{24,16},{1,9},{9,1},{17,25},{25,17},{2,10},{10... | collective-permute-start | bytes 589832 | tf_op jit(solution)/shard_map/ppermute | solution.py:544
  8.7 8.4 %collective-permute-start.7 = (bf16[384,256]{1,0:T(8,128)(2,1)}, bf16[384,256]{1,0:T(8,128)(2,1)S(1)}, u32[]{:S(2)}, u32[]{:S(2)}) collective-permute-start(bf16[384,256]{1,0:T(8,128)(2,1)} %get-tuple-element.28), channel_id=1, source_target_pairs={{0,24},{8,16},{16,8},{24,0},{1,25},{9,17},{17,9},{25,1},{2,26},{10... | collective-permute-start | bytes 589832 | tf_op jit(solution)/shard_map/ppermute | solution.py:544
  8.9 11.0 %collective-permute-start.4 = (bf16[384,128]{1,0:T(8,128)(2,1)}, bf16[384,128]{1,0:T(8,128)(2,1)S(1)}, u32[]{:S(2)}, u32[]{:S(2)}) collective-permute-start(bf16[384,128]{1,0:T(8,128)(2,1)} %get-tuple-element.25), channel_id=1, source_target_pairs={{0,16},{8,24},{16,0},{24,8},{1,17},{9,25},{17,1},{25,9},{2,18},{10... | collective-permute-start | bytes 294920 | tf_op jit(solution)/shard_map/ppermute | solution.py:544
  10.8 9.1 %collective-permute-start.5 = (bf16[384,128]{1,0:T(8,128)(2,1)}, bf16[384,128]{1,0:T(8,128)(2,1)S(1)}, u32[]{:S(2)}, u32[]{:S(2)}) collective-permute-start(bf16[384,128]{1,0:T(8,128)(2,1)} %get-tuple-element.26), channel_id=1, source_target_pairs={{0,24},{8,16},{16,8},{24,0},{1,25},{9,17},{17,9},{25,1},{2,26},{10... | collective-permute-start | bytes 294920 | tf_op jit(solution)/shard_map/ppermute | solution.py:544
  11.0 1.4 %copy-start = (bf16[384,4,512]{2,1,0:T(4,128)(2,1)S(1)}, bf16[384,4,512]{2,1,0:T(4,128)(2,1)}, u32[]{:S(2)}) copy-start(bf16[384,4,512]{2,1,0:T(4,128)(2,1)} %x_hbm.5) | copy-start | bytes 4718596
  12.5 0.9 %copy-start.3 = (bf16[384,256]{1,0:T(8,128)(2,1)S(1)}, bf16[384,256]{1,0:T(8,128)(2,1)}, u32[]{:S(2)}) copy-start(bf16[384,256]{1,0:T(8,128)(2,1)} %get-tuple-element.20.refs_1_.refs_0_) | copy-start | bytes 589828
  14.7 7.4 %collective-permute-start.2 = (bf16[384,128]{1,0:T(8,128)(2,1)S(1)}, bf16[384,128]{1,0:T(8,128)(2,1)S(1)}, u32[]{:S(2)}, u32[]{:S(2)}) collective-permute-start(bf16[384,128]{1,0:T(8,128)(2,1)S(1)} %get-tuple-element.23), channel_id=1, source_target_pairs={{0,24},{8,16},{16,8},{24,0},{1,25},{9,17},{17,9},{25,1},{2,26},{10... | collective-permute-start | bytes 294920 | tf_op jit(solution)/shard_map/ppermute | solution.py:544
  16.3 8.3 %collective-permute-start.3 = (bf16[384,128]{1,0:T(8,128)(2,1)S(1)}, bf16[384,128]{1,0:T(8,128)(2,1)S(1)}, u32[]{:S(2)}, u32[]{:S(2)}) collective-permute-start(bf16[384,128]{1,0:T(8,128)(2,1)S(1)} %get-tuple-element.24), channel_id=1, source_target_pairs={{0,16},{8,24},{16,0},{24,8},{1,17},{9,25},{17,1},{25,9},{2,18},{10... | collective-permute-start | bytes 294920 | tf_op jit(solution)/shard_map/ppermute | solution.py:544
  17.0 2.9 %collective-permute-start.1 = (bf16[384,256]{1,0:T(8,128)(2,1)S(1)}, bf16[384,256]{1,0:T(8,128)(2,1)S(1)}, u32[]{:S(2)}, u32[]{:S(2)}) collective-permute-start(bf16[384,256]{1,0:T(8,128)(2,1)S(1)} %get-tuple-element.22), channel_id=1, source_target_pairs={{0,8},{8,0},{16,24},{24,16},{1,9},{9,1},{17,25},{25,17},{2,10},{10... | collective-permute-start | bytes 589832 | tf_op jit(solution)/shard_map/ppermute | solution.py:544
  26.3 1.2 %collective-permute-start.8 = (bf16[64,128]{1,0:T(8,128)(2,1)S(1)}, bf16[64,128]{1,0:T(8,128)(2,1)S(1)}, u32[]{:S(2)}, u32[]{:S(2)}) collective-permute-start(bf16[64,128]{1,0:T(8,128)(2,1)S(1)} %get-tuple-element.30), channel_id=1, source_target_pairs={{0,8},{1,9},{2,10},{3,11},{4,12},{5,13},{6,14},{7,15},{8,0},{9,1},... | collective-permute-start | bytes 49160 | tf_op jit(solution)/shard_map/ppermute | solution.py:544
  27.6 6.0 %collective-permute-start.11 = (bf16[64,128]{1,0:T(8,128)(2,1)S(1)}, bf16[64,128]{1,0:T(8,128)(2,1)S(1)}, u32[]{:S(2)}, u32[]{:S(2)}) collective-permute-start(bf16[64,128]{1,0:T(8,128)(2,1)S(1)} %add_convert_fusion), channel_id=1, source_target_pairs={{0,17},{1,16},{2,19},{3,18},{4,21},{5,20},{6,23},{7,22},{8,25},{9,... | collective-permute-start | bytes 49160 | tf_op jit(solution)/shard_map/ppermute | solution.py:544
  29.4 4.1 %collective-permute-start.10 = (bf16[64,128]{1,0:T(8,128)(2,1)S(1)}, bf16[64,128]{1,0:T(8,128)(2,1)S(1)}, u32[]{:S(2)}, u32[]{:S(2)}) collective-permute-start(bf16[64,128]{1,0:T(8,128)(2,1)S(1)} %add_convert_fusion), channel_id=1, source_target_pairs={{0,1},{1,0},{2,3},{3,2},{4,5},{5,4},{6,7},{7,6},{8,9},{9,8},{10,11... | collective-permute-start | bytes 49160 | tf_op jit(solution)/shard_map/ppermute | solution.py:544
  29.9 3.7 %collective-permute-start.9 = (bf16[64,128]{1,0:T(8,128)(2,1)S(1)}, bf16[64,128]{1,0:T(8,128)(2,1)S(1)}, u32[]{:S(2)}, u32[]{:S(2)}) collective-permute-start(bf16[64,128]{1,0:T(8,128)(2,1)S(1)} %add_convert_fusion), channel_id=1, source_target_pairs={{0,16},{1,17},{2,18},{3,19},{4,20},{5,21},{6,22},{7,23},{8,24},{9,... | collective-permute-start | bytes 49160 | tf_op jit(solution)/shard_map/ppermute | solution.py:544
  33.7 9.6 %copy-start.4 = (bf16[2,128,256]{2,1,0:T(8,128)(2,1)S(1)}, bf16[2,128,256]{2,1,0:T(8,128)(2,1)}, u32[]{:S(2)}) copy-start(bf16[2,128,256]{2,1,0:T(8,128)(2,1)} %constant.8.clone.spread_ref) | copy-start | bytes 393220
  33.7 6.1 %collective-permute-start.13 = (bf16[64,128]{1,0:T(8,128)(2,1)S(1)}, bf16[64,128]{1,0:T(8,128)(2,1)S(1)}, u32[]{:S(2)}, u32[]{:S(2)}) collective-permute-start(bf16[64,128]{1,0:T(8,128)(2,1)S(1)} %add_add_fusion.1), channel_id=1, source_target_pairs={{0,6},{1,7},{2,4},{3,5},{4,2},{5,3},{6,0},{7,1},{8,14},{9,15},{10,... | collective-permute-start | bytes 49160 | tf_op jit(solution)/shard_map/ppermute | solution.py:544
  37.4 4.6 %collective-permute-start.12 = (bf16[64,128]{1,0:T(8,128)(2,1)S(1)}, bf16[64,128]{1,0:T(8,128)(2,1)S(1)}, u32[]{:S(2)}, u32[]{:S(2)}) collective-permute-start(bf16[64,128]{1,0:T(8,128)(2,1)S(1)} %add_add_fusion.1), channel_id=1, source_target_pairs={{0,4},{1,5},{2,6},{3,7},{4,0},{5,1},{6,2},{7,3},{8,12},{9,13},{10,... | collective-permute-start | bytes 49160 | tf_op jit(solution)/shard_map/ppermute | solution.py:544
  37.4 4.6 %collective-permute-start.14 = (bf16[64,128]{1,0:T(8,128)(2,1)S(1)}, bf16[64,128]{1,0:T(8,128)(2,1)S(1)}, u32[]{:S(2)}, u32[]{:S(2)}) collective-permute-start(bf16[64,128]{1,0:T(8,128)(2,1)S(1)} %add_add_fusion.1), channel_id=1, source_target_pairs={{0,2},{1,3},{2,0},{3,1},{4,6},{5,7},{6,4},{7,5},{8,10},{9,11},{10,... | collective-permute-start | bytes 49160 | tf_op jit(solution)/shard_map/ppermute | solution.py:544
  42.0 1.3 %collective-permute-start.15 = (f32[64,128]{1,0:T(8,128)S(1)}, f32[64,128]{1,0:T(8,128)S(1)}, u32[]{:S(2)}, u32[]{:S(2)}) collective-permute-start(f32[64,128]{1,0:T(8,128)S(1)} %add_add_fusion.half_ref), channel_id=1, source_target_pairs={{0,8},{1,9},{2,10},{3,11},{4,12},{5,13},{6,14},{7,15},{8,0},{9,1},... | collective-permute-start | bytes 98312 | tf_op jit(solution)/shard_map/ppermute | solution.py:544

commit v18 on v16

--- a/solution.py
+++ b/solution.py
@@ -597,7 +597,7 @@
         masks = bits[at : at + 2]
         if len(masks) == 2:
             masks.append(masks[0] ^ masks[1])
-            masks = masks[1:] + masks[:1] if at > 1 else masks
+            masks = masks[1:] + masks[:1] if at > 1 else masks[::-1]
         half = half.astype(BF16)
         terms = [half] + [swap(half, axes, mask, size) for mask in masks]
         terms = [t.astype(F32) for t in terms]

time: 48 us -> 48.9 us (1.019)
  waiting for transfers between devices: 5.99 us -> 6.92 us
    ppermute x16, waiting for transfers between devices: 5.99 us -> 6.92 us  [swap(): return lax.ppermute(x, axes, [(i, i ^ mask) for i in range(size)])]
where the time goes in v18:
time: 48.9 us; the launch traced here: 48.7 us
  Pallas kernels  22.3 us (46%)
  starting transfers between devices  16.2 us (33%)
  waiting for transfers between devices  6.92 us (14%)
  local copies, waits for them, and re-layouts  2.38 us (5%)
  between operations  0.87 us (2%)
    ppermute x16, starting transfers between devices, swap(): return lax.ppermute(x, axes, [(i, i ^ mask) for i in range(size)])  16.2 us
    ppermute x16, waiting for transfers between devices, swap(): return lax.ppermute(x, axes, [(i, i ^ mask) for i in range(size)])  6.92 us
    pallas_call x3, Pallas kernels, gram_part(): pl.pallas_call(functools.partial(gram_kernel, lanes, base, scale, last),...  6.61 us
    pallas_call x3, Pallas kernels, pack(): pl.pallas_call(functools.partial(pack_kernel, jobs, parts, len(after)), o...  6.15 us
    pallas_call x1, Pallas kernels, mode_fields(): pl.pallas_call(functools.partial(mode_kernel, len(spectra), share), out_s...  4.78 us
    pallas_call x3, Pallas kernels, spectrum(): pl.pallas_call(functools.partial(spectrum_kernel, lanes, base), out_shape...  4.06 us
    unnamed x18, local copies, waits for them, and re-layouts  2.38 us
  transfers between devices with their start and end apart: 16, of which 7 were waited for; matrix products, arithmetic and copies ran while one was open for 0% of the time, Pallas kernels for 28%

profile of v18, /device:TPU:0, one launch (start us, length us, event | category | flops | bytes accessed | tf_op | source)
XLA Modules:
  0.0 48.7 jit_solution(13127890921434416043)
XLA Ops:
  0.6 2.2 %shard_map.95.refs_0_ = bf16[384,256]{1,0:T(8,128)(2,1)} custom-call(s32[1,4]{1,0:T(1,128)} %owner_hbm.5, bf16[384,4,512]{2,1,0:T(4,128)(2,1)} %x_hbm.5), custom_call_target="tpu_custom_call" | custom-call | flops 1000 | bytes 1000 | tf_op jit(solution)/shard_map/pallas_call | solution.py:150
  2.8 0.0 copy-start.7
  2.8 0.0 copy-start.8
  2.9 0.0 copy-start.1
  2.9 0.0 copy-start.2
  2.9 0.0 copy-start.5
  2.9 0.0 copy-start.6
  2.9 3.0 %collective-permute-start = (bf16[384,256]{1,0:T(8,128)(2,1)}, bf16[384,256]{1,0:T(8,128)(2,1)S(1)}, u32[]{:S(2)}, u32[]{:S(2)}) collective-permute-start(bf16[384,256]{1,0:T(8,128)(2,1)} %shard_map.95.refs_0_), channel_id=1, source_target_pairs={{0,16},{8,24},{16,0},{24,8},{1,17},{9,25},{17,1},{25,9},{2,18},{10... | collective-permute-start | bytes 589832 | tf_op jit(solution)/shard_map/ppermute | solution.py:543
  5.9 2.7 %shard_map.96 = (bf16[384,256]{1,0:T(8,128)(2,1)}, bf16[384,256]{1,0:T(8,128)(2,1)}, bf16[384,256]{1,0:T(8,128)(2,1)}, bf16[384,128]{1,0:T(8,128)(2,1)}, bf16[384,128]{1,0:T(8,128)(2,1)}) custom-call(s32[1,4]{1,0:T(1,128)} %owner_hbm.5, bf16[384,4,512]{2,1,0:T(4,128)(2,1)} %x_hbm.5, bf16[384,256]{1,0:T(8,128)(2,1)} %shard_map.95.refs_0_), custom_call_target="tpu_custom_call" | custom-call | flops 1000 | bytes 1000 | tf_op jit(solution)/shard_map/pallas_call | solution.py:150
  8.6 0.1 collective-permute-start.6
  8.7 0.2 collective-permute-start.7
  8.9 1.9 %collective-permute-start.4 = (bf16[384,128]{1,0:T(8,128)(2,1)}, bf16[384,128]{1,0:T(8,128)(2,1)S(1)}, u32[]{:S(2)}, u32[]{:S(2)}) collective-permute-start(bf16[384,128]{1,0:T(8,128)(2,1)} %get-tuple-element.25), channel_id=1, source_target_pairs={{0,16},{8,24},{16,0},{24,8},{1,17},{9,25},{17,1},{25,9},{2,18},{10... | collective-permute-start | bytes 294920 | tf_op jit(solution)/shard_map/ppermute | solution.py:543
  10.8 0.0 collective-permute-start.5
  10.8 0.2 collective-permute-done.refs_0_.refs_2_
  11.0 0.0 copy-done.7
  11.0 0.0 copy-start
  11.0 1.4 %copy-done = bf16[384,4,512]{2,1,0:T(4,128)(2,1)S(1)} copy-done((bf16[384,4,512]{2,1,0:T(4,128)(2,1)S(1)}, bf16[384,4,512]{2,1,0:T(4,128)(2,1)}, u32[]{:S(2)}) %copy-start) | copy-done | bytes 1572888
  12.5 0.0 copy-start.3
  12.5 0.9 %copy-done.3 = bf16[384,256]{1,0:T(8,128)(2,1)S(1)} copy-done((bf16[384,256]{1,0:T(8,128)(2,1)S(1)}, bf16[384,256]{1,0:T(8,128)(2,1)}, u32[]{:S(2)}) %copy-start.3) | copy-done | bytes 196632
  13.4 1.3 %shard_map.97 = (bf16[384,256]{1,0:T(8,128)(2,1)S(1)}, bf16[384,256]{1,0:T(8,128)(2,1)S(1)}, bf16[384,128]{1,0:T(8,128)(2,1)S(1)}, bf16[384,128]{1,0:T(8,128)(2,1)S(1)}) custom-call(s32[1,4]{1,0:T(1,128)S(1)} %copy-done.7, bf16[384,4,512]{2,1,0:T(4,128)(2,1)S(1)} %copy-done, bf16[384,256]{1,0:T(8,128)(2,1)S(1)} %collective-permute-done.refs_0_.refs_2_, ...), custom_call_target="tpu_custom_call" | custom-call | flops 1000 | bytes 1000 | tf_op jit(solution)/shard_map/pallas_call | solution.py:150
  14.7 2.3 %collective-permute-start.2 = (bf16[384,128]{1,0:T(8,128)(2,1)S(1)}, bf16[384,128]{1,0:T(8,128)(2,1)S(1)}, u32[]{:S(2)}, u32[]{:S(2)}) collective-permute-start(bf16[384,128]{1,0:T(8,128)(2,1)S(1)} %get-tuple-element.23), channel_id=1, source_target_pairs={{0,16},{8,24},{16,0},{24,8},{1,17},{9,25},{17,1},{25,9},{2,18},{10... | collective-permute-start | bytes 294920 | tf_op jit(solution)/shard_map/ppermute | solution.py:543
  17.0 0.0 collective-permute-done.6.refs_1_
  17.0 0.0 collective-permute-start.3
  17.0 0.0 collective-permute-done.7.refs_3_
  17.0 0.2 collective-permute-start.1
  17.2 0.0 copy-done.8
  17.2 0.0 copy-done.1
  17.2 0.0 copy-done.2
  17.2 0.0 copy-done.5
  17.2 0.0 copy-done.6
  17.2 2.7 %shard_map.98.refs_4_ = f32[128,128]{1,0:T(8,128)S(1)} custom-call(s32[4]{0:T(128)S(1)} %copy-done.5, s32[11]{0:T(128)S(1)} %copy-done.6, f32[1,256]{1,0:T(1,128)S(1)} %slice.14.w_ref, bf16[512,256]{1,0:T(8,128)(2,1)S(1)} %copy-done.1, bf16[2816,128]{1,0:T(8,128)(2,1)S(1)} %copy-done.2, bf16[384,256]{1,0:T(8,128)(2,1)S(1)} %copy-done.3, ...), custom_call_target="tpu_custom_call" | custom-call | flops 1000 | bytes 1000 | tf_op jit(solution)/shard_map/pallas_call | solution.py:256
  19.9 0.0 collective-permute-done.4.refs_2_
  19.9 0.0 collective-permute-done.5.refs_3_
  19.9 0.0 collective-permute-done.1.refs_1_
  19.9 2.2 %shard_map.99.refs_4_.before_ref = f32[128,128]{1,0:T(8,128)S(1)} custom-call(s32[4]{0:T(128)S(1)} %copy-done.5, s32[11]{0:T(128)S(1)} %copy-done.6, f32[1,128]{1,0:T(1,128)S(1)} %get-tuple-element.40.w_ref, bf16[512,256]{1,0:T(8,128)(2,1)S(1)} %copy-done.1, bf16[2816,128]{1,0:T(8,128)(2,1)S(1)} %copy-done.2, ...), custom_call_target="tpu_custom_call" | custom-call | flops 1000 | bytes 1000 | tf_op jit(solution)/shard_map/pallas_call | solution.py:256
  22.2 0.9 %collective-permute-done.2.refs_2_ = bf16[384,128]{1,0:T(8,128)(2,1)S(1)} collective-permute-done((bf16[384,128]{1,0:T(8,128)(2,1)S(1)}, bf16[384,128]{1,0:T(8,128)(2,1)S(1)}, u32[]{:S(2)}, u32[]{:S(2)}) %collective-permute-start.2) | collective-permute-done | bytes 98336 | tf_op jit(solution)/shard_map/ppermute | solution.py:543
  23.0 1.0 %collective-permute-done.3.refs_3_ = bf16[384,128]{1,0:T(8,128)(2,1)S(1)} collective-permute-done((bf16[384,128]{1,0:T(8,128)(2,1)S(1)}, bf16[384,128]{1,0:T(8,128)(2,1)S(1)}, u32[]{:S(2)}, u32[]{:S(2)}) %collective-permute-start.3) | collective-permute-done | bytes 98336 | tf_op jit(solution)/shard_map/ppermute | solution.py:543
  24.0 1.7 %shard_map.100 = (bf16[64,128]{1,0:T(8,128)(2,1)S(1)}, f32[22,128,128]{2,1,0:T(8,128)S(1)}) custom-call(s32[4]{0:T(128)S(1)} %copy-done.5, s32[11]{0:T(128)S(1)} %copy-done.6, f32[1,128]{1,0:T(1,128)S(1)} %get-tuple-element.41.w_ref, bf16[512,256]{1,0:T(8,128)(2,1)S(1)} %copy-done.1, bf16[2816,128]{1,0:T(8,128)(2,1)S(1)} %copy-done.2, ...), custom_call_target="tpu_custom_call" | custom-call | flops 1000 | bytes 1000 | tf_op jit(solution)/shard_map/pallas_call | solution.py:256
  25.7 0.5 collective-permute-start.8
  26.2 0.7 %shard_map.101.refs_4_ = bf16[64,128]{1,0:T(8,128)(2,1)S(1)} custom-call(f32[22,128,128]{2,1,0:T(8,128)S(1)} %get-tuple-element.29.s_ref, bf16[2816,128]{1,0:T(8,128)(2,1)S(1)} %copy-done.2, f32[128,128]{1,0:T(8,128)S(1)} %shard_map.99.refs_4_.before_ref), custom_call_target="tpu_custom_call" | custom-call | flops 1000000000 | bytes 3000000 | tf_op jit(solution)/shard_map/pallas_call | solution.py:274
  26.8 0.2 collective-permute-done.8
  27.0 1.0 %collective-permute-start.11 = (bf16[64,128]{1,0:T(8,128)(2,1)S(1)}, bf16[64,128]{1,0:T(8,128)(2,1)S(1)}, u32[]{:S(2)}, u32[]{:S(2)}) collective-permute-start(bf16[64,128]{1,0:T(8,128)(2,1)S(1)} %add_convert_fusion), channel_id=1, source_target_pairs={{0,16},{1,17},{2,18},{3,19},{4,20},{5,21},{6,22},{7,23},{8,24},{9,... | collective-permute-start | bytes 49160 | tf_op jit(solution)/shard_map/ppermute | solution.py:543
  28.0 1.7 %collective-permute-start.10 = (bf16[64,128]{1,0:T(8,128)(2,1)S(1)}, bf16[64,128]{1,0:T(8,128)(2,1)S(1)}, u32[]{:S(2)}, u32[]{:S(2)}) collective-permute-start(bf16[64,128]{1,0:T(8,128)(2,1)S(1)} %add_convert_fusion), channel_id=1, source_target_pairs={{0,1},{1,0},{2,3},{3,2},{4,5},{5,4},{6,7},{7,6},{8,9},{9,8},{10,11... | collective-permute-start | bytes 49160 | tf_op jit(solution)/shard_map/ppermute | solution.py:543
  29.7 0.9 %collective-permute-start.9 = (bf16[64,128]{1,0:T(8,128)(2,1)S(1)}, bf16[64,128]{1,0:T(8,128)(2,1)S(1)}, u32[]{:S(2)}, u32[]{:S(2)}) collective-permute-start(bf16[64,128]{1,0:T(8,128)(2,1)S(1)} %add_convert_fusion), channel_id=1, source_target_pairs={{0,17},{1,16},{2,19},{3,18},{4,21},{5,20},{6,23},{7,22},{8,25},{9,... | collective-permute-start | bytes 49160 | tf_op jit(solution)/shard_map/ppermute | solution.py:543
  30.6 1.2 %shard_map.103.refs_2_ = f32[22,128,128]{2,1,0:T(8,128)S(1)} custom-call(s32[4]{0:T(128)S(1)} %copy-done.5, s32[11]{0:T(128)S(1)} %copy-done.6, bf16[512,256]{1,0:T(8,128)(2,1)S(1)} %copy-done.1, bf16[384,256]{1,0:T(8,128)(2,1)S(1)} %get-tuple-element.21.refs_0_, bf16[384,256]{1,0:T(8,128)(2,1)S(1)} %collective-permute-done.1.refs_1_, ...), custom_call_target="tpu_custom_call" | custom-call | flops 1000 | bytes 1000 | tf_op jit(solution)/shard_map/pallas_call | solution.py:295
  31.8 1.2 %shard_map.102.refs_1_ = f32[22,128,128]{2,1,0:T(8,128)S(1)} custom-call(s32[4]{0:T(128)S(1)} %copy-done.5, s32[11]{0:T(128)S(1)} %copy-done.6, bf16[512,256]{1,0:T(8,128)(2,1)S(1)} %copy-done.1, bf16[384,256]{1,0:T(8,128)(2,1)S(1)} %get-tuple-element.21.refs_0_, bf16[384,256]{1,0:T(8,128)(2,1)S(1)} %collective-permute-done.1.refs_1_, ...), custom_call_target="tpu_custom_call" | custom-call | flops 1000 | bytes 1000 | tf_op jit(solution)/shard_map/pallas_call | solution.py:295
  33.0 0.0 collective-permute-done.11
  33.0 0.0 collective-permute-done.10
  33.1 1.3 %collective-permute-done.9 = bf16[64,128]{1,0:T(8,128)(2,1)S(1)} collective-permute-done((bf16[64,128]{1,0:T(8,128)(2,1)S(1)}, bf16[64,128]{1,0:T(8,128)(2,1)S(1)}, u32[]{:S(2)}, u32[]{:S(2)}) %collective-permute-start.9) | collective-permute-done | bytes 16416 | tf_op jit(solution)/shard_map/ppermute | solution.py:543
  34.3 0.0 copy-start.4
  34.3 3.7 %collective-permute-start.13 = (bf16[64,128]{1,0:T(8,128)(2,1)S(1)}, bf16[64,128]{1,0:T(8,128)(2,1)S(1)}, u32[]{:S(2)}, u32[]{:S(2)}) collective-permute-start(bf16[64,128]{1,0:T(8,128)(2,1)S(1)} %add_add_fusion.1), channel_id=1, source_target_pairs={{0,6},{1,7},{2,4},{3,5},{4,2},{5,3},{6,0},{7,1},{8,14},{9,15},{10,... | collective-permute-start | bytes 49160 | tf_op jit(solution)/shard_map/ppermute | solution.py:543
  38.0 0.0 collective-permute-start.12
  38.0 0.8 %collective-permute-start.14 = (bf16[64,128]{1,0:T(8,128)(2,1)S(1)}, bf16[64,128]{1,0:T(8,128)(2,1)S(1)}, u32[]{:S(2)}, u32[]{:S(2)}) collective-permute-start(bf16[64,128]{1,0:T(8,128)(2,1)S(1)} %add_add_fusion.1), channel_id=1, source_target_pairs={{0,2},{1,3},{2,0},{3,1},{4,6},{5,7},{6,4},{7,5},{8,10},{9,11},{10,... | collective-permute-start | bytes 49160 | tf_op jit(solution)/shard_map/ppermute | solution.py:543
  38.8 1.6 %shard_map.104.refs_0_ = f32[22,128,256]{2,1,0:T(8,128)S(1)} custom-call(s32[4]{0:T(128)S(1)} %copy-done.5, s32[11]{0:T(128)S(1)} %copy-done.6, bf16[512,256]{1,0:T(8,128)(2,1)S(1)} %copy-done.1, bf16[384,256]{1,0:T(8,128)(2,1)S(1)} %copy-done.3, bf16[384,256]{1,0:T(8,128)(2,1)S(1)} %collective-permute-done.6.refs_1_, ...), custom_call_target="tpu_custom_call" | custom-call | flops 1000 | bytes 1000 | tf_op jit(solution)/shard_map/pallas_call | solution.py:295
  40.4 0.0 collective-permute-done.13
  40.4 2.2 %collective-permute-done.12 = bf16[64,128]{1,0:T(8,128)(2,1)S(1)} collective-permute-done((bf16[64,128]{1,0:T(8,128)(2,1)S(1)}, bf16[64,128]{1,0:T(8,128)(2,1)S(1)}, u32[]{:S(2)}, u32[]{:S(2)}) %collective-permute-start.12) | collective-permute-done | bytes 16416 | tf_op jit(solution)/shard_map/ppermute | solution.py:543
  42.6 0.0 collective-permute-done.14
  42.7 0.1 collective-permute-start.15
  42.7 1.2 %collective-permute-done.15.other_ref = f32[64,128]{1,0:T(8,128)S(1)} collective-permute-done((f32[64,128]{1,0:T(8,128)S(1)}, f32[64,128]{1,0:T(8,128)S(1)}, u32[]{:S(2)}, u32[]{:S(2)}) %collective-permute-start.15) | collective-permute-done | bytes 32800 | tf_op jit(solution)/shard_map/ppermute | solution.py:543
  43.9 0.0 copy-done.4
  43.9 4.8 %shard_map.105 = (bf16[2,11,128,512]{3,2,1,0:T(8,128)(2,1)}, f32[11,11,2,16]{3,2,1,0:T(2,128)}) custom-call(f32[64,128]{1,0:T(8,128)S(1)} %add_add_fusion.half_ref, f32[64,128]{1,0:T(8,128)S(1)} %collective-permute-done.15.other_ref, bf16[2,128,256]{2,1,0:T(8,128)(2,1)S(1)} %copy-done.4, f32[22,128,256]{2,1,0:T(8,128)S(1)} %shard_map.104.refs_0_, ...), custom_call_target="tpu_custom_call" | custom-call | tf_op jit(solution)/shard_map/pallas_call | solution.py:516
  (5 shorter events, 0.0 us)
Async XLA Ops:
  2.8 8.2 %copy-start.7 = (s32[1,4]{1,0:T(1,128)S(1)}, s32[1,4]{1,0:T(1,128)}, u32[]{:S(2)}) copy-start(s32[1,4]{1,0:T(1,128)} %owner_hbm.5) | copy-start | bytes 52
  2.8 14.3 %copy-start.8 = (f32[512]{0:T(512)S(1)}, f32[512]{0:T(512)}, u32[]{:S(2)}) copy-start(f32[512]{0:T(512)} %param.9) | copy-start | bytes 6148
  2.9 14.3 %copy-start.1 = (bf16[512,256]{1,0:T(8,128)(2,1)S(1)}, bf16[512,256]{1,0:T(8,128)(2,1)}, u32[]{:S(2)}) copy-start(bf16[512,256]{1,0:T(8,128)(2,1)} %constant.6.clone.f_ref) | copy-start | bytes 786436
  2.9 14.3 %copy-start.2 = (bf16[2816,128]{1,0:T(8,128)(2,1)S(1)}, bf16[2816,128]{1,0:T(8,128)(2,1)}, u32[]{:S(2)}) copy-start(bf16[2816,128]{1,0:T(8,128)(2,1)} %constant.7.clone.pick_ref) | copy-start | bytes 2162692
  2.9 14.3 %copy-start.5 = (s32[4]{0:T(128)S(1)}, s32[4]{0:T(128)}, u32[]{:S(2)}) copy-start(s32[4]{0:T(128)} %order_ref.11) | copy-start | bytes 52
  2.9 14.3 %copy-start.6 = (s32[11]{0:T(128)S(1)}, s32[11]{0:T(128)}, u32[]{:S(2)}) copy-start(s32[11]{0:T(128)} %offsets_ref.11) | copy-start | bytes 136
  2.9 8.1 %collective-permute-start = (bf16[384,256]{1,0:T(8,128)(2,1)}, bf16[384,256]{1,0:T(8,128)(2,1)S(1)}, u32[]{:S(2)}, u32[]{:S(2)}) collective-permute-start(bf16[384,256]{1,0:T(8,128)(2,1)} %shard_map.95.refs_0_), channel_id=1, source_target_pairs={{0,16},{8,24},{16,0},{24,8},{1,17},{9,25},{17,1},{25,9},{2,18},{10... | collective-permute-start | bytes 589832 | tf_op jit(solution)/shard_map/ppermute | solution.py:543
  8.6 8.4 %collective-permute-start.6 = (bf16[384,256]{1,0:T(8,128)(2,1)}, bf16[384,256]{1,0:T(8,128)(2,1)S(1)}, u32[]{:S(2)}, u32[]{:S(2)}) collective-permute-start(bf16[384,256]{1,0:T(8,128)(2,1)} %get-tuple-element.27), channel_id=1, source_target_pairs={{0,8},{8,0},{16,24},{24,16},{1,9},{9,1},{17,25},{25,17},{2,10},{10... | collective-permute-start | bytes 589832 | tf_op jit(solution)/shard_map/ppermute | solution.py:543
  8.7 8.3 %collective-permute-start.7 = (bf16[384,256]{1,0:T(8,128)(2,1)}, bf16[384,256]{1,0:T(8,128)(2,1)S(1)}, u32[]{:S(2)}, u32[]{:S(2)}) collective-permute-start(bf16[384,256]{1,0:T(8,128)(2,1)} %get-tuple-element.28), channel_id=1, source_target_pairs={{0,24},{8,16},{16,8},{24,0},{1,25},{9,17},{17,9},{25,1},{2,26},{10... | collective-permute-start | bytes 589832 | tf_op jit(solution)/shard_map/ppermute | solution.py:543
  8.9 11.0 %collective-permute-start.4 = (bf16[384,128]{1,0:T(8,128)(2,1)}, bf16[384,128]{1,0:T(8,128)(2,1)S(1)}, u32[]{:S(2)}, u32[]{:S(2)}) collective-permute-start(bf16[384,128]{1,0:T(8,128)(2,1)} %get-tuple-element.25), channel_id=1, source_target_pairs={{0,16},{8,24},{16,0},{24,8},{1,17},{9,25},{17,1},{25,9},{2,18},{10... | collective-permute-start | bytes 294920 | tf_op jit(solution)/shard_map/ppermute | solution.py:543
  10.8 9.1 %collective-permute-start.5 = (bf16[384,128]{1,0:T(8,128)(2,1)}, bf16[384,128]{1,0:T(8,128)(2,1)S(1)}, u32[]{:S(2)}, u32[]{:S(2)}) collective-permute-start(bf16[384,128]{1,0:T(8,128)(2,1)} %get-tuple-element.26), channel_id=1, source_target_pairs={{0,24},{8,16},{16,8},{24,0},{1,25},{9,17},{17,9},{25,1},{2,26},{10... | collective-permute-start | bytes 294920 | tf_op jit(solution)/shard_map/ppermute | solution.py:543
  11.0 1.4 %copy-start = (bf16[384,4,512]{2,1,0:T(4,128)(2,1)S(1)}, bf16[384,4,512]{2,1,0:T(4,128)(2,1)}, u32[]{:S(2)}) copy-start(bf16[384,4,512]{2,1,0:T(4,128)(2,1)} %x_hbm.5) | copy-start | bytes 4718596
  12.5 0.9 %copy-start.3 = (bf16[384,256]{1,0:T(8,128)(2,1)S(1)}, bf16[384,256]{1,0:T(8,128)(2,1)}, u32[]{:S(2)}) copy-start(bf16[384,256]{1,0:T(8,128)(2,1)} %get-tuple-element.20.refs_1_.refs_0_) | copy-start | bytes 589828
  14.7 8.4 %collective-permute-start.2 = (bf16[384,128]{1,0:T(8,128)(2,1)S(1)}, bf16[384,128]{1,0:T(8,128)(2,1)S(1)}, u32[]{:S(2)}, u32[]{:S(2)}) collective-permute-start(bf16[384,128]{1,0:T(8,128)(2,1)S(1)} %get-tuple-element.23), channel_id=1, source_target_pairs={{0,16},{8,24},{16,0},{24,8},{1,17},{9,25},{17,1},{25,9},{2,18},{10... | collective-permute-start | bytes 294920 | tf_op jit(solution)/shard_map/ppermute | solution.py:543
  17.0 7.0 %collective-permute-start.3 = (bf16[384,128]{1,0:T(8,128)(2,1)S(1)}, bf16[384,128]{1,0:T(8,128)(2,1)S(1)}, u32[]{:S(2)}, u32[]{:S(2)}) collective-permute-start(bf16[384,128]{1,0:T(8,128)(2,1)S(1)} %get-tuple-element.24), channel_id=1, source_target_pairs={{0,24},{8,16},{16,8},{24,0},{1,25},{9,17},{17,9},{25,1},{2,26},{10... | collective-permute-start | bytes 294920 | tf_op jit(solution)/shard_map/ppermute | solution.py:543
  17.0 3.0 %collective-permute-start.1 = (bf16[384,256]{1,0:T(8,128)(2,1)S(1)}, bf16[384,256]{1,0:T(8,128)(2,1)S(1)}, u32[]{:S(2)}, u32[]{:S(2)}) collective-permute-start(bf16[384,256]{1,0:T(8,128)(2,1)S(1)} %get-tuple-element.22), channel_id=1, source_target_pairs={{0,8},{8,0},{16,24},{24,16},{1,9},{9,1},{17,25},{25,17},{2,10},{10... | collective-permute-start | bytes 589832 | tf_op jit(solution)/shard_map/ppermute | solution.py:543
  25.7 1.3 %collective-permute-start.8 = (bf16[64,128]{1,0:T(8,128)(2,1)S(1)}, bf16[64,128]{1,0:T(8,128)(2,1)S(1)}, u32[]{:S(2)}, u32[]{:S(2)}) collective-permute-start(bf16[64,128]{1,0:T(8,128)(2,1)S(1)} %get-tuple-element.30), channel_id=1, source_target_pairs={{0,8},{1,9},{2,10},{3,11},{4,12},{5,13},{6,14},{7,15},{8,0},{9,1},... | collective-permute-start | bytes 49160 | tf_op jit(solution)/shard_map/ppermute | solution.py:543
  27.0 6.0 %collective-permute-start.11 = (bf16[64,128]{1,0:T(8,128)(2,1)S(1)}, bf16[64,128]{1,0:T(8,128)(2,1)S(1)}, u32[]{:S(2)}, u32[]{:S(2)}) collective-permute-start(bf16[64,128]{1,0:T(8,128)(2,1)S(1)} %add_convert_fusion), channel_id=1, source_target_pairs={{0,16},{1,17},{2,18},{3,19},{4,20},{5,21},{6,22},{7,23},{8,24},{9,... | collective-permute-start | bytes 49160 | tf_op jit(solution)/shard_map/ppermute | solution.py:543
  28.0 5.0 %collective-permute-start.10 = (bf16[64,128]{1,0:T(8,128)(2,1)S(1)}, bf16[64,128]{1,0:T(8,128)(2,1)S(1)}, u32[]{:S(2)}, u32[]{:S(2)}) collective-permute-start(bf16[64,128]{1,0:T(8,128)(2,1)S(1)} %add_convert_fusion), channel_id=1, source_target_pairs={{0,1},{1,0},{2,3},{3,2},{4,5},{5,4},{6,7},{7,6},{8,9},{9,8},{10,11... | collective-permute-start | bytes 49160 | tf_op jit(solution)/shard_map/ppermute | solution.py:543
  29.7 4.6 %collective-permute-start.9 = (bf16[64,128]{1,0:T(8,128)(2,1)S(1)}, bf16[64,128]{1,0:T(8,128)(2,1)S(1)}, u32[]{:S(2)}, u32[]{:S(2)}) collective-permute-start(bf16[64,128]{1,0:T(8,128)(2,1)S(1)} %add_convert_fusion), channel_id=1, source_target_pairs={{0,17},{1,16},{2,19},{3,18},{4,21},{5,20},{6,23},{7,22},{8,25},{9,... | collective-permute-start | bytes 49160 | tf_op jit(solution)/shard_map/ppermute | solution.py:543
  34.3 9.6 %copy-start.4 = (bf16[2,128,256]{2,1,0:T(8,128)(2,1)S(1)}, bf16[2,128,256]{2,1,0:T(8,128)(2,1)}, u32[]{:S(2)}) copy-start(bf16[2,128,256]{2,1,0:T(8,128)(2,1)} %constant.8.clone.spread_ref) | copy-start | bytes 393220
  34.3 6.1 %collective-permute-start.13 = (bf16[64,128]{1,0:T(8,128)(2,1)S(1)}, bf16[64,128]{1,0:T(8,128)(2,1)S(1)}, u32[]{:S(2)}, u32[]{:S(2)}) collective-permute-start(bf16[64,128]{1,0:T(8,128)(2,1)S(1)} %add_add_fusion.1), channel_id=1, source_target_pairs={{0,6},{1,7},{2,4},{3,5},{4,2},{5,3},{6,0},{7,1},{8,14},{9,15},{10,... | collective-permute-start | bytes 49160 | tf_op jit(solution)/shard_map/ppermute | solution.py:543
  38.0 4.6 %collective-permute-start.12 = (bf16[64,128]{1,0:T(8,128)(2,1)S(1)}, bf16[64,128]{1,0:T(8,128)(2,1)S(1)}, u32[]{:S(2)}, u32[]{:S(2)}) collective-permute-start(bf16[64,128]{1,0:T(8,128)(2,1)S(1)} %add_add_fusion.1), channel_id=1, source_target_pairs={{0,4},{1,5},{2,6},{3,7},{4,0},{5,1},{6,2},{7,3},{8,12},{9,13},{10,... | collective-permute-start | bytes 49160 | tf_op jit(solution)/shard_map/ppermute | solution.py:543
  38.0 4.6 %collective-permute-start.14 = (bf16[64,128]{1,0:T(8,128)(2,1)S(1)}, bf16[64,128]{1,0:T(8,128)(2,1)S(1)}, u32[]{:S(2)}, u32[]{:S(2)}) collective-permute-start(bf16[64,128]{1,0:T(8,128)(2,1)S(1)} %add_add_fusion.1), channel_id=1, source_target_pairs={{0,2},{1,3},{2,0},{3,1},{4,6},{5,7},{6,4},{7,5},{8,10},{9,11},{10,... | collective-permute-start | bytes 49160 | tf_op jit(solution)/shard_map/ppermute | solution.py:543
  42.7 1.3 %collective-permute-start.15 = (f32[64,128]{1,0:T(8,128)S(1)}, f32[64,128]{1,0:T(8,128)S(1)}, u32[]{:S(2)}, u32[]{:S(2)}) collective-permute-start(f32[64,128]{1,0:T(8,128)S(1)} %add_add_fusion.half_ref), channel_id=1, source_target_pairs={{0,8},{1,9},{2,10},{3,11},{4,12},{5,13},{6,14},{7,15},{8,0},{9,1},... | collective-permute-start | bytes 98312 | tf_op jit(solution)/shard_map/ppermute | solution.py:543
